TPU v7x, 256 devices: a whole 4x4x8 slice. The times are simulated.
256 devices in a mesh: wide: 64 (over z_hi, y, x, core), narrow: 4 (over z_lo).
Axes of the slice: x: 4, y: 4, z: 8 (z_hi: 2, z_lo: 4; z = z_hi * 4 + z_lo), core: 2. Of those that a mesh axis runs over, the one named last changes fastest.
Arguments:
- latent: bfloat16 [128, 256, 640], P('wide', 'narrow'), may hold values from -16 to 16
- conv_fine: bfloat16 [3, 3, 640, 640], P(None, None, None, 'narrow'), may hold values from -0.078125 to 0.078125
- conv_deep: bfloat16 [3, 3, 640, 1280], P(None, None, None, 'narrow'), may hold values from -0.078125 to 0.078125
- upstream: bfloat16 [64, 128, 1280], P('wide', None, 'narrow'), may hold values from -6 to 6
Outputs:
- output: bfloat16 [64, 128, 1280], P('wide', None, 'narrow')
- grad_latent: bfloat16 [128, 256, 640], P('wide', 'narrow')
- grad_fine: float32 [3, 3, 640, 640], P(None, None, 'wide', 'narrow')
- grad_deep: float32 [3, 3, 640, 1280], P(None, None, 'wide', 'narrow')
All inputs are finite; a program needn't handle non-finite values.
Results may differ from a plain program's by a relative error of at most 0.018.
Values may be sent and summed in bfloat16 or wider, within the bound.
No kernel may reach another device: no remote copies, remote signals or barrier semaphores. Data moves between devices by JAX's collectives and lax.ppermute only.
A program may use at most 128 MiB of HBM per device.

v0:
```python
import jax
import jax.numpy as jnp
from jax import lax
from jax.sharding import PartitionSpec as P


def padded_2(block, sides, width):
    for axis, dim in sides:
        count = lax.axis_size(axis)
        forward = [(i, i + 1) for i in range(count - 1)]
        backward = [(target, source) for source, target in forward]
        low = lax.ppermute(
            lax.slice_in_dim(block, block.shape[dim] - width, None, axis=dim), axis, forward
        )
        high = lax.ppermute(lax.slice_in_dim(block, 0, width, axis=dim), axis, backward)
        block = jnp.concatenate([low, block, high], axis=dim)
    return block


def forward_taps(padded, kernel):
    out_rows = padded.shape[0] - 2
    out_cols = padded.shape[1] - 2
    running = jnp.zeros((out_rows * out_cols, kernel.shape[3]), jnp.float32)
    for row_tap in range(3):
        for col_tap in range(3):
            window = padded[row_tap : row_tap + out_rows, col_tap : col_tap + out_cols].reshape(
                out_rows * out_cols, -1
            )
            running = running + jnp.dot(
                window, kernel[row_tap, col_tap], preferred_element_type=jnp.float32
            )
    return running.reshape(out_rows, out_cols, -1)


def transpose_taps(padded, kernel):
    out_rows = padded.shape[0] - 2
    out_cols = padded.shape[1] - 2
    running = jnp.zeros((out_rows * out_cols, kernel.shape[2]), jnp.float32)
    for row_tap in range(3):
        for col_tap in range(3):
            window = padded[
                2 - row_tap : 2 - row_tap + out_rows, 2 - col_tap : 2 - col_tap + out_cols
            ].reshape(out_rows * out_cols, -1)
            running = running + lax.dot_general(
                window,
                kernel[row_tap, col_tap],
                (((1,), (1,)), ((), ())),
                preferred_element_type=jnp.float32,
            )
    return running.reshape(out_rows, out_cols, -1)


def tap_folder(slab, piece):
    piece_rows = piece.shape[0]
    piece_cols = piece.shape[1]
    flat_in = piece.reshape(piece_rows * piece_cols, -1)
    taps_list = []
    for row_tap in range(3):
        band = lax.dynamic_slice_in_dim(slab, row_tap, piece_rows, 0)
        row_list = []
        for col_tap in range(3):
            window = band[:, col_tap : col_tap + piece_cols].reshape(piece_rows * piece_cols, -1)
            row_list.append(
                lax.dot_general(
                    window, flat_in, (((0,), (0,)), ((), ())), preferred_element_type=jnp.float32
                )
            )
        taps_list.append(jnp.stack(row_list))
    return jnp.stack(taps_list)


def pad_columns(field):
    return jnp.pad(field, ((0, 0), (1, 1), (0, 0)))


def pad_both(field):
    return jnp.pad(field, ((1, 1), (1, 1), (0, 0)))


def pool_pairs(field):
    half_rows = field.shape[0] // 2
    half_cols = field.shape[1] // 2
    return field.reshape(half_rows, 2, half_cols, 2, field.shape[2]).mean(axis=(1, 3))


def spread_pairs(field):
    half_rows, half_cols, depth = field.shape
    grown = jnp.broadcast_to(field[:, None, :, None, :], (half_rows, 2, half_cols, 2, depth))
    return grown.reshape(2 * half_rows, 2 * half_cols, depth) * 0.25


def silu_slope(preact):
    sigma = jax.nn.sigmoid(preact)
    return sigma * (1.0 + preact * (1.0 - sigma))


def on_device(latent, conv_fine, conv_deep, upstream):
    kernels = lax.all_gather(conv_fine, "narrow", axis=3, tiled=True)
    padded = padded_2(latent, (("wide", 0), ("narrow", 1)), 1)
    pooled = pool_pairs(forward_taps(padded, kernels)).astype(jnp.bfloat16)
    deep_input = lax.all_gather(pooled, "narrow", axis=1, tiled=True)
    deep_pad = pad_columns(padded_2(deep_input, (("wide", 0),), 1))
    preact = forward_taps(deep_pad, conv_deep)
    output = jax.nn.silu(preact).astype(jnp.bfloat16)
    grad_pre = (upstream.astype(jnp.float32) * silu_slope(preact)).astype(jnp.bfloat16)
    deep_slab = pad_both(
        lax.all_to_all(deep_input, "wide", split_axis=2, concat_axis=0, tiled=True)
    )
    grad_deep = tap_folder(deep_slab, lax.all_gather(grad_pre, "wide", axis=0, tiled=True))
    grad_pad = pad_columns(padded_2(grad_pre, (("wide", 0),), 1))
    partial_pool = transpose_taps(grad_pad, conv_deep)
    grad_pool = lax.psum_scatter(
        partial_pool.astype(jnp.bfloat16), "narrow", scatter_dimension=1, tiled=True
    )
    grad_act = spread_pairs(grad_pool)
    back_pad = padded_2(grad_act, (("wide", 0), ("narrow", 1)), 1)
    grad_latent = transpose_taps(back_pad, kernels).astype(jnp.bfloat16)
    sliced = lax.all_to_all(latent, "wide", split_axis=2, concat_axis=0, tiled=True)
    fine_slab = pad_both(lax.all_gather(sliced, "narrow", axis=1, tiled=True))
    act_quarter = lax.all_to_all(grad_act, "narrow", split_axis=2, concat_axis=1, tiled=True)
    grad_fine = tap_folder(fine_slab, lax.all_gather(act_quarter, "wide", axis=0, tiled=True))
    return (output, grad_latent, grad_fine, grad_deep)


def solution(mesh):
    return jax.shard_map(
        on_device,
        mesh=mesh,
        in_specs=(
            P("wide", "narrow", None),
            P(None, None, None, "narrow"),
            P(None, None, None, "narrow"),
            P("wide", None, "narrow"),
        ),
        out_specs=(
            P("wide", None, "narrow"),
            P("wide", "narrow", None),
            P(None, None, "wide", "narrow"),
            P(None, None, "wide", "narrow"),
        ),
        check_vma=False,
    )
```

profile of v0, /device:TPU:32, one launch (start us, length us, event | category | flops | bytes accessed | tf_op | source)
XLA Modules:
  0.0 518.0 jit_solution(17601449561791145387)
XLA Ops:
  8.9 1.7 collective-permute-start
  12.0 3.1 collective-permute-done.1
  16.2 4.0 collective-permute-start.2
  20.2 2.0 collective-permute-start.3
  22.2 3.5 collective-permute-done.3
  25.9 123.7 %all-gather.5.cloned.1.call-done = bf16[3,3,640,640]{2,3,1,0:T(8,128)(2,1)} async-done(((bf16[3,3,640,160]{2,3,1,0:T(8,128)(2,1)}), bf16[3,3,640,640]{2,3,1,0:T(8,128)(2,1)}) %all-gather.5.cloned.1.call-update) | async-done | bytes 7372816 | tf_op jit(solution)/shard_map/all_gather | solution.py:98
  163.7 11.7 %all-gather = bf16[128,640]{1,0:T(8,128)(2,1)S(1)} all-gather(bf16[32,640]{1,0:T(8,128)(2,1)S(1)} %multiply_convert_fusion.1), channel_id=2, replica_groups=mesh['wide'=64,'narrow'=4] {'narrow'}, dimensions={0}, use_global_device_ids=true | all-gather | bytes 204800 | tf_op jit(solution)/shard_map/all_gather | solution.py:101
  176.7 3.0 collective-permute-start.4
  193.8 4.2 collective-permute-start.6
  209.8 2.0 fusion.6
  212.6 40.7 %reduce-scatter.2.cloned.1.call-done = bf16[1,32,640]{2,1,0:T(8,128)(2,1)} async-done(((bf16[1,128,640]{2,1,0:T(8,128)(2,1)}), bf16[1,32,640]{2,1,0:T(8,128)(2,1)}) %reduce-scatter.2.cloned.1.call-update) | async-done | bytes 40976 | tf_op jit(solution)/shard_map/reduce_scatter | solution.py:112
  254.8 11.1 %all_to_all.54 = bf16[4,2,10240]{2,1,0:T(2,128)(2,1)S(1)} all-to-all(bf16[4,2,10240]{2,1,0:T(2,128)(2,1)S(1)} %reshape.249), channel_id=1, replica_groups=mesh['wide'=64,'narrow'=4] {'narrow'}, dimensions={0} | all-to-all | bytes 327680 | tf_op jit(solution)/shard_map/all_to_all | solution.py:120
  268.0 26.1 %all_to_all.55 = bf16[64,2,640]{2,1,0:T(2,128)(2,1)S(1)} all-to-all(bf16[64,2,640]{2,1,0:T(2,128)(2,1)S(1)} %reshape.251), channel_id=1, replica_groups=mesh['wide'=64,'narrow'=4] {'wide'}, dimensions={0} | all-to-all | bytes 327680 | tf_op jit(solution)/shard_map/all_to_all | solution.py:118
  295.5 1.6 reduce.3
  297.8 4.8 all-to-all-start.2
  302.7 16.1 %all_gather.17 = bf16[128,256,10]{0,1,2:T(8,128)(2,1)S(1)} all-gather(bf16[128,64,10]{0,1,2:T(8,128)(2,1)S(1)} %copy.29), channel_id=1, replica_groups=mesh['wide'=64,'narrow'=4] {'narrow'}, dimensions={1}, use_global_device_ids=true | all-gather | bytes 819200 | tf_op jit(solution)/shard_map/all_gather | solution.py:119
  321.9 3.0 collective-permute-start.8
  326.2 5.3 %collective-permute-start.10 = (bf16[4,1,640]{2,1,0:T(2,128)(2,1)S(1)}, bf16[4,1,640]{2,1,0:T(2,128)(2,1)S(1)}, u32[]{:S(2)}, u32[]{:S(2)}) collective-permute-start(bf16[4,1,640]{2,1,0:T(2,128)(2,1)S(1)} %get-tuple-element.34), channel_id=1, source_target_pairs={{1,0},{2,1},{3,2},{5,4},{6,5},{7,6},{9,8},{10,9},{11,10},{13,12},{... | collective-permute-start | bytes 15368 | tf_op jit(solution)/shard_map/ppermute | solution.py:15
  331.5 1.9 collective-permute-start.11
  347.6 2.1 fusion.5
  349.7 9.0 %all-gather.9.cloned.1.call-done = bf16[64,128,320]{1,2,0:T(8,128)(2,1)} async-done(((bf16[1,128,320]{1,2,0:T(8,128)(2,1)}), bf16[64,128,320]{1,2,0:T(8,128)(2,1)}) %all-gather.9.cloned.1.call-update) | async-done | bytes 5242896 | tf_op jit(solution)/shard_map/all_gather | solution.py:109
  358.7 4.1 convolution_bitcast_fusion
  375.4 105.4 %all-gather.7.cloned.1.call-done = bf16[128,256,160]{1,2,0:T(8,128)(2,1)} async-done(((bf16[2,256,160]{1,2,0:T(8,128)(2,1)}), bf16[128,256,160]{1,2,0:T(8,128)(2,1)}) %all-gather.7.cloned.1.call-update) | async-done | bytes 10485776 | tf_op jit(solution)/shard_map/all_gather | solution.py:121
  480.8 6.9 %convolution_bitcast_fusion.9 = f32[1,10,160]{2,1,0:T(8,128)S(1)} fusion(bf16[128,256,160]{1,2,0:T(8,128)(2,1)} %all-gather.7.cloned.1.call-done, bf16[128,256,10]{1,2,0:T(8,128)(2,1)S(1)} %copy.30), kind=kOutput, calls=%fused_computation.56 | convolution fusion | flops 104857600 | bytes 11147520 | tf_op jit(solution)/shard_map/dot_general | solution.py:64
  487.8 2.8 convolution_bitcast_fusion.10
  490.6 2.8 convolution_bitcast_fusion.11
  493.5 3.0 convolution_bitcast_fusion.15
  496.5 2.9 convolution_bitcast_fusion.16
  499.3 2.8 convolution_bitcast_fusion.17
  502.1 2.9 convolution_bitcast_fusion.12
  505.0 2.8 convolution_bitcast_fusion.13
  507.9 2.8 convolution_bitcast_fusion.14
  (125 shorter events, 83.5 us)
Async XLA Ops:
  7.2 142.5 %all-gather.5.cloned.1.call-start = ((), (), s32[]{:S(2)}) async-start(), calls=%async_computation.4 | async-start | bytes 9216000 | tf_op jit(solution)/shard_map/all_gather | solution.py:98
  7.9 245.4 %reduce-scatter.2.cloned.1.call-start = ((), (), s32[]{:S(2)}) async-start(), calls=%async_computation.5 | async-start | bytes 204800 | tf_op jit(solution)/shard_map/reduce_scatter | solution.py:112
  8.9 3.1 collective-permute-start
  10.6 4.4 collective-permute-start.1
  16.1 142.6 %copy-start.2 = (bf16[2,64,640]{2,1,0:T(8,128)(2,1)S(1)}, bf16[2,64,640]{2,1,0:T(8,128)(2,1)}, u32[]{:S(2)}) copy-start(bf16[2,64,640]{2,1,0:T(8,128)(2,1)} %param.4) | copy-start | bytes 491524
  16.2 6.0 %collective-permute-start.2 = (bf16[4,1,640]{2,1,0:T(2,128)(2,1)S(1)}, bf16[4,1,640]{2,1,0:T(2,128)(2,1)S(1)}, u32[]{:S(2)}, u32[]{:S(2)}) collective-permute-start(bf16[4,1,640]{2,1,0:T(2,128)(2,1)S(1)} %get-tuple-element.39), channel_id=1, source_target_pairs={{0,1},{1,2},{2,3},{4,5},{5,6},{6,7},{8,9},{9,10},{10,11},{12,13},{... | collective-permute-start | bytes 15368 | tf_op jit(solution)/shard_map/ppermute | solution.py:12
  20.2 5.6 %collective-permute-start.3 = (bf16[4,1,640]{2,1,0:T(2,128)(2,1)S(1)}, bf16[4,1,640]{2,1,0:T(2,128)(2,1)S(1)}, u32[]{:S(2)}, u32[]{:S(2)}) collective-permute-start(bf16[4,1,640]{2,1,0:T(2,128)(2,1)S(1)} %get-tuple-element.40), channel_id=1, source_target_pairs={{1,0},{2,1},{3,2},{5,4},{6,5},{7,6},{9,8},{10,9},{11,10},{13,12},{... | collective-permute-start | bytes 15368 | tf_op jit(solution)/shard_map/ppermute | solution.py:15
  163.3 27.9 %copy-start.4 = (bf16[1,128,320]{1,2,0:T(8,128)(2,1)S(1)}, bf16[1,128,320]{1,2,0:T(8,128)(2,1)}, u32[]{:S(2)}) copy-start(bf16[1,128,320]{1,2,0:T(8,128)(2,1)} %param.7) | copy-start | bytes 245764
  175.4 4.3 collective-permute-start.5
  176.7 4.0 collective-permute-start.4
  192.5 19.3 %copy-start.3 = (bf16[1,128,320]{1,2,0:T(8,128)(2,1)}, bf16[1,128,320]{1,2,0:T(8,128)(2,1)S(1)}, u32[]{:S(2)}) copy-start(bf16[1,128,320]{1,2,0:T(8,128)(2,1)S(1)} %get-tuple-element.48) | copy-start | bytes 245764
  192.5 5.5 %collective-permute-start.7 = (bf16[1,128,320]{1,2,0:T(8,128)(2,1)S(1)}, bf16[1,128,320]{1,2,0:T(8,128)(2,1)S(1)}, u32[]{:S(2)}, u32[]{:S(2)}) collective-permute-start(bf16[1,128,320]{1,2,0:T(8,128)(2,1)S(1)} %get-tuple-element.48), channel_id=1, source_target_pairs={{4,0},{8,4},{12,8},{16,12},{20,16},{24,20},{28,24},{32,28},{36,32}... | collective-permute-start | bytes 245768 | tf_op jit(solution)/shard_map/ppermute | solution.py:15
  193.8 5.1 collective-permute-start.6
  211.8 146.9 %all-gather.9.cloned.1.call-start = ((), (), s32[]{:S(2)}) async-start(), calls=%async_computation.7 | async-start | bytes 5324800 | tf_op jit(solution)/shard_map/all_gather | solution.py:109
  212.6 268.2 %all-gather.7.cloned.1.call-start = ((), (), s32[]{:S(2)}) async-start(), calls=%async_computation.6 | async-start | bytes 10649600 | tf_op jit(solution)/shard_map/all_gather | solution.py:121
  297.8 22.6 %all-to-all-start.2 = ((bf16[64,2,640]{2,1,0:T(2,128)(2,1)}), bf16[64,2,640]{2,1,0:T(2,128)(2,1)S(1)}, u32[]{:S(2)}, u32[]{:S(2)}) async-start(bf16[64,2,640]{2,1,0:T(2,128)(2,1)} %reshape.253), calls=%async_computation.3 | async-start | bytes 327680 | tf_op jit(solution)/shard_map/all_to_all | solution.py:107
  320.6 5.5 %collective-permute-start.9 = (bf16[1,64,640]{2,1,0:T(8,128)(2,1)S(1)}, bf16[1,64,640]{2,1,0:T(8,128)(2,1)S(1)}, u32[]{:S(2)}, u32[]{:S(2)}) collective-permute-start(bf16[1,64,640]{2,1,0:T(8,128)(2,1)S(1)} %mul.54), channel_id=1, source_target_pairs={{4,0},{8,4},{12,8},{16,12},{20,16},{24,20},{28,24},{32,28},{36,32}... | collective-permute-start | bytes 245768 | tf_op jit(solution)/shard_map/ppermute | solution.py:15
  321.9 4.2 collective-permute-start.8
  326.2 10.0 %collective-permute-start.10 = (bf16[4,1,640]{2,1,0:T(2,128)(2,1)S(1)}, bf16[4,1,640]{2,1,0:T(2,128)(2,1)S(1)}, u32[]{:S(2)}, u32[]{:S(2)}) collective-permute-start(bf16[4,1,640]{2,1,0:T(2,128)(2,1)S(1)} %get-tuple-element.34), channel_id=1, source_target_pairs={{1,0},{2,1},{3,2},{5,4},{6,5},{7,6},{9,8},{10,9},{11,10},{13,12},{... | collective-permute-start | bytes 15368 | tf_op jit(solution)/shard_map/ppermute | solution.py:15
  331.5 5.6 %collective-permute-start.11 = (bf16[4,1,640]{2,1,0:T(2,128)(2,1)S(1)}, bf16[4,1,640]{2,1,0:T(2,128)(2,1)S(1)}, u32[]{:S(2)}, u32[]{:S(2)}) collective-permute-start(bf16[4,1,640]{2,1,0:T(2,128)(2,1)S(1)} %get-tuple-element.35), channel_id=1, source_target_pairs={{0,1},{1,2},{2,3},{4,5},{5,6},{6,7},{8,9},{9,10},{10,11},{12,13},{... | collective-permute-start | bytes 15368 | tf_op jit(solution)/shard_map/ppermute | solution.py:12
  358.7 4.1 copy-start.1
  480.8 7.0 %copy-start = (bf16[128,256,160]{1,2,0:T(8,128)(2,1)S(1)}, bf16[128,256,160]{1,2,0:T(8,128)(2,1)}, u32[]{:S(2)}) copy-start(bf16[128,256,160]{1,2,0:T(8,128)(2,1)} %all-gather.7.cloned.1.call-done) | copy-start | bytes 31457284
Sparse Core Ops, SparseCore 0:
  9.8 139.7 all-gather.4
  211.9 41.3 reduce-scatter.1
  258.0 100.6 all-gather.8
  362.7 118.0 all-gather.6
where the time goes:
time: 523 us; the launch traced here: 518 us
  waiting for transfers between devices  291 us (56%)
  matrix products  97.1 us (19%)
  blocking collectives  64.9 us (12%)
  starting transfers between devices  35.3 us (7%)
  between operations  14.5 us (3%)
  local copies, waits for them, and re-layouts  9.97 us (2%)
  other arithmetic  5.29 us (1%)
    all_gather x1, waiting for transfers between devices, on_device(): kernels = lax.all_gather(conv_fine, 'narrow', axis=3, tiled=True)  124 us
    all_gather x1, waiting for transfers between devices, on_device(): lax.all_gather(act_quarter, 'wide', axis=0, tiled=True)  105 us
    dot_general x18, matrix products, tap_folder(): lax.dot_general(window, flat_in, (((0,), (0,)), ((), ())), preferred_elem...  45.7 us
    reduce_scatter x1, waiting for transfers between devices, on_device(): lax.psum_scatter(partial_pool.astype(jnp.bfloat16), 'narrow', scatter_dim...  40.7 us
    dot_general x18, matrix products, transpose_taps(): lax.dot_general(window, kernel[row_tap, col_tap], (((1,), (1,)), ((), ())...  26.4 us
    all_to_all x1, blocking collectives, on_device(): lax.all_to_all(latent, 'wide', split_axis=2, concat_axis=0, tiled=True)  26.1 us
    dot_general x18, matrix products, forward_taps(): jnp.dot(window, kernel[row_tap, col_tap], preferred_element_type=jnp.floa...  25.1 us
    ppermute x6, starting transfers between devices, padded_2(): lax.ppermute(lax.slice_in_dim(block, block.shape[dim] - width, None, axis...  17.9 us
  transfers between devices with their start and end apart: 17, of which 10 were waited for; matrix products, arithmetic and copies ran while one was open for 8% of the time, Pallas kernels for 0%

commit v1 on v0

v1 whole, which is shorter than its diff:
```python
import jax
import jax.numpy as jnp
import numpy as np
from jax import lax
from jax.sharding import PartitionSpec as P

BF = jnp.bfloat16
F32 = jnp.float32
GRAIN = 16


def mm(a, b):
    return jnp.dot(a, b, preferred_element_type=F32)


def mm_t(a, b):
    return lax.dot_general(a, b, (((1,), (1,)), ((), ())), preferred_element_type=F32)


def box_matrix(cols, pieces):
    deep = cols // 2
    part = cols // pieces
    table = np.zeros((3, 3, deep, pieces, 2, part), np.float32)
    for a, rows in enumerate(((0,), (0, 1), (1,))):
        for b in range(3):
            for j in range(deep):
                for p in (2 * j + b - 1, 2 * j + b):
                    if 0 <= p < cols:
                        for r in rows:
                            table[a, b, j, p // part, r, p % part] = 0.25
    return table.reshape(9 * deep, 2 * cols)


def spread_matrix(cols):
    deep = cols // 2
    table = np.zeros((3, cols, deep), np.float32)
    for p in range(cols):
        for j, b in ((p // 2, 1), ((p + 1) // 2, 0), (p // 2 - 1 + p % 2, 2)):
            if 0 <= j < deep:
                table[b, p, j] = 0.25
    return table


def channel_matrix(depth, groups, members):
    grain = depth // (groups * members)
    table = np.zeros((members, depth, groups * GRAIN), np.float32)
    for c in range(depth):
        g, j, k = c // (members * grain), c // grain % members, c % grain
        table[j, c, g * GRAIN + k] = 1.0
    return table


def later(y):
    return jnp.concatenate([jnp.zeros_like(y[:1]), y[:-1]], axis=0)


def sooner(y):
    return jnp.concatenate([y[1:], jnp.zeros_like(y[:1])], axis=0)


def fine_forward(x, box, w):
    deep = box.shape[0] // 9
    u = mm(box, x).astype(BF)
    u = [u[t * deep : (t + 1) * deep] for t in range(9)]
    own = sum(mm(u[t], w[t]) for t in range(9))
    up = sum(mm(u[b], w[6 + b]) for b in range(3))
    down = sum(mm(u[6 + b], w[b]) for b in range(3))
    return own, up, down


def deep_forward(before, mine, after, w, upstream):
    y = [sum(mm(row, w[3 * a + b]) for a, row in enumerate((before, mine, after))) for b in range(3)]
    preact = y[1] + later(y[0]) + sooner(y[2])
    sigma = jax.nn.sigmoid(preact)
    output = (preact * sigma).astype(BF)
    grad = upstream.astype(F32) * (sigma * (1.0 + preact * (1.0 - sigma)))
    return output, grad.astype(BF)


def deep_backward(before, mine, after, w, pieces):
    part = w.shape[1] // pieces
    outs = []
    for k in range(pieces):
        z = [
            sum(mm_t(row, w[3 * a + b, k * part : (k + 1) * part]) for a, row in enumerate((after, mine, before)))
            for b in range(3)
        ]
        outs.append((z[1] + sooner(z[0]) + later(z[2])).astype(BF))
    return jnp.stack(outs)


def fine_backward(before, mine, after, spread, w, pieces):
    h = [[mm(spread[b], row).astype(BF) for b in range(3)] for row in (before, mine, after)]
    part = spread.shape[1] // pieces
    y0 = sum(mm_t(h[(1, 1, 0)[a]][b], w[3 * a + b]) for a in range(3) for b in range(3))
    y1 = sum(mm_t(h[(2, 1, 1)[a]][b], w[3 * a + b]) for a in range(3) for b in range(3))
    y = jnp.stack([y0, y1]).astype(BF).reshape(2, pieces, part, -1)
    return y.transpose(1, 0, 2, 3)


def on_device(latent, conv_fine, conv_deep, upstream):
    wide = lax.axis_size("wide")
    pieces = lax.axis_size("narrow")
    members = 8
    groups = wide // members
    near = [[members * g + j for j in range(members)] for g in range(groups)]
    far = [[members * g + j for g in range(groups)] for j in range(members)]
    onward = lambda s: [(i, i + s) for i in range(wide - s)]
    back = lambda s: [(i + s, i) for i in range(wide - s)]
    rows, part, depth = latent.shape
    cols = part * pieces
    deep = cols // 2
    grain = depth // wide
    w_fine = conv_fine.reshape(9, depth, -1)
    w_deep = conv_deep.reshape(9, depth, -1)
    mine_fine = w_fine.shape[2]
    mine_deep = w_deep.shape[2]
    box = jnp.asarray(box_matrix(cols, pieces), BF)
    spread = jnp.asarray(spread_matrix(cols), BF)
    lanes = jnp.asarray(channel_matrix(depth, groups, members), BF)

    def everyone(v):
        return lax.all_to_all(jnp.broadcast_to(v[None], (pieces,) + v.shape), "narrow", 0, 0)

    def both_sides(v, s=1):
        return lax.ppermute(v, "wide", onward(s)), lax.ppermute(v, "wide", back(s))

    x = everyone(latent).reshape(pieces * rows * part, depth)
    own, up, down = fine_forward(x, box, w_fine)
    up = lax.ppermute(up, "wide", back(1))
    down = lax.ppermute(down, "wide", onward(1))
    pooled = (own + up + down).astype(BF)
    pooled = everyone(pooled).transpose(1, 0, 2).reshape(deep, depth)
    before, after = both_sides(pooled)
    output, grad_pre = deep_forward(before, pooled, after, w_deep, upstream[0])

    before, after = both_sides(grad_pre)
    partial = deep_backward(before, grad_pre, after, w_deep, pieces)
    partial = lax.all_to_all(partial, "narrow", 0, 0)
    grad_pool = jnp.sum(partial.astype(F32), axis=0).astype(BF)
    before, after = both_sides(grad_pool)
    partial = fine_backward(before, grad_pool, after, spread, w_fine, pieces)
    partial = lax.all_to_all(partial, "narrow", 0, 0)
    grad_latent = jnp.sum(partial.astype(F32), axis=0).astype(BF)

    def owners(part):
        part = part.astype(BF).reshape(3, 3, groups, GRAIN, -1)[:, :, :, :grain]
        part = part.transpose(2, 0, 1, 3, 4)
        got = lax.all_to_all(part, "wide", 0, 0, axis_index_groups=far)
        return jnp.sum(got.astype(F32), axis=0)

    slab = jnp.stack([mm(pooled, lanes[j]).astype(BF) for j in range(members)])
    slab = lax.all_to_all(slab, "wide", 0, 0, axis_index_groups=near)
    first = lax.ppermute(slab[-1], "wide", onward(members))
    last = lax.ppermute(slab[0], "wide", back(members))
    slab = jnp.concatenate([first[None], slab, last[None]])
    grads = lax.all_gather(grad_pre, "wide", axis_index_groups=near)
    shifted = jnp.pad(grads, ((0, 0), (1, 1), (0, 0)))
    grad_deep = owners(
        jnp.stack(
            [
                jnp.einsum(
                    "ijc,ijo->co",
                    slab[a : a + members],
                    shifted[:, 2 - b : 2 - b + deep],
                    preferred_element_type=F32,
                )
                for a in range(3)
                for b in range(3)
            ]
        )
    )

    slab = jnp.stack([mm(x, lanes[j]).astype(BF) for j in range(members)])
    slab = lax.all_to_all(slab, "wide", 0, 0, axis_index_groups=near)
    flat = slab.reshape(members, pieces, rows, part, -1)
    first = lax.ppermute(flat[-1, :, 1], "wide", onward(members)).reshape(cols, -1)
    last = lax.ppermute(flat[0, :, 0], "wide", back(members)).reshape(cols, -1)
    u = jnp.einsum("ts,isc->itc", box, slab, preferred_element_type=F32)
    u = u.reshape(members, 3, 3 * deep, -1)
    edge = box.reshape(3, 3 * deep, pieces, rows, part)
    first = mm(edge[0, :, :, 0].reshape(3 * deep, cols), first)
    last = mm(edge[0, :, :, 0].reshape(3 * deep, cols), last)
    low = u[:, 0] + jnp.concatenate([first[None], u[:-1, 2]])
    high = u[:, 2] + jnp.concatenate([u[1:, 0], last[None]])
    m = jnp.stack([low, u[:, 1], high], axis=1).astype(BF).reshape(members, 9, deep, -1)
    grads = lax.all_gather(grad_pool, "wide", axis_index_groups=near)
    grad_fine = owners(jnp.einsum("itjc,ijo->tco", m, grads, preferred_element_type=F32))
    return output[None], grad_latent, grad_fine, grad_deep


def solution(mesh):
    return jax.shard_map(
        on_device,
        mesh=mesh,
        in_specs=(
            P("wide", "narrow", None),
            P(None, None, None, "narrow"),
            P(None, None, None, "narrow"),
            P("wide", None, "narrow"),
        ),
        out_specs=(
            P("wide", None, "narrow"),
            P("wide", "narrow", None),
            P(None, None, "wide", "narrow"),
            P(None, None, "wide", "narrow"),
        ),
        check_vma=False,
    )
```

time: 523 us -> 322 us (0.62)
  waiting for transfers between devices: 291 us -> 40.3 us
  starting transfers between devices: 35.3 us -> 93.7 us
  local copies, waits for them, and re-layouts: 9.97 us -> 26.8 us
  between operations: 14.5 us -> 1.98 us
  blocking collectives: 64.9 us -> 55.9 us
  matrix products: 97.1 us -> 88.9 us
    all_gather x3 -> x0, waiting for transfers between devices: 238 us -> none  [the longest x1 124 us: on_device(): kernels = lax.all_gather(conv_fine, 'narrow', axis=3, tiled=True)]
    all_to_all x1 -> x7, starting transfers between devices: 4.8 us -> 58.6 us  [the longest x2 33.7 us: owners(): got = lax.all_to_all(part, 'wide', 0, 0, axis_index_groups=far)]
    reduce_scatter x1 -> x0, waiting for transfers between devices: 40.7 us -> none  [on_device(): lax.psum_scatter(partial_pool.astype(jnp.bfloat16), 'narrow', scatter_dim...]
    all_to_all x1 -> x7, waiting for transfers between devices: 0.01 us -> 38.6 us  [the longest x2 22.3 us: owners(): got = lax.all_to_all(part, 'wide', 0, 0, axis_index_groups=far)]
    all_to_all x2 -> x1, blocking collectives: 37.2 us -> 21.3 us  [everyone(): lax.all_to_all(jnp.broadcast_to(v[None], (pieces,) + v.shape), 'narrow',...]
    ppermute x12, waiting for transfers between devices: 10.7 us -> 1.69 us  [the longest x1 1.66 us: on_device(): lax.ppermute(flat[-1, :, 1], 'wide', onward(members)).reshape(cols, -1)]
    transpose x0 -> x5, local copies, waits for them, and re-layouts: none -> 8.66 us  [the longest x1 6.09 us: on_device(): u = jnp.einsum('ts,isc->itc', box, slab, preferred_element_type=F32)]
    dot_general x54 -> x108, matrix products: 97.1 us -> 88.9 us  [the longest x51 42.7 us: mm_t(): lax.dot_general(a, b, (((1,), (1,)), ((), ())), preferred_element_type=F32)]
  transfers between devices with their start and end apart: 17 -> 19, of which waited for: 10 -> 5; matrix products, arithmetic and copies ran while one was open for 8% -> 36% of each run, Pallas kernels for 0% -> 0%
where the time goes in v1:
time: 322 us; the launch traced here: 316 us
  starting transfers between devices  93.7 us (29%)
  matrix products  88.9 us (28%)
  blocking collectives  55.9 us (17%)
  waiting for transfers between devices  40.3 us (13%)
  local copies, waits for them, and re-layouts  26.8 us (8%)
  other arithmetic  8.75 us (3%)
    dot_general x51, matrix products, mm_t(): lax.dot_general(a, b, (((1,), (1,)), ((), ())), preferred_element_type=F32)  42.7 us
    all_to_all x2, starting transfers between devices, owners(): got = lax.all_to_all(part, 'wide', 0, 0, axis_index_groups=far)  33.7 us
    dot_general x46, matrix products, mm(): return jnp.dot(a, b, preferred_element_type=F32)  31 us
    all_to_all x2, waiting for transfers between devices, owners(): got = lax.all_to_all(part, 'wide', 0, 0, axis_index_groups=far)  22.3 us
    all_to_all x1, blocking collectives, everyone(): lax.all_to_all(jnp.broadcast_to(v[None], (pieces,) + v.shape), 'narrow',...  21.3 us
    all_gather x1, blocking collectives, on_device(): grads = lax.all_gather(grad_pool, 'wide', axis_index_groups=near)  21 us
    all_gather x1, blocking collectives, on_device(): grads = lax.all_gather(grad_pre, 'wide', axis_index_groups=near)  13.6 us
    all_to_all x2, starting transfers between devices, on_device(): slab = lax.all_to_all(slab, 'wide', 0, 0, axis_index_groups=near)  11.3 us
  transfers between devices with their start and end apart: 19, of which 5 were waited for; matrix products, arithmetic and copies ran while one was open for 36% of the time, Pallas kernels for 0%

profile of v1, /device:TPU:32, one launch (start us, length us, event | category | flops | bytes accessed | tf_op | source)
XLA Modules:
  0.0 316.2 jit_solution(10929325864239676632)
XLA Ops:
  1.7 21.3 %all_to_all.40 = bf16[4,2,64,640]{3,2,1,0:T(8,128)(2,1)S(1)} all-to-all(bf16[4,2,64,640]{3,2,1,0:T(8,128)(2,1)S(1)} %broadcast_in_dim.10), channel_id=1, replica_groups=mesh['wide'=64,'narrow'=4] {'narrow'}, dimensions={0} | all-to-all | bytes 1310720 | tf_op jit(solution)/shard_map/all_to_all | solution.py:123
  28.9 3.2 %collective-permute-start.1 = (f32[128,160]{0,1:T(8,128)S(1)}, f32[128,160]{0,1:T(8,128)S(1)}, u32[]{:S(2)}, u32[]{:S(2)}) collective-permute-start(f32[128,160]{0,1:T(8,128)S(1)} %convolution_add_fusion.15), channel_id=1, source_target_pairs={{0,4},{4,8},{8,12},{12,16},{16,20},{20,24},{24,28},{28,32},{32,36}... | collective-permute-start | bytes 245768 | tf_op jit(solution)/shard_map/ppermute | solution.py:131
  36.4 5.1 %all-to-all-start.1 = ((bf16[4,128,160]{1,2,0:T(8,128)(2,1)}), bf16[4,128,160]{1,2,0:T(8,128)(2,1)S(1)}, u32[]{:S(2)}, u32[]{:S(2)}) async-start(bf16[4,128,160]{1,2,0:T(8,128)(2,1)} %broadcast_in_dim.11), calls=%async_computation.1 | async-start | bytes 327680 | tf_op jit(solution)/shard_map/all_to_all | solution.py:123
  42.5 5.6 %all-to-all-done.1 = bf16[4,128,160]{1,2,0:T(8,128)(2,1)S(1)} async-done(((bf16[4,128,160]{1,2,0:T(8,128)(2,1)}), bf16[4,128,160]{1,2,0:T(8,128)(2,1)S(1)}, u32[]{:S(2)}, u32[]{:S(2)}) %all-to-all-start.1) | async-done | bytes 163872 | tf_op jit(solution)/shard_map/all_to_all | solution.py:123
  50.3 3.0 collective-permute-start.2
  55.9 1.8 fusion.84
  59.4 1.8 fusion.88
  64.7 6.9 %all-to-all-start.6 = ((bf16[8,128,128]{2,1,0:T(8,128)(2,1)}), bf16[8,128,128]{2,1,0:T(8,128)(2,1)S(1)}, u32[]{:S(2)}, u32[]{:S(2)}) async-start(bf16[8,128,128]{2,1,0:T(8,128)(2,1)} %fusion.96), calls=%async_computation.6 | async-start | bytes 524288 | tf_op jit(solution)/shard_map/all_to_all | solution.py:153
  79.7 13.6 %all-gather.1 = bf16[1024,320]{0,1:T(8,128)(2,1)S(1)} all-gather(bf16[128,320]{0,1:T(8,128)(2,1)S(1)} %get-tuple-element.20), channel_id=3, replica_groups={{0,4,8,12,16,20,24,28},{32,36,40,44,48,52,56,60},{64,68,72,76,80,84,88,..., dimensions={0}, use_global_device_ids=true | all-gather | bytes 737280 | tf_op jit(solution)/shard_map/all_gather | solution.py:157
  93.3 2.2 collective-permute-start.5
  106.4 8.2 %collective-permute-start.10 = (bf16[128,128]{1,0:T(8,128)(2,1)}, bf16[128,128]{1,0:T(8,128)(2,1)}, u32[]{:S(2)}, u32[]{:S(2)}) collective-permute-start(bf16[128,128]{1,0:T(8,128)(2,1)} %get-tuple-element.19), channel_id=1, source_target_pairs={{0,32},{4,36},{8,40},{12,44},{16,48},{20,52},{24,56},{28,60},{32,6... | collective-permute-start | bytes 98312 | tf_op jit(solution)/shard_map/ppermute | solution.py:154
  135.2 4.9 %all-to-all-start.2 = ((bf16[4,128,160]{1,2,0:T(8,128)(2,1)}), bf16[4,128,160]{1,2,0:T(8,128)(2,1)}, u32[]{:S(2)}, u32[]{:S(2)}) async-start(bf16[4,128,160]{1,2,0:T(8,128)(2,1)} %pad_maximum_fusion.3), calls=%async_computation.2 | async-start | bytes 327680 | tf_op jit(solution)/shard_map/all_to_all | solution.py:139
  152.1 4.4 %all-to-all-start.4 = ((bf16[8,512,128]{1,2,0:T(8,128)(2,1)}), bf16[8,512,128]{1,2,0:T(8,128)(2,1)}, u32[]{:S(2)}, u32[]{:S(2)}) async-start(bf16[8,512,128]{1,2,0:T(8,128)(2,1)} %fusion.29), calls=%async_computation.4 | async-start | bytes 2097152 | tf_op jit(solution)/shard_map/all_to_all | solution.py:175
  159.6 2.9 collective-permute-start.6
  167.8 21.0 %all-gather = bf16[1024,160]{0,1:T(8,128)(2,1)S(1)} all-gather(bf16[128,160]{0,1:T(8,128)(2,1)} %reduce_sum.42), channel_id=2, replica_groups={{0,4,8,12,16,20,24,28},{32,36,40,44,48,52,56,60},{64,68,72,76,80,84,88,..., dimensions={0}, use_global_device_ids=true | all-gather | bytes 368640 | tf_op jit(solution)/shard_map/all_gather | solution.py:187
  191.0 2.4 convolution_add_fusion.4
  193.5 2.7 fusion.4
  197.5 5.3 %convolution_bitcast_fusion = f32[8,1152,128]{1,2,0:T(8,128)} fusion(bf16[8,512,128]{1,2,0:T(8,128)(2,1)} %all-to-all-done.4, bf16[1152,512,1]{1,0,2:T(8,128)(2,1)} %constant.69), kind=kOutput, calls=%fused_computation | convolution fusion | flops 1207959552 | bytes 6946816 | tf_op jit(solution)/shard_map/ts,isc->itc/dot_general | solution.py:179
  202.9 6.1 %copy.47 = f32[8,1152,128]{2,1,0:T(8,128)} copy(f32[8,1152,128]{1,2,0:T(8,128)} %convolution_bitcast_fusion) | data formatting | bytes 9437184 | tf_op jit(solution)/shard_map/ts,isc->itc/transpose | solution.py:179
  209.0 2.3 copy.48
  213.4 2.1 fusion.174
  216.7 7.5 %collective-permute-start.8 = (bf16[4,64,128]{2,1,0:T(8,128)(2,1)S(1)}, bf16[4,64,128]{2,1,0:T(8,128)(2,1)S(1)}, u32[]{:S(2)}, u32[]{:S(2)}) collective-permute-start(bf16[4,64,128]{2,1,0:T(8,128)(2,1)S(1)} %get-tuple-element.16), channel_id=1, source_target_pairs={{0,32},{4,36},{8,40},{12,44},{16,48},{20,52},{24,56},{28,60},{32,6... | collective-permute-start | bytes 196616 | tf_op jit(solution)/shard_map/ppermute | solution.py:177
  229.7 2.4 reshape.88
  232.1 30.2 %all-to-all-start.5 = ((bf16[8,2,7200]{2,1,0:T(2,128)(2,1)}), bf16[8,2,7200]{2,1,0:T(2,128)(2,1)S(1)}, u32[]{:S(2)}, u32[]{:S(2)}) async-start(bf16[8,2,7200]{2,1,0:T(2,128)(2,1)} %reshape.88), calls=%async_computation.5 | async-start | bytes 466944 | tf_op jit(solution)/shard_map/all_to_all | solution.py:149
  264.9 10.7 %all-to-all-done.5 = bf16[8,2,7200]{2,1,0:T(2,128)(2,1)S(1)} async-done(((bf16[8,2,7200]{2,1,0:T(2,128)(2,1)}), bf16[8,2,7200]{2,1,0:T(2,128)(2,1)S(1)}, u32[]{:S(2)}, u32[]{:S(2)}) %all-to-all-start.5) | async-done | bytes 230432 | tf_op jit(solution)/shard_map/all_to_all | solution.py:149
  275.6 3.5 %all-to-all-start.7 = ((bf16[8,3,3,10,320]{4,2,3,1,0:T(4,128)(2,1)}), bf16[8,3,3,10,320]{4,2,3,1,0:T(4,128)(2,1)S(1)}, u32[]{:S(2)}, u32[]{:S(2)}) async-start(bf16[8,3,3,10,320]{4,2,3,1,0:T(4,128)(2,1)} %copy.59), calls=%async_computation.7 | async-start | bytes 1474560 | tf_op jit(solution)/shard_map/all_to_all | solution.py:149
  279.2 2.1 fusion.10
  281.3 2.2 convolution_add_fusion.6
  285.1 1.9 maximum_bitcast_fusion
  287.0 11.5 %all-to-all-done.7 = bf16[8,3,3,10,320]{4,2,3,1,0:T(4,128)(2,1)S(1)} async-done(((bf16[8,3,3,10,320]{4,2,3,1,0:T(4,128)(2,1)}), bf16[8,3,3,10,320]{4,2,3,1,0:T(4,128)(2,1)S(1)}, u32[]{:S(2)}, u32[]{:S(2)}) %all-to-all-start.7) | async-done | bytes 460832 | tf_op jit(solution)/shard_map/all_to_all | solution.py:149
  298.6 3.5 %all-to-all-start.3 = ((bf16[4,2,64,640]{3,2,1,0:T(8,128)(2,1)}), bf16[4,2,64,640]{3,2,1,0:T(8,128)(2,1)S(1)}, u32[]{:S(2)}, u32[]{:S(2)}) async-start(bf16[4,2,64,640]{3,2,1,0:T(8,128)(2,1)} %maximum_bitcast_fusion), calls=%async_computation.3 | async-start | bytes 1310720 | tf_op jit(solution)/shard_map/all_to_all | solution.py:143
  304.7 10.7 %all-to-all-done.3 = bf16[4,2,64,640]{3,2,1,0:T(8,128)(2,1)S(1)} async-done(((bf16[4,2,64,640]{3,2,1,0:T(8,128)(2,1)}), bf16[4,2,64,640]{3,2,1,0:T(8,128)(2,1)S(1)}, u32[]{:S(2)}, u32[]{:S(2)}) %all-to-all-start.3) | async-done | bytes 655392 | tf_op jit(solution)/shard_map/all_to_all | solution.py:143
  (222 shorter events, 101.0 us)
Async XLA Ops:
  0.6 22.4 %copy-start.33 = (bf16[1152,512]{1,0:T(8,128)(2,1)S(1)}, bf16[1152,512]{1,0:T(8,128)(2,1)}, u32[]{:S(2)}) copy-start(bf16[1152,512]{1,0:T(8,128)(2,1)} %constant.17.clone) | copy-start | bytes 3538948
  27.0 7.9 %collective-permute-start = (f32[128,160]{0,1:T(8,128)S(1)}, f32[128,160]{0,1:T(8,128)S(1)}, u32[]{:S(2)}, u32[]{:S(2)}) collective-permute-start(f32[128,160]{0,1:T(8,128)S(1)} %convolution_add_fusion.17), channel_id=1, source_target_pairs={{4,0},{8,4},{12,8},{16,12},{20,16},{24,20},{28,24},{32,28},{36,32}... | collective-permute-start | bytes 245768 | tf_op jit(solution)/shard_map/ppermute | solution.py:130
  28.9 6.1 %collective-permute-start.1 = (f32[128,160]{0,1:T(8,128)S(1)}, f32[128,160]{0,1:T(8,128)S(1)}, u32[]{:S(2)}, u32[]{:S(2)}) collective-permute-start(f32[128,160]{0,1:T(8,128)S(1)} %convolution_add_fusion.15), channel_id=1, source_target_pairs={{0,4},{4,8},{8,12},{12,16},{16,20},{20,24},{24,28},{28,32},{32,36}... | collective-permute-start | bytes 245768 | tf_op jit(solution)/shard_map/ppermute | solution.py:131
  34.4 13.8 %copy-start.22 = (bf16[640,128]{1,0:T(8,128)(2,1)S(1)}, bf16[640,128]{1,0:T(8,128)(2,1)}, u32[]{:S(2)}) copy-start(bf16[640,128]{1,0:T(8,128)(2,1)} %constant.51) | copy-start | bytes 491524
  36.4 11.7 %all-to-all-start.1 = ((bf16[4,128,160]{1,2,0:T(8,128)(2,1)}), bf16[4,128,160]{1,2,0:T(8,128)(2,1)S(1)}, u32[]{:S(2)}, u32[]{:S(2)}) async-start(bf16[4,128,160]{1,2,0:T(8,128)(2,1)} %broadcast_in_dim.11), calls=%async_computation.1 | async-start | bytes 327680 | tf_op jit(solution)/shard_map/all_to_all | solution.py:123
  49.0 23.9 %collective-permute-start.3 = (bf16[128,640]{0,1:T(8,128)(2,1)S(1)}, bf16[128,640]{0,1:T(8,128)(2,1)S(1)}, u32[]{:S(2)}, u32[]{:S(2)}) collective-permute-start(bf16[128,640]{0,1:T(8,128)(2,1)S(1)} %bitcast.588), channel_id=1, source_target_pairs={{4,0},{8,4},{12,8},{16,12},{20,16},{24,20},{28,24},{32,28},{36,32}... | collective-permute-start | bytes 491528 | tf_op jit(solution)/shard_map/ppermute | solution.py:126
  50.3 25.4 %collective-permute-start.2 = (bf16[128,640]{0,1:T(8,128)(2,1)S(1)}, bf16[128,640]{0,1:T(8,128)(2,1)S(1)}, u32[]{:S(2)}, u32[]{:S(2)}) collective-permute-start(bf16[128,640]{0,1:T(8,128)(2,1)S(1)} %bitcast.589), channel_id=1, source_target_pairs={{0,4},{4,8},{8,12},{12,16},{16,20},{20,24},{24,28},{28,32},{32,36}... | collective-permute-start | bytes 491528 | tf_op jit(solution)/shard_map/ppermute | solution.py:126
  64.7 41.1 %all-to-all-start.6 = ((bf16[8,128,128]{2,1,0:T(8,128)(2,1)}), bf16[8,128,128]{2,1,0:T(8,128)(2,1)S(1)}, u32[]{:S(2)}, u32[]{:S(2)}) async-start(bf16[8,128,128]{2,1,0:T(8,128)(2,1)} %fusion.96), calls=%async_computation.6 | async-start | bytes 524288 | tf_op jit(solution)/shard_map/all_to_all | solution.py:153
  93.3 22.7 %collective-permute-start.5 = (bf16[128,320]{0,1:T(8,128)(2,1)S(1)}, bf16[128,320]{0,1:T(8,128)(2,1)S(1)}, u32[]{:S(2)}, u32[]{:S(2)}) collective-permute-start(bf16[128,320]{0,1:T(8,128)(2,1)S(1)} %get-tuple-element.20), channel_id=1, source_target_pairs={{0,4},{4,8},{8,12},{12,16},{16,20},{20,24},{24,28},{28,32},{32,36}... | collective-permute-start | bytes 245768 | tf_op jit(solution)/shard_map/ppermute | solution.py:126
  95.6 21.8 %collective-permute-start.4 = (bf16[128,320]{0,1:T(8,128)(2,1)S(1)}, bf16[128,320]{0,1:T(8,128)(2,1)S(1)}, u32[]{:S(2)}, u32[]{:S(2)}) collective-permute-start(bf16[128,320]{0,1:T(8,128)(2,1)S(1)} %get-tuple-element.20), channel_id=1, source_target_pairs={{4,0},{8,4},{12,8},{16,12},{20,16},{24,20},{28,24},{32,28},{36,32}... | collective-permute-start | bytes 245768 | tf_op jit(solution)/shard_map/ppermute | solution.py:126
  105.7 22.6 %copy-start.26 = (bf16[8,128,128]{2,1,0:T(8,128)(2,1)}, bf16[8,128,128]{2,1,0:T(8,128)(2,1)S(1)}, u32[]{:S(2)}) copy-start(bf16[8,128,128]{2,1,0:T(8,128)(2,1)S(1)} %all-to-all-done.6) | copy-start | bytes 786436
  105.7 19.8 %copy-start.31 = (f32[128,160]{0,1:T(8,128)S(1)}, f32[128,160]{0,1:T(8,128)}, u32[]{:S(2)}) copy-start(f32[128,160]{0,1:T(8,128)} %fusion.129) | copy-start | bytes 245764
  105.8 22.6 %copy-start.30 = (f32[128,160]{0,1:T(8,128)S(1)}, f32[128,160]{0,1:T(8,128)}, u32[]{:S(2)}) copy-start(f32[128,160]{0,1:T(8,128)} %fusion.126) | copy-start | bytes 245764
  106.4 33.8 %collective-permute-start.10 = (bf16[128,128]{1,0:T(8,128)(2,1)}, bf16[128,128]{1,0:T(8,128)(2,1)}, u32[]{:S(2)}, u32[]{:S(2)}) collective-permute-start(bf16[128,128]{1,0:T(8,128)(2,1)} %get-tuple-element.19), channel_id=1, source_target_pairs={{0,32},{4,36},{8,40},{12,44},{16,48},{20,52},{24,56},{28,60},{32,6... | collective-permute-start | bytes 98312 | tf_op jit(solution)/shard_map/ppermute | solution.py:154
  114.6 31.4 %collective-permute-start.11 = (bf16[128,128]{1,0:T(8,128)(2,1)S(1)}, bf16[128,128]{1,0:T(8,128)(2,1)}, u32[]{:S(2)}, u32[]{:S(2)}) collective-permute-start(bf16[128,128]{1,0:T(8,128)(2,1)S(1)} %get-tuple-element.18), channel_id=1, source_target_pairs={{32,0},{36,4},{40,8},{44,12},{48,16},{52,20},{56,24},{60,28},{64,3... | collective-permute-start | bytes 98312 | tf_op jit(solution)/shard_map/ppermute | solution.py:155
  116.0 12.4 %copy-start.2 = (bf16[3,3,640,320]{2,3,1,0:T(8,128)(2,1)S(1)}, bf16[3,3,640,320]{2,3,1,0:T(8,128)(2,1)}, u32[]{:S(2)}) copy-start(bf16[3,3,640,320]{2,3,1,0:T(8,128)(2,1)} %param.9) | copy-start | bytes 11059204
  119.6 9.6 %copy-start.29 = (f32[128,160]{0,1:T(8,128)S(1)}, f32[128,160]{0,1:T(8,128)}, u32[]{:S(2)}) copy-start(f32[128,160]{0,1:T(8,128)} %fusion.121) | copy-start | bytes 245764
  135.2 16.9 %all-to-all-start.2 = ((bf16[4,128,160]{1,2,0:T(8,128)(2,1)}), bf16[4,128,160]{1,2,0:T(8,128)(2,1)}, u32[]{:S(2)}, u32[]{:S(2)}) async-start(bf16[4,128,160]{1,2,0:T(8,128)(2,1)} %pad_maximum_fusion.3), calls=%async_computation.2 | async-start | bytes 327680 | tf_op jit(solution)/shard_map/all_to_all | solution.py:139
  152.1 11.7 %copy-start.24 = (bf16[256,128]{1,0:T(8,128)(2,1)S(1)}, bf16[256,128]{1,0:T(8,128)(2,1)}, u32[]{:S(2)}) copy-start(bf16[256,128]{1,0:T(8,128)(2,1)} %constant.47) | copy-start | bytes 196612
  152.1 45.5 %all-to-all-start.4 = ((bf16[8,512,128]{1,2,0:T(8,128)(2,1)}), bf16[8,512,128]{1,2,0:T(8,128)(2,1)}, u32[]{:S(2)}, u32[]{:S(2)}) async-start(bf16[8,512,128]{1,2,0:T(8,128)(2,1)} %fusion.29), calls=%async_computation.4 | async-start | bytes 2097152 | tf_op jit(solution)/shard_map/all_to_all | solution.py:175
  159.6 103.8 %collective-permute-start.6 = (bf16[128,160]{0,1:T(8,128)(2,1)}, bf16[128,160]{0,1:T(8,128)(2,1)}, u32[]{:S(2)}, u32[]{:S(2)}) collective-permute-start(bf16[128,160]{0,1:T(8,128)(2,1)} %reduce_sum.42), channel_id=1, source_target_pairs={{0,4},{4,8},{8,12},{12,16},{16,20},{20,24},{24,28},{28,32},{32,36}... | collective-permute-start | bytes 122888 | tf_op jit(solution)/shard_map/ppermute | solution.py:126
  162.5 27.2 %collective-permute-start.7 = (bf16[128,160]{0,1:T(8,128)(2,1)}, bf16[128,160]{0,1:T(8,128)(2,1)S(1)}, u32[]{:S(2)}, u32[]{:S(2)}) collective-permute-start(bf16[128,160]{0,1:T(8,128)(2,1)} %reduce_sum.42), channel_id=1, source_target_pairs={{4,0},{8,4},{12,8},{16,12},{20,16},{24,20},{28,24},{32,28},{36,32}... | collective-permute-start | bytes 122888 | tf_op jit(solution)/shard_map/ppermute | solution.py:126
  166.7 22.2 %copy-start.4 = (f32[256,640]{1,0:T(8,128)}, f32[256,640]{1,0:T(8,128)S(1)}, u32[]{:S(2)}) copy-start(f32[256,640]{1,0:T(8,128)S(1)} %fusion.108) | copy-start | bytes 1966084
  212.1 12.2 %collective-permute-start.9 = (bf16[4,64,128]{2,1,0:T(8,128)(2,1)S(1)}, bf16[4,64,128]{2,1,0:T(8,128)(2,1)S(1)}, u32[]{:S(2)}, u32[]{:S(2)}) collective-permute-start(bf16[4,64,128]{2,1,0:T(8,128)(2,1)S(1)} %get-tuple-element.17), channel_id=1, source_target_pairs={{32,0},{36,4},{40,8},{44,12},{48,16},{52,20},{56,24},{60,28},{64,3... | collective-permute-start | bytes 196616 | tf_op jit(solution)/shard_map/ppermute | solution.py:178
  213.4 10.9 %copy-start.12 = (bf16[384,256]{1,0:T(8,128)(2,1)S(1)}, bf16[384,256]{1,0:T(8,128)(2,1)}, u32[]{:S(2)}) copy-start(bf16[384,256]{1,0:T(8,128)(2,1)} %constant.68) | copy-start | bytes 589828
  216.7 9.4 %collective-permute-start.8 = (bf16[4,64,128]{2,1,0:T(8,128)(2,1)S(1)}, bf16[4,64,128]{2,1,0:T(8,128)(2,1)S(1)}, u32[]{:S(2)}, u32[]{:S(2)}) collective-permute-start(bf16[4,64,128]{2,1,0:T(8,128)(2,1)S(1)} %get-tuple-element.16), channel_id=1, source_target_pairs={{0,32},{4,36},{8,40},{12,44},{16,48},{20,52},{24,56},{28,60},{32,6... | collective-permute-start | bytes 196616 | tf_op jit(solution)/shard_map/ppermute | solution.py:177
  228.6 33.7 %copy-start.10 = (bf16[160,256]{1,0:T(8,128)(2,1)S(1)}, bf16[160,256]{1,0:T(8,128)(2,1)}, u32[]{:S(2)}) copy-start(bf16[160,256]{1,0:T(8,128)(2,1)} %copy-done.9) | copy-start | bytes 245764
  228.6 34.8 %copy-start.5 = (f32[256,640]{1,0:T(8,128)S(1)}, f32[256,640]{1,0:T(8,128)}, u32[]{:S(2)}) copy-start(f32[256,640]{1,0:T(8,128)} %fusion.7) | copy-start | bytes 1966084
  232.1 43.5 %all-to-all-start.5 = ((bf16[8,2,7200]{2,1,0:T(2,128)(2,1)}), bf16[8,2,7200]{2,1,0:T(2,128)(2,1)S(1)}, u32[]{:S(2)}, u32[]{:S(2)}) async-start(bf16[8,2,7200]{2,1,0:T(2,128)(2,1)} %reshape.88), calls=%async_computation.5 | async-start | bytes 466944 | tf_op jit(solution)/shard_map/all_to_all | solution.py:149
  263.5 15.7 %copy-start.8 = (bf16[160,256]{1,0:T(8,128)(2,1)S(1)}, bf16[160,256]{1,0:T(8,128)(2,1)}, u32[]{:S(2)}) copy-start(bf16[160,256]{1,0:T(8,128)(2,1)} %copy-done.7) | copy-start | bytes 245764
  275.6 23.0 %all-to-all-start.7 = ((bf16[8,3,3,10,320]{4,2,3,1,0:T(4,128)(2,1)}), bf16[8,3,3,10,320]{4,2,3,1,0:T(4,128)(2,1)S(1)}, u32[]{:S(2)}, u32[]{:S(2)}) async-start(bf16[8,3,3,10,320]{4,2,3,1,0:T(4,128)(2,1)} %copy.59), calls=%async_computation.7 | async-start | bytes 1474560 | tf_op jit(solution)/shard_map/all_to_all | solution.py:149
  298.6 16.9 %all-to-all-start.3 = ((bf16[4,2,64,640]{3,2,1,0:T(8,128)(2,1)}), bf16[4,2,64,640]{3,2,1,0:T(8,128)(2,1)S(1)}, u32[]{:S(2)}, u32[]{:S(2)}) async-start(bf16[4,2,64,640]{3,2,1,0:T(8,128)(2,1)} %maximum_bitcast_fusion), calls=%async_computation.3 | async-start | bytes 1310720 | tf_op jit(solution)/shard_map/all_to_all | solution.py:143
  (21 other events, 83.9 us)

commit v2 on v1

v2 whole, which is shorter than its diff:
```python
import functools

import jax
import jax.numpy as jnp
import numpy as np
from jax import lax
from jax.experimental import pallas as pl
from jax.experimental.pallas import tpu as pltpu
from jax.sharding import PartitionSpec as P

BF = jnp.bfloat16
F32 = jnp.float32
GRAIN = 16
MEMBERS = 8


def mm(a, b):
    return jnp.dot(a, b, preferred_element_type=F32)


def mm_t(a, b):
    return lax.dot_general(a, b, (((1,), (1,)), ((), ())), preferred_element_type=F32)


def box_matrix(cols, pieces):
    deep = cols // 2
    part = cols // pieces
    table = np.zeros((3, 3, deep, pieces, 2, part), np.float32)
    for a, rows in enumerate(((0,), (0, 1), (1,))):
        for b in range(3):
            for j in range(deep):
                for p in (2 * j + b - 1, 2 * j + b):
                    if 0 <= p < cols:
                        for r in rows:
                            table[a, b, j, p // part, r, p % part] = 0.25
    return table.reshape(9 * deep, 2 * cols)


def spread_matrix(cols):
    deep = cols // 2
    table = np.zeros((3, cols, deep), np.float32)
    for p in range(cols):
        for j, b in ((p // 2, 1), ((p + 1) // 2, 0), (p // 2 - 1 + p % 2, 2)):
            if 0 <= j < deep:
                table[b, p, j] = 0.25
    return table


def channel_matrix(depth, groups):
    grain = depth // (groups * MEMBERS)
    table = np.zeros((MEMBERS, depth, groups * GRAIN), np.float32)
    for c in range(depth):
        g, j, k = c // (MEMBERS * grain), c // grain % MEMBERS, c % grain
        table[j, c, g * GRAIN + k] = 1.0
    return table


def pack_matrix(groups, grain):
    table = np.zeros((groups * grain, groups * GRAIN), np.float32)
    for g in range(groups):
        for k in range(grain):
            table[g * grain + k, g * GRAIN + k] = 1.0
    return table


def owner_matrix(groups, grain, block):
    table = np.zeros((groups * block, 9 * groups * grain), np.float32)
    for t in range(9):
        for g in range(groups):
            for k in range(grain):
                table[g * block + t * grain + k, (t * groups + g) * grain + k] = 1.0
    return table


def moved(y, step):
    rows = y.shape[0]
    place = lax.broadcasted_iota(jnp.int32, y.shape, 0)
    edge = 0 if step == 1 else rows - 1
    return jnp.where(place == edge, 0.0, pltpu.roll(y, step % rows, 0))


def call(body, outs, args, scratch=(), flops=0):
    size = sum(a.size * a.dtype.itemsize for a in args)
    smem = pl.BlockSpec(memory_space=pltpu.SMEM)
    vmem = pl.BlockSpec(memory_space=pltpu.VMEM)
    return pl.pallas_call(
        body,
        out_shape=outs,
        in_specs=[smem if a.dtype == jnp.int32 else vmem for a in args],
        out_specs=jax.tree.map(lambda _: vmem, outs),
        scratch_shapes=list(scratch),
        compiler_params=pltpu.CompilerParams(vmem_limit_bytes=40 * 2**20),
        cost_estimate=pl.CostEstimate(flops=flops, bytes_accessed=size, transcendentals=0),
    )(*args)


def shape(dims, dtype=BF):
    return jax.ShapeDtypeStruct(dims, dtype)


def fine_forward(odd, x, box, w, own, partner, other):
    deep = own.shape[0]
    u = [mm(box[t * deep : (t + 1) * deep], x[...]).astype(BF) for t in range(9)]
    mine = sum(mm(u[3 + b], w[3 + b]) for b in range(3))
    pair = [jnp.concatenate([u[b], u[6 + b]]) for b in range(3)]
    first = sum(mm(pair[b], w[b]) for b in range(3))
    last = sum(mm(pair[b], w[6 + b]) for b in range(3))
    own[...] = mine + first[:deep] + last[deep:]
    down = first[deep:]
    up = last[:deep]

    @pl.when(odd[0] == 0)
    def _():
        partner[...] = down
        other[...] = up

    @pl.when(odd[0] == 1)
    def _():
        partner[...] = up
        other[...] = down


def side_rows(odd, partner, other, rows):
    rows[odd[0]] = other[...]
    rows[1 - odd[0]] = partner[...]
    return rows[0], rows[1]


def deep_forward(odd, partner, mine, other, w, upstream, output, grad, rows):
    before, after = side_rows(odd, partner, other, rows)
    y = [sum(mm(row, w[3 * a + b]) for a, row in enumerate((before, mine[...], after))) for b in range(3)]
    preact = y[1] + moved(y[0], 1) + moved(y[2], -1)
    sigma = jax.nn.sigmoid(preact)
    output[...] = (preact * sigma).astype(BF)
    grad[...] = (upstream[...].astype(F32) * (sigma * (1.0 + preact * (1.0 - sigma)))).astype(BF)


def deep_backward(odd, partner, mine, other, w, out, rows):
    before, after = side_rows(odd, partner, other, rows)
    part = out.shape[2]
    z = [sum(mm_t(row, w[3 * a + b]) for a, row in enumerate((after, mine[...], before))) for b in range(3)]
    z = (z[1] + moved(z[0], -1) + moved(z[2], 1)).astype(BF)
    for k in range(out.shape[0]):
        out[k] = z[:, k * part : (k + 1) * part]


def fine_backward(odd, partner, mine, other, spread, w, out, rows):
    before, after = side_rows(odd, partner, other, rows)
    h = [[mm(spread[b], row).astype(BF) for b in range(3)] for row in (before, mine[...], after)]
    pieces, _, part, _ = out.shape
    for r, order in enumerate(((1, 1, 0), (2, 1, 1))):
        y = sum(mm_t(h[order[a]][b], w[3 * a + b]) for a in range(3) for b in range(3)).astype(BF)
        for k in range(pieces):
            out[k, r] = y[k * part : (k + 1) * part]


def slices(x, lanes, out):
    for j in range(MEMBERS):
        out[j] = mm(x[...], lanes[j]).astype(BF)


def deep_table(slab, first, last, pack, table):
    deep = slab.shape[1]
    size = pack.shape[0]
    place = lax.broadcasted_iota(jnp.int32, (size, deep), 1)
    for i in range(-1, MEMBERS + 1):
        row = first[...] if i < 0 else last[...] if i == MEMBERS else slab[i]
        flat = mm_t(pack[...], row)
        turned = (
            jnp.where(place == 0, 0.0, pltpu.roll(flat, 1, 1)).astype(BF),
            flat.astype(BF),
            jnp.where(place == deep - 1, 0.0, pltpu.roll(flat, deep - 1, 1)).astype(BF),
        )
        for a in range(3):
            home = i + 1 - a
            if 0 <= home < MEMBERS:
                for b in range(3):
                    t = 3 * a + b
                    table[t * size : (t + 1) * size, home * deep : (home + 1) * deep] = turned[b]


def fine_table(slab, first, last, box, pack, table):
    size = pack.shape[0]
    deep = box.shape[0] // 9
    wide = 3 * deep

    def boxed(block):
        return mm_t(mm_t(pack[...], block).astype(BF), box[...])

    u = [boxed(first[...])] + [boxed(slab[i]) for i in range(MEMBERS)] + [boxed(last[...])]
    for i in range(MEMBERS):
        here = u[i + 1]
        rows = (
            here[:, :wide] + u[i][:, 2 * wide :],
            here[:, wide : 2 * wide],
            here[:, 2 * wide :] + u[i + 2][:, :wide],
        )
        for a in range(3):
            value = rows[a].astype(BF)
            for b in range(3):
                t = 3 * a + b
                table[t * size : (t + 1) * size, i * deep : (i + 1) * deep] = value[:, b * deep : (b + 1) * deep]


def weight_part(table, grads, order, out):
    out[...] = mm(order[...], mm(table[...], grads[...]).astype(BF)).astype(BF)


def weight_sum(parts, out):
    total = parts[0].astype(F32)
    for g in range(1, parts.shape[0]):
        total = total + parts[g].astype(F32)
    grain = out.shape[1]
    for t in range(9):
        out[t] = total[t * grain : (t + 1) * grain]


def on_device(latent, conv_fine, conv_deep, upstream):
    wide = lax.axis_size("wide")
    pieces = lax.axis_size("narrow")
    groups = wide // MEMBERS
    near = [[MEMBERS * g + j for j in range(MEMBERS)] for g in range(groups)]
    far = [[MEMBERS * g + j for g in range(groups)] for j in range(MEMBERS)]
    odd = (lax.axis_index("wide") % 2).astype(jnp.int32).reshape(1)
    rows, part, depth = latent.shape
    cols = part * pieces
    deep = cols // 2
    grain = depth // wide
    block = -(-9 * grain // 16) * 16
    w_fine = conv_fine.reshape(9, depth, -1)
    w_deep = conv_deep.reshape(9, depth, -1)
    fine = w_fine.shape[2]
    full = w_deep.shape[2]
    box = jnp.asarray(box_matrix(cols, pieces), BF)
    spread = jnp.asarray(spread_matrix(cols), BF)
    lanes = jnp.asarray(channel_matrix(depth, groups), BF)
    pack = jnp.asarray(pack_matrix(groups, grain), BF)
    order = jnp.asarray(owner_matrix(groups, grain, block), BF)

    def everyone(v, count, **which):
        return lax.all_to_all(jnp.broadcast_to(v[None], (count,) + v.shape), split_axis=0, concat_axis=0, **which)

    def pairs(to_partner, to_other):
        partner = lax.ppermute(to_partner, "wide", [(i, i ^ 1) for i in range(wide)])
        other = lax.ppermute(
            to_other, "wide", [(i, i - 1 + 2 * (i % 2)) for i in range(1, wide - 1)]
        )
        return partner, other

    def around(first, last):
        return (
            lax.ppermute(last, "wide", [(i, i + MEMBERS) for i in range(wide - MEMBERS)]),
            lax.ppermute(first, "wide", [(i + MEMBERS, i) for i in range(wide - MEMBERS)]),
        )

    x = everyone(latent, pieces, axis_name="narrow").reshape(pieces * rows * part, depth)
    own, partner, other = call(
        fine_forward,
        [shape((deep, fine), F32)] * 3,
        (odd, x, box, w_fine),
        flops=2 * 9 * deep * depth * (2 * cols + 2 * fine),
    )
    partner, other = pairs(partner, other)
    pooled = (own + partner + other).astype(BF)
    pooled = everyone(pooled, pieces, axis_name="narrow").transpose(1, 0, 2).reshape(deep, depth)
    partner, other = pairs(pooled, pooled)
    output, grad_pre = call(
        deep_forward,
        [shape((deep, full))] * 2,
        (odd, partner, pooled, other, w_deep, upstream[0]),
        [pltpu.VMEM((2, deep, depth), BF)],
        flops=2 * 9 * deep * depth * full,
    )
    partner, other = pairs(grad_pre, grad_pre)
    partial = call(
        deep_backward,
        shape((pieces, deep, fine)),
        (odd, partner, grad_pre, other, w_deep),
        [pltpu.VMEM((2, deep, full), BF)],
        flops=2 * 9 * deep * depth * full,
    )
    partial = lax.all_to_all(partial, "narrow", 0, 0)
    grad_pool = jnp.sum(partial.astype(F32), axis=0).astype(BF)
    partner, other = pairs(grad_pool, grad_pool)
    partial = call(
        fine_backward,
        shape((pieces, rows, part, depth)),
        (odd, partner, grad_pool, other, spread, w_fine),
        [pltpu.VMEM((2, deep, fine), BF)],
        flops=2 * 18 * cols * depth * fine,
    )
    partial = lax.all_to_all(partial, "narrow", 0, 0)
    grad_latent = jnp.sum(partial.astype(F32), axis=0).astype(BF)

    def owners(table, grads):
        width = grads.shape[-1]
        grads = everyone(grads, MEMBERS, axis_name="wide", axis_index_groups=near)
        got = call(
            weight_part,
            shape((groups * block, width)),
            (table, grads.reshape(MEMBERS * deep, width), order),
            flops=2 * 9 * groups * grain * MEMBERS * deep * width,
        )
        got = got.reshape(groups, block, width)
        got = lax.all_to_all(got, "wide", 0, 0, axis_index_groups=far)
        total = call(weight_sum, shape((9, grain, width), F32), (got,))
        return total.reshape(3, 3, grain, width)

    table_shape = shape((9 * groups * grain, MEMBERS * deep))
    slab = call(slices, shape((MEMBERS, deep, groups * GRAIN)), (pooled, lanes))
    slab = lax.all_to_all(slab, "wide", 0, 0, axis_index_groups=near)
    first, last = around(slab[0], slab[-1])
    table = call(deep_table, table_shape, (slab, first, last, pack))
    grad_deep = owners(table, grad_pre)

    slab = call(slices, shape((MEMBERS, rows * cols, groups * GRAIN)), (x, lanes))
    slab = lax.all_to_all(slab, "wide", 0, 0, axis_index_groups=near)
    first, last = around(slab[0], slab[-1])
    table = call(fine_table, table_shape, (slab, first, last, box, pack))
    grad_fine = owners(table, grad_pool)
    return output[None], grad_latent, grad_fine, grad_deep


def solution(mesh):
    return jax.shard_map(
        on_device,
        mesh=mesh,
        in_specs=(
            P("wide", "narrow", None),
            P(None, None, None, "narrow"),
            P(None, None, None, "narrow"),
            P("wide", None, "narrow"),
        ),
        out_specs=(
            P("wide", None, "narrow"),
            P("wide", "narrow", None),
            P(None, None, "wide", "narrow"),
            P(None, None, "wide", "narrow"),
        ),
        check_vma=False,
    )
```

time: 322 us -> 257 us (0.80); the launches traced: 316 us -> 255 us
  matrix products: 88.9 us -> 0 us
  blocking collectives: 55.9 us -> 12.3 us
  waiting for transfers between devices: 40.3 us -> 72 us
  Pallas kernels: 0 us -> 22 us
  local copies, waits for them, and re-layouts: 26.8 us -> 43.2 us
  starting transfers between devices: 93.7 us -> 103 us
  other arithmetic: 8.75 us -> 1.94 us
    dot_general x108 -> x0, matrix products: 88.9 us -> none  [the longest x51 42.7 us: mm_t(): lax.dot_general(a, b, (((1,), (1,)), ((), ())), preferred_element_type=F32)]
    all_gather x2 -> x0, blocking collectives: 34.6 us -> none  [the longest x1 21 us: on_device(): grads = lax.all_gather(grad_pool, 'wide', axis_index_groups=near)]
    unnamed x73 -> x54, local copies, waits for them, and re-layouts: 8.05 us -> 30.8 us
    pallas_call x0 -> x12, Pallas kernels: none -> 22 us  [call(): pl.pallas_call(body, out_shape=outs, in_specs=[smem if a.dtype == jnp.int...]
    all_to_all x3 -> x5, starting transfers between devices: 38.8 us -> 58.4 us  [the longest x2 44.2 us: owners(): got = lax.all_to_all(got, 'wide', 0, 0, axis_index_groups=far)]
    ppermute x12, starting transfers between devices: 35.1 us -> 16.7 us  [the longest x2 6.74 us: around(): lax.ppermute(last, 'wide', [(i, i + MEMBERS) for i in range(wide - MEMBER...]
    ppermute x12, waiting for transfers between devices: 1.69 us -> 18.2 us  [the longest x2 14.4 us: around(): lax.ppermute(first, 'wide', [(i + MEMBERS, i) for i in range(wide - MEMBE...]
    all_to_all x2, waiting for transfers between devices: 0.01 us -> 16 us  [on_device(): slab = lax.all_to_all(slab, 'wide', 0, 0, axis_index_groups=near)]
  transfers between devices with their start and end apart: 19 -> 21, of which waited for: 5 -> 13; matrix products, arithmetic and copies ran while one was open for 36% -> 9% of each run, Pallas kernels for 0% -> 7%
where the time goes in v2:
time: 257 us; the launch traced here: 255 us
  starting transfers between devices  103 us (40%)
  waiting for transfers between devices  72 us (28%)
  local copies, waits for them, and re-layouts  43.2 us (17%)
  Pallas kernels  22 us (9%)
  blocking collectives  12.3 us (5%)
    all_to_all x2, starting transfers between devices, owners(): got = lax.all_to_all(got, 'wide', 0, 0, axis_index_groups=far)  44.2 us
    unnamed x54, local copies, waits for them, and re-layouts  30.8 us
    pallas_call x12, Pallas kernels, call(): pl.pallas_call(body, out_shape=outs, in_specs=[smem if a.dtype == jnp.int...  22 us
    all_to_all x2, starting transfers between devices, on_device(): slab = lax.all_to_all(slab, 'wide', 0, 0, axis_index_groups=near)  19.1 us
    all_to_all x2, waiting for transfers between devices, owners(): got = lax.all_to_all(got, 'wide', 0, 0, axis_index_groups=far)  18.8 us
    all_to_all x3, waiting for transfers between devices, everyone(): lax.all_to_all(jnp.broadcast_to(v[None], (count,) + v.shape), split_axis=...  18.4 us
    all_to_all x2, waiting for transfers between devices, on_device(): slab = lax.all_to_all(slab, 'wide', 0, 0, axis_index_groups=near)  16 us
    ppermute x2, waiting for transfers between devices, around(): lax.ppermute(first, 'wide', [(i + MEMBERS, i) for i in range(wide - MEMBE...  14.4 us
  transfers between devices with their start and end apart: 21, of which 13 were waited for; matrix products, arithmetic and copies ran while one was open for 9% of the time, Pallas kernels for 7%

profile of v2, /device:TPU:32, one launch (start us, length us, event | category | flops | bytes accessed | tf_op | source)
XLA Modules:
  0.0 255.4 jit_solution(9984233579424669769)
XLA Ops:
  2.5 6.0 %all-to-all-start = ((bf16[4,2,64,640]{3,2,1,0:T(8,128)(2,1)}), bf16[4,2,64,640]{3,2,1,0:T(8,128)(2,1)}, u32[]{:S(2)}, u32[]{:S(2)}) async-start(bf16[4,2,64,640]{3,2,1,0:T(8,128)(2,1)} %broadcast_in_dim.10), calls=%async_computation | async-start | bytes 1310720 | tf_op jit(solution)/shard_map/all_to_all | solution.py:241
  8.5 3.7 %copy.48 = bf16[3,3,640,160]{3,2,1,0:T(8,128)(2,1)S(1)} copy(bf16[3,3,640,160]{2,3,1,0:T(8,128)(2,1)} %param.10) | data formatting | bytes 3686400 | tf_op args[1]
  12.2 10.3 %all-to-all-done = bf16[4,2,64,640]{3,2,1,0:T(8,128)(2,1)} async-done(((bf16[4,2,64,640]{3,2,1,0:T(8,128)(2,1)}), bf16[4,2,64,640]{3,2,1,0:T(8,128)(2,1)}, u32[]{:S(2)}, u32[]{:S(2)}) %all-to-all-start) | async-done | bytes 655392 | tf_op jit(solution)/shard_map/all_to_all | solution.py:241
  23.8 2.9 %shard_map.120 = (f32[128,160]{1,0:T(8,128)S(1)}, f32[128,160]{1,0:T(8,128)S(1)}, f32[128,160]{1,0:T(8,128)S(1)}) custom-call(s32[1]{0:T(128)} %bitcast.odd, bf16[512,640]{1,0:T(8,128)(2,1)} %bitcast.1.x, bf16[1152,512]{1,0:T(8,128)(2,1)S(1)} %copy-done.6, bf16[9,640,160]{2,1,0:T(8,128)(2,1)S(1)} %bitcast.25), custom_call_target="tpu_custom_call" | custom-call | flops 1226833920 | bytes 3678212 | tf_op jit(solution)/shard_map/pallas_call | solution.py:86
  27.4 2.9 %collective-permute-start = (f32[128,160]{1,0:T(8,128)S(1)}, f32[128,160]{1,0:T(8,128)S(1)}, u32[]{:S(2)}, u32[]{:S(2)}) collective-permute-start(f32[128,160]{1,0:T(8,128)S(1)} %get-tuple-element.10), channel_id=1, source_target_pairs={{0,4},{4,0},{8,12},{12,8},{16,20},{20,16},{24,28},{28,24},{32,36},... | collective-permute-start | bytes 245768 | tf_op jit(solution)/shard_map/ppermute | solution.py:244
  31.5 12.3 %all_to_all.50 = bf16[4,128,160]{1,2,0:T(8,128)(2,1)S(1)} all-to-all(bf16[4,128,160]{1,2,0:T(8,128)(2,1)S(1)} %broadcast_in_dim.11), channel_id=1, replica_groups=mesh['wide'=64,'narrow'=4] {'narrow'}, dimensions={0} | all-to-all | bytes 327680 | tf_op jit(solution)/shard_map/all_to_all | solution.py:241
  48.1 8.5 %all-to-all-start.7 = ((bf16[8,128,128]{2,1,0:T(8,128)(2,1)}), bf16[8,128,128]{2,1,0:T(8,128)(2,1)S(1)}, u32[]{:S(2)}, u32[]{:S(2)}) async-start(bf16[8,128,128]{2,1,0:T(8,128)(2,1)} %copy-done.16), calls=%async_computation.7 | async-start | bytes 524288 | tf_op jit(solution)/shard_map/all_to_all | solution.py:311
  56.6 7.8 %copy.52 = bf16[3,3,640,320]{3,2,1,0:T(8,128)(2,1)} copy(bf16[3,3,640,320]{2,3,1,0:T(8,128)(2,1)} %param.11) | data formatting | bytes 7372800 | tf_op args[2]
  64.6 2.2 copy-done
  66.8 2.3 shard_map.121
  74.2 4.6 %all-to-all-start.2 = ((bf16[4,128,160]{1,2,0:T(8,128)(2,1)}), bf16[4,128,160]{1,2,0:T(8,128)(2,1)S(1)}, u32[]{:S(2)}, u32[]{:S(2)}) async-start(bf16[4,128,160]{1,2,0:T(8,128)(2,1)} %copy.55), calls=%async_computation.2 | async-start | bytes 327680 | tf_op jit(solution)/shard_map/all_to_all | solution.py:282
  80.2 2.6 %shard_map.124 = bf16[8,512,128]{2,1,0:T(8,128)(2,1)S(1)} custom-call(bf16[512,640]{1,0:T(8,128)(2,1)} %bitcast.1.x, bf16[8,640,128]{2,1,0:T(8,128)(2,1)S(1)} %copy-done.5), custom_call_target="tpu_custom_call" | custom-call | bytes 1966080 | tf_op jit(solution)/shard_map/pallas_call | solution.py:86
  84.3 10.6 %all-to-all-start.4 = ((bf16[8,512,128]{2,1,0:T(8,128)(2,1)}), bf16[8,512,128]{2,1,0:T(8,128)(2,1)}, u32[]{:S(2)}, u32[]{:S(2)}) async-start(bf16[8,512,128]{2,1,0:T(8,128)(2,1)} %copy-done.10), calls=%async_computation.4 | async-start | bytes 2097152 | tf_op jit(solution)/shard_map/all_to_all | solution.py:317
  94.9 16.0 %all-to-all-done.4.slab = bf16[8,512,128]{2,1,0:T(8,128)(2,1)} async-done(((bf16[8,512,128]{2,1,0:T(8,128)(2,1)}), bf16[8,512,128]{2,1,0:T(8,128)(2,1)}, u32[]{:S(2)}, u32[]{:S(2)}) %all-to-all-start.4) | async-done | bytes 1048608 | tf_op jit(solution)/shard_map/all_to_all | solution.py:317
  111.7 4.1 %all-to-all-start.5 = ((bf16[8,128,160]{1,2,0:T(8,128)(2,1)}), bf16[8,128,160]{1,2,0:T(8,128)(2,1)}, u32[]{:S(2)}, u32[]{:S(2)}) async-start(bf16[8,128,160]{1,2,0:T(8,128)(2,1)} %broadcast_in_dim.13), calls=%async_computation.5 | async-start | bytes 655360 | tf_op jit(solution)/shard_map/all_to_all | solution.py:241
  115.9 8.1 %all-to-all-done.5 = bf16[8,128,160]{1,2,0:T(8,128)(2,1)} async-done(((bf16[8,128,160]{1,2,0:T(8,128)(2,1)}), bf16[8,128,160]{1,2,0:T(8,128)(2,1)}, u32[]{:S(2)}, u32[]{:S(2)}) %all-to-all-start.5) | async-done | bytes 327712 | tf_op jit(solution)/shard_map/all_to_all | solution.py:241
  124.9 4.2 %all-to-all-start.8 = ((bf16[8,128,320]{1,2,0:T(8,128)(2,1)}), bf16[8,128,320]{1,2,0:T(8,128)(2,1)}, u32[]{:S(2)}, u32[]{:S(2)}) async-start(bf16[8,128,320]{1,2,0:T(8,128)(2,1)} %broadcast_in_dim.14), calls=%async_computation.8 | async-start | bytes 1310720 | tf_op jit(solution)/shard_map/all_to_all | solution.py:241
  130.1 4.2 %collective-permute-start.8 = (bf16[512,128]{1,0:T(8,128)(2,1)S(1)}, bf16[512,128]{1,0:T(8,128)(2,1)S(1)}, u32[]{:S(2)}, u32[]{:S(2)}) collective-permute-start(bf16[512,128]{1,0:T(8,128)(2,1)S(1)} %get-tuple-element.31), channel_id=1, source_target_pairs={{0,32},{4,36},{8,40},{12,44},{16,48},{20,52},{24,56},{28,60},{32,6... | collective-permute-start | bytes 393224 | tf_op jit(solution)/shard_map/ppermute | solution.py:252
  137.6 10.1 %collective-permute-done.9.last = bf16[512,128]{1,0:T(8,128)(2,1)S(1)} collective-permute-done((bf16[512,128]{1,0:T(8,128)(2,1)S(1)}, bf16[512,128]{1,0:T(8,128)(2,1)S(1)}, u32[]{:S(2)}, u32[]{:S(2)}) %collective-permute-start.9) | collective-permute-done | bytes 131104 | tf_op jit(solution)/shard_map/ppermute | solution.py:253
  148.9 5.0 %shard_map.125.table = bf16[720,1024]{1,0:T(8,128)(2,1)S(1)} custom-call(bf16[8,512,128]{2,1,0:T(8,128)(2,1)} %all-to-all-done.4.slab, bf16[512,128]{1,0:T(8,128)(2,1)S(1)} %collective-permute-done.8.first, bf16[512,128]{1,0:T(8,128)(2,1)S(1)} %collective-permute-done.9.last, bf16[1152,512]{1,0:T(8,128)(2,1)S(1)} %copy-done.7, bf16[80,128]{1,0:T(8,128)(2,1)S(1)} %copy-done.22), custom_call_target="tpu_custom_call" | custom-call | bytes 2510848 | tf_op jit(solution)/shard_map/pallas_call | solution.py:86
  161.1 2.0 copy.60
  163.1 23.3 %all-to-all-start.6 = ((bf16[8,96,160]{1,2,0:T(8,128)(2,1)}), bf16[8,96,160]{1,2,0:T(8,128)(2,1)}, u32[]{:S(2)}, u32[]{:S(2)}) async-start(bf16[8,96,160]{1,2,0:T(8,128)(2,1)} %copy.60), calls=%async_computation.6 | async-start | bytes 655360 | tf_op jit(solution)/shard_map/all_to_all | solution.py:305
  187.8 2.7 %shard_map.123 = bf16[4,2,64,640]{3,2,1,0:T(8,128)(2,1)S(1)} custom-call(s32[1]{0:T(128)} %bitcast.odd, bf16[128,160]{1,0:T(8,128)(2,1)S(1)} %collective-permute-done.6.partner, bf16[128,160]{1,0:T(8,128)(2,1)S(1)} %copy.56.mine, bf16[128,160]{1,0:T(8,128)(2,1)S(1)} %collective-permute-done.7.other, bf16[3,256,128]{2,1,0:T(8,128)(2,1)S(1)} %copy-done.19, ...), custom_call_target="tpu_custom_call" | custom-call | flops 943718400 | bytes 2162692 | tf_op jit(solution)/shard_map/pallas_call | solution.py:86
  191.4 8.1 %all-to-all-done.6 = bf16[8,96,160]{1,2,0:T(8,128)(2,1)} async-done(((bf16[8,96,160]{1,2,0:T(8,128)(2,1)}), bf16[8,96,160]{1,2,0:T(8,128)(2,1)}, u32[]{:S(2)}, u32[]{:S(2)}) %all-to-all-start.6) | async-done | bytes 245792 | tf_op jit(solution)/shard_map/all_to_all | solution.py:305
  199.4 4.2 %all-to-all-start.3 = ((bf16[4,2,64,640]{3,2,1,0:T(8,128)(2,1)}), bf16[4,2,64,640]{3,2,1,0:T(8,128)(2,1)}, u32[]{:S(2)}, u32[]{:S(2)}) async-start(bf16[4,2,64,640]{3,2,1,0:T(8,128)(2,1)} %copy-done.12), calls=%async_computation.3 | async-start | bytes 1310720 | tf_op jit(solution)/shard_map/all_to_all | solution.py:292
  203.6 2.6 %collective-permute-start.10 = (bf16[128,128]{1,0:T(8,128)(2,1)S(1)}, bf16[128,128]{1,0:T(8,128)(2,1)S(1)}, u32[]{:S(2)}, u32[]{:S(2)}) collective-permute-start(bf16[128,128]{1,0:T(8,128)(2,1)S(1)} %get-tuple-element.33), channel_id=1, source_target_pairs={{0,32},{4,36},{8,40},{12,44},{16,48},{20,52},{24,56},{28,60},{32,6... | collective-permute-start | bytes 98312 | tf_op jit(solution)/shard_map/ppermute | solution.py:252
  207.8 4.4 %collective-permute-done.11.last = bf16[128,128]{1,0:T(8,128)(2,1)S(1)} collective-permute-done((bf16[128,128]{1,0:T(8,128)(2,1)S(1)}, bf16[128,128]{1,0:T(8,128)(2,1)S(1)}, u32[]{:S(2)}, u32[]{:S(2)}) %collective-permute-start.11) | collective-permute-done | bytes 32800 | tf_op jit(solution)/shard_map/ppermute | solution.py:253
  212.6 2.3 copy.64
  216.0 2.4 shard_map.130
  218.4 20.9 %all-to-all-start.9 = ((bf16[8,96,320]{2,1,0:T(8,128)(2,1)}), bf16[8,96,320]{2,1,0:T(8,128)(2,1)S(1)}, u32[]{:S(2)}, u32[]{:S(2)}) async-start(bf16[8,96,320]{2,1,0:T(8,128)(2,1)} %bitcast.16), calls=%async_computation.9 | async-start | bytes 1179648 | tf_op jit(solution)/shard_map/all_to_all | solution.py:305
  242.0 1.9 reduce_sum.25
  243.8 10.7 %all-to-all-done.9.parts = bf16[8,96,320]{2,1,0:T(8,128)(2,1)S(1)} async-done(((bf16[8,96,320]{2,1,0:T(8,128)(2,1)}), bf16[8,96,320]{2,1,0:T(8,128)(2,1)S(1)}, u32[]{:S(2)}, u32[]{:S(2)}) %all-to-all-start.9) | async-done | bytes 491552 | tf_op jit(solution)/shard_map/all_to_all | solution.py:305
  (95 shorter events, 40.7 us)
Async XLA Ops:
  2.5 20.0 %all-to-all-start = ((bf16[4,2,64,640]{3,2,1,0:T(8,128)(2,1)}), bf16[4,2,64,640]{3,2,1,0:T(8,128)(2,1)}, u32[]{:S(2)}, u32[]{:S(2)}) async-start(bf16[4,2,64,640]{3,2,1,0:T(8,128)(2,1)} %broadcast_in_dim.10), calls=%async_computation | async-start | bytes 1310720 | tf_op jit(solution)/shard_map/all_to_all | solution.py:241
  26.7 3.6 %collective-permute-start.1 = (f32[128,160]{1,0:T(8,128)S(1)}, f32[128,160]{1,0:T(8,128)S(1)}, u32[]{:S(2)}, u32[]{:S(2)}) collective-permute-start(f32[128,160]{1,0:T(8,128)S(1)} %get-tuple-element.11), channel_id=1, source_target_pairs={{4,8},{8,4},{12,16},{16,12},{20,24},{24,20},{28,32},{32,28},{36,40... | collective-permute-start | bytes 245768 | tf_op jit(solution)/shard_map/ppermute | solution.py:245
  27.4 3.9 %collective-permute-start = (f32[128,160]{1,0:T(8,128)S(1)}, f32[128,160]{1,0:T(8,128)S(1)}, u32[]{:S(2)}, u32[]{:S(2)}) collective-permute-start(f32[128,160]{1,0:T(8,128)S(1)} %get-tuple-element.10), channel_id=1, source_target_pairs={{0,4},{4,0},{8,12},{12,8},{16,20},{20,16},{24,28},{28,24},{32,36},... | collective-permute-start | bytes 245768 | tf_op jit(solution)/shard_map/ppermute | solution.py:244
  44.0 20.6 %collective-permute-start.2 = (bf16[128,640]{1,0:T(8,128)(2,1)S(1)}, bf16[128,640]{1,0:T(8,128)(2,1)}, u32[]{:S(2)}, u32[]{:S(2)}) collective-permute-start(bf16[128,640]{1,0:T(8,128)(2,1)S(1)} %copy.50.mine.x), channel_id=1, source_target_pairs={{0,4},{4,0},{8,12},{12,8},{16,20},{20,16},{24,28},{28,24},{32,36},... | collective-permute-start | bytes 491528 | tf_op jit(solution)/shard_map/ppermute | solution.py:244
  44.2 20.3 %collective-permute-start.3 = (bf16[128,640]{1,0:T(8,128)(2,1)S(1)}, bf16[128,640]{1,0:T(8,128)(2,1)}, u32[]{:S(2)}, u32[]{:S(2)}) collective-permute-start(bf16[128,640]{1,0:T(8,128)(2,1)S(1)} %copy.50.mine.x), channel_id=1, source_target_pairs={{4,8},{8,4},{12,16},{16,12},{20,24},{24,20},{28,32},{32,28},{36,40... | collective-permute-start | bytes 491528 | tf_op jit(solution)/shard_map/ppermute | solution.py:245
  48.1 26.2 %all-to-all-start.7 = ((bf16[8,128,128]{2,1,0:T(8,128)(2,1)}), bf16[8,128,128]{2,1,0:T(8,128)(2,1)S(1)}, u32[]{:S(2)}, u32[]{:S(2)}) async-start(bf16[8,128,128]{2,1,0:T(8,128)(2,1)} %copy-done.16), calls=%async_computation.7 | async-start | bytes 524288 | tf_op jit(solution)/shard_map/all_to_all | solution.py:311
  56.6 7.8 %copy-start.23 = (bf16[1,128,320]{1,2,0:T(8,128)(2,1)S(1)}, bf16[1,128,320]{1,2,0:T(8,128)(2,1)}, u32[]{:S(2)}) copy-start(bf16[1,128,320]{1,2,0:T(8,128)(2,1)} %param.12) | copy-start | bytes 245764
  64.6 2.3 copy-start
  66.8 4.4 %copy-start.1 = (bf16[3,3,640,320]{3,2,1,0:T(8,128)(2,1)S(1)}, bf16[3,3,640,320]{3,2,1,0:T(8,128)(2,1)}, u32[]{:S(2)}) copy-start(bf16[3,3,640,320]{3,2,1,0:T(8,128)(2,1)} %copy.52) | copy-start | bytes 11059204
  69.7 1.4 collective-permute-start.4
  70.2 0.9 collective-permute-start.5
  74.2 8.5 %copy-start.14 = (bf16[8,128,128]{2,1,0:T(8,128)(2,1)}, bf16[8,128,128]{2,1,0:T(8,128)(2,1)S(1)}, u32[]{:S(2)}) copy-start(bf16[8,128,128]{2,1,0:T(8,128)(2,1)S(1)} %all-to-all-done.7.slab) | copy-start | bytes 786436
  74.2 10.0 %all-to-all-start.2 = ((bf16[4,128,160]{1,2,0:T(8,128)(2,1)}), bf16[4,128,160]{1,2,0:T(8,128)(2,1)S(1)}, u32[]{:S(2)}, u32[]{:S(2)}) async-start(bf16[4,128,160]{1,2,0:T(8,128)(2,1)} %copy.55), calls=%async_computation.2 | async-start | bytes 327680 | tf_op jit(solution)/shard_map/all_to_all | solution.py:282
  83.8 32.0 %copy-start.18 = (bf16[128,320]{1,0:T(8,128)(2,1)S(1)}, bf16[128,320]{1,0:T(8,128)(2,1)}, u32[]{:S(2)}) copy-start(bf16[128,320]{1,0:T(8,128)(2,1)} %copy-done.17) | copy-start | bytes 245764
  84.3 26.6 %all-to-all-start.4 = ((bf16[8,512,128]{2,1,0:T(8,128)(2,1)}), bf16[8,512,128]{2,1,0:T(8,128)(2,1)}, u32[]{:S(2)}, u32[]{:S(2)}) async-start(bf16[8,512,128]{2,1,0:T(8,128)(2,1)} %copy-done.10), calls=%async_computation.4 | async-start | bytes 2097152 | tf_op jit(solution)/shard_map/all_to_all | solution.py:317
  111.7 12.3 %all-to-all-start.5 = ((bf16[8,128,160]{1,2,0:T(8,128)(2,1)}), bf16[8,128,160]{1,2,0:T(8,128)(2,1)}, u32[]{:S(2)}, u32[]{:S(2)}) async-start(bf16[8,128,160]{1,2,0:T(8,128)(2,1)} %broadcast_in_dim.13), calls=%async_computation.5 | async-start | bytes 655360 | tf_op jit(solution)/shard_map/all_to_all | solution.py:241
  115.8 31.9 %copy-start.22 = (bf16[80,128]{1,0:T(8,128)(2,1)S(1)}, bf16[80,128]{1,0:T(8,128)(2,1)}, u32[]{:S(2)}) copy-start(bf16[80,128]{1,0:T(8,128)(2,1)} %constant.36.clone.pack) | copy-start | bytes 61444
  124.9 38.2 %all-to-all-start.8 = ((bf16[8,128,320]{1,2,0:T(8,128)(2,1)}), bf16[8,128,320]{1,2,0:T(8,128)(2,1)}, u32[]{:S(2)}, u32[]{:S(2)}) async-start(bf16[8,128,320]{1,2,0:T(8,128)(2,1)} %broadcast_in_dim.14), calls=%async_computation.8 | async-start | bytes 1310720 | tf_op jit(solution)/shard_map/all_to_all | solution.py:241
  130.1 7.4 %collective-permute-start.8 = (bf16[512,128]{1,0:T(8,128)(2,1)S(1)}, bf16[512,128]{1,0:T(8,128)(2,1)S(1)}, u32[]{:S(2)}, u32[]{:S(2)}) collective-permute-start(bf16[512,128]{1,0:T(8,128)(2,1)S(1)} %get-tuple-element.31), channel_id=1, source_target_pairs={{0,32},{4,36},{8,40},{12,44},{16,48},{20,52},{24,56},{28,60},{32,6... | collective-permute-start | bytes 393224 | tf_op jit(solution)/shard_map/ppermute | solution.py:252
  134.3 13.3 %collective-permute-start.9 = (bf16[512,128]{1,0:T(8,128)(2,1)S(1)}, bf16[512,128]{1,0:T(8,128)(2,1)S(1)}, u32[]{:S(2)}, u32[]{:S(2)}) collective-permute-start(bf16[512,128]{1,0:T(8,128)(2,1)S(1)} %get-tuple-element.30), channel_id=1, source_target_pairs={{32,0},{36,4},{40,8},{44,12},{48,16},{52,20},{56,24},{60,28},{64,3... | collective-permute-start | bytes 393224 | tf_op jit(solution)/shard_map/ppermute | solution.py:253
  156.3 1.4 copy-start.3
  161.1 26.7 %copy-start.19 = (bf16[3,256,128]{2,1,0:T(8,128)(2,1)S(1)}, bf16[3,256,128]{2,1,0:T(8,128)(2,1)}, u32[]{:S(2)}) copy-start(bf16[3,256,128]{2,1,0:T(8,128)(2,1)} %constant.34.clone.spread) | copy-start | bytes 589828
  163.1 36.4 %all-to-all-start.6 = ((bf16[8,96,160]{1,2,0:T(8,128)(2,1)}), bf16[8,96,160]{1,2,0:T(8,128)(2,1)}, u32[]{:S(2)}, u32[]{:S(2)}) async-start(bf16[8,96,160]{1,2,0:T(8,128)(2,1)} %copy.60), calls=%async_computation.6 | async-start | bytes 655360 | tf_op jit(solution)/shard_map/all_to_all | solution.py:305
  186.5 17.1 %copy-start.15 = (bf16[8,128,128]{2,1,0:T(8,128)(2,1)S(1)}, bf16[8,128,128]{2,1,0:T(8,128)(2,1)}, u32[]{:S(2)}) copy-start(bf16[8,128,128]{2,1,0:T(8,128)(2,1)} %copy-done.14) | copy-start | bytes 786436
  186.5 1.3 collective-permute-start.6
  186.6 1.2 collective-permute-start.7
  199.4 18.9 %all-to-all-start.3 = ((bf16[4,2,64,640]{3,2,1,0:T(8,128)(2,1)}), bf16[4,2,64,640]{3,2,1,0:T(8,128)(2,1)}, u32[]{:S(2)}, u32[]{:S(2)}) async-start(bf16[4,2,64,640]{3,2,1,0:T(8,128)(2,1)} %copy-done.12), calls=%async_computation.3 | async-start | bytes 1310720 | tf_op jit(solution)/shard_map/all_to_all | solution.py:292
  203.6 4.2 %collective-permute-start.10 = (bf16[128,128]{1,0:T(8,128)(2,1)S(1)}, bf16[128,128]{1,0:T(8,128)(2,1)S(1)}, u32[]{:S(2)}, u32[]{:S(2)}) collective-permute-start(bf16[128,128]{1,0:T(8,128)(2,1)S(1)} %get-tuple-element.33), channel_id=1, source_target_pairs={{0,32},{4,36},{8,40},{12,44},{16,48},{20,52},{24,56},{28,60},{32,6... | collective-permute-start | bytes 98312 | tf_op jit(solution)/shard_map/ppermute | solution.py:252
  206.2 8.7 %copy-start.9 = (bf16[768,720]{1,0:T(8,128)(2,1)S(1)}, bf16[768,720]{1,0:T(8,128)(2,1)}, u32[]{:S(2)}) copy-start(bf16[768,720]{1,0:T(8,128)(2,1)} %constant.37.clone.order) | copy-start | bytes 3317764
  206.2 5.9 %collective-permute-start.11 = (bf16[128,128]{1,0:T(8,128)(2,1)S(1)}, bf16[128,128]{1,0:T(8,128)(2,1)S(1)}, u32[]{:S(2)}, u32[]{:S(2)}) collective-permute-start(bf16[128,128]{1,0:T(8,128)(2,1)S(1)} %get-tuple-element.32), channel_id=1, source_target_pairs={{32,0},{36,4},{40,8},{44,12},{48,16},{52,20},{56,24},{60,28},{64,3... | collective-permute-start | bytes 98312 | tf_op jit(solution)/shard_map/ppermute | solution.py:253
  216.0 23.3 %copy-start.21 = (bf16[128,320]{1,0:T(8,128)(2,1)S(1)}, bf16[128,320]{1,0:T(8,128)(2,1)}, u32[]{:S(2)}) copy-start(bf16[128,320]{1,0:T(8,128)(2,1)} %copy-done.20) | copy-start | bytes 245764
  218.4 36.2 %all-to-all-start.9 = ((bf16[8,96,320]{2,1,0:T(8,128)(2,1)}), bf16[8,96,320]{2,1,0:T(8,128)(2,1)S(1)}, u32[]{:S(2)}, u32[]{:S(2)}) async-start(bf16[8,96,320]{2,1,0:T(8,128)(2,1)} %bitcast.16), calls=%async_computation.9 | async-start | bytes 1179648 | tf_op jit(solution)/shard_map/all_to_all | solution.py:305
  (13 other events, 13.3 us)

commit v3 on v2

v3 whole, which is shorter than its diff:
```python
import functools

import jax
import jax.numpy as jnp
import numpy as np
from jax import lax
from jax.experimental import pallas as pl
from jax.experimental.pallas import tpu as pltpu
from jax.sharding import PartitionSpec as P

BF = jnp.bfloat16
F32 = jnp.float32
MEMBERS = 8


def mm(a, b):
    return jnp.dot(a, b, preferred_element_type=F32)


def mm_t(a, b):
    return lax.dot_general(a, b, (((1,), (1,)), ((), ())), preferred_element_type=F32)


def box_matrix(cols, pieces):
    deep = cols // 2
    part = cols // pieces
    table = np.zeros((3, 3, deep, pieces, 2, part), np.float32)
    for a, rows in enumerate(((0,), (0, 1), (1,))):
        for b in range(3):
            for j in range(deep):
                for p in (2 * j + b - 1, 2 * j + b):
                    if 0 <= p < cols:
                        for r in rows:
                            table[a, b, j, p // part, r, p % part] = 0.25
    return table.reshape(9 * deep, 2 * cols)


def spread_matrix(cols):
    deep = cols // 2
    table = np.zeros((3, cols, deep), np.float32)
    for p in range(cols):
        for j, b in ((p // 2, 1), ((p + 1) // 2, 0), (p // 2 - 1 + p % 2, 2)):
            if 0 <= j < deep:
                table[b, p, j] = 0.25
    return table


def channel_matrix(depth, groups):
    grain = depth // (groups * MEMBERS)
    table = np.zeros((MEMBERS, groups, grain, depth), np.float32)
    for c in range(depth):
        table[c // grain % MEMBERS, c // (MEMBERS * grain), c % grain, c] = 1.0
    return table.reshape(depth, depth)


def owner_matrix(groups, grain, block):
    table = np.zeros((groups * block, 9 * groups * grain), np.float32)
    for t in range(9):
        for g in range(groups):
            for k in range(grain):
                table[g * block + t * grain + k, (t * groups + g) * grain + k] = 1.0
    return table


def moved(y, step, axis):
    size = y.shape[axis]
    place = lax.broadcasted_iota(jnp.int32, y.shape, axis)
    edge = 0 if step == 1 else size - 1
    return jnp.where(place == edge, 0.0, pltpu.roll(y, step % size, axis))


def shape(dims, dtype=BF):
    return jax.ShapeDtypeStruct(dims, dtype)


def call(body, outs, args, scratch=(), flops=0, behind=()):
    size = sum(a.size * a.dtype.itemsize for a in args)
    smem = pl.BlockSpec(memory_space=pltpu.SMEM)
    vmem = pl.BlockSpec(memory_space=pltpu.VMEM)
    aside = pl.BlockSpec(memory_space=pl.ANY)
    count = len(args)

    def kernel(*refs):
        body(*refs[:count], *refs[count + len(behind) :])

    return pl.pallas_call(
        kernel,
        out_shape=outs,
        in_specs=[smem if a.dtype == jnp.int32 else vmem for a in args] + [aside] * len(behind),
        out_specs=jax.tree.map(lambda _: vmem, outs),
        scratch_shapes=list(scratch),
        compiler_params=pltpu.CompilerParams(vmem_limit_bytes=40 * 2**20),
        cost_estimate=pl.CostEstimate(flops=flops, bytes_accessed=size, transcendentals=0),
    )(*args, *behind)


def fine_forward(at, x, box, w, own, partner, other):
    deep = own.shape[1]
    u = [mm(box[t * deep : (t + 1) * deep], x[...]).astype(BF) for t in range(9)]
    pair = [jnp.concatenate([u[b], u[6 + b]]) for b in range(3)]
    mine = sum(mm_t(w[3 + b], u[3 + b]) for b in range(3))
    first = sum(mm_t(w[b], pair[b]) for b in range(3))
    last = sum(mm_t(w[6 + b], pair[b]) for b in range(3))
    own[...] = mine + first[:, :deep] + last[:, deep:]
    down = first[:, deep:]
    up = last[:, :deep]

    @pl.when(at[0] == 0)
    def _():
        partner[...] = down
        other[...] = up

    @pl.when(at[0] == 1)
    def _():
        partner[...] = up
        other[...] = down


def side_rows(at, partner, other, rows):
    rows[at[0]] = other[...]
    rows[1 - at[0]] = partner[...]
    return rows[0], rows[1]


def deep_forward(at, partner, mine, other, w, upstream, output, grad, rows):
    before, after = side_rows(at, partner, other, rows)
    y = [sum(mm(w[3 * a + b], row) for a, row in enumerate((before, mine[...], after))) for b in range(3)]
    preact = y[1] + moved(y[0], 1, 1) + moved(y[2], -1, 1)
    sigma = jax.nn.sigmoid(preact)
    output[...] = (preact * sigma).astype(BF)
    grad[...] = (upstream[...].astype(F32) * (sigma * (1.0 + preact * (1.0 - sigma)))).astype(BF)


def deep_backward(at, partner, mine, other, unit, w, out, rows):
    before, after = side_rows(at, partner, other, rows)
    turned = [mm_t(unit[...], row).astype(BF) for row in (after, mine[...], before)]
    z = [sum(mm(row, w[3 * a + b]) for a, row in enumerate(turned)) for b in range(3)]
    z = z[1] + moved(z[0], -1, 0) + moved(z[2], 1, 0)
    out[...] = z.T.astype(BF)


def fine_backward(at, partner, mine, other, spread, w, out, rows):
    before, after = side_rows(at, partner, other, rows)
    h = [[mm_t(spread[b], row).astype(BF) for b in range(3)] for row in (before, mine[...], after)]
    pieces, _, part, _ = out.shape
    for r, order in enumerate(((1, 1, 0), (2, 1, 1))):
        y = sum(mm(h[order[a]][b], w[3 * a + b]) for a in range(3) for b in range(3)).astype(BF)
        for k in range(pieces):
            out[k, r] = y[k * part : (k + 1) * part]


def slices(x, pooled, pick, out):
    size = out.shape[1]
    wide = x.shape[0]
    for j in range(MEMBERS):
        rows = pick[j * size : (j + 1) * size]
        out[j, :, :wide] = mm_t(rows, x[...]).astype(BF)
        out[j, :, wide:] = mm(rows, pooled[...]).astype(BF)


def edges(slab, first, last):
    first[...] = slab[0]
    last[...] = slab[MEMBERS - 1]


def tables(slab, first, last, box, fine, deep):
    size = slab.shape[1]
    cols = deep.shape[1] // MEMBERS
    wide = box.shape[1]
    blocks = [first[...]] + [slab[i] for i in range(MEMBERS)] + [last[...]]
    for i, block in enumerate(blocks):
        row = block[:, wide:].astype(F32)
        turned = [moved(row, 1, 1).astype(BF), block[:, wide:], moved(row, -1, 1).astype(BF)]
        for a in range(3):
            home = i - a
            if 0 <= home < MEMBERS:
                for b in range(3):
                    t = 3 * a + b
                    deep[t * size : (t + 1) * size, home * cols : (home + 1) * cols] = turned[b]
    stack = jnp.concatenate([block[:, :wide] for block in blocks])
    for b in range(3):
        u = [mm_t(stack, box[(3 * a + b) * cols : (3 * a + b + 1) * cols]) for a in range(3)]
        u = [[v[i * size : (i + 1) * size] for i in range(MEMBERS + 2)] for v in u]
        for i in range(MEMBERS):
            rows = (u[0][i + 1] + u[2][i], u[1][i + 1], u[2][i + 1] + u[0][i + 2])
            for a in range(3):
                t = 3 * a + b
                fine[t * size : (t + 1) * size, i * cols : (i + 1) * cols] = rows[a].astype(BF)


def weight_part(at, one, two, four, eight, table, order, out0, out1, out2, out3, grads, parts):
    cols = one.shape[1]
    blocks = [one[...], two[...]] + [four[i] for i in range(2)] + [eight[i] for i in range(4)]
    for r, block in enumerate(blocks):
        grads[jnp.bitwise_xor(at[1], r)] = block
    total = sum(mm_t(table[:, i * cols : (i + 1) * cols], grads[i]) for i in range(MEMBERS))
    parts[...] = mm(order[...], total.astype(BF)).astype(BF)
    size = out0.shape[1]
    for step, out in enumerate((out0, out1, out2, out3)):
        for half in range(2):
            place = (half * 4 + jnp.bitwise_and(at[2] + step, 3)) * size
            out[half] = parts[pl.ds(pl.multiple_of(place, 32), size)]


def weight_half(at, own, got1, got2, got3, keep, send):
    def total(half):
        return sum(v[half].astype(F32) for v in (own, got1, got2, got3))

    keep[...] = total(at[3])
    send[...] = total(1 - at[3]).astype(BF)


def weight_sum(keep, got, out):
    total = keep[...] + got[...].astype(F32)
    grain = out.shape[1]
    for t in range(9):
        out[t] = total[t * grain : (t + 1) * grain]


def on_device(latent, conv_fine, conv_deep, upstream):
    wide = lax.axis_size("wide")
    pieces = lax.axis_size("narrow")
    groups = wide // MEMBERS
    near = [[MEMBERS * g + j for j in range(MEMBERS)] for g in range(groups)]
    me = lax.axis_index("wide").astype(jnp.int32)
    at = jnp.stack([me % 2, me % 8, me // 8 % 4, me // 32])
    rows, part, depth = latent.shape
    cols = part * pieces
    deep = cols // 2
    grain = depth // wide
    size = groups * grain
    block = -(-9 * grain // 32) * 32
    w_fine = conv_fine.transpose(0, 1, 3, 2).reshape(9, -1, depth)
    w_deep = conv_deep.transpose(0, 1, 3, 2).reshape(9, -1, depth)
    fine = w_fine.shape[1]
    full = w_deep.shape[1]
    box = jnp.asarray(box_matrix(cols, pieces), BF)
    spread = jnp.asarray(spread_matrix(cols), BF)
    pick = jnp.asarray(channel_matrix(depth, groups), BF)
    order = jnp.asarray(owner_matrix(groups, grain, block), BF)
    unit = jnp.asarray(np.eye(deep), BF)

    def everyone(v):
        return lax.all_to_all(jnp.broadcast_to(v[None], (pieces,) + v.shape), "narrow", 0, 0)

    def swap(v, bit):
        return lax.ppermute(v, "wide", [(i, i ^ bit) for i in range(wide)])

    def pairs(to_partner, to_other):
        other = lax.ppermute(to_other, "wide", [(i, i - 1 + 2 * (i % 2)) for i in range(1, wide - 1)])
        return swap(to_partner, 1), other

    x = everyone(latent).reshape(pieces * rows * part, depth)
    own, partner, other = call(
        fine_forward,
        [shape((fine, deep), F32)] * 3,
        (at, x, box, w_fine),
        flops=2 * 9 * deep * depth * (2 * cols + 2 * fine),
    )
    partner, other = pairs(partner, other)
    pooled = everyone((own + partner + other).astype(BF)).reshape(depth, deep)
    partner, other = pairs(pooled, pooled)
    output, grad_pre = call(
        deep_forward,
        [shape((full, deep))] * 2,
        (at, partner, pooled, other, w_deep, upstream[0].T),
        [pltpu.VMEM((2, depth, deep), BF)],
        flops=2 * 9 * deep * depth * full,
    )
    pre_partner, other = pairs(grad_pre, grad_pre)
    partial = call(
        deep_backward,
        shape((depth, deep)),
        (at, pre_partner, grad_pre, other, unit, w_deep),
        [pltpu.VMEM((2, full, deep), BF)],
        flops=2 * 9 * deep * depth * full,
    )
    partial = lax.all_to_all(partial.reshape(pieces, fine, deep), "narrow", 0, 0)
    grad_pool = jnp.sum(partial.astype(F32), axis=0).astype(BF)
    pool_partner, other = pairs(grad_pool, grad_pool)
    back = call(
        fine_backward,
        shape((pieces, rows, part, depth)),
        (at, pool_partner, grad_pool, other, spread, w_fine),
        [pltpu.VMEM((2, fine, deep), BF)],
        flops=2 * 18 * cols * depth * fine,
    )
    partial = lax.all_to_all(back, "narrow", 0, 0)
    grad_latent = jnp.sum(partial.astype(F32), axis=0).astype(BF)

    slab = call(
        slices,
        shape((MEMBERS, size, rows * cols + deep)),
        (x, pooled, pick),
        flops=2 * depth * depth * (rows * cols + deep),
        behind=(grad_pre,),
    )
    slab = lax.all_to_all(slab, "wide", 0, 0, axis_index_groups=near)
    first, last = call(edges, [shape(slab.shape[1:])] * 2, (slab,), behind=(grad_pool,))
    first, last = (
        lax.ppermute(last, "wide", [(i, i + MEMBERS) for i in range(wide - MEMBERS)]),
        lax.ppermute(first, "wide", [(i + MEMBERS, i) for i in range(wide - MEMBERS)]),
    )
    fine_table, deep_table = call(
        tables,
        [shape((9 * size, MEMBERS * deep))] * 2,
        (slab, first, last, box),
        flops=2 * 10 * size * box.size,
    )

    def owners(table, one, two, behind):
        width = one.shape[0]
        four = swap(jnp.stack([one, two]), 2)
        eight = swap(jnp.concatenate([one[None], two[None], four]), 4)
        parts = call(
            weight_part,
            [shape((2, block, width))] * 4,
            (at, one, two, four, eight, table, order),
            [pltpu.VMEM((MEMBERS, width, deep), BF), pltpu.VMEM((groups * block, width), BF)],
            flops=2 * 9 * size * MEMBERS * deep * width,
            behind=behind,
        )
        got = [
            lax.ppermute(
                parts[s], "wide", [(i, i // 32 * 32 + (i // 8 + s) % 4 * 8 + i % 8) for i in range(wide)]
            )
            for s in (1, 2, 3)
        ]
        keep, send = call(weight_half, [shape((block, width), F32), shape((block, width))], (at, parts[0], *got))
        total = call(weight_sum, shape((9, grain, width), F32), (keep, swap(send, 32)))
        return total.reshape(3, 3, grain, width)

    grad_deep = owners(deep_table, grad_pre, pre_partner, (back,))
    grad_fine = owners(fine_table, grad_pool, pool_partner, ())
    return output.T[None], grad_latent, grad_fine, grad_deep


def solution(mesh):
    return jax.shard_map(
        on_device,
        mesh=mesh,
        in_specs=(
            P("wide", "narrow", None),
            P(None, None, None, "narrow"),
            P(None, None, None, "narrow"),
            P("wide", None, "narrow"),
        ),
        out_specs=(
            P("wide", None, "narrow"),
            P("wide", "narrow", None),
            P(None, None, "wide", "narrow"),
            P(None, None, "wide", "narrow"),
        ),
        check_vma=False,
    )
```

time: 257 us -> 184 us (0.72)
  local copies, waits for them, and re-layouts: 43.2 us -> 6.44 us
  waiting for transfers between devices: 72 us -> 40.5 us
  starting transfers between devices: 103 us -> 100 us
    ppermute x8 -> x18, starting transfers between devices: 13.4 us -> 69.9 us  [the longest x6 39.1 us: owners(): lax.ppermute(parts[s], 'wide', [(i, i // 32 * 32 + (i // 8 + s) % 4 * 8 +...]
    all_to_all x7 -> x3, starting transfers between devices: 67.2 us -> 15.1 us  [the longest x1 6 us: everyone(): lax.all_to_all(jnp.broadcast_to(v[None], (pieces,) + v.shape), 'narrow',...]
    unnamed x54 -> x20, local copies, waits for them, and re-layouts: 30.8 us -> 4.5 us
    all_to_all x7 -> x3, waiting for transfers between devices: 37.7 us -> 16.6 us  [the longest x1 13.9 us: everyone(): lax.all_to_all(jnp.broadcast_to(v[None], (pieces,) + v.shape), 'narrow',...]
    all_to_all x2 -> x1, waiting for transfers between devices: 16 us -> 6.89 us  [on_device(): slab = lax.all_to_all(slab, 'wide', 0, 0, axis_index_groups=near)]
    all_to_all x2 -> x1, starting transfers between devices: 19.1 us -> 12.6 us  [on_device(): slab = lax.all_to_all(slab, 'wide', 0, 0, axis_index_groups=near)]
    all_to_all x3 -> x0, local copies, waits for them, and re-layouts: 4.6 us -> none  [the longest x2 3.43 us: everyone(): lax.all_to_all(jnp.broadcast_to(v[None], (count,) + v.shape), split_axis=...]
    ppermute x8 -> x18, waiting for transfers between devices: 18.2 us -> 17.1 us  [the longest x10 13.4 us: swap(): return lax.ppermute(v, 'wide', [(i, i ^ bit) for i in range(wide)])]
  transfers between devices with their start and end apart: 21 -> 26, of which waited for: 13 -> 13; matrix products, arithmetic and copies ran while one was open for 9% -> 1% of each run, Pallas kernels for 7% -> 9%
where the time goes in v3:
time: 184 us; the launch traced here: 183 us
  starting transfers between devices  100 us (54%)
  waiting for transfers between devices  40.5 us (22%)
  Pallas kernels  23.1 us (13%)
  blocking collectives  11.2 us (6%)
  local copies, waits for them, and re-layouts  6.44 us (4%)
    ppermute x6, starting transfers between devices, owners(): lax.ppermute(parts[s], 'wide', [(i, i // 32 * 32 + (i // 8 + s) % 4 * 8 +...  39.1 us
    ppermute x10, starting transfers between devices, swap(): return lax.ppermute(v, 'wide', [(i, i ^ bit) for i in range(wide)])  24.9 us
    pallas_call x13, Pallas kernels, call(): pl.pallas_call(kernel, out_shape=outs, in_specs=[smem if a.dtype == jnp.i...  23.1 us
    all_to_all x1, waiting for transfers between devices, everyone(): lax.all_to_all(jnp.broadcast_to(v[None], (pieces,) + v.shape), 'narrow',...  13.9 us
    ppermute x10, waiting for transfers between devices, swap(): return lax.ppermute(v, 'wide', [(i, i ^ bit) for i in range(wide)])  13.4 us
    all_to_all x1, starting transfers between devices, on_device(): slab = lax.all_to_all(slab, 'wide', 0, 0, axis_index_groups=near)  12.6 us
    all_to_all x1, blocking collectives, everyone(): lax.all_to_all(jnp.broadcast_to(v[None], (pieces,) + v.shape), 'narrow',...  11.2 us
    all_to_all x1, waiting for transfers between devices, on_device(): slab = lax.all_to_all(slab, 'wide', 0, 0, axis_index_groups=near)  6.89 us
  transfers between devices with their start and end apart: 26, of which 13 were waited for; matrix products, arithmetic and copies ran while one was open for 1% of the time, Pallas kernels for 9%

profile of v3, /device:TPU:32, one launch (start us, length us, event | category | flops | bytes accessed | tf_op | source)
XLA Modules:
  0.0 183.4 jit_solution(16399620452575338)
XLA Ops:
  0.6 1.9 %broadcast_in_dim.6 = bf16[4,2,64,640]{3,2,1,0:T(8,128)(2,1)} broadcast(bf16[2,64,640]{2,1,0:T(8,128)(2,1)} %param.9), dimensions={1,2,3} | broadcast | bytes 819200 | tf_op jit(solution)/shard_map/broadcast_in_dim | solution.py:244
  2.6 6.0 %all-to-all-start = ((bf16[4,2,64,640]{3,2,1,0:T(8,128)(2,1)}), bf16[4,2,64,640]{3,2,1,0:T(8,128)(2,1)S(1)}, u32[]{:S(2)}, u32[]{:S(2)}) async-start(bf16[4,2,64,640]{3,2,1,0:T(8,128)(2,1)} %broadcast_in_dim.6), calls=%async_computation | async-start | bytes 1310720 | tf_op jit(solution)/shard_map/all_to_all | solution.py:244
  8.6 13.9 %all-to-all-done = bf16[4,2,64,640]{3,2,1,0:T(8,128)(2,1)S(1)} async-done(((bf16[4,2,64,640]{3,2,1,0:T(8,128)(2,1)}), bf16[4,2,64,640]{3,2,1,0:T(8,128)(2,1)S(1)}, u32[]{:S(2)}, u32[]{:S(2)}) %all-to-all-start) | async-done | bytes 655392 | tf_op jit(solution)/shard_map/all_to_all | solution.py:244
  24.1 2.4 %shard_map.120 = (f32[160,128]{1,0:T(8,128)S(1)}, f32[160,128]{1,0:T(8,128)S(1)}, f32[160,128]{1,0:T(8,128)S(1)}) custom-call(s32[4]{0:T(128)S(1)} %pad_add_fusion.refs_0_, bf16[512,640]{1,0:T(8,128)(2,1)S(1)} %bitcast.27, bf16[1152,512]{1,0:T(8,128)(2,1)S(1)} %copy-done.7, bf16[9,160,640]{2,1,0:T(8,128)(2,1)S(1)} %bitcast.44), custom_call_target="tpu_custom_call" | custom-call | flops 1226833920 | bytes 3678224 | tf_op jit(solution)/shard_map/pallas_call | solution.py:86
  28.0 11.2 %all_to_all.25 = bf16[4,160,128]{2,1,0:T(8,128)(2,1)S(1)} all-to-all(bf16[4,160,128]{2,1,0:T(8,128)(2,1)S(1)} %broadcast_in_dim.7), channel_id=1, replica_groups=mesh['wide'=64,'narrow'=4] {'narrow'}, dimensions={0} | all-to-all | bytes 327680 | tf_op jit(solution)/shard_map/all_to_all | solution.py:244
  39.2 3.9 %collective-permute-start.2 = (bf16[640,128]{1,0:T(8,128)(2,1)S(1)}, bf16[640,128]{1,0:T(8,128)(2,1)S(1)}, u32[]{:S(2)}, u32[]{:S(2)}) collective-permute-start(bf16[640,128]{1,0:T(8,128)(2,1)S(1)} %bitcast.31), channel_id=1, source_target_pairs={{0,4},{4,0},{8,12},{12,8},{16,20},{20,16},{24,28},{28,24},{32,36},... | collective-permute-start | bytes 491528 | tf_op jit(solution)/shard_map/ppermute | solution.py:247
  44.1 2.4 %shard_map.121 = (bf16[320,128]{1,0:T(8,128)(2,1)}, bf16[320,128]{1,0:T(8,128)(2,1)S(1)}) custom-call(s32[4]{0:T(128)S(1)} %pad_add_fusion.refs_0_, bf16[640,128]{1,0:T(8,128)(2,1)S(1)} %collective-permute-done.2.refs_1_, bf16[640,128]{1,0:T(8,128)(2,1)S(1)} %bitcast.33, bf16[640,128]{1,0:T(8,128)(2,1)S(1)} %collective-permute-done.3.refs_3_, ...), custom_call_target="tpu_custom_call" | custom-call | flops 471859200 | bytes 4259856 | tf_op jit(solution)/shard_map/pallas_call | solution.py:86
  46.6 6.7 %collective-permute-start.4 = (bf16[320,128]{1,0:T(8,128)(2,1)S(1)}, bf16[320,128]{1,0:T(8,128)(2,1)S(1)}, u32[]{:S(2)}, u32[]{:S(2)}) collective-permute-start(bf16[320,128]{1,0:T(8,128)(2,1)S(1)} %get-tuple-element.29.refs_2_.refs_3_.refs_1_), channel_id=1, source_target_pairs={{0,4},{4,0},{8,12},{12,8},{16,20},{20,16},{24,28},{28,24},{32,36},... | collective-permute-start | bytes 245768 | tf_op jit(solution)/shard_map/ppermute | solution.py:247
  54.2 2.6 %shard_map.122 = bf16[640,128]{1,0:T(8,128)(2,1)} custom-call(s32[4]{0:T(128)S(1)} %pad_add_fusion.refs_0_, bf16[320,128]{1,0:T(8,128)(2,1)S(1)} %collective-permute-done.4.refs_1_.refs_2_, bf16[320,128]{1,0:T(8,128)(2,1)S(1)} %get-tuple-element.29.refs_2_.refs_3_.refs_1_, bf16[320,128]{1,0:T(8,128)(2,1)S(1)} %collective-permute-done.5.refs_3_, ...), custom_call_target="tpu_custom_call" | custom-call | flops 471859200 | bytes 3964944 | tf_op jit(solution)/shard_map/pallas_call | solution.py:86
  56.8 4.7 %all-to-all-start.2 = ((bf16[4,160,128]{2,1,0:T(8,128)(2,1)}), bf16[4,160,128]{2,1,0:T(8,128)(2,1)S(1)}, u32[]{:S(2)}, u32[]{:S(2)}) async-start(bf16[4,160,128]{2,1,0:T(8,128)(2,1)} %bitcast.15), calls=%async_computation.2 | async-start | bytes 327680 | tf_op jit(solution)/shard_map/all_to_all | solution.py:278
  61.4 2.8 %shard_map.124 = bf16[8,80,640]{2,1,0:T(8,128)(2,1)} custom-call(bf16[512,640]{1,0:T(8,128)(2,1)S(1)} %bitcast.28, bf16[640,128]{1,0:T(8,128)(2,1)S(1)} %bitcast.34, bf16[640,640]{1,0:T(8,128)(2,1)S(1)} %copy-done.2, bf16[320,128]{1,0:T(8,128)(2,1)S(1)} %get-tuple-element.29.refs_2_.refs_3_.refs_1_), custom_call_target="tpu_custom_call" | custom-call | flops 524288000 | bytes 1638400 | tf_op jit(solution)/shard_map/pallas_call | solution.py:86
  64.2 2.6 %all-to-all-done.2 = bf16[4,160,128]{2,1,0:T(8,128)(2,1)S(1)} async-done(((bf16[4,160,128]{2,1,0:T(8,128)(2,1)}), bf16[4,160,128]{2,1,0:T(8,128)(2,1)S(1)}, u32[]{:S(2)}, u32[]{:S(2)}) %all-to-all-start.2) | async-done | bytes 163872 | tf_op jit(solution)/shard_map/all_to_all | solution.py:278
  66.9 12.6 %all-to-all-start.4 = ((bf16[8,80,640]{2,1,0:T(8,128)(2,1)}), bf16[8,80,640]{2,1,0:T(8,128)(2,1)S(1)}, u32[]{:S(2)}, u32[]{:S(2)}) async-start(bf16[8,80,640]{2,1,0:T(8,128)(2,1)} %shard_map.124), calls=%async_computation.4 | async-start | bytes 1638400 | tf_op jit(solution)/shard_map/all_to_all | solution.py:298
  82.5 4.1 %shard_map.123.refs_7_ = bf16[4,2,64,640]{3,2,1,0:T(8,128)(2,1)} custom-call(s32[4]{0:T(128)S(1)} %pad_add_fusion.refs_0_, bf16[160,128]{1,0:T(8,128)(2,1)S(1)} %collective-permute-done.6.refs_1_.refs_2_, bf16[160,128]{1,0:T(8,128)(2,1)S(1)} %reduce_sum.24.refs_2_.refs_1_, bf16[160,128]{1,0:T(8,128)(2,1)S(1)} %collective-permute-done.7.refs_3_, ...), custom_call_target="tpu_custom_call" | custom-call | flops 943718400 | bytes 2162704 | tf_op jit(solution)/shard_map/pallas_call | solution.py:86
  86.6 6.9 %all-to-all-done.4.refs_0_ = bf16[8,80,640]{2,1,0:T(8,128)(2,1)S(1)} async-done(((bf16[8,80,640]{2,1,0:T(8,128)(2,1)}), bf16[8,80,640]{2,1,0:T(8,128)(2,1)S(1)}, u32[]{:S(2)}, u32[]{:S(2)}) %all-to-all-start.4) | async-done | bytes 819232 | tf_op jit(solution)/shard_map/all_to_all | solution.py:298
  93.5 4.5 %all-to-all-start.3 = ((bf16[4,2,64,640]{3,2,1,0:T(8,128)(2,1)}), bf16[4,2,64,640]{3,2,1,0:T(8,128)(2,1)S(1)}, u32[]{:S(2)}, u32[]{:S(2)}) async-start(bf16[4,2,64,640]{3,2,1,0:T(8,128)(2,1)} %shard_map.123.refs_7_), calls=%async_computation.3 | async-start | bytes 1310720 | tf_op jit(solution)/shard_map/all_to_all | solution.py:288
  98.0 4.6 %collective-permute-start.16 = (bf16[2,320,128]{2,1,0:T(8,128)(2,1)S(1)}, bf16[2,320,128]{2,1,0:T(8,128)(2,1)S(1)}, u32[]{:S(2)}, u32[]{:S(2)}) collective-permute-start(bf16[2,320,128]{2,1,0:T(8,128)(2,1)S(1)} %pad_maximum_fusion.2), channel_id=1, source_target_pairs={{0,8},{4,12},{8,0},{12,4},{16,24},{20,28},{24,16},{28,20},{32,40},... | collective-permute-start | bytes 491528 | tf_op jit(solution)/shard_map/ppermute | solution.py:247
  102.5 4.6 %collective-permute-done.16.refs_3_ = bf16[2,320,128]{2,1,0:T(8,128)(2,1)S(1)} collective-permute-done((bf16[2,320,128]{2,1,0:T(8,128)(2,1)S(1)}, bf16[2,320,128]{2,1,0:T(8,128)(2,1)S(1)}, u32[]{:S(2)}, u32[]{:S(2)}) %collective-permute-start.16) | collective-permute-done | bytes 163872 | tf_op jit(solution)/shard_map/ppermute | solution.py:247
  107.2 3.4 %collective-permute-start.17 = (bf16[4,320,128]{2,1,0:T(8,128)(2,1)S(1)}, bf16[4,320,128]{2,1,0:T(8,128)(2,1)S(1)}, u32[]{:S(2)}, u32[]{:S(2)}) collective-permute-start(bf16[4,320,128]{2,1,0:T(8,128)(2,1)S(1)} %pad_maximum_fusion), channel_id=1, source_target_pairs={{0,16},{4,20},{8,24},{12,28},{16,0},{20,4},{24,8},{28,12},{32,48},... | collective-permute-start | bytes 983048 | tf_op jit(solution)/shard_map/ppermute | solution.py:247
  110.9 4.6 %collective-permute-start.10 = (bf16[80,640]{1,0:T(8,128)(2,1)S(1)}, bf16[80,640]{1,0:T(8,128)(2,1)S(1)}, u32[]{:S(2)}, u32[]{:S(2)}) collective-permute-start(bf16[80,640]{1,0:T(8,128)(2,1)S(1)} %get-tuple-element.30), channel_id=1, source_target_pairs={{0,32},{4,36},{8,40},{12,44},{16,48},{20,52},{24,56},{28,60},{32,6... | collective-permute-start | bytes 307208 | tf_op jit(solution)/shard_map/ppermute | solution.py:301
  116.8 2.2 %collective-permute-done.8.refs_3_ = bf16[2,160,128]{2,1,0:T(8,128)(2,1)S(1)} collective-permute-done((bf16[2,160,128]{2,1,0:T(8,128)(2,1)S(1)}, bf16[2,160,128]{2,1,0:T(8,128)(2,1)S(1)}, u32[]{:S(2)}, u32[]{:S(2)}) %collective-permute-start.8) | collective-permute-done | bytes 81952 | tf_op jit(solution)/shard_map/ppermute | solution.py:247
  119.0 1.9 %collective-permute-start.9 = (bf16[4,160,128]{2,1,0:T(8,128)(2,1)S(1)}, bf16[4,160,128]{2,1,0:T(8,128)(2,1)S(1)}, u32[]{:S(2)}, u32[]{:S(2)}) collective-permute-start(bf16[4,160,128]{2,1,0:T(8,128)(2,1)S(1)} %pad_maximum_fusion.1), channel_id=1, source_target_pairs={{0,16},{4,20},{8,24},{12,28},{16,0},{20,4},{24,8},{28,12},{32,48},... | collective-permute-start | bytes 491528 | tf_op jit(solution)/shard_map/ppermute | solution.py:247
  122.1 2.1 %shard_map.126 = (bf16[720,1024]{1,0:T(8,128)(2,1)S(1)}, bf16[720,1024]{1,0:T(8,128)(2,1)S(1)}) custom-call(bf16[8,80,640]{2,1,0:T(8,128)(2,1)S(1)} %all-to-all-done.4.refs_0_, bf16[80,640]{1,0:T(8,128)(2,1)S(1)} %collective-permute-done.10.refs_1_, bf16[80,640]{1,0:T(8,128)(2,1)S(1)} %collective-permute-done.11.refs_2_, bf16[1152,512]{1,0:T(8,128)(2,1)S(1)} %copy-done.7), custom_call_target="tpu_custom_call" | custom-call | flops 943718400 | bytes 2203648 | tf_op jit(solution)/shard_map/pallas_call | solution.py:86
  124.2 2.9 %shard_map.130 = (bf16[2,96,320]{2,1,0:T(8,128)(2,1)S(1)}, bf16[2,96,320]{2,1,0:T(8,128)(2,1)S(1)}, bf16[2,96,320]{2,1,0:T(8,128)(2,1)S(1)}, bf16[2,96,320]{2,1,0:T(8,128)(2,1)S(1)}) custom-call(s32[4]{0:T(128)S(1)} %pad_add_fusion.refs_0_, bf16[320,128]{1,0:T(8,128)(2,1)S(1)} %get-tuple-element.29.refs_2_.refs_3_.refs_1_, ...), custom_call_target="tpu_custom_call" | custom-call | flops 471859200 | bytes 3235856 | tf_op jit(solution)/shard_map/pallas_call | solution.py:86
  127.1 18.5 %collective-permute-start.18 = (bf16[2,96,320]{2,1,0:T(8,128)(2,1)S(1)}, bf16[2,96,320]{2,1,0:T(8,128)(2,1)S(1)}, u32[]{:S(2)}, u32[]{:S(2)}) collective-permute-start(bf16[2,96,320]{2,1,0:T(8,128)(2,1)S(1)} %get-tuple-element.41), channel_id=1, source_target_pairs={{0,32},{4,36},{8,40},{12,44},{16,48},{20,52},{24,56},{28,60},{32,6... | collective-permute-start | bytes 368648 | tf_op jit(solution)/shard_map/ppermute | solution.py:324
  145.6 15.7 %collective-permute-start.19 = (bf16[2,96,320]{2,1,0:T(8,128)(2,1)S(1)}, bf16[2,96,320]{2,1,0:T(8,128)(2,1)S(1)}, u32[]{:S(2)}, u32[]{:S(2)}) collective-permute-start(bf16[2,96,320]{2,1,0:T(8,128)(2,1)S(1)} %get-tuple-element.42), channel_id=1, source_target_pairs={{0,64},{4,68},{8,72},{12,76},{16,80},{20,84},{24,88},{28,92},{32,9... | collective-permute-start | bytes 368648 | tf_op jit(solution)/shard_map/ppermute | solution.py:324
  161.3 2.4 %shard_map.127 = (bf16[2,96,160]{2,1,0:T(8,128)(2,1)S(1)}, bf16[2,96,160]{2,1,0:T(8,128)(2,1)S(1)}, bf16[2,96,160]{2,1,0:T(8,128)(2,1)S(1)}, bf16[2,96,160]{2,1,0:T(8,128)(2,1)S(1)}) custom-call(s32[4]{0:T(128)S(1)} %pad_add_fusion.refs_0_, bf16[160,128]{1,0:T(8,128)(2,1)S(1)} %reduce_sum.24.refs_2_.refs_1_, ...), custom_call_target="tpu_custom_call" | custom-call | flops 235929600 | bytes 2908176 | tf_op jit(solution)/shard_map/pallas_call | solution.py:86
  163.8 2.1 %collective-permute-start.12 = (bf16[2,96,160]{2,1,0:T(8,128)(2,1)S(1)}, bf16[2,96,160]{2,1,0:T(8,128)(2,1)S(1)}, u32[]{:S(2)}, u32[]{:S(2)}) collective-permute-start(bf16[2,96,160]{2,1,0:T(8,128)(2,1)S(1)} %get-tuple-element.34), channel_id=1, source_target_pairs={{0,32},{4,36},{8,40},{12,44},{16,48},{20,52},{24,56},{28,60},{32,6... | collective-permute-start | bytes 184328 | tf_op jit(solution)/shard_map/ppermute | solution.py:324
  165.9 2.8 %collective-permute-start.14 = (bf16[2,96,160]{2,1,0:T(8,128)(2,1)S(1)}, bf16[2,96,160]{2,1,0:T(8,128)(2,1)S(1)}, u32[]{:S(2)}, u32[]{:S(2)}) collective-permute-start(bf16[2,96,160]{2,1,0:T(8,128)(2,1)S(1)} %get-tuple-element.36), channel_id=1, source_target_pairs={{0,96},{4,100},{8,104},{12,108},{16,112},{20,116},{24,120},{28,124... | collective-permute-start | bytes 184328 | tf_op jit(solution)/shard_map/ppermute | solution.py:324
  169.7 2.3 %collective-permute-done.13.refs_3_ = bf16[2,96,160]{2,1,0:T(8,128)(2,1)S(1)} collective-permute-done((bf16[2,96,160]{2,1,0:T(8,128)(2,1)S(1)}, bf16[2,96,160]{2,1,0:T(8,128)(2,1)S(1)}, u32[]{:S(2)}, u32[]{:S(2)}) %collective-permute-start.13) | collective-permute-done | bytes 61472 | tf_op jit(solution)/shard_map/ppermute | solution.py:324
  172.6 3.4 %collective-permute-start.15 = (bf16[96,160]{1,0:T(8,128)(2,1)S(1)}, bf16[96,160]{1,0:T(8,128)(2,1)S(1)}, u32[]{:S(2)}, u32[]{:S(2)}) collective-permute-start(bf16[96,160]{1,0:T(8,128)(2,1)S(1)} %get-tuple-element.38), channel_id=1, source_target_pairs={{0,128},{4,132},{8,136},{12,140},{16,144},{20,148},{24,152},{28,15... | collective-permute-start | bytes 92168 | tf_op jit(solution)/shard_map/ppermute | solution.py:247
  176.0 5.1 %collective-permute-done.15.refs_1_ = bf16[96,160]{1,0:T(8,128)(2,1)S(1)} collective-permute-done((bf16[96,160]{1,0:T(8,128)(2,1)S(1)}, bf16[96,160]{1,0:T(8,128)(2,1)S(1)}, u32[]{:S(2)}, u32[]{:S(2)}) %collective-permute-start.15) | collective-permute-done | bytes 30752 | tf_op jit(solution)/shard_map/ppermute | solution.py:247
  (64 shorter events, 14.6 us)
Async XLA Ops:
  0.6 22.0 %copy-start.7 = (bf16[1152,512]{1,0:T(8,128)(2,1)S(1)}, bf16[1152,512]{1,0:T(8,128)(2,1)}, u32[]{:S(2)}) copy-start(bf16[1152,512]{1,0:T(8,128)(2,1)} %constant.75.clone.refs_2_.refs_3_) | copy-start | bytes 3538948
  2.6 20.0 %all-to-all-start = ((bf16[4,2,64,640]{3,2,1,0:T(8,128)(2,1)}), bf16[4,2,64,640]{3,2,1,0:T(8,128)(2,1)S(1)}, u32[]{:S(2)}, u32[]{:S(2)}) async-start(bf16[4,2,64,640]{3,2,1,0:T(8,128)(2,1)} %broadcast_in_dim.6), calls=%async_computation | async-start | bytes 1310720 | tf_op jit(solution)/shard_map/all_to_all | solution.py:244
  24.1 20.0 %copy-start = (bf16[3,3,640,320]{2,3,1,0:T(8,128)(2,1)S(1)}, bf16[3,3,640,320]{2,3,1,0:T(8,128)(2,1)}, u32[]{:S(2)}) copy-start(bf16[3,3,640,320]{2,3,1,0:T(8,128)(2,1)} %param.11) | copy-start | bytes 11059204
  24.1 20.0 %copy-start.3 = (bf16[1,128,320]{1,2,0:T(8,128)(2,1)S(1)}, bf16[1,128,320]{1,2,0:T(8,128)(2,1)}, u32[]{:S(2)}) copy-start(bf16[1,128,320]{1,2,0:T(8,128)(2,1)} %param.12) | copy-start | bytes 245764
  26.5 1.4 collective-permute-start
  26.6 1.3 collective-permute-start.1
  39.2 4.9 %collective-permute-start.2 = (bf16[640,128]{1,0:T(8,128)(2,1)S(1)}, bf16[640,128]{1,0:T(8,128)(2,1)S(1)}, u32[]{:S(2)}, u32[]{:S(2)}) collective-permute-start(bf16[640,128]{1,0:T(8,128)(2,1)S(1)} %bitcast.31), channel_id=1, source_target_pairs={{0,4},{4,0},{8,12},{12,8},{16,20},{20,16},{24,28},{28,24},{32,36},... | collective-permute-start | bytes 491528 | tf_op jit(solution)/shard_map/ppermute | solution.py:247
  43.1 1.0 collective-permute-start.3
  44.1 10.1 %copy-start.4 = (bf16[128,128]{1,0:T(8,128)(2,1)S(1)}, bf16[128,128]{1,0:T(8,128)(2,1)}, u32[]{:S(2)}) copy-start(bf16[128,128]{1,0:T(8,128)(2,1)} %constant.79.clone.refs_4_) | copy-start | bytes 98308
  46.6 14.9 %copy-start.2 = (bf16[640,640]{1,0:T(8,128)(2,1)S(1)}, bf16[640,640]{1,0:T(8,128)(2,1)}, u32[]{:S(2)}) copy-start(bf16[640,640]{1,0:T(8,128)(2,1)} %constant.77.clone.refs_2_) | copy-start | bytes 2457604
  46.6 7.6 %collective-permute-start.4 = (bf16[320,128]{1,0:T(8,128)(2,1)S(1)}, bf16[320,128]{1,0:T(8,128)(2,1)S(1)}, u32[]{:S(2)}, u32[]{:S(2)}) collective-permute-start(bf16[320,128]{1,0:T(8,128)(2,1)S(1)} %get-tuple-element.29.refs_2_.refs_3_.refs_1_), channel_id=1, source_target_pairs={{0,4},{4,0},{8,12},{12,8},{16,20},{20,16},{24,28},{28,24},{32,36},... | collective-permute-start | bytes 245768 | tf_op jit(solution)/shard_map/ppermute | solution.py:247
  53.3 0.9 collective-permute-start.5
  56.8 10.1 %all-to-all-start.2 = ((bf16[4,160,128]{2,1,0:T(8,128)(2,1)}), bf16[4,160,128]{2,1,0:T(8,128)(2,1)S(1)}, u32[]{:S(2)}, u32[]{:S(2)}) async-start(bf16[4,160,128]{2,1,0:T(8,128)(2,1)} %bitcast.15), calls=%async_computation.2 | async-start | bytes 327680 | tf_op jit(solution)/shard_map/all_to_all | solution.py:278
  64.2 16.8 %copy-start.8 = (bf16[3,256,128]{2,1,0:T(8,128)(2,1)S(1)}, bf16[3,256,128]{2,1,0:T(8,128)(2,1)}, u32[]{:S(2)}) copy-start(bf16[3,256,128]{2,1,0:T(8,128)(2,1)} %constant.76.clone.refs_4_) | copy-start | bytes 589828
  66.9 26.6 %all-to-all-start.4 = ((bf16[8,80,640]{2,1,0:T(8,128)(2,1)}), bf16[8,80,640]{2,1,0:T(8,128)(2,1)S(1)}, u32[]{:S(2)}, u32[]{:S(2)}) async-start(bf16[8,80,640]{2,1,0:T(8,128)(2,1)} %shard_map.124), calls=%async_computation.4 | async-start | bytes 1638400 | tf_op jit(solution)/shard_map/all_to_all | solution.py:298
  79.5 1.5 collective-permute-start.6
  80.1 0.9 collective-permute-start.7
  93.5 89.1 %all-to-all-start.3 = ((bf16[4,2,64,640]{3,2,1,0:T(8,128)(2,1)}), bf16[4,2,64,640]{3,2,1,0:T(8,128)(2,1)S(1)}, u32[]{:S(2)}, u32[]{:S(2)}) async-start(bf16[4,2,64,640]{3,2,1,0:T(8,128)(2,1)} %shard_map.123.refs_7_), calls=%async_computation.3 | async-start | bytes 1310720 | tf_op jit(solution)/shard_map/all_to_all | solution.py:288
  98.0 9.2 %collective-permute-start.16 = (bf16[2,320,128]{2,1,0:T(8,128)(2,1)S(1)}, bf16[2,320,128]{2,1,0:T(8,128)(2,1)S(1)}, u32[]{:S(2)}, u32[]{:S(2)}) collective-permute-start(bf16[2,320,128]{2,1,0:T(8,128)(2,1)S(1)} %pad_maximum_fusion.2), channel_id=1, source_target_pairs={{0,8},{4,12},{8,0},{12,4},{16,24},{20,28},{24,16},{28,20},{32,40},... | collective-permute-start | bytes 491528 | tf_op jit(solution)/shard_map/ppermute | solution.py:247
  107.2 17.0 %collective-permute-start.17 = (bf16[4,320,128]{2,1,0:T(8,128)(2,1)S(1)}, bf16[4,320,128]{2,1,0:T(8,128)(2,1)S(1)}, u32[]{:S(2)}, u32[]{:S(2)}) collective-permute-start(bf16[4,320,128]{2,1,0:T(8,128)(2,1)S(1)} %pad_maximum_fusion), channel_id=1, source_target_pairs={{0,16},{4,20},{8,24},{12,28},{16,0},{20,4},{24,8},{28,12},{32,48},... | collective-permute-start | bytes 983048 | tf_op jit(solution)/shard_map/ppermute | solution.py:247
  110.6 8.4 %collective-permute-start.8 = (bf16[2,160,128]{2,1,0:T(8,128)(2,1)S(1)}, bf16[2,160,128]{2,1,0:T(8,128)(2,1)S(1)}, u32[]{:S(2)}, u32[]{:S(2)}) collective-permute-start(bf16[2,160,128]{2,1,0:T(8,128)(2,1)S(1)} %pad_maximum_fusion.3), channel_id=1, source_target_pairs={{0,8},{4,12},{8,0},{12,4},{16,24},{20,28},{24,16},{28,20},{32,40},... | collective-permute-start | bytes 245768 | tf_op jit(solution)/shard_map/ppermute | solution.py:247
  110.9 10.1 %collective-permute-start.10 = (bf16[80,640]{1,0:T(8,128)(2,1)S(1)}, bf16[80,640]{1,0:T(8,128)(2,1)S(1)}, u32[]{:S(2)}, u32[]{:S(2)}) collective-permute-start(bf16[80,640]{1,0:T(8,128)(2,1)S(1)} %get-tuple-element.30), channel_id=1, source_target_pairs={{0,32},{4,36},{8,40},{12,44},{16,48},{20,52},{24,56},{28,60},{32,6... | collective-permute-start | bytes 307208 | tf_op jit(solution)/shard_map/ppermute | solution.py:301
  115.5 6.6 %collective-permute-start.11 = (bf16[80,640]{1,0:T(8,128)(2,1)S(1)}, bf16[80,640]{1,0:T(8,128)(2,1)S(1)}, u32[]{:S(2)}, u32[]{:S(2)}) collective-permute-start(bf16[80,640]{1,0:T(8,128)(2,1)S(1)} %get-tuple-element.31), channel_id=1, source_target_pairs={{32,0},{36,4},{40,8},{44,12},{48,16},{52,20},{56,24},{60,28},{64,3... | collective-permute-start | bytes 307208 | tf_op jit(solution)/shard_map/ppermute | solution.py:302
  119.0 42.3 %collective-permute-start.9 = (bf16[4,160,128]{2,1,0:T(8,128)(2,1)S(1)}, bf16[4,160,128]{2,1,0:T(8,128)(2,1)S(1)}, u32[]{:S(2)}, u32[]{:S(2)}) collective-permute-start(bf16[4,160,128]{2,1,0:T(8,128)(2,1)S(1)} %pad_maximum_fusion.1), channel_id=1, source_target_pairs={{0,16},{4,20},{8,24},{12,28},{16,0},{20,4},{24,8},{28,12},{32,48},... | collective-permute-start | bytes 491528 | tf_op jit(solution)/shard_map/ppermute | solution.py:247
  127.1 38.8 %collective-permute-start.18 = (bf16[2,96,320]{2,1,0:T(8,128)(2,1)S(1)}, bf16[2,96,320]{2,1,0:T(8,128)(2,1)S(1)}, u32[]{:S(2)}, u32[]{:S(2)}) collective-permute-start(bf16[2,96,320]{2,1,0:T(8,128)(2,1)S(1)} %get-tuple-element.41), channel_id=1, source_target_pairs={{0,32},{4,36},{8,40},{12,44},{16,48},{20,52},{24,56},{28,60},{32,6... | collective-permute-start | bytes 368648 | tf_op jit(solution)/shard_map/ppermute | solution.py:324
  145.6 23.0 %collective-permute-start.19 = (bf16[2,96,320]{2,1,0:T(8,128)(2,1)S(1)}, bf16[2,96,320]{2,1,0:T(8,128)(2,1)S(1)}, u32[]{:S(2)}, u32[]{:S(2)}) collective-permute-start(bf16[2,96,320]{2,1,0:T(8,128)(2,1)S(1)} %get-tuple-element.42), channel_id=1, source_target_pairs={{0,64},{4,68},{8,72},{12,76},{16,80},{20,84},{24,88},{28,92},{32,9... | collective-permute-start | bytes 368648 | tf_op jit(solution)/shard_map/ppermute | solution.py:324
  161.3 7.3 %collective-permute-start.20 = (bf16[2,96,320]{2,1,0:T(8,128)(2,1)S(1)}, bf16[2,96,320]{2,1,0:T(8,128)(2,1)S(1)}, u32[]{:S(2)}, u32[]{:S(2)}) collective-permute-start(bf16[2,96,320]{2,1,0:T(8,128)(2,1)S(1)} %get-tuple-element.43), channel_id=1, source_target_pairs={{0,96},{4,100},{8,104},{12,108},{16,112},{20,116},{24,120},{28,124... | collective-permute-start | bytes 368648 | tf_op jit(solution)/shard_map/ppermute | solution.py:324
  163.8 5.9 %collective-permute-start.12 = (bf16[2,96,160]{2,1,0:T(8,128)(2,1)S(1)}, bf16[2,96,160]{2,1,0:T(8,128)(2,1)S(1)}, u32[]{:S(2)}, u32[]{:S(2)}) collective-permute-start(bf16[2,96,160]{2,1,0:T(8,128)(2,1)S(1)} %get-tuple-element.34), channel_id=1, source_target_pairs={{0,32},{4,36},{8,40},{12,44},{16,48},{20,52},{24,56},{28,60},{32,6... | collective-permute-start | bytes 184328 | tf_op jit(solution)/shard_map/ppermute | solution.py:324
  165.9 6.1 %collective-permute-start.13 = (bf16[2,96,160]{2,1,0:T(8,128)(2,1)S(1)}, bf16[2,96,160]{2,1,0:T(8,128)(2,1)S(1)}, u32[]{:S(2)}, u32[]{:S(2)}) collective-permute-start(bf16[2,96,160]{2,1,0:T(8,128)(2,1)S(1)} %get-tuple-element.35), channel_id=1, source_target_pairs={{0,64},{4,68},{8,72},{12,76},{16,80},{20,84},{24,88},{28,92},{32,9... | collective-permute-start | bytes 184328 | tf_op jit(solution)/shard_map/ppermute | solution.py:324
  165.9 6.1 %collective-permute-start.14 = (bf16[2,96,160]{2,1,0:T(8,128)(2,1)S(1)}, bf16[2,96,160]{2,1,0:T(8,128)(2,1)S(1)}, u32[]{:S(2)}, u32[]{:S(2)}) collective-permute-start(bf16[2,96,160]{2,1,0:T(8,128)(2,1)S(1)} %get-tuple-element.36), channel_id=1, source_target_pairs={{0,96},{4,100},{8,104},{12,108},{16,112},{20,116},{24,120},{28,124... | collective-permute-start | bytes 184328 | tf_op jit(solution)/shard_map/ppermute | solution.py:324
  169.3 12.5 %collective-permute-start.21 = (bf16[96,320]{1,0:T(8,128)(2,1)S(1)}, bf16[96,320]{1,0:T(8,128)(2,1)S(1)}, u32[]{:S(2)}, u32[]{:S(2)}) collective-permute-start(bf16[96,320]{1,0:T(8,128)(2,1)S(1)} %get-tuple-element.45), channel_id=1, source_target_pairs={{0,128},{4,132},{8,136},{12,140},{16,144},{20,148},{24,152},{28,15... | collective-permute-start | bytes 184328 | tf_op jit(solution)/shard_map/ppermute | solution.py:247
  172.6 8.5 %collective-permute-start.15 = (bf16[96,160]{1,0:T(8,128)(2,1)S(1)}, bf16[96,160]{1,0:T(8,128)(2,1)S(1)}, u32[]{:S(2)}, u32[]{:S(2)}) collective-permute-start(bf16[96,160]{1,0:T(8,128)(2,1)S(1)} %get-tuple-element.38), channel_id=1, source_target_pairs={{0,128},{4,132},{8,136},{12,140},{16,144},{20,148},{24,152},{28,15... | collective-permute-start | bytes 92168 | tf_op jit(solution)/shard_map/ppermute | solution.py:247
  (3 other events, 8.2 us)

commit v4 on v3

v4 whole, which is shorter than its diff:
```python
import functools

import jax
import jax.numpy as jnp
import numpy as np
from jax import lax
from jax.experimental import pallas as pl
from jax.experimental.pallas import tpu as pltpu
from jax.sharding import PartitionSpec as P

BF = jnp.bfloat16
F32 = jnp.float32
MEMBERS = 8


def mm(a, b):
    return jnp.dot(a, b, preferred_element_type=F32)


def mm_t(a, b):
    return lax.dot_general(a, b, (((1,), (1,)), ((), ())), preferred_element_type=F32)


def channel_matrix(depth, groups):
    grain = depth // (groups * MEMBERS)
    table = np.zeros((MEMBERS, groups, grain, depth), np.float32)
    for c in range(depth):
        table[c // grain % MEMBERS, c // (MEMBERS * grain), c % grain, c] = 1.0
    return table.reshape(depth, depth)


def owner_matrix(groups, grain, block):
    table = np.zeros((groups * block, 9 * groups * grain), np.float32)
    for t in range(9):
        for g in range(groups):
            for k in range(grain):
                table[g * block + t * grain + k, (t * groups + g) * grain + k] = 1.0
    return table


def moved(y, step, axis):
    size = y.shape[axis]
    place = lax.broadcasted_iota(jnp.int32, y.shape, axis)
    edge = 0 if step == 1 else size - 1
    return jnp.where(place == edge, 0.0, pltpu.roll(y, step % size, axis))


def shape(dims, dtype=BF):
    return jax.ShapeDtypeStruct(dims, dtype)


def call(body, outs, args, scratch=(), flops=0, behind=()):
    size = sum(a.size * a.dtype.itemsize for a in args)
    smem = pl.BlockSpec(memory_space=pltpu.SMEM)
    vmem = pl.BlockSpec(memory_space=pltpu.VMEM)
    aside = pl.BlockSpec(memory_space=pl.ANY)
    count = len(args)

    def kernel(*refs):
        body(*refs[:count], *refs[count + len(behind) :])

    return pl.pallas_call(
        kernel,
        out_shape=outs,
        in_specs=[smem if a.dtype == jnp.int32 else vmem for a in args] + [aside] * len(behind),
        out_specs=jax.tree.map(lambda _: vmem, outs),
        scratch_shapes=list(scratch),
        compiler_params=pltpu.CompilerParams(vmem_limit_bytes=40 * 2**20),
        cost_estimate=pl.CostEstimate(flops=flops, bytes_accessed=size, transcendentals=0),
    )(*args, *behind)


def column_box(cols, b):
    low = 2 * lax.broadcasted_iota(jnp.int32, (cols // 2, cols), 0) + (b - 1)
    gap = lax.broadcasted_iota(jnp.int32, (cols // 2, cols), 1) - low
    return jnp.where((gap == 0) | (gap == 1), 0.25, 0.0).astype(BF)


def unit(size):
    row = lax.broadcasted_iota(jnp.int32, (size, size), 0)
    return jnp.where(row == lax.broadcasted_iota(jnp.int32, (size, size), 1), 1.0, 0.0).astype(BF)


def interleave(cols):
    place = lax.broadcasted_iota(jnp.int32, (cols, cols), 0)
    source = place // 2 + (place % 2) * (cols // 2)
    return jnp.where(source == lax.broadcasted_iota(jnp.int32, (cols, cols), 1), 1.0, 0.0).astype(BF)


def fine_rows(x):
    pieces = x.shape[0]
    return [jnp.concatenate([x[k, r] for k in range(pieces)]) for r in range(2)]


def to_sides(at, up, down, partner, other):
    up = up.astype(BF)
    down = down.astype(BF)

    @pl.when(at[0] == 0)
    def _():
        partner[...] = down
        other[...] = up

    @pl.when(at[0] == 1)
    def _():
        partner[...] = up
        other[...] = down


def fine_forward(at, x, w, own, partner, other):
    deep = own.shape[1]
    rows = fine_rows(x)
    u0, us, u1 = [], [], []
    for b in range(3):
        box = column_box(2 * deep, b)
        u = [mm(box, row) for row in rows]
        u0.append(u[0].astype(BF))
        u1.append(u[1].astype(BF))
        us.append((u[0] + u[1]).astype(BF))
    pair = [jnp.concatenate([u0[b], u1[b]]) for b in range(3)]
    mine = sum(mm_t(w[3 + b], us[b]) for b in range(3))
    first = sum(mm_t(w[b], pair[b]) for b in range(3))
    last = sum(mm_t(w[6 + b], pair[b]) for b in range(3))
    own[...] = mine + first[:, :deep] + last[:, deep:]
    to_sides(at, last[:, :deep], first[:, deep:], partner, other)


def side_rows(at, partner, other, rows):
    rows[at[0]] = other[...]
    rows[1 - at[0]] = partner[...]
    return rows[0], rows[1]


def deep_taps(w, a, row):
    y = [mm(w[3 * a + b], row) for b in range(3)]
    return y[1] + moved(y[0], 1, 1) + moved(y[2], -1, 1)


def deep_sides(at, own, got1, got2, got3, w, pooled, partner, other):
    size = own.shape[0]
    for s, piece in enumerate((own, got1, got2, got3)):
        place = jnp.bitwise_and(at[4] - s, 3) * size
        pooled[pl.ds(pl.multiple_of(place, 32), size)] = piece[...]
    row = pooled[...]
    to_sides(at, deep_taps(w, 2, row), deep_taps(w, 0, row), partner, other)


def deep_own(pooled, w, preact):
    preact[...] = deep_taps(w, 1, pooled[...])


def deep_forward(own, partner, other, upstream, output, grad):
    preact = own[...] + partner[...].astype(F32) + other[...].astype(F32)
    sigma = jax.nn.sigmoid(preact)
    output[...] = (preact * sigma).astype(BF)
    grad[...] = (upstream[...].astype(F32) * (sigma * (1.0 + preact * (1.0 - sigma)))).astype(BF)


def deep_backward(at, partner, mine, other, w, out0, out1, out2, out3, rows, whole):
    before, after = side_rows(at, partner, other, rows)
    turn = unit(mine.shape[1])
    turned = [mm_t(turn, row).astype(BF) for row in (after, mine[...], before)]
    z = [sum(mm(row, w[3 * a + b]) for a, row in enumerate(turned)) for b in range(3)]
    z = z[1] + moved(z[0], -1, 0) + moved(z[2], 1, 0)
    whole[...] = z.T.astype(BF)
    size = out0.shape[0]
    for s, out in enumerate((out0, out1, out2, out3)):
        place = jnp.bitwise_and(at[4] + s, 3) * size
        out[...] = whole[pl.ds(pl.multiple_of(place, 32), size)]


def pool_add(own, partner, other, out):
    out[...] = (own[...] + partner[...].astype(F32) + other[...].astype(F32)).astype(BF)


def pool_sum(own, got1, got2, got3, out):
    out[...] = sum(v[...].astype(F32) for v in (own, got1, got2, got3)).astype(BF)


def fine_backward(at, partner, mine, other, w, out, rows):
    before, after = side_rows(at, partner, other, rows)
    deep = mine.shape[1]
    turn = unit(deep)
    before, here, after = [mm_t(turn, row).astype(BF) for row in (before, mine[...], after)]
    weave = interleave(2 * deep)
    pieces, _, part, _ = out.shape
    top = jnp.concatenate([here, after])
    low = jnp.concatenate([before, here])
    z = []
    for b in range(3):
        both = mm(top, w[b]) + mm(low, w[6 + b])
        mid = mm(here, w[3 + b])
        z.append((both[:deep] + mid, both[deep:] + mid))
    for r in range(2):
        even = z[1][r] + z[0][r] + moved(z[2][r], 1, 0)
        late = z[1][r] + moved(z[0][r], -1, 0) + z[2][r]
        y = jnp.concatenate([(0.25 * even).astype(BF), (0.25 * late).astype(BF)])
        y = mm(weave, y).astype(BF)
        for k in range(pieces):
            out[k, r] = y[k * part : (k + 1) * part]


def fine_slices(x, pick, out):
    size = out.shape[1]
    for r, row in enumerate(fine_rows(x)):
        cols = row.shape[0]
        for j in range(MEMBERS):
            out[j, :, r * cols : (r + 1) * cols] = mm_t(pick[j * size : (j + 1) * size], row).astype(BF)


def deep_slices(pooled, pick, out):
    size = out.shape[1]
    for j in range(MEMBERS):
        out[j] = mm(pick[j * size : (j + 1) * size], pooled[...]).astype(BF)


def edges(fine, deep, first, last):
    cols = fine.shape[2] // 2
    first[:, :cols] = fine[0, :, :cols]
    first[:, cols:] = deep[0]
    last[:, :cols] = fine[MEMBERS - 1, :, cols:]
    last[:, cols:] = deep[MEMBERS - 1]


def tables(fine_slab, deep_slab, before, after, fine, deep):
    size = fine_slab.shape[1]
    cols = deep_slab.shape[2]
    wide = 2 * cols
    blocks = [before[:, wide:]] + [deep_slab[i] for i in range(MEMBERS)] + [after[:, wide:]]
    for i, block in enumerate(blocks):
        row = block.astype(F32)
        turned = [moved(row, 1, 1).astype(BF), block, moved(row, -1, 1).astype(BF)]
        for a in range(3):
            home = i - a
            if 0 <= home < MEMBERS:
                for b in range(3):
                    t = 3 * a + b
                    deep[t * size : (t + 1) * size, home * cols : (home + 1) * cols] = turned[b]
    slab = [fine_slab[i] for i in range(MEMBERS)]
    evens = jnp.concatenate([row[:, :wide] for row in slab] + [after[:, :wide]])
    odds = jnp.concatenate([before[:, :wide]] + [row[:, wide:] for row in slab])
    for b in range(3):
        box = column_box(wide, b)
        even = mm_t(evens, box)
        late = mm_t(odds, box)
        even = [even[i * size : (i + 1) * size] for i in range(MEMBERS + 1)]
        late = [late[i * size : (i + 1) * size] for i in range(MEMBERS + 1)]
        for i in range(MEMBERS):
            rows = (late[i] + even[i], even[i] + late[i + 1], late[i + 1] + even[i + 1])
            for a in range(3):
                t = 3 * a + b
                fine[t * size : (t + 1) * size, i * cols : (i + 1) * cols] = rows[a].astype(BF)


def weight_part(at, own, partner, near, far, rest, table, order, out0, out1, out2, out3, grads, parts):
    cols = own.shape[1]
    blocks = (own[...], partner[...], near[...], rest[0], far[0], rest[1], far[1], rest[2])
    for r, block in enumerate(blocks):
        grads[jnp.bitwise_xor(at[1], r)] = block
    total = sum(mm_t(table[:, i * cols : (i + 1) * cols], grads[i]) for i in range(MEMBERS))
    parts[...] = mm(order[...], total.astype(BF)).astype(BF)
    size = out0.shape[1]
    for step, out in enumerate((out0, out1, out2, out3)):
        for half in range(2):
            place = (half * 4 + jnp.bitwise_and(at[2] + step, 3)) * size
            out[half] = parts[pl.ds(pl.multiple_of(place, 32), size)]


def weight_half(at, own, got1, got2, got3, keep, send):
    def total(half):
        return sum(v[half].astype(F32) for v in (own, got1, got2, got3))

    keep[...] = total(at[3])
    send[...] = total(1 - at[3]).astype(BF)


def weight_sum(keep, got, out):
    total = keep[...] + got[...].astype(F32)
    grain = out.shape[1]
    for t in range(9):
        out[t] = total[t * grain : (t + 1) * grain]


def on_device(latent, conv_fine, conv_deep, upstream):
    wide = lax.axis_size("wide")
    pieces = lax.axis_size("narrow")
    groups = wide // MEMBERS
    near = [[MEMBERS * g + j for j in range(MEMBERS)] for g in range(groups)]
    me = lax.axis_index("wide").astype(jnp.int32)
    at = jnp.stack([me % 2, me % 8, me // 8 % 4, me // 32, lax.axis_index("narrow").astype(jnp.int32)])
    rows, part, depth = latent.shape
    cols = part * pieces
    deep = cols // 2
    grain = depth // wide
    size = groups * grain
    block = -(-9 * grain // 32) * 32
    w_fine = conv_fine.transpose(0, 1, 3, 2).reshape(9, -1, depth)
    w_deep = conv_deep.transpose(0, 1, 3, 2).reshape(9, -1, depth)
    fine = w_fine.shape[1]
    full = w_deep.shape[1]
    pick = jnp.asarray(channel_matrix(depth, groups), BF)
    order = jnp.asarray(owner_matrix(groups, grain, block), BF)

    def across(v, step):
        return lax.ppermute(v, "narrow", [(i, (i + step) % pieces) for i in range(pieces)])

    def swap(v, bit):
        return lax.ppermute(v, "wide", [(i, i ^ bit) for i in range(wide)])

    def pairs(to_partner, to_other):
        other = lax.ppermute(to_other, "wide", [(i, i - 1 + 2 * (i % 2)) for i in range(1, wide - 1)])
        return swap(to_partner, 1), other

    x = lax.all_to_all(jnp.broadcast_to(latent[None], (pieces,) + latent.shape), "narrow", 0, 0)
    own, partner, other = call(
        fine_forward,
        [shape((fine, deep), F32), shape((fine, deep)), shape((fine, deep))],
        (at, x, w_fine),
        flops=2 * 9 * deep * depth * (2 * cols + 2 * fine),
    )
    partner, other = pairs(partner, other)
    fine_slab = call(
        fine_slices,
        shape((MEMBERS, size, rows * cols)),
        (x, pick),
        flops=2 * depth * depth * rows * cols,
        behind=(own,),
    )
    fine_slab = lax.all_to_all(fine_slab, "wide", 0, 0, axis_index_groups=near)
    mine = call(pool_add, shape((fine, deep)), (own, partner, other))
    got = [across(mine, s) for s in (1, 2, 3)]
    pooled, partner, other = call(
        deep_sides,
        [shape((depth, deep)), shape((full, deep)), shape((full, deep))],
        (at, mine, *got, w_deep),
        flops=2 * 6 * deep * depth * full,
    )
    partner, other = pairs(partner, other)
    preact = call(
        deep_own, shape((full, deep), F32), (pooled, w_deep), flops=2 * 3 * deep * depth * full, behind=(pooled,)
    )
    output, grad_pre = call(deep_forward, [shape((full, deep))] * 2, (preact, partner, other, upstream[0].T))

    pre_partner, other = pairs(grad_pre, grad_pre)
    pre_near = swap(grad_pre, 2)
    parts = call(
        deep_backward,
        [shape((fine, deep))] * 4,
        (at, pre_partner, grad_pre, other, w_deep),
        [pltpu.VMEM((2, full, deep), BF), pltpu.VMEM((depth, deep), BF)],
        flops=2 * 9 * deep * depth * full,
        behind=(pre_near,),
    )
    pre_far = swap(jnp.stack([grad_pre, pre_near]), 4)
    deep_slab = call(
        deep_slices,
        shape((MEMBERS, size, deep)),
        (pooled, pick),
        flops=2 * depth * depth * deep,
        behind=(parts[0],),
    )
    deep_slab = lax.all_to_all(deep_slab, "wide", 0, 0, axis_index_groups=near)
    got = [across(parts[s], s) for s in (1, 2, 3)]
    grad_pool = call(pool_sum, shape((fine, deep)), (parts[0], *got), behind=(pre_far,))
    pool_partner, other = pairs(grad_pool, grad_pool)
    pool_near = swap(grad_pool, 2)
    pre_rest = swap(jnp.concatenate([pre_near[None], pre_far]), 1)
    back = call(
        fine_backward,
        shape((pieces, rows, part, depth)),
        (at, pool_partner, grad_pool, other, w_fine),
        [pltpu.VMEM((2, fine, deep), BF)],
        flops=2 * 18 * cols * depth * fine,
        behind=(pool_near,),
    )
    partial = lax.all_to_all(back, "narrow", 0, 0)
    grad_latent = jnp.sum(partial.astype(F32), axis=0).astype(BF)

    first, last = call(
        edges, [shape((size, cols + deep))] * 2, (fine_slab, deep_slab), behind=(grad_pool,)
    )
    before = lax.ppermute(last, "wide", [(i, i + MEMBERS) for i in range(wide - MEMBERS)])
    after = lax.ppermute(first, "wide", [(i + MEMBERS, i) for i in range(wide - MEMBERS)])
    pool_far = swap(jnp.stack([grad_pool, pool_near]), 4)
    pool_rest = swap(jnp.concatenate([pool_near[None], pool_far]), 1)
    fine_table, deep_table = call(
        tables,
        [shape((9 * size, MEMBERS * deep))] * 2,
        (fine_slab, deep_slab, before, after),
        flops=2 * 9 * size * 6 * deep * 2 * deep,
        behind=(back,),
    )

    def owners(table, *grads):
        width = grads[0].shape[0]
        parts = call(
            weight_part,
            [shape((2, block, width))] * 4,
            (at, *grads, table, order),
            [pltpu.VMEM((MEMBERS, width, deep), BF), pltpu.VMEM((groups * block, width), BF)],
            flops=2 * 9 * size * MEMBERS * deep * width,
        )
        got = [
            lax.ppermute(
                parts[s], "wide", [(i, i // 32 * 32 + (i // 8 + s) % 4 * 8 + i % 8) for i in range(wide)]
            )
            for s in (1, 2, 3)
        ]
        keep, send = call(weight_half, [shape((block, width), F32), shape((block, width))], (at, parts[0], *got))
        total = call(weight_sum, shape((9, grain, width), F32), (keep, swap(send, 32)))
        return total.reshape(3, 3, grain, width)

    grad_deep = owners(deep_table, grad_pre, pre_partner, pre_near, pre_far, pre_rest)
    grad_fine = owners(fine_table, grad_pool, pool_partner, pool_near, pool_far, pool_rest)
    return output.T[None], grad_latent, grad_fine, grad_deep


def solution(mesh):
    return jax.shard_map(
        on_device,
        mesh=mesh,
        in_specs=(
            P("wide", "narrow", None),
            P(None, None, None, "narrow"),
            P(None, None, None, "narrow"),
            P("wide", None, "narrow"),
        ),
        out_specs=(
            P("wide", None, "narrow"),
            P("wide", "narrow", None),
            P(None, None, "wide", "narrow"),
            P(None, None, "wide", "narrow"),
        ),
        check_vma=False,
    )
```

time: 184 us -> 184 us (level)
  waiting for transfers between devices: 40.5 us -> 65 us
  starting transfers between devices: 100 us -> 88.8 us
  blocking collectives: 11.2 us -> 0 us
  Pallas kernels: 23.1 us -> 20.4 us
    ppermute x1, waiting for transfers between devices: 1.08 us -> 20.8 us  [on_device(): lax.ppermute(first, 'wide', [(i + MEMBERS, i) for i in range(wide - MEMBE...]
    ppermute x6, starting transfers between devices: 39.1 us -> 24.8 us  [owners(): lax.ppermute(parts[s], 'wide', [(i, i // 32 * 32 + (i // 8 + s) % 4 * 8 +...]
    all_to_all x1 -> x0, blocking collectives: 11.2 us -> none  [everyone(): lax.all_to_all(jnp.broadcast_to(v[None], (pieces,) + v.shape), 'narrow',...]
    ppermute x0 -> x6, starting transfers between devices: none -> 9.59 us  [across(): lax.ppermute(v, 'narrow', [(i, (i + step) % pieces) for i in range(pieces)])]
    ppermute x0 -> x6, waiting for transfers between devices: none -> 6.67 us  [across(): lax.ppermute(v, 'narrow', [(i, (i + step) % pieces) for i in range(pieces)])]
    all_to_all x3, starting transfers between devices: 23.3 us -> 16.8 us  [the longest x1 7.27 us: on_device(): deep_slab = lax.all_to_all(deep_slab, 'wide', 0, 0, axis_index_groups=near)]
    all_to_all x3, waiting for transfers between devices: 23.5 us -> 17.9 us  [the longest x1 13.9 us: on_device(): lax.all_to_all(jnp.broadcast_to(latent[None], (pieces,) + latent.shape),...]
    ppermute x10 -> x12, waiting for transfers between devices: 13.4 us -> 16.6 us  [swap(): return lax.ppermute(v, 'wide', [(i, i ^ bit) for i in range(wide)])]
  transfers between devices with their start and end apart: 26 -> 34, of which waited for: 13 -> 16; matrix products, arithmetic and copies ran while one was open for 1% -> 1% of each run, Pallas kernels for 9% -> 7%
where the time goes in v4:
time: 184 us; the launch traced here: 183 us
  starting transfers between devices  88.8 us (48%)
  waiting for transfers between devices  65 us (35%)
  Pallas kernels  20.4 us (11%)
  local copies, waits for them, and re-layouts  6.76 us (4%)
    ppermute x12, starting transfers between devices, swap(): return lax.ppermute(v, 'wide', [(i, i ^ bit) for i in range(wide)])  25 us
    ppermute x6, starting transfers between devices, owners(): lax.ppermute(parts[s], 'wide', [(i, i // 32 * 32 + (i // 8 + s) % 4 * 8 +...  24.8 us
    ppermute x1, waiting for transfers between devices, on_device(): lax.ppermute(first, 'wide', [(i + MEMBERS, i) for i in range(wide - MEMBE...  20.8 us
    pallas_call x18, Pallas kernels, call(): pl.pallas_call(kernel, out_shape=outs, in_specs=[smem if a.dtype == jnp.i...  20.4 us
    ppermute x12, waiting for transfers between devices, swap(): return lax.ppermute(v, 'wide', [(i, i ^ bit) for i in range(wide)])  16.6 us
    all_to_all x1, waiting for transfers between devices, on_device(): lax.all_to_all(jnp.broadcast_to(latent[None], (pieces,) + latent.shape),...  13.9 us
    ppermute x6, starting transfers between devices, across(): lax.ppermute(v, 'narrow', [(i, (i + step) % pieces) for i in range(pieces)])  9.59 us
    all_to_all x1, starting transfers between devices, on_device(): deep_slab = lax.all_to_all(deep_slab, 'wide', 0, 0, axis_index_groups=near)  7.27 us
  transfers between devices with their start and end apart: 34, of which 16 were waited for; matrix products, arithmetic and copies ran while one was open for 1% of the time, Pallas kernels for 7%

profile of v4, /device:TPU:32, one launch (start us, length us, event | category | flops | bytes accessed | tf_op | source)
XLA Modules:
  0.0 182.6 jit_solution(8662856194567389377)
XLA Ops:
  0.6 1.8 broadcast_in_dim.4
  2.4 6.0 %all-to-all-start = ((bf16[4,2,64,640]{3,2,1,0:T(8,128)(2,1)}), bf16[4,2,64,640]{3,2,1,0:T(8,128)(2,1)S(1)}, u32[]{:S(2)}, u32[]{:S(2)}) async-start(bf16[4,2,64,640]{3,2,1,0:T(8,128)(2,1)} %broadcast_in_dim.4), calls=%async_computation | async-start | bytes 1310720 | tf_op jit(solution)/shard_map/all_to_all | solution.py:314
  8.5 13.9 %all-to-all-done.refs_1_.refs_0_ = bf16[4,2,64,640]{3,2,1,0:T(8,128)(2,1)S(1)} async-done(((bf16[4,2,64,640]{3,2,1,0:T(8,128)(2,1)}), bf16[4,2,64,640]{3,2,1,0:T(8,128)(2,1)S(1)}, u32[]{:S(2)}, u32[]{:S(2)}) %all-to-all-start) | async-done | bytes 655392 | tf_op jit(solution)/shard_map/all_to_all | solution.py:314
  28.6 4.2 %collective-permute-start.3 = (bf16[160,128]{1,0:T(8,128)(2,1)S(1)}, bf16[160,128]{1,0:T(8,128)(2,1)S(1)}, u32[]{:S(2)}, u32[]{:S(2)}) collective-permute-start(bf16[160,128]{1,0:T(8,128)(2,1)S(1)} %shard_map.94.refs_1_), channel_id=1, source_target_pairs={{0,2},{1,3},{2,0},{3,1},{4,6},{5,7},{6,4},{7,5},{8,10},{9,11},{10,... | collective-permute-start | bytes 122888 | tf_op jit(solution)/shard_map/ppermute | solution.py:305
  32.8 2.4 %collective-permute-done.3.refs_3_ = bf16[160,128]{1,0:T(8,128)(2,1)S(1)} collective-permute-done((bf16[160,128]{1,0:T(8,128)(2,1)S(1)}, bf16[160,128]{1,0:T(8,128)(2,1)S(1)}, u32[]{:S(2)}, u32[]{:S(2)}) %collective-permute-start.3) | collective-permute-done | bytes 40992 | tf_op jit(solution)/shard_map/ppermute | solution.py:305
  38.2 3.7 %collective-permute-start.5 = (bf16[320,128]{1,0:T(8,128)(2,1)S(1)}, bf16[320,128]{1,0:T(8,128)(2,1)S(1)}, u32[]{:S(2)}, u32[]{:S(2)}) collective-permute-start(bf16[320,128]{1,0:T(8,128)(2,1)S(1)} %get-tuple-element.36), channel_id=1, source_target_pairs={{0,4},{4,0},{8,12},{12,8},{16,20},{20,16},{24,28},{28,24},{32,36},... | collective-permute-start | bytes 245768 | tf_op jit(solution)/shard_map/ppermute | solution.py:308
  44.2 4.6 %collective-permute-start.7 = (bf16[320,128]{1,0:T(8,128)(2,1)S(1)}, bf16[320,128]{1,0:T(8,128)(2,1)S(1)}, u32[]{:S(2)}, u32[]{:S(2)}) collective-permute-start(bf16[320,128]{1,0:T(8,128)(2,1)S(1)} %get-tuple-element.39.refs_2_.refs_1_), channel_id=1, source_target_pairs={{0,4},{4,0},{8,12},{12,8},{16,20},{20,16},{24,28},{28,24},{32,36},... | collective-permute-start | bytes 245768 | tf_op jit(solution)/shard_map/ppermute | solution.py:308
  49.4 3.4 %collective-permute-start.9 = (bf16[320,128]{1,0:T(8,128)(2,1)S(1)}, bf16[320,128]{1,0:T(8,128)(2,1)S(1)}, u32[]{:S(2)}, u32[]{:S(2)}) collective-permute-start(bf16[320,128]{1,0:T(8,128)(2,1)S(1)} %get-tuple-element.39.refs_2_.refs_1_), channel_id=1, source_target_pairs={{0,8},{4,12},{8,0},{12,4},{16,24},{20,28},{24,16},{28,20},{32,40},... | collective-permute-start | bytes 245768 | tf_op jit(solution)/shard_map/ppermute | solution.py:308
  52.9 3.6 %collective-permute-done.9.refs_5_.refs_3_ = bf16[320,128]{1,0:T(8,128)(2,1)S(1)} collective-permute-done((bf16[320,128]{1,0:T(8,128)(2,1)S(1)}, bf16[320,128]{1,0:T(8,128)(2,1)S(1)}, u32[]{:S(2)}, u32[]{:S(2)}) %collective-permute-start.9) | collective-permute-done | bytes 81952 | tf_op jit(solution)/shard_map/ppermute | solution.py:308
  56.5 1.9 %shard_map.98 = (bf16[160,128]{1,0:T(8,128)(2,1)S(1)}, bf16[160,128]{1,0:T(8,128)(2,1)S(1)}, bf16[160,128]{1,0:T(8,128)(2,1)S(1)}, bf16[160,128]{1,0:T(8,128)(2,1)S(1)}) custom-call(s32[5]{0:T(128)S(1)} %stack.41.refs_0_, bf16[320,128]{1,0:T(8,128)(2,1)S(1)} %collective-permute-done.7.refs_1_.refs_2_, ...), custom_call_target="tpu_custom_call" | custom-call | flops 471859200 | bytes 3932180 | tf_op jit(solution)/shard_map/pallas_call | solution.py:62
  59.5 7.3 %all-to-all-start.3 = ((bf16[8,80,128]{2,1,0:T(8,128)(2,1)}), bf16[8,80,128]{2,1,0:T(8,128)(2,1)S(1)}, u32[]{:S(2)}, u32[]{:S(2)}) async-start(bf16[8,80,128]{2,1,0:T(8,128)(2,1)} %shard_map.102), calls=%async_computation.3 | async-start | bytes 327680 | tf_op jit(solution)/shard_map/all_to_all | solution.py:362
  66.8 2.6 %shard_map.101 = bf16[8,80,512]{2,1,0:T(8,128)(2,1)} custom-call(bf16[4,2,64,640]{3,2,1,0:T(8,128)(2,1)S(1)} %all-to-all-done.refs_1_.refs_0_, bf16[640,640]{1,0:T(8,128)(2,1)S(1)} %copy-done.2, f32[160,128]{1,0:T(8,128)S(1)} %get-tuple-element.32.refs_0_.refs_2_), custom_call_target="tpu_custom_call" | custom-call | flops 419430400 | bytes 1474560 | tf_op jit(solution)/shard_map/pallas_call | solution.py:62
  69.4 3.9 %all-to-all-done.3.refs_1_ = bf16[8,80,128]{2,1,0:T(8,128)(2,1)S(1)} async-done(((bf16[8,80,128]{2,1,0:T(8,128)(2,1)}), bf16[8,80,128]{2,1,0:T(8,128)(2,1)S(1)}, u32[]{:S(2)}, u32[]{:S(2)}) %all-to-all-start.3) | async-done | bytes 163872 | tf_op jit(solution)/shard_map/all_to_all | solution.py:362
  73.3 3.5 %all-to-all-start.2 = ((bf16[8,80,512]{2,1,0:T(8,128)(2,1)}), bf16[8,80,512]{2,1,0:T(8,128)(2,1)S(1)}, u32[]{:S(2)}, u32[]{:S(2)}) async-start(bf16[8,80,512]{2,1,0:T(8,128)(2,1)} %shard_map.101), calls=%async_computation.2 | async-start | bytes 1310720 | tf_op jit(solution)/shard_map/all_to_all | solution.py:329
  76.9 3.5 %collective-permute-start.13 = (bf16[2,320,128]{2,1,0:T(8,128)(2,1)S(1)}, bf16[2,320,128]{2,1,0:T(8,128)(2,1)S(1)}, u32[]{:S(2)}, u32[]{:S(2)}) collective-permute-start(bf16[2,320,128]{2,1,0:T(8,128)(2,1)S(1)} %pad_maximum_fusion.1), channel_id=1, source_target_pairs={{0,16},{4,20},{8,24},{12,28},{16,0},{20,4},{24,8},{28,12},{32,48},... | collective-permute-start | bytes 491528 | tf_op jit(solution)/shard_map/ppermute | solution.py:308
  80.4 2.5 %collective-permute-start.11 = (bf16[160,128]{1,0:T(8,128)(2,1)S(1)}, bf16[160,128]{1,0:T(8,128)(2,1)S(1)}, u32[]{:S(2)}, u32[]{:S(2)}) collective-permute-start(bf16[160,128]{1,0:T(8,128)(2,1)S(1)} %get-tuple-element.42), channel_id=1, source_target_pairs={{0,2},{1,3},{2,0},{3,1},{4,6},{5,7},{6,4},{7,5},{8,10},{9,11},{10,... | collective-permute-start | bytes 122888 | tf_op jit(solution)/shard_map/ppermute | solution.py:305
  86.9 5.1 %collective-permute-done.13.refs_4_ = bf16[2,320,128]{2,1,0:T(8,128)(2,1)S(1)} collective-permute-done((bf16[2,320,128]{2,1,0:T(8,128)(2,1)S(1)}, bf16[2,320,128]{2,1,0:T(8,128)(2,1)S(1)}, u32[]{:S(2)}, u32[]{:S(2)}) %collective-permute-start.13) | collective-permute-done | bytes 163872 | tf_op jit(solution)/shard_map/ppermute | solution.py:308
  92.8 3.4 %collective-permute-start.16 = (bf16[160,128]{1,0:T(8,128)(2,1)S(1)}, bf16[160,128]{1,0:T(8,128)(2,1)S(1)}, u32[]{:S(2)}, u32[]{:S(2)}) collective-permute-start(bf16[160,128]{1,0:T(8,128)(2,1)S(1)} %shard_map.99.refs_2_.refs_1_), channel_id=1, source_target_pairs={{0,8},{4,12},{8,0},{12,4},{16,24},{20,28},{24,16},{28,20},{32,40},... | collective-permute-start | bytes 122888 | tf_op jit(solution)/shard_map/ppermute | solution.py:308
  96.3 2.5 %collective-permute-done.16.refs_5_.refs_3_ = bf16[160,128]{1,0:T(8,128)(2,1)S(1)} collective-permute-done((bf16[160,128]{1,0:T(8,128)(2,1)S(1)}, bf16[160,128]{1,0:T(8,128)(2,1)S(1)}, u32[]{:S(2)}, u32[]{:S(2)}) %collective-permute-start.16) | collective-permute-done | bytes 40992 | tf_op jit(solution)/shard_map/ppermute | solution.py:308
  100.2 3.0 %shard_map.100.refs_4_ = bf16[4,2,64,640]{3,2,1,0:T(8,128)(2,1)} custom-call(s32[5]{0:T(128)S(1)} %stack.41.refs_0_, bf16[160,128]{1,0:T(8,128)(2,1)S(1)} %collective-permute-done.14.refs_1_.refs_2_, bf16[160,128]{1,0:T(8,128)(2,1)S(1)} %shard_map.99.refs_2_.refs_1_, bf16[160,128]{1,0:T(8,128)(2,1)S(1)} %collective-permute-done.15.refs_3_, ...), custom_call_target="tpu_custom_call" | custom-call | flops 943718400 | bytes 1966100 | tf_op jit(solution)/shard_map/pallas_call | solution.py:62
  103.2 4.6 %all-to-all-start.1 = ((bf16[4,2,64,640]{3,2,1,0:T(8,128)(2,1)}), bf16[4,2,64,640]{3,2,1,0:T(8,128)(2,1)S(1)}, u32[]{:S(2)}, u32[]{:S(2)}) async-start(bf16[4,2,64,640]{3,2,1,0:T(8,128)(2,1)} %shard_map.100.refs_4_), calls=%async_computation.1 | async-start | bytes 1310720 | tf_op jit(solution)/shard_map/all_to_all | solution.py:376
  108.0 2.5 %collective-permute-start.17 = (bf16[2,160,128]{2,1,0:T(8,128)(2,1)S(1)}, bf16[2,160,128]{2,1,0:T(8,128)(2,1)S(1)}, u32[]{:S(2)}, u32[]{:S(2)}) collective-permute-start(bf16[2,160,128]{2,1,0:T(8,128)(2,1)S(1)} %pad_maximum_fusion.3), channel_id=1, source_target_pairs={{0,16},{4,20},{8,24},{12,28},{16,0},{20,4},{24,8},{28,12},{32,48},... | collective-permute-start | bytes 245768 | tf_op jit(solution)/shard_map/ppermute | solution.py:308
  110.5 4.0 %collective-permute-start.19 = (bf16[80,384]{1,0:T(8,128)(2,1)S(1)}, bf16[80,384]{1,0:T(8,128)(2,1)S(1)}, u32[]{:S(2)}, u32[]{:S(2)}) collective-permute-start(bf16[80,384]{1,0:T(8,128)(2,1)S(1)} %get-tuple-element.44), channel_id=1, source_target_pairs={{0,32},{4,36},{8,40},{12,44},{16,48},{20,52},{24,56},{28,60},{32,6... | collective-permute-start | bytes 184328 | tf_op jit(solution)/shard_map/ppermute | solution.py:382
  116.3 20.8 %collective-permute-done.20.refs_3_ = bf16[80,384]{1,0:T(8,128)(2,1)S(1)} collective-permute-done((bf16[80,384]{1,0:T(8,128)(2,1)S(1)}, bf16[80,384]{1,0:T(8,128)(2,1)S(1)}, u32[]{:S(2)}, u32[]{:S(2)}) %collective-permute-start.20) | collective-permute-done | bytes 61472 | tf_op jit(solution)/shard_map/ppermute | solution.py:383
  137.9 2.9 %shard_map.108 = (bf16[2,96,320]{2,1,0:T(8,128)(2,1)S(1)}, bf16[2,96,320]{2,1,0:T(8,128)(2,1)S(1)}, bf16[2,96,320]{2,1,0:T(8,128)(2,1)S(1)}, bf16[2,96,320]{2,1,0:T(8,128)(2,1)S(1)}) custom-call(s32[5]{0:T(128)S(1)} %stack.41.refs_0_, bf16[320,128]{1,0:T(8,128)(2,1)S(1)} %get-tuple-element.39.refs_2_.refs_1_, ...), custom_call_target="tpu_custom_call" | custom-call | flops 471859200 | bytes 3235860 | tf_op jit(solution)/shard_map/pallas_call | solution.py:62
  140.8 5.1 %collective-permute-start.26 = (bf16[2,96,320]{2,1,0:T(8,128)(2,1)S(1)}, bf16[2,96,320]{2,1,0:T(8,128)(2,1)S(1)}, u32[]{:S(2)}, u32[]{:S(2)}) collective-permute-start(bf16[2,96,320]{2,1,0:T(8,128)(2,1)S(1)} %get-tuple-element.55), channel_id=1, source_target_pairs={{0,32},{4,36},{8,40},{12,44},{16,48},{20,52},{24,56},{28,60},{32,6... | collective-permute-start | bytes 368648 | tf_op jit(solution)/shard_map/ppermute | solution.py:404
  145.9 14.9 %collective-permute-start.27 = (bf16[2,96,320]{2,1,0:T(8,128)(2,1)S(1)}, bf16[2,96,320]{2,1,0:T(8,128)(2,1)S(1)}, u32[]{:S(2)}, u32[]{:S(2)}) collective-permute-start(bf16[2,96,320]{2,1,0:T(8,128)(2,1)S(1)} %get-tuple-element.56), channel_id=1, source_target_pairs={{0,64},{4,68},{8,72},{12,76},{16,80},{20,84},{24,88},{28,92},{32,9... | collective-permute-start | bytes 368648 | tf_op jit(solution)/shard_map/ppermute | solution.py:404
  160.8 2.4 %shard_map.105 = (bf16[2,96,160]{2,1,0:T(8,128)(2,1)S(1)}, bf16[2,96,160]{2,1,0:T(8,128)(2,1)S(1)}, bf16[2,96,160]{2,1,0:T(8,128)(2,1)S(1)}, bf16[2,96,160]{2,1,0:T(8,128)(2,1)S(1)}) custom-call(s32[5]{0:T(128)S(1)} %stack.41.refs_0_, bf16[160,128]{1,0:T(8,128)(2,1)S(1)} %shard_map.99.refs_2_.refs_1_, ...), custom_call_target="tpu_custom_call" | custom-call | flops 235929600 | bytes 2908180 | tf_op jit(solution)/shard_map/pallas_call | solution.py:62
  163.2 2.1 %collective-permute-start.21 = (bf16[2,96,160]{2,1,0:T(8,128)(2,1)S(1)}, bf16[2,96,160]{2,1,0:T(8,128)(2,1)S(1)}, u32[]{:S(2)}, u32[]{:S(2)}) collective-permute-start(bf16[2,96,160]{2,1,0:T(8,128)(2,1)S(1)} %get-tuple-element.48), channel_id=1, source_target_pairs={{0,32},{4,36},{8,40},{12,44},{16,48},{20,52},{24,56},{28,60},{32,6... | collective-permute-start | bytes 184328 | tf_op jit(solution)/shard_map/ppermute | solution.py:404
  165.3 2.8 %collective-permute-start.23 = (bf16[2,96,160]{2,1,0:T(8,128)(2,1)S(1)}, bf16[2,96,160]{2,1,0:T(8,128)(2,1)S(1)}, u32[]{:S(2)}, u32[]{:S(2)}) collective-permute-start(bf16[2,96,160]{2,1,0:T(8,128)(2,1)S(1)} %get-tuple-element.50), channel_id=1, source_target_pairs={{0,96},{4,100},{8,104},{12,108},{16,112},{20,116},{24,120},{28,124... | collective-permute-start | bytes 184328 | tf_op jit(solution)/shard_map/ppermute | solution.py:404
  172.1 3.4 %collective-permute-start.24 = (bf16[96,160]{1,0:T(8,128)(2,1)S(1)}, bf16[96,160]{1,0:T(8,128)(2,1)S(1)}, u32[]{:S(2)}, u32[]{:S(2)}) collective-permute-start(bf16[96,160]{1,0:T(8,128)(2,1)S(1)} %get-tuple-element.52), channel_id=1, source_target_pairs={{0,128},{4,132},{8,136},{12,140},{16,144},{20,148},{24,152},{28,15... | collective-permute-start | bytes 92168 | tf_op jit(solution)/shard_map/ppermute | solution.py:308
  175.5 4.9 %collective-permute-done.24.refs_1_ = bf16[96,160]{1,0:T(8,128)(2,1)S(1)} collective-permute-done((bf16[96,160]{1,0:T(8,128)(2,1)S(1)}, bf16[96,160]{1,0:T(8,128)(2,1)S(1)}, u32[]{:S(2)}, u32[]{:S(2)}) %collective-permute-start.24) | collective-permute-done | bytes 30752 | tf_op jit(solution)/shard_map/ppermute | solution.py:308
  (75 shorter events, 28.4 us)
Async XLA Ops:
  2.4 20.0 %all-to-all-start = ((bf16[4,2,64,640]{3,2,1,0:T(8,128)(2,1)}), bf16[4,2,64,640]{3,2,1,0:T(8,128)(2,1)S(1)}, u32[]{:S(2)}, u32[]{:S(2)}) async-start(bf16[4,2,64,640]{3,2,1,0:T(8,128)(2,1)} %broadcast_in_dim.4), calls=%async_computation | async-start | bytes 1310720 | tf_op jit(solution)/shard_map/all_to_all | solution.py:314
  25.8 1.3 collective-permute-start
  27.1 5.7 %collective-permute-start.2 = (bf16[160,128]{1,0:T(8,128)(2,1)S(1)}, bf16[160,128]{1,0:T(8,128)(2,1)S(1)}, u32[]{:S(2)}, u32[]{:S(2)}) collective-permute-start(bf16[160,128]{1,0:T(8,128)(2,1)S(1)} %shard_map.94.refs_1_), channel_id=1, source_target_pairs={{0,1},{1,2},{2,3},{3,0},{4,5},{5,6},{6,7},{7,4},{8,9},{9,10},{10,1... | collective-permute-start | bytes 122888 | tf_op jit(solution)/shard_map/ppermute | solution.py:305
  28.6 6.6 %collective-permute-start.3 = (bf16[160,128]{1,0:T(8,128)(2,1)S(1)}, bf16[160,128]{1,0:T(8,128)(2,1)S(1)}, u32[]{:S(2)}, u32[]{:S(2)}) collective-permute-start(bf16[160,128]{1,0:T(8,128)(2,1)S(1)} %shard_map.94.refs_1_), channel_id=1, source_target_pairs={{0,2},{1,3},{2,0},{3,1},{4,6},{5,7},{6,4},{7,5},{8,10},{9,11},{10,... | collective-permute-start | bytes 122888 | tf_op jit(solution)/shard_map/ppermute | solution.py:305
  32.8 4.0 %collective-permute-start.4 = (bf16[160,128]{1,0:T(8,128)(2,1)S(1)}, bf16[160,128]{1,0:T(8,128)(2,1)S(1)}, u32[]{:S(2)}, u32[]{:S(2)}) collective-permute-start(bf16[160,128]{1,0:T(8,128)(2,1)S(1)} %shard_map.94.refs_1_), channel_id=1, source_target_pairs={{0,3},{1,0},{2,1},{3,2},{4,7},{5,4},{6,5},{7,6},{8,11},{9,8},{10,9... | collective-permute-start | bytes 122888 | tf_op jit(solution)/shard_map/ppermute | solution.py:305
  38.2 4.9 %collective-permute-start.5 = (bf16[320,128]{1,0:T(8,128)(2,1)S(1)}, bf16[320,128]{1,0:T(8,128)(2,1)S(1)}, u32[]{:S(2)}, u32[]{:S(2)}) collective-permute-start(bf16[320,128]{1,0:T(8,128)(2,1)S(1)} %get-tuple-element.36), channel_id=1, source_target_pairs={{0,4},{4,0},{8,12},{12,8},{16,20},{20,16},{24,28},{28,24},{32,36},... | collective-permute-start | bytes 245768 | tf_op jit(solution)/shard_map/ppermute | solution.py:308
  44.2 8.7 %collective-permute-start.7 = (bf16[320,128]{1,0:T(8,128)(2,1)S(1)}, bf16[320,128]{1,0:T(8,128)(2,1)S(1)}, u32[]{:S(2)}, u32[]{:S(2)}) collective-permute-start(bf16[320,128]{1,0:T(8,128)(2,1)S(1)} %get-tuple-element.39.refs_2_.refs_1_), channel_id=1, source_target_pairs={{0,4},{4,0},{8,12},{12,8},{16,20},{20,16},{24,28},{28,24},{32,36},... | collective-permute-start | bytes 245768 | tf_op jit(solution)/shard_map/ppermute | solution.py:308
  48.7 4.1 %collective-permute-start.8 = (bf16[320,128]{1,0:T(8,128)(2,1)S(1)}, bf16[320,128]{1,0:T(8,128)(2,1)S(1)}, u32[]{:S(2)}, u32[]{:S(2)}) collective-permute-start(bf16[320,128]{1,0:T(8,128)(2,1)S(1)} %get-tuple-element.39.refs_2_.refs_1_), channel_id=1, source_target_pairs={{4,8},{8,4},{12,16},{16,12},{20,24},{24,20},{28,32},{32,28},{36,40... | collective-permute-start | bytes 245768 | tf_op jit(solution)/shard_map/ppermute | solution.py:311
  49.4 7.1 %collective-permute-start.9 = (bf16[320,128]{1,0:T(8,128)(2,1)S(1)}, bf16[320,128]{1,0:T(8,128)(2,1)S(1)}, u32[]{:S(2)}, u32[]{:S(2)}) collective-permute-start(bf16[320,128]{1,0:T(8,128)(2,1)S(1)} %get-tuple-element.39.refs_2_.refs_1_), channel_id=1, source_target_pairs={{0,8},{4,12},{8,0},{12,4},{16,24},{20,28},{24,16},{28,20},{32,40},... | collective-permute-start | bytes 245768 | tf_op jit(solution)/shard_map/ppermute | solution.py:308
  59.5 13.8 %all-to-all-start.3 = ((bf16[8,80,128]{2,1,0:T(8,128)(2,1)}), bf16[8,80,128]{2,1,0:T(8,128)(2,1)S(1)}, u32[]{:S(2)}, u32[]{:S(2)}) async-start(bf16[8,80,128]{2,1,0:T(8,128)(2,1)} %shard_map.102), calls=%async_computation.3 | async-start | bytes 327680 | tf_op jit(solution)/shard_map/all_to_all | solution.py:362
  73.3 30.0 %all-to-all-start.2 = ((bf16[8,80,512]{2,1,0:T(8,128)(2,1)}), bf16[8,80,512]{2,1,0:T(8,128)(2,1)S(1)}, u32[]{:S(2)}, u32[]{:S(2)}) async-start(bf16[8,80,512]{2,1,0:T(8,128)(2,1)} %shard_map.101), calls=%async_computation.2 | async-start | bytes 1310720 | tf_op jit(solution)/shard_map/all_to_all | solution.py:329
  76.9 15.2 %collective-permute-start.13 = (bf16[2,320,128]{2,1,0:T(8,128)(2,1)S(1)}, bf16[2,320,128]{2,1,0:T(8,128)(2,1)S(1)}, u32[]{:S(2)}, u32[]{:S(2)}) collective-permute-start(bf16[2,320,128]{2,1,0:T(8,128)(2,1)S(1)} %pad_maximum_fusion.1), channel_id=1, source_target_pairs={{0,16},{4,20},{8,24},{12,28},{16,0},{20,4},{24,8},{28,12},{32,48},... | collective-permute-start | bytes 491528 | tf_op jit(solution)/shard_map/ppermute | solution.py:308
  80.4 4.0 %collective-permute-start.10 = (bf16[160,128]{1,0:T(8,128)(2,1)S(1)}, bf16[160,128]{1,0:T(8,128)(2,1)S(1)}, u32[]{:S(2)}, u32[]{:S(2)}) collective-permute-start(bf16[160,128]{1,0:T(8,128)(2,1)S(1)} %get-tuple-element.41), channel_id=1, source_target_pairs={{0,1},{1,2},{2,3},{3,0},{4,5},{5,6},{6,7},{7,4},{8,9},{9,10},{10,1... | collective-permute-start | bytes 122888 | tf_op jit(solution)/shard_map/ppermute | solution.py:305
  80.4 5.1 %collective-permute-start.11 = (bf16[160,128]{1,0:T(8,128)(2,1)S(1)}, bf16[160,128]{1,0:T(8,128)(2,1)S(1)}, u32[]{:S(2)}, u32[]{:S(2)}) collective-permute-start(bf16[160,128]{1,0:T(8,128)(2,1)S(1)} %get-tuple-element.42), channel_id=1, source_target_pairs={{0,2},{1,3},{2,0},{3,1},{4,6},{5,7},{6,4},{7,5},{8,10},{9,11},{10,... | collective-permute-start | bytes 122888 | tf_op jit(solution)/shard_map/ppermute | solution.py:305
  82.9 4.0 %collective-permute-start.12 = (bf16[160,128]{1,0:T(8,128)(2,1)S(1)}, bf16[160,128]{1,0:T(8,128)(2,1)S(1)}, u32[]{:S(2)}, u32[]{:S(2)}) collective-permute-start(bf16[160,128]{1,0:T(8,128)(2,1)S(1)} %get-tuple-element.43), channel_id=1, source_target_pairs={{0,3},{1,0},{2,1},{3,2},{4,7},{5,4},{6,5},{7,6},{8,11},{9,8},{10,9... | collective-permute-start | bytes 122888 | tf_op jit(solution)/shard_map/ppermute | solution.py:305
  92.0 4.2 %collective-permute-start.14 = (bf16[160,128]{1,0:T(8,128)(2,1)S(1)}, bf16[160,128]{1,0:T(8,128)(2,1)S(1)}, u32[]{:S(2)}, u32[]{:S(2)}) collective-permute-start(bf16[160,128]{1,0:T(8,128)(2,1)S(1)} %shard_map.99.refs_2_.refs_1_), channel_id=1, source_target_pairs={{0,4},{4,0},{8,12},{12,8},{16,20},{20,16},{24,28},{28,24},{32,36},... | collective-permute-start | bytes 122888 | tf_op jit(solution)/shard_map/ppermute | solution.py:308
  92.1 4.1 %collective-permute-start.15 = (bf16[160,128]{1,0:T(8,128)(2,1)S(1)}, bf16[160,128]{1,0:T(8,128)(2,1)S(1)}, u32[]{:S(2)}, u32[]{:S(2)}) collective-permute-start(bf16[160,128]{1,0:T(8,128)(2,1)S(1)} %shard_map.99.refs_2_.refs_1_), channel_id=1, source_target_pairs={{4,8},{8,4},{12,16},{16,12},{20,24},{24,20},{28,32},{32,28},{36,40... | collective-permute-start | bytes 122888 | tf_op jit(solution)/shard_map/ppermute | solution.py:311
  92.8 5.9 %collective-permute-start.16 = (bf16[160,128]{1,0:T(8,128)(2,1)S(1)}, bf16[160,128]{1,0:T(8,128)(2,1)S(1)}, u32[]{:S(2)}, u32[]{:S(2)}) collective-permute-start(bf16[160,128]{1,0:T(8,128)(2,1)S(1)} %shard_map.99.refs_2_.refs_1_), channel_id=1, source_target_pairs={{0,8},{4,12},{8,0},{12,4},{16,24},{20,28},{24,16},{28,20},{32,40},... | collective-permute-start | bytes 122888 | tf_op jit(solution)/shard_map/ppermute | solution.py:308
  103.2 78.6 %all-to-all-start.1 = ((bf16[4,2,64,640]{3,2,1,0:T(8,128)(2,1)}), bf16[4,2,64,640]{3,2,1,0:T(8,128)(2,1)S(1)}, u32[]{:S(2)}, u32[]{:S(2)}) async-start(bf16[4,2,64,640]{3,2,1,0:T(8,128)(2,1)} %shard_map.100.refs_4_), calls=%async_computation.1 | async-start | bytes 1310720 | tf_op jit(solution)/shard_map/all_to_all | solution.py:376
  107.9 30.0 %collective-permute-start.25 = (bf16[3,320,128]{2,1,0:T(8,128)(2,1)S(1)}, bf16[3,320,128]{2,1,0:T(8,128)(2,1)S(1)}, u32[]{:S(2)}, u32[]{:S(2)}) collective-permute-start(bf16[3,320,128]{2,1,0:T(8,128)(2,1)S(1)} %pad_maximum_fusion), channel_id=1, source_target_pairs={{0,4},{4,0},{8,12},{12,8},{16,20},{20,16},{24,28},{28,24},{32,36},... | collective-permute-start | bytes 737288 | tf_op jit(solution)/shard_map/ppermute | solution.py:308
  108.0 7.8 %collective-permute-start.17 = (bf16[2,160,128]{2,1,0:T(8,128)(2,1)S(1)}, bf16[2,160,128]{2,1,0:T(8,128)(2,1)S(1)}, u32[]{:S(2)}, u32[]{:S(2)}) collective-permute-start(bf16[2,160,128]{2,1,0:T(8,128)(2,1)S(1)} %pad_maximum_fusion.3), channel_id=1, source_target_pairs={{0,16},{4,20},{8,24},{12,28},{16,0},{20,4},{24,8},{28,12},{32,48},... | collective-permute-start | bytes 245768 | tf_op jit(solution)/shard_map/ppermute | solution.py:308
  110.5 5.9 %collective-permute-start.19 = (bf16[80,384]{1,0:T(8,128)(2,1)S(1)}, bf16[80,384]{1,0:T(8,128)(2,1)S(1)}, u32[]{:S(2)}, u32[]{:S(2)}) collective-permute-start(bf16[80,384]{1,0:T(8,128)(2,1)S(1)} %get-tuple-element.44), channel_id=1, source_target_pairs={{0,32},{4,36},{8,40},{12,44},{16,48},{20,52},{24,56},{28,60},{32,6... | collective-permute-start | bytes 184328 | tf_op jit(solution)/shard_map/ppermute | solution.py:382
  114.5 22.6 %collective-permute-start.20 = (bf16[80,384]{1,0:T(8,128)(2,1)S(1)}, bf16[80,384]{1,0:T(8,128)(2,1)S(1)}, u32[]{:S(2)}, u32[]{:S(2)}) collective-permute-start(bf16[80,384]{1,0:T(8,128)(2,1)S(1)} %get-tuple-element.45), channel_id=1, source_target_pairs={{32,0},{36,4},{40,8},{44,12},{48,16},{52,20},{56,24},{60,28},{64,3... | collective-permute-start | bytes 184328 | tf_op jit(solution)/shard_map/ppermute | solution.py:383
  115.8 45.0 %collective-permute-start.18 = (bf16[3,160,128]{2,1,0:T(8,128)(2,1)S(1)}, bf16[3,160,128]{2,1,0:T(8,128)(2,1)S(1)}, u32[]{:S(2)}, u32[]{:S(2)}) collective-permute-start(bf16[3,160,128]{2,1,0:T(8,128)(2,1)S(1)} %pad_maximum_fusion.2), channel_id=1, source_target_pairs={{0,4},{4,0},{8,12},{12,8},{16,20},{20,16},{24,28},{28,24},{32,36},... | collective-permute-start | bytes 368648 | tf_op jit(solution)/shard_map/ppermute | solution.py:308
  140.8 24.5 %collective-permute-start.26 = (bf16[2,96,320]{2,1,0:T(8,128)(2,1)S(1)}, bf16[2,96,320]{2,1,0:T(8,128)(2,1)S(1)}, u32[]{:S(2)}, u32[]{:S(2)}) collective-permute-start(bf16[2,96,320]{2,1,0:T(8,128)(2,1)S(1)} %get-tuple-element.55), channel_id=1, source_target_pairs={{0,32},{4,36},{8,40},{12,44},{16,48},{20,52},{24,56},{28,60},{32,6... | collective-permute-start | bytes 368648 | tf_op jit(solution)/shard_map/ppermute | solution.py:404
  145.9 22.2 %collective-permute-start.27 = (bf16[2,96,320]{2,1,0:T(8,128)(2,1)S(1)}, bf16[2,96,320]{2,1,0:T(8,128)(2,1)S(1)}, u32[]{:S(2)}, u32[]{:S(2)}) collective-permute-start(bf16[2,96,320]{2,1,0:T(8,128)(2,1)S(1)} %get-tuple-element.56), channel_id=1, source_target_pairs={{0,64},{4,68},{8,72},{12,76},{16,80},{20,84},{24,88},{28,92},{32,9... | collective-permute-start | bytes 368648 | tf_op jit(solution)/shard_map/ppermute | solution.py:404
  160.8 7.3 %collective-permute-start.28 = (bf16[2,96,320]{2,1,0:T(8,128)(2,1)S(1)}, bf16[2,96,320]{2,1,0:T(8,128)(2,1)S(1)}, u32[]{:S(2)}, u32[]{:S(2)}) collective-permute-start(bf16[2,96,320]{2,1,0:T(8,128)(2,1)S(1)} %get-tuple-element.57), channel_id=1, source_target_pairs={{0,96},{4,100},{8,104},{12,108},{16,112},{20,116},{24,120},{28,124... | collective-permute-start | bytes 368648 | tf_op jit(solution)/shard_map/ppermute | solution.py:404
  163.2 7.0 %collective-permute-start.21 = (bf16[2,96,160]{2,1,0:T(8,128)(2,1)S(1)}, bf16[2,96,160]{2,1,0:T(8,128)(2,1)S(1)}, u32[]{:S(2)}, u32[]{:S(2)}) collective-permute-start(bf16[2,96,160]{2,1,0:T(8,128)(2,1)S(1)} %get-tuple-element.48), channel_id=1, source_target_pairs={{0,32},{4,36},{8,40},{12,44},{16,48},{20,52},{24,56},{28,60},{32,6... | collective-permute-start | bytes 184328 | tf_op jit(solution)/shard_map/ppermute | solution.py:404
  165.3 6.1 %collective-permute-start.22 = (bf16[2,96,160]{2,1,0:T(8,128)(2,1)S(1)}, bf16[2,96,160]{2,1,0:T(8,128)(2,1)S(1)}, u32[]{:S(2)}, u32[]{:S(2)}) collective-permute-start(bf16[2,96,160]{2,1,0:T(8,128)(2,1)S(1)} %get-tuple-element.49), channel_id=1, source_target_pairs={{0,64},{4,68},{8,72},{12,76},{16,80},{20,84},{24,88},{28,92},{32,9... | collective-permute-start | bytes 184328 | tf_op jit(solution)/shard_map/ppermute | solution.py:404
  165.3 6.1 %collective-permute-start.23 = (bf16[2,96,160]{2,1,0:T(8,128)(2,1)S(1)}, bf16[2,96,160]{2,1,0:T(8,128)(2,1)S(1)}, u32[]{:S(2)}, u32[]{:S(2)}) collective-permute-start(bf16[2,96,160]{2,1,0:T(8,128)(2,1)S(1)} %get-tuple-element.50), channel_id=1, source_target_pairs={{0,96},{4,100},{8,104},{12,108},{16,112},{20,116},{24,120},{28,124... | collective-permute-start | bytes 184328 | tf_op jit(solution)/shard_map/ppermute | solution.py:404
  168.8 12.3 %collective-permute-start.29 = (bf16[96,320]{1,0:T(8,128)(2,1)S(1)}, bf16[96,320]{1,0:T(8,128)(2,1)S(1)}, u32[]{:S(2)}, u32[]{:S(2)}) collective-permute-start(bf16[96,320]{1,0:T(8,128)(2,1)S(1)} %get-tuple-element.59), channel_id=1, source_target_pairs={{0,128},{4,132},{8,136},{12,140},{16,144},{20,148},{24,152},{28,15... | collective-permute-start | bytes 184328 | tf_op jit(solution)/shard_map/ppermute | solution.py:308
  172.1 8.3 %collective-permute-start.24 = (bf16[96,160]{1,0:T(8,128)(2,1)S(1)}, bf16[96,160]{1,0:T(8,128)(2,1)S(1)}, u32[]{:S(2)}, u32[]{:S(2)}) collective-permute-start(bf16[96,160]{1,0:T(8,128)(2,1)S(1)} %get-tuple-element.52), channel_id=1, source_target_pairs={{0,128},{4,132},{8,136},{12,140},{16,144},{20,148},{24,152},{28,15... | collective-permute-start | bytes 92168 | tf_op jit(solution)/shard_map/ppermute | solution.py:308
  (8 other events, 63.5 us)

commit v5 on v4

--- a/solution.py
+++ b/solution.py
@@ -49,7 +49,7 @@
     return jax.ShapeDtypeStruct(dims, dtype)
 
 
-def call(body, outs, args, scratch=(), flops=0, behind=()):
+def call(body, outs, args, scratch=(), flops=0, behind=(), remote=()):
     size = sum(a.size * a.dtype.itemsize for a in args)
     smem = pl.BlockSpec(memory_space=pltpu.SMEM)
     vmem = pl.BlockSpec(memory_space=pltpu.VMEM)
@@ -62,7 +62,10 @@
     return pl.pallas_call(
         kernel,
         out_shape=outs,
-        in_specs=[smem if a.dtype == jnp.int32 else vmem for a in args] + [aside] * len(behind),
+        in_specs=[
+            smem if a.dtype == jnp.int32 else aside if i in remote else vmem for i, a in enumerate(args)
+        ]
+        + [aside] * len(behind),
         out_specs=jax.tree.map(lambda _: vmem, outs),
         scratch_shapes=list(scratch),
         compiler_params=pltpu.CompilerParams(vmem_limit_bytes=40 * 2**20),
@@ -87,6 +90,13 @@
     return jnp.where(source == lax.broadcasted_iota(jnp.int32, (cols, cols), 1), 1.0, 0.0).astype(BF)
 
 
+def fetch(source, target, sems):
+    copies = [pltpu.make_async_copy(source.at[t], target.at[t], sems.at[t]) for t in range(source.shape[0])]
+    for copy in copies:
+        copy.start()
+    return copies
+
+
 def fine_rows(x):
     pieces = x.shape[0]
     return [jnp.concatenate([x[k, r] for k in range(pieces)]) for r in range(2)]
@@ -107,7 +117,8 @@
         other[...] = down
 
 
-def fine_forward(at, x, w, own, partner, other):
+def fine_forward(at, x, weights, own, partner, other, w, sems):
+    copies = fetch(weights, w, sems)
     deep = own.shape[1]
     rows = fine_rows(x)
     u0, us, u1 = [], [], []
@@ -118,6 +129,8 @@
         u1.append(u[1].astype(BF))
         us.append((u[0] + u[1]).astype(BF))
     pair = [jnp.concatenate([u0[b], u1[b]]) for b in range(3)]
+    for copy in copies:
+        copy.wait()
     mine = sum(mm_t(w[3 + b], us[b]) for b in range(3))
     first = sum(mm_t(w[b], pair[b]) for b in range(3))
     last = sum(mm_t(w[6 + b], pair[b]) for b in range(3))
@@ -177,7 +190,8 @@
     out[...] = sum(v[...].astype(F32) for v in (own, got1, got2, got3)).astype(BF)
 
 
-def fine_backward(at, partner, mine, other, w, out, rows):
+def fine_backward(at, partner, mine, other, weights, out, rows, w, sems):
+    copies = fetch(weights, w, sems)
     before, after = side_rows(at, partner, other, rows)
     deep = mine.shape[1]
     turn = unit(deep)
@@ -187,6 +201,8 @@
     top = jnp.concatenate([here, after])
     low = jnp.concatenate([before, here])
     z = []
+    for copy in copies:
+        copy.wait()
     for b in range(3):
         both = mm(top, w[b]) + mm(low, w[6 + b])
         mid = mm(here, w[3 + b])
@@ -316,7 +332,9 @@
         fine_forward,
         [shape((fine, deep), F32), shape((fine, deep)), shape((fine, deep))],
         (at, x, w_fine),
+        [pltpu.VMEM(w_fine.shape, BF), pltpu.SemaphoreType.DMA((9,))],
         flops=2 * 9 * deep * depth * (2 * cols + 2 * fine),
+        remote=(2,),
     )
     partner, other = pairs(partner, other)
     fine_slab = call(
@@ -326,20 +344,33 @@
         flops=2 * depth * depth * rows * cols,
         behind=(own,),
     )
+    mine = call(pool_add, shape((fine, deep)), (own, partner, other), behind=(fine_slab,))
     fine_slab = lax.all_to_all(fine_slab, "wide", 0, 0, axis_index_groups=near)
-    mine = call(pool_add, shape((fine, deep)), (own, partner, other))
     got = [across(mine, s) for s in (1, 2, 3)]
     pooled, partner, other = call(
         deep_sides,
         [shape((depth, deep)), shape((full, deep)), shape((full, deep))],
         (at, mine, *got, w_deep),
         flops=2 * 6 * deep * depth * full,
+        behind=(fine_slab,),
     )
     partner, other = pairs(partner, other)
+    deep_slab = call(
+        deep_slices, shape((MEMBERS, size, deep)), (pooled, pick), flops=2 * depth * depth * deep
+    )
     preact = call(
         deep_own, shape((full, deep), F32), (pooled, w_deep), flops=2 * 3 * deep * depth * full, behind=(pooled,)
     )
-    output, grad_pre = call(deep_forward, [shape((full, deep))] * 2, (preact, partner, other, upstream[0].T))
+    output, grad_pre = call(
+        deep_forward,
+        [shape((full, deep))] * 2,
+        (preact, partner, other, upstream[0].T),
+        behind=(deep_slab,),
+    )
+    deep_slab = lax.all_to_all(deep_slab, "wide", 0, 0, axis_index_groups=near)
+    first, last = call(edges, [shape((size, cols + deep))] * 2, (fine_slab, deep_slab))
+    before = lax.ppermute(last, "wide", [(i, i + MEMBERS) for i in range(wide - MEMBERS)])
+    after = lax.ppermute(first, "wide", [(i + MEMBERS, i) for i in range(wide - MEMBERS)])
 
     pre_partner, other = pairs(grad_pre, grad_pre)
     pre_near = swap(grad_pre, 2)
@@ -349,57 +380,36 @@
         (at, pre_partner, grad_pre, other, w_deep),
         [pltpu.VMEM((2, full, deep), BF), pltpu.VMEM((depth, deep), BF)],
         flops=2 * 9 * deep * depth * full,
-        behind=(pre_near,),
+        behind=(pre_near, before, after),
     )
     pre_far = swap(jnp.stack([grad_pre, pre_near]), 4)
-    deep_slab = call(
-        deep_slices,
-        shape((MEMBERS, size, deep)),
-        (pooled, pick),
-        flops=2 * depth * depth * deep,
-        behind=(parts[0],),
-    )
-    deep_slab = lax.all_to_all(deep_slab, "wide", 0, 0, axis_index_groups=near)
-    got = [across(parts[s], s) for s in (1, 2, 3)]
-    grad_pool = call(pool_sum, shape((fine, deep)), (parts[0], *got), behind=(pre_far,))
-    pool_partner, other = pairs(grad_pool, grad_pool)
-    pool_near = swap(grad_pool, 2)
-    pre_rest = swap(jnp.concatenate([pre_near[None], pre_far]), 1)
-    back = call(
-        fine_backward,
-        shape((pieces, rows, part, depth)),
-        (at, pool_partner, grad_pool, other, w_fine),
-        [pltpu.VMEM((2, fine, deep), BF)],
-        flops=2 * 18 * cols * depth * fine,
-        behind=(pool_near,),
-    )
-    partial = lax.all_to_all(back, "narrow", 0, 0)
-    grad_latent = jnp.sum(partial.astype(F32), axis=0).astype(BF)
-
-    first, last = call(
-        edges, [shape((size, cols + deep))] * 2, (fine_slab, deep_slab), behind=(grad_pool,)
-    )
-    before = lax.ppermute(last, "wide", [(i, i + MEMBERS) for i in range(wide - MEMBERS)])
-    after = lax.ppermute(first, "wide", [(i + MEMBERS, i) for i in range(wide - MEMBERS)])
-    pool_far = swap(jnp.stack([grad_pool, pool_near]), 4)
-    pool_rest = swap(jnp.concatenate([pool_near[None], pool_far]), 1)
     fine_table, deep_table = call(
         tables,
         [shape((9 * size, MEMBERS * deep))] * 2,
         (fine_slab, deep_slab, before, after),
         flops=2 * 9 * size * 6 * deep * 2 * deep,
-        behind=(back,),
-    )
-
-    def owners(table, *grads):
+        behind=(parts[0],),
+    )
+    got = [across(parts[s], s) for s in (1, 2, 3)]
+    grad_pool = call(pool_sum, shape((fine, deep)), (parts[0], *got), behind=(pre_far, deep_table))
+    pool_partner, other = pairs(grad_pool, grad_pool)
+    pool_near = swap(grad_pool, 2)
+    pre_rest = swap(jnp.concatenate([pre_near[None], pre_far]), 1)
+    pool_far = swap(jnp.stack([grad_pool, pool_near]), 4)
+    pool_rest = swap(jnp.concatenate([pool_near[None], pool_far]), 1)
+
+    def products(table, *grads):
         width = grads[0].shape[0]
-        parts = call(
+        return call(
             weight_part,
             [shape((2, block, width))] * 4,
             (at, *grads, table, order),
             [pltpu.VMEM((MEMBERS, width, deep), BF), pltpu.VMEM((groups * block, width), BF)],
             flops=2 * 9 * size * MEMBERS * deep * width,
         )
+
+    def owners(parts):
+        width = parts[0].shape[2]
         got = [
             lax.ppermute(
                 parts[s], "wide", [(i, i // 32 * 32 + (i // 8 + s) % 4 * 8 + i % 8) for i in range(wide)]
@@ -410,8 +420,22 @@
         total = call(weight_sum, shape((9, grain, width), F32), (keep, swap(send, 32)))
         return total.reshape(3, 3, grain, width)
 
-    grad_deep = owners(deep_table, grad_pre, pre_partner, pre_near, pre_far, pre_rest)
-    grad_fine = owners(fine_table, grad_pool, pool_partner, pool_near, pool_far, pool_rest)
+    deep_parts = products(deep_table, grad_pre, pre_partner, pre_near, pre_far, pre_rest)
+    fine_parts = products(fine_table, grad_pool, pool_partner, pool_near, pool_far, pool_rest)
+    back = call(
+        fine_backward,
+        shape((pieces, rows, part, depth)),
+        (at, pool_partner, grad_pool, other, w_fine),
+        [pltpu.VMEM((2, fine, deep), BF), pltpu.VMEM(w_fine.shape, BF), pltpu.SemaphoreType.DMA((9,))],
+        flops=2 * 18 * cols * depth * fine,
+        behind=(deep_parts[0], fine_parts[0]),
+        remote=(4,),
+    )
+    partial = lax.all_to_all(back, "narrow", 0, 0)
+    grad_latent = jnp.sum(partial.astype(F32), axis=0).astype(BF)
+
+    grad_deep = owners(deep_parts)
+    grad_fine = owners(fine_parts)
     return output.T[None], grad_latent, grad_fine, grad_deep
 
 

time: 184 us -> 178 us (0.967)
  waiting for transfers between devices: 65 us -> 40.1 us
  starting transfers between devices: 88.8 us -> 101 us
  Pallas kernels: 20.4 us -> 26.2 us
    ppermute x1, waiting for transfers between devices: 20.8 us -> 4.27 us  [on_device(): lax.ppermute(first, 'wide', [(i + MEMBERS, i) for i in range(wide - MEMBE...]
    ppermute x12, starting transfers between devices: 25 us -> 34.8 us  [swap(): return lax.ppermute(v, 'wide', [(i, i ^ bit) for i in range(wide)])]
    pallas_call x18, Pallas kernels: 20.4 us -> 26.2 us  [call(): pl.pallas_call(kernel, out_shape=outs, in_specs=[smem if a.dtype == jnp.i...]
    ppermute x12, waiting for transfers between devices: 16.6 us -> 11 us  [swap(): return lax.ppermute(v, 'wide', [(i, i ^ bit) for i in range(wide)])]
    all_to_all x1, waiting for transfers between devices: 3.91 us -> 0.25 us  [on_device(): deep_slab = lax.all_to_all(deep_slab, 'wide', 0, 0, axis_index_groups=near)]
    ppermute x6, starting transfers between devices: 24.8 us -> 27.5 us  [owners(): lax.ppermute(parts[s], 'wide', [(i, i // 32 * 32 + (i // 8 + s) % 4 * 8 +...]
    unnamed x14 -> x16, local copies, waits for them, and re-layouts: 4.86 us -> 5.95 us
where the time goes in v5:
time: 178 us; the launch traced here: 177 us
  starting transfers between devices  101 us (57%)
  waiting for transfers between devices  40.1 us (23%)
  Pallas kernels  26.2 us (15%)
  local copies, waits for them, and re-layouts  8 us (4%)
    ppermute x12, starting transfers between devices, swap(): return lax.ppermute(v, 'wide', [(i, i ^ bit) for i in range(wide)])  34.8 us
    ppermute x6, starting transfers between devices, owners(): lax.ppermute(parts[s], 'wide', [(i, i // 32 * 32 + (i // 8 + s) % 4 * 8 +...  27.5 us
    pallas_call x18, Pallas kernels, call(): pl.pallas_call(kernel, out_shape=outs, in_specs=[smem if a.dtype == jnp.i...  26.2 us
    all_to_all x1, waiting for transfers between devices, on_device(): lax.all_to_all(jnp.broadcast_to(latent[None], (pieces,) + latent.shape),...  13.9 us
    ppermute x12, waiting for transfers between devices, swap(): return lax.ppermute(v, 'wide', [(i, i ^ bit) for i in range(wide)])  11 us
    ppermute x6, starting transfers between devices, across(): lax.ppermute(v, 'narrow', [(i, (i + step) % pieces) for i in range(pieces)])  9.63 us
    all_to_all x1, starting transfers between devices, on_device(): deep_slab = lax.all_to_all(deep_slab, 'wide', 0, 0, axis_index_groups=near)  6.33 us
    ppermute x6, waiting for transfers between devices, across(): lax.ppermute(v, 'narrow', [(i, (i + step) % pieces) for i in range(pieces)])  6.04 us
  transfers between devices with their start and end apart: 34, of which 16 were waited for; matrix products, arithmetic and copies ran while one was open for 1% of the time, Pallas kernels for 7%

profile of v5, /device:TPU:32, one launch (start us, length us, event | category | flops | bytes accessed | tf_op | source)
XLA Modules:
  0.0 177.4 jit_solution(12709189011167328797)
XLA Ops:
  2.6 6.0 %all-to-all-start = ((bf16[4,2,64,640]{3,2,1,0:T(8,128)(2,1)}), bf16[4,2,64,640]{3,2,1,0:T(8,128)(2,1)S(1)}, u32[]{:S(2)}, u32[]{:S(2)}) async-start(bf16[4,2,64,640]{3,2,1,0:T(8,128)(2,1)} %broadcast_in_dim.4), calls=%async_computation | async-start | bytes 1310720 | tf_op jit(solution)/shard_map/all_to_all | solution.py:330
  8.7 13.9 %all-to-all-done.refs_1_.refs_0_ = bf16[4,2,64,640]{3,2,1,0:T(8,128)(2,1)S(1)} async-done(((bf16[4,2,64,640]{3,2,1,0:T(8,128)(2,1)}), bf16[4,2,64,640]{3,2,1,0:T(8,128)(2,1)S(1)}, u32[]{:S(2)}, u32[]{:S(2)}) %all-to-all-start) | async-done | bytes 655392 | tf_op jit(solution)/shard_map/all_to_all | solution.py:330
  22.6 4.4 %shard_map.93 = (f32[160,128]{1,0:T(8,128)S(1)}, bf16[160,128]{1,0:T(8,128)(2,1)S(1)}, bf16[160,128]{1,0:T(8,128)(2,1)S(1)}) custom-call(s32[5]{0:T(128)S(1)} %stack.41.refs_0_, bf16[4,2,64,640]{3,2,1,0:T(8,128)(2,1)S(1)} %all-to-all-done.refs_1_.refs_0_, bf16[9,160,640]{2,1,0:T(8,128)(2,1)S(1)} %bitcast.35), custom_call_target="tpu_custom_call" | custom-call | flops 1226833920 | bytes 2498580 | tf_op jit(solution)/shard_map/pallas_call | solution.py:62
  27.1 2.6 %shard_map.94.refs_3_ = bf16[8,80,512]{2,1,0:T(8,128)(2,1)} custom-call(bf16[4,2,64,640]{3,2,1,0:T(8,128)(2,1)S(1)} %all-to-all-done.refs_1_.refs_0_, bf16[640,640]{1,0:T(8,128)(2,1)S(1)} %copy-done.4, f32[160,128]{1,0:T(8,128)S(1)} %get-tuple-element.32.refs_2_.refs_0_), custom_call_target="tpu_custom_call" | custom-call | flops 419430400 | bytes 1474560 | tf_op jit(solution)/shard_map/pallas_call | solution.py:62
  29.6 4.3 %all-to-all-start.1 = ((bf16[8,80,512]{2,1,0:T(8,128)(2,1)}), bf16[8,80,512]{2,1,0:T(8,128)(2,1)S(1)}, u32[]{:S(2)}, u32[]{:S(2)}) async-start(bf16[8,80,512]{2,1,0:T(8,128)(2,1)} %shard_map.94.refs_3_), calls=%async_computation.1 | async-start | bytes 1310720 | tf_op jit(solution)/shard_map/all_to_all | solution.py:348
  36.9 4.2 %collective-permute-start.3 = (bf16[160,128]{1,0:T(8,128)(2,1)S(1)}, bf16[160,128]{1,0:T(8,128)(2,1)S(1)}, u32[]{:S(2)}, u32[]{:S(2)}) collective-permute-start(bf16[160,128]{1,0:T(8,128)(2,1)S(1)} %shard_map.95.refs_1_), channel_id=1, source_target_pairs={{0,2},{1,3},{2,0},{3,1},{4,6},{5,7},{6,4},{7,5},{8,10},{9,11},{10,... | collective-permute-start | bytes 122888 | tf_op jit(solution)/shard_map/ppermute | solution.py:321
  41.1 2.4 %collective-permute-done.3.refs_3_ = bf16[160,128]{1,0:T(8,128)(2,1)S(1)} collective-permute-done((bf16[160,128]{1,0:T(8,128)(2,1)S(1)}, bf16[160,128]{1,0:T(8,128)(2,1)S(1)}, u32[]{:S(2)}, u32[]{:S(2)}) %collective-permute-start.3) | collective-permute-done | bytes 40992 | tf_op jit(solution)/shard_map/ppermute | solution.py:321
  46.2 2.0 %copy-done = bf16[3,3,640,320]{2,3,1,0:T(8,128)(2,1)S(1)} copy-done((bf16[3,3,640,320]{2,3,1,0:T(8,128)(2,1)S(1)}, bf16[3,3,640,320]{2,3,1,0:T(8,128)(2,1)}, u32[]{:S(2)}) %copy-start) | copy-done | bytes 3686424
  49.6 6.7 %collective-permute-start.5 = (bf16[320,128]{1,0:T(8,128)(2,1)S(1)}, bf16[320,128]{1,0:T(8,128)(2,1)S(1)}, u32[]{:S(2)}, u32[]{:S(2)}) collective-permute-start(bf16[320,128]{1,0:T(8,128)(2,1)S(1)} %get-tuple-element.36), channel_id=1, source_target_pairs={{0,4},{4,0},{8,12},{12,8},{16,20},{20,16},{24,28},{28,24},{32,36},... | collective-permute-start | bytes 245768 | tf_op jit(solution)/shard_map/ppermute | solution.py:324
  59.6 5.1 %collective-permute-start.9 = (bf16[320,128]{1,0:T(8,128)(2,1)S(1)}, bf16[320,128]{1,0:T(8,128)(2,1)S(1)}, u32[]{:S(2)}, u32[]{:S(2)}) collective-permute-start(bf16[320,128]{1,0:T(8,128)(2,1)S(1)} %get-tuple-element.39.refs_2_.refs_1_), channel_id=1, source_target_pairs={{0,8},{4,12},{8,0},{12,4},{16,24},{20,28},{24,16},{28,20},{32,40},... | collective-permute-start | bytes 245768 | tf_op jit(solution)/shard_map/ppermute | solution.py:324
  64.8 6.3 %all-to-all-start.2 = ((bf16[8,80,128]{2,1,0:T(8,128)(2,1)}), bf16[8,80,128]{2,1,0:T(8,128)(2,1)S(1)}, u32[]{:S(2)}, u32[]{:S(2)}) async-start(bf16[8,80,128]{2,1,0:T(8,128)(2,1)} %shard_map.98.refs_4_), calls=%async_computation.2 | async-start | bytes 327680 | tf_op jit(solution)/shard_map/all_to_all | solution.py:370
  72.3 5.0 %collective-permute-start.15 = (bf16[2,320,128]{2,1,0:T(8,128)(2,1)S(1)}, bf16[2,320,128]{2,1,0:T(8,128)(2,1)S(1)}, u32[]{:S(2)}, u32[]{:S(2)}) collective-permute-start(bf16[2,320,128]{2,1,0:T(8,128)(2,1)S(1)} %pad_maximum_fusion.1), channel_id=1, source_target_pairs={{0,16},{4,20},{8,24},{12,28},{16,0},{20,4},{24,8},{28,12},{32,48},... | collective-permute-start | bytes 491528 | tf_op jit(solution)/shard_map/ppermute | solution.py:324
  77.6 3.5 %collective-permute-start.10 = (bf16[80,384]{1,0:T(8,128)(2,1)S(1)}, bf16[80,384]{1,0:T(8,128)(2,1)S(1)}, u32[]{:S(2)}, u32[]{:S(2)}) collective-permute-start(bf16[80,384]{1,0:T(8,128)(2,1)S(1)} %get-tuple-element.40), channel_id=1, source_target_pairs={{0,32},{4,36},{8,40},{12,44},{16,48},{20,52},{24,56},{28,60},{32,6... | collective-permute-start | bytes 184328 | tf_op jit(solution)/shard_map/ppermute | solution.py:372
  82.9 4.3 %collective-permute-done.11.refs_7_.refs_3_ = bf16[80,384]{1,0:T(8,128)(2,1)S(1)} collective-permute-done((bf16[80,384]{1,0:T(8,128)(2,1)S(1)}, bf16[80,384]{1,0:T(8,128)(2,1)S(1)}, u32[]{:S(2)}, u32[]{:S(2)}) %collective-permute-start.11) | collective-permute-done | bytes 61472 | tf_op jit(solution)/shard_map/ppermute | solution.py:373
  87.2 2.0 %copy-done.2 = bf16[3,3,640,320]{2,3,1,0:T(8,128)(2,1)S(1)} copy-done((bf16[3,3,640,320]{2,3,1,0:T(8,128)(2,1)S(1)}, bf16[3,3,640,320]{2,3,1,0:T(8,128)(2,1)}, u32[]{:S(2)}) %copy-start.2) | copy-done | bytes 3686424
  91.5 2.4 %collective-permute-start.13 = (bf16[160,128]{1,0:T(8,128)(2,1)S(1)}, bf16[160,128]{1,0:T(8,128)(2,1)S(1)}, u32[]{:S(2)}, u32[]{:S(2)}) collective-permute-start(bf16[160,128]{1,0:T(8,128)(2,1)S(1)} %get-tuple-element.44), channel_id=1, source_target_pairs={{0,2},{1,3},{2,0},{3,1},{4,6},{5,7},{6,4},{7,5},{8,10},{9,11},{10,... | collective-permute-start | bytes 122888 | tf_op jit(solution)/shard_map/ppermute | solution.py:321
  98.7 3.4 %collective-permute-done.19.refs_3_ = bf16[160,128]{1,0:T(8,128)(2,1)S(1)} collective-permute-done((bf16[160,128]{1,0:T(8,128)(2,1)S(1)}, bf16[160,128]{1,0:T(8,128)(2,1)S(1)}, u32[]{:S(2)}, u32[]{:S(2)}) %collective-permute-start.19) | collective-permute-done | bytes 40992 | tf_op jit(solution)/shard_map/ppermute | solution.py:324
  102.1 2.1 %collective-permute-start.20 = (bf16[2,160,128]{2,1,0:T(8,128)(2,1)S(1)}, bf16[2,160,128]{2,1,0:T(8,128)(2,1)S(1)}, u32[]{:S(2)}, u32[]{:S(2)}) collective-permute-start(bf16[2,160,128]{2,1,0:T(8,128)(2,1)S(1)} %pad_maximum_fusion.3), channel_id=1, source_target_pairs={{0,16},{4,20},{8,24},{12,28},{16,0},{20,4},{24,8},{28,12},{32,48},... | collective-permute-start | bytes 245768 | tf_op jit(solution)/shard_map/ppermute | solution.py:324
  104.2 2.1 %collective-permute-start.18 = (bf16[3,320,128]{2,1,0:T(8,128)(2,1)S(1)}, bf16[3,320,128]{2,1,0:T(8,128)(2,1)S(1)}, u32[]{:S(2)}, u32[]{:S(2)}) collective-permute-start(bf16[3,320,128]{2,1,0:T(8,128)(2,1)S(1)} %pad_maximum_fusion), channel_id=1, source_target_pairs={{0,4},{4,0},{8,12},{12,8},{16,20},{20,16},{24,28},{28,24},{32,36},... | collective-permute-start | bytes 737288 | tf_op jit(solution)/shard_map/ppermute | solution.py:324
  108.2 2.9 %collective-permute-start.21 = (bf16[3,160,128]{2,1,0:T(8,128)(2,1)S(1)}, bf16[3,160,128]{2,1,0:T(8,128)(2,1)S(1)}, u32[]{:S(2)}, u32[]{:S(2)}) collective-permute-start(bf16[3,160,128]{2,1,0:T(8,128)(2,1)S(1)} %pad_maximum_fusion.2), channel_id=1, source_target_pairs={{0,4},{4,0},{8,12},{12,8},{16,20},{20,16},{24,28},{28,24},{32,36},... | collective-permute-start | bytes 368648 | tf_op jit(solution)/shard_map/ppermute | solution.py:324
  112.3 3.1 %shard_map.105 = (bf16[2,96,160]{2,1,0:T(8,128)(2,1)S(1)}, bf16[2,96,160]{2,1,0:T(8,128)(2,1)}, bf16[2,96,160]{2,1,0:T(8,128)(2,1)S(1)}, bf16[2,96,160]{2,1,0:T(8,128)(2,1)S(1)}) custom-call(s32[5]{0:T(128)S(1)} %stack.41.refs_0_, bf16[160,128]{1,0:T(8,128)(2,1)S(1)} %shard_map.103.refs_1_.refs_2_, ...), custom_call_target="tpu_custom_call" | custom-call | flops 235929600 | bytes 2908180 | tf_op jit(solution)/shard_map/pallas_call | solution.py:62
  115.3 2.9 %shard_map.104 = (bf16[2,96,320]{2,1,0:T(8,128)(2,1)S(1)}, bf16[2,96,320]{2,1,0:T(8,128)(2,1)S(1)}, bf16[2,96,320]{2,1,0:T(8,128)(2,1)S(1)}, bf16[2,96,320]{2,1,0:T(8,128)(2,1)S(1)}) custom-call(s32[5]{0:T(128)S(1)} %stack.41.refs_0_, bf16[320,128]{1,0:T(8,128)(2,1)S(1)} %get-tuple-element.39.refs_2_.refs_1_, ...), custom_call_target="tpu_custom_call" | custom-call | flops 471859200 | bytes 3235860 | tf_op jit(solution)/shard_map/pallas_call | solution.py:62
  118.2 5.5 %shard_map.106 = bf16[4,2,64,640]{3,2,1,0:T(8,128)(2,1)} custom-call(s32[5]{0:T(128)S(1)} %stack.41.refs_0_, bf16[160,128]{1,0:T(8,128)(2,1)S(1)} %collective-permute-done.16.refs_2_.refs_1_, bf16[160,128]{1,0:T(8,128)(2,1)S(1)} %shard_map.103.refs_1_.refs_2_, bf16[160,128]{1,0:T(8,128)(2,1)S(1)} %collective-permute-done.17.refs_3_, ...), custom_call_target="tpu_custom_call" | custom-call | flops 943718400 | bytes 1966100 | tf_op jit(solution)/shard_map/pallas_call | solution.py:62
  123.8 5.4 %all-to-all-start.3 = ((bf16[4,2,64,640]{3,2,1,0:T(8,128)(2,1)}), bf16[4,2,64,640]{3,2,1,0:T(8,128)(2,1)S(1)}, u32[]{:S(2)}, u32[]{:S(2)}) async-start(bf16[4,2,64,640]{3,2,1,0:T(8,128)(2,1)} %shard_map.106), calls=%async_computation.3 | async-start | bytes 1310720 | tf_op jit(solution)/shard_map/all_to_all | solution.py:434
  129.2 7.4 %collective-permute-start.26 = (bf16[2,96,320]{2,1,0:T(8,128)(2,1)S(1)}, bf16[2,96,320]{2,1,0:T(8,128)(2,1)S(1)}, u32[]{:S(2)}, u32[]{:S(2)}) collective-permute-start(bf16[2,96,320]{2,1,0:T(8,128)(2,1)S(1)} %get-tuple-element.55), channel_id=1, source_target_pairs={{0,32},{4,36},{8,40},{12,44},{16,48},{20,52},{24,56},{28,60},{32,6... | collective-permute-start | bytes 368648 | tf_op jit(solution)/shard_map/ppermute | solution.py:414
  136.6 15.1 %collective-permute-start.27 = (bf16[2,96,320]{2,1,0:T(8,128)(2,1)S(1)}, bf16[2,96,320]{2,1,0:T(8,128)(2,1)S(1)}, u32[]{:S(2)}, u32[]{:S(2)}) collective-permute-start(bf16[2,96,320]{2,1,0:T(8,128)(2,1)S(1)} %get-tuple-element.56), channel_id=1, source_target_pairs={{0,64},{4,68},{8,72},{12,76},{16,80},{20,84},{24,88},{28,92},{32,9... | collective-permute-start | bytes 368648 | tf_op jit(solution)/shard_map/ppermute | solution.py:414
  151.8 2.0 %collective-permute-start.22 = (bf16[2,96,160]{2,1,0:T(8,128)(2,1)}, bf16[2,96,160]{2,1,0:T(8,128)(2,1)S(1)}, u32[]{:S(2)}, u32[]{:S(2)}) collective-permute-start(bf16[2,96,160]{2,1,0:T(8,128)(2,1)} %get-tuple-element.50), channel_id=1, source_target_pairs={{0,32},{4,36},{8,40},{12,44},{16,48},{20,52},{24,56},{28,60},{32,6... | collective-permute-start | bytes 184328 | tf_op jit(solution)/shard_map/ppermute | solution.py:414
  154.1 2.9 %collective-permute-start.24 = (bf16[2,96,160]{2,1,0:T(8,128)(2,1)S(1)}, bf16[2,96,160]{2,1,0:T(8,128)(2,1)S(1)}, u32[]{:S(2)}, u32[]{:S(2)}) collective-permute-start(bf16[2,96,160]{2,1,0:T(8,128)(2,1)S(1)} %get-tuple-element.52), channel_id=1, source_target_pairs={{0,96},{4,100},{8,104},{12,108},{16,112},{20,116},{24,120},{28,124... | collective-permute-start | bytes 184328 | tf_op jit(solution)/shard_map/ppermute | solution.py:414
  157.0 2.6 %collective-permute-done.27.refs_3_ = bf16[2,96,320]{2,1,0:T(8,128)(2,1)S(1)} collective-permute-done((bf16[2,96,320]{2,1,0:T(8,128)(2,1)S(1)}, bf16[2,96,320]{2,1,0:T(8,128)(2,1)S(1)}, u32[]{:S(2)}, u32[]{:S(2)}) %collective-permute-start.27) | collective-permute-done | bytes 122912 | tf_op jit(solution)/shard_map/ppermute | solution.py:414
  160.3 6.1 %collective-permute-start.29 = (bf16[96,320]{1,0:T(8,128)(2,1)S(1)}, bf16[96,320]{1,0:T(8,128)(2,1)S(1)}, u32[]{:S(2)}, u32[]{:S(2)}) collective-permute-start(bf16[96,320]{1,0:T(8,128)(2,1)S(1)} %get-tuple-element.59), channel_id=1, source_target_pairs={{0,128},{4,132},{8,136},{12,140},{16,144},{20,148},{24,152},{28,15... | collective-permute-start | bytes 184328 | tf_op jit(solution)/shard_map/ppermute | solution.py:324
  167.0 3.1 %collective-permute-start.25 = (bf16[96,160]{1,0:T(8,128)(2,1)S(1)}, bf16[96,160]{1,0:T(8,128)(2,1)S(1)}, u32[]{:S(2)}, u32[]{:S(2)}) collective-permute-start(bf16[96,160]{1,0:T(8,128)(2,1)S(1)} %get-tuple-element.54), channel_id=1, source_target_pairs={{0,128},{4,132},{8,136},{12,140},{16,144},{20,148},{24,152},{28,15... | collective-permute-start | bytes 92168 | tf_op jit(solution)/shard_map/ppermute | solution.py:324
  170.1 5.0 %collective-permute-done.25.refs_1_ = bf16[96,160]{1,0:T(8,128)(2,1)S(1)} collective-permute-done((bf16[96,160]{1,0:T(8,128)(2,1)S(1)}, bf16[96,160]{1,0:T(8,128)(2,1)S(1)}, u32[]{:S(2)}, u32[]{:S(2)}) %collective-permute-start.25) | collective-permute-done | bytes 30752 | tf_op jit(solution)/shard_map/ppermute | solution.py:324
  (77 shorter events, 29.6 us)
Async XLA Ops:
  2.6 20.0 %all-to-all-start = ((bf16[4,2,64,640]{3,2,1,0:T(8,128)(2,1)}), bf16[4,2,64,640]{3,2,1,0:T(8,128)(2,1)S(1)}, u32[]{:S(2)}, u32[]{:S(2)}) async-start(bf16[4,2,64,640]{3,2,1,0:T(8,128)(2,1)} %broadcast_in_dim.4), calls=%async_computation | async-start | bytes 1310720 | tf_op jit(solution)/shard_map/all_to_all | solution.py:330
  29.6 16.5 %all-to-all-start.1 = ((bf16[8,80,512]{2,1,0:T(8,128)(2,1)}), bf16[8,80,512]{2,1,0:T(8,128)(2,1)S(1)}, u32[]{:S(2)}, u32[]{:S(2)}) async-start(bf16[8,80,512]{2,1,0:T(8,128)(2,1)} %shard_map.94.refs_3_), calls=%async_computation.1 | async-start | bytes 1310720 | tf_op jit(solution)/shard_map/all_to_all | solution.py:348
  34.0 1.4 collective-permute-start
  35.4 5.7 %collective-permute-start.2 = (bf16[160,128]{1,0:T(8,128)(2,1)S(1)}, bf16[160,128]{1,0:T(8,128)(2,1)S(1)}, u32[]{:S(2)}, u32[]{:S(2)}) collective-permute-start(bf16[160,128]{1,0:T(8,128)(2,1)S(1)} %shard_map.95.refs_1_), channel_id=1, source_target_pairs={{0,1},{1,2},{2,3},{3,0},{4,5},{5,6},{6,7},{7,4},{8,9},{9,10},{10,1... | collective-permute-start | bytes 122888 | tf_op jit(solution)/shard_map/ppermute | solution.py:321
  36.9 6.6 %collective-permute-start.3 = (bf16[160,128]{1,0:T(8,128)(2,1)S(1)}, bf16[160,128]{1,0:T(8,128)(2,1)S(1)}, u32[]{:S(2)}, u32[]{:S(2)}) collective-permute-start(bf16[160,128]{1,0:T(8,128)(2,1)S(1)} %shard_map.95.refs_1_), channel_id=1, source_target_pairs={{0,2},{1,3},{2,0},{3,1},{4,6},{5,7},{6,4},{7,5},{8,10},{9,11},{10,... | collective-permute-start | bytes 122888 | tf_op jit(solution)/shard_map/ppermute | solution.py:321
  41.1 4.0 %collective-permute-start.4 = (bf16[160,128]{1,0:T(8,128)(2,1)S(1)}, bf16[160,128]{1,0:T(8,128)(2,1)S(1)}, u32[]{:S(2)}, u32[]{:S(2)}) collective-permute-start(bf16[160,128]{1,0:T(8,128)(2,1)S(1)} %shard_map.95.refs_1_), channel_id=1, source_target_pairs={{0,3},{1,0},{2,1},{3,2},{4,7},{5,4},{6,5},{7,6},{8,11},{9,8},{10,9... | collective-permute-start | bytes 122888 | tf_op jit(solution)/shard_map/ppermute | solution.py:321
  49.6 8.9 %collective-permute-start.5 = (bf16[320,128]{1,0:T(8,128)(2,1)S(1)}, bf16[320,128]{1,0:T(8,128)(2,1)S(1)}, u32[]{:S(2)}, u32[]{:S(2)}) collective-permute-start(bf16[320,128]{1,0:T(8,128)(2,1)S(1)} %get-tuple-element.36), channel_id=1, source_target_pairs={{0,4},{4,0},{8,12},{12,8},{16,20},{20,16},{24,28},{28,24},{32,36},... | collective-permute-start | bytes 245768 | tf_op jit(solution)/shard_map/ppermute | solution.py:324
  56.3 2.2 %collective-permute-start.6 = (bf16[320,128]{1,0:T(8,128)(2,1)S(1)}, bf16[320,128]{1,0:T(8,128)(2,1)S(1)}, u32[]{:S(2)}, u32[]{:S(2)}) collective-permute-start(bf16[320,128]{1,0:T(8,128)(2,1)S(1)} %get-tuple-element.37), channel_id=1, source_target_pairs={{4,8},{8,4},{12,16},{16,12},{20,24},{24,20},{28,32},{32,28},{36,40... | collective-permute-start | bytes 245768 | tf_op jit(solution)/shard_map/ppermute | solution.py:327
  59.6 12.6 %collective-permute-start.9 = (bf16[320,128]{1,0:T(8,128)(2,1)S(1)}, bf16[320,128]{1,0:T(8,128)(2,1)S(1)}, u32[]{:S(2)}, u32[]{:S(2)}) collective-permute-start(bf16[320,128]{1,0:T(8,128)(2,1)S(1)} %get-tuple-element.39.refs_2_.refs_1_), channel_id=1, source_target_pairs={{0,8},{4,12},{8,0},{12,4},{16,24},{20,28},{24,16},{28,20},{32,40},... | collective-permute-start | bytes 245768 | tf_op jit(solution)/shard_map/ppermute | solution.py:324
  64.8 12.8 %all-to-all-start.2 = ((bf16[8,80,128]{2,1,0:T(8,128)(2,1)}), bf16[8,80,128]{2,1,0:T(8,128)(2,1)S(1)}, u32[]{:S(2)}, u32[]{:S(2)}) async-start(bf16[8,80,128]{2,1,0:T(8,128)(2,1)} %shard_map.98.refs_4_), calls=%async_computation.2 | async-start | bytes 327680 | tf_op jit(solution)/shard_map/all_to_all | solution.py:370
  71.1 11.3 %collective-permute-start.7 = (bf16[320,128]{1,0:T(8,128)(2,1)S(1)}, bf16[320,128]{1,0:T(8,128)(2,1)S(1)}, u32[]{:S(2)}, u32[]{:S(2)}) collective-permute-start(bf16[320,128]{1,0:T(8,128)(2,1)S(1)} %get-tuple-element.39.refs_2_.refs_1_), channel_id=1, source_target_pairs={{0,4},{4,0},{8,12},{12,8},{16,20},{20,16},{24,28},{28,24},{32,36},... | collective-permute-start | bytes 245768 | tf_op jit(solution)/shard_map/ppermute | solution.py:324
  71.6 10.8 %collective-permute-start.8 = (bf16[320,128]{1,0:T(8,128)(2,1)S(1)}, bf16[320,128]{1,0:T(8,128)(2,1)S(1)}, u32[]{:S(2)}, u32[]{:S(2)}) collective-permute-start(bf16[320,128]{1,0:T(8,128)(2,1)S(1)} %get-tuple-element.39.refs_2_.refs_1_), channel_id=1, source_target_pairs={{4,8},{8,4},{12,16},{16,12},{20,24},{24,20},{28,32},{32,28},{36,40... | collective-permute-start | bytes 245768 | tf_op jit(solution)/shard_map/ppermute | solution.py:327
  72.3 25.7 %collective-permute-start.15 = (bf16[2,320,128]{2,1,0:T(8,128)(2,1)S(1)}, bf16[2,320,128]{2,1,0:T(8,128)(2,1)S(1)}, u32[]{:S(2)}, u32[]{:S(2)}) collective-permute-start(bf16[2,320,128]{2,1,0:T(8,128)(2,1)S(1)} %pad_maximum_fusion.1), channel_id=1, source_target_pairs={{0,16},{4,20},{8,24},{12,28},{16,0},{20,4},{24,8},{28,12},{32,48},... | collective-permute-start | bytes 491528 | tf_op jit(solution)/shard_map/ppermute | solution.py:324
  77.6 5.3 %collective-permute-start.10 = (bf16[80,384]{1,0:T(8,128)(2,1)S(1)}, bf16[80,384]{1,0:T(8,128)(2,1)S(1)}, u32[]{:S(2)}, u32[]{:S(2)}) collective-permute-start(bf16[80,384]{1,0:T(8,128)(2,1)S(1)} %get-tuple-element.40), channel_id=1, source_target_pairs={{0,32},{4,36},{8,40},{12,44},{16,48},{20,52},{24,56},{28,60},{32,6... | collective-permute-start | bytes 184328 | tf_op jit(solution)/shard_map/ppermute | solution.py:372
  81.1 6.1 %collective-permute-start.11 = (bf16[80,384]{1,0:T(8,128)(2,1)S(1)}, bf16[80,384]{1,0:T(8,128)(2,1)S(1)}, u32[]{:S(2)}, u32[]{:S(2)}) collective-permute-start(bf16[80,384]{1,0:T(8,128)(2,1)S(1)} %get-tuple-element.41), channel_id=1, source_target_pairs={{32,0},{36,4},{40,8},{44,12},{48,16},{52,20},{56,24},{60,28},{64,3... | collective-permute-start | bytes 184328 | tf_op jit(solution)/shard_map/ppermute | solution.py:373
  91.2 4.7 %collective-permute-start.12 = (bf16[160,128]{1,0:T(8,128)(2,1)S(1)}, bf16[160,128]{1,0:T(8,128)(2,1)S(1)}, u32[]{:S(2)}, u32[]{:S(2)}) collective-permute-start(bf16[160,128]{1,0:T(8,128)(2,1)S(1)} %get-tuple-element.43), channel_id=1, source_target_pairs={{0,1},{1,2},{2,3},{3,0},{4,5},{5,6},{6,7},{7,4},{8,9},{9,10},{10,1... | collective-permute-start | bytes 122888 | tf_op jit(solution)/shard_map/ppermute | solution.py:321
  91.5 5.2 %collective-permute-start.13 = (bf16[160,128]{1,0:T(8,128)(2,1)S(1)}, bf16[160,128]{1,0:T(8,128)(2,1)S(1)}, u32[]{:S(2)}, u32[]{:S(2)}) collective-permute-start(bf16[160,128]{1,0:T(8,128)(2,1)S(1)} %get-tuple-element.44), channel_id=1, source_target_pairs={{0,2},{1,3},{2,0},{3,1},{4,6},{5,7},{6,4},{7,5},{8,10},{9,11},{10,... | collective-permute-start | bytes 122888 | tf_op jit(solution)/shard_map/ppermute | solution.py:321
  94.0 4.0 %collective-permute-start.14 = (bf16[160,128]{1,0:T(8,128)(2,1)S(1)}, bf16[160,128]{1,0:T(8,128)(2,1)S(1)}, u32[]{:S(2)}, u32[]{:S(2)}) collective-permute-start(bf16[160,128]{1,0:T(8,128)(2,1)S(1)} %get-tuple-element.45), channel_id=1, source_target_pairs={{0,3},{1,0},{2,1},{3,2},{4,7},{5,4},{6,5},{7,6},{8,11},{9,8},{10,9... | collective-permute-start | bytes 122888 | tf_op jit(solution)/shard_map/ppermute | solution.py:321
  98.0 4.1 %collective-permute-start.19 = (bf16[160,128]{1,0:T(8,128)(2,1)S(1)}, bf16[160,128]{1,0:T(8,128)(2,1)S(1)}, u32[]{:S(2)}, u32[]{:S(2)}) collective-permute-start(bf16[160,128]{1,0:T(8,128)(2,1)S(1)} %shard_map.103.refs_1_.refs_2_), channel_id=1, source_target_pairs={{0,8},{4,12},{8,0},{12,4},{16,24},{20,28},{24,16},{28,20},{32,40},... | collective-permute-start | bytes 122888 | tf_op jit(solution)/shard_map/ppermute | solution.py:324
  102.1 6.0 %collective-permute-start.20 = (bf16[2,160,128]{2,1,0:T(8,128)(2,1)S(1)}, bf16[2,160,128]{2,1,0:T(8,128)(2,1)S(1)}, u32[]{:S(2)}, u32[]{:S(2)}) collective-permute-start(bf16[2,160,128]{2,1,0:T(8,128)(2,1)S(1)} %pad_maximum_fusion.3), channel_id=1, source_target_pairs={{0,16},{4,20},{8,24},{12,28},{16,0},{20,4},{24,8},{28,12},{32,48},... | collective-permute-start | bytes 245768 | tf_op jit(solution)/shard_map/ppermute | solution.py:324
  104.2 11.1 %collective-permute-start.18 = (bf16[3,320,128]{2,1,0:T(8,128)(2,1)S(1)}, bf16[3,320,128]{2,1,0:T(8,128)(2,1)S(1)}, u32[]{:S(2)}, u32[]{:S(2)}) collective-permute-start(bf16[3,320,128]{2,1,0:T(8,128)(2,1)S(1)} %pad_maximum_fusion), channel_id=1, source_target_pairs={{0,4},{4,0},{8,12},{12,8},{16,20},{20,16},{24,28},{28,24},{32,36},... | collective-permute-start | bytes 737288 | tf_op jit(solution)/shard_map/ppermute | solution.py:324
  108.2 4.1 %collective-permute-start.21 = (bf16[3,160,128]{2,1,0:T(8,128)(2,1)S(1)}, bf16[3,160,128]{2,1,0:T(8,128)(2,1)S(1)}, u32[]{:S(2)}, u32[]{:S(2)}) collective-permute-start(bf16[3,160,128]{2,1,0:T(8,128)(2,1)S(1)} %pad_maximum_fusion.2), channel_id=1, source_target_pairs={{0,4},{4,0},{8,12},{12,8},{16,20},{20,16},{24,28},{28,24},{32,36},... | collective-permute-start | bytes 368648 | tf_op jit(solution)/shard_map/ppermute | solution.py:324
  111.1 7.1 %collective-permute-start.17 = (bf16[160,128]{1,0:T(8,128)(2,1)S(1)}, bf16[160,128]{1,0:T(8,128)(2,1)S(1)}, u32[]{:S(2)}, u32[]{:S(2)}) collective-permute-start(bf16[160,128]{1,0:T(8,128)(2,1)S(1)} %shard_map.103.refs_1_.refs_2_), channel_id=1, source_target_pairs={{4,8},{8,4},{12,16},{16,12},{20,24},{24,20},{28,32},{32,28},{36,40... | collective-permute-start | bytes 122888 | tf_op jit(solution)/shard_map/ppermute | solution.py:327
  123.8 52.8 %all-to-all-start.3 = ((bf16[4,2,64,640]{3,2,1,0:T(8,128)(2,1)}), bf16[4,2,64,640]{3,2,1,0:T(8,128)(2,1)S(1)}, u32[]{:S(2)}, u32[]{:S(2)}) async-start(bf16[4,2,64,640]{3,2,1,0:T(8,128)(2,1)} %shard_map.106), calls=%async_computation.3 | async-start | bytes 1310720 | tf_op jit(solution)/shard_map/all_to_all | solution.py:434
  129.2 24.9 %collective-permute-start.26 = (bf16[2,96,320]{2,1,0:T(8,128)(2,1)S(1)}, bf16[2,96,320]{2,1,0:T(8,128)(2,1)S(1)}, u32[]{:S(2)}, u32[]{:S(2)}) collective-permute-start(bf16[2,96,320]{2,1,0:T(8,128)(2,1)S(1)} %get-tuple-element.55), channel_id=1, source_target_pairs={{0,32},{4,36},{8,40},{12,44},{16,48},{20,52},{24,56},{28,60},{32,6... | collective-permute-start | bytes 368648 | tf_op jit(solution)/shard_map/ppermute | solution.py:414
  136.6 23.1 %collective-permute-start.27 = (bf16[2,96,320]{2,1,0:T(8,128)(2,1)S(1)}, bf16[2,96,320]{2,1,0:T(8,128)(2,1)S(1)}, u32[]{:S(2)}, u32[]{:S(2)}) collective-permute-start(bf16[2,96,320]{2,1,0:T(8,128)(2,1)S(1)} %get-tuple-element.56), channel_id=1, source_target_pairs={{0,64},{4,68},{8,72},{12,76},{16,80},{20,84},{24,88},{28,92},{32,9... | collective-permute-start | bytes 368648 | tf_op jit(solution)/shard_map/ppermute | solution.py:414
  151.7 7.9 %collective-permute-start.28 = (bf16[2,96,320]{2,1,0:T(8,128)(2,1)S(1)}, bf16[2,96,320]{2,1,0:T(8,128)(2,1)S(1)}, u32[]{:S(2)}, u32[]{:S(2)}) collective-permute-start(bf16[2,96,320]{2,1,0:T(8,128)(2,1)S(1)} %get-tuple-element.57), channel_id=1, source_target_pairs={{0,96},{4,100},{8,104},{12,108},{16,112},{20,116},{24,120},{28,124... | collective-permute-start | bytes 368648 | tf_op jit(solution)/shard_map/ppermute | solution.py:414
  151.8 14.6 %collective-permute-start.22 = (bf16[2,96,160]{2,1,0:T(8,128)(2,1)}, bf16[2,96,160]{2,1,0:T(8,128)(2,1)S(1)}, u32[]{:S(2)}, u32[]{:S(2)}) collective-permute-start(bf16[2,96,160]{2,1,0:T(8,128)(2,1)} %get-tuple-element.50), channel_id=1, source_target_pairs={{0,32},{4,36},{8,40},{12,44},{16,48},{20,52},{24,56},{28,60},{32,6... | collective-permute-start | bytes 184328 | tf_op jit(solution)/shard_map/ppermute | solution.py:414
  153.8 12.6 %collective-permute-start.23 = (bf16[2,96,160]{2,1,0:T(8,128)(2,1)S(1)}, bf16[2,96,160]{2,1,0:T(8,128)(2,1)S(1)}, u32[]{:S(2)}, u32[]{:S(2)}) collective-permute-start(bf16[2,96,160]{2,1,0:T(8,128)(2,1)S(1)} %get-tuple-element.51), channel_id=1, source_target_pairs={{0,64},{4,68},{8,72},{12,76},{16,80},{20,84},{24,88},{28,92},{32,9... | collective-permute-start | bytes 184328 | tf_op jit(solution)/shard_map/ppermute | solution.py:414
  154.1 12.3 %collective-permute-start.24 = (bf16[2,96,160]{2,1,0:T(8,128)(2,1)S(1)}, bf16[2,96,160]{2,1,0:T(8,128)(2,1)S(1)}, u32[]{:S(2)}, u32[]{:S(2)}) collective-permute-start(bf16[2,96,160]{2,1,0:T(8,128)(2,1)S(1)} %get-tuple-element.52), channel_id=1, source_target_pairs={{0,96},{4,100},{8,104},{12,108},{16,112},{20,116},{24,120},{28,124... | collective-permute-start | bytes 184328 | tf_op jit(solution)/shard_map/ppermute | solution.py:414
  160.3 15.5 %collective-permute-start.29 = (bf16[96,320]{1,0:T(8,128)(2,1)S(1)}, bf16[96,320]{1,0:T(8,128)(2,1)S(1)}, u32[]{:S(2)}, u32[]{:S(2)}) collective-permute-start(bf16[96,320]{1,0:T(8,128)(2,1)S(1)} %get-tuple-element.59), channel_id=1, source_target_pairs={{0,128},{4,132},{8,136},{12,140},{16,144},{20,148},{24,152},{28,15... | collective-permute-start | bytes 184328 | tf_op jit(solution)/shard_map/ppermute | solution.py:324
  167.0 8.1 %collective-permute-start.25 = (bf16[96,160]{1,0:T(8,128)(2,1)S(1)}, bf16[96,160]{1,0:T(8,128)(2,1)S(1)}, u32[]{:S(2)}, u32[]{:S(2)}) collective-permute-start(bf16[96,160]{1,0:T(8,128)(2,1)S(1)} %get-tuple-element.54), channel_id=1, source_target_pairs={{0,128},{4,132},{8,136},{12,140},{16,144},{20,148},{24,152},{28,15... | collective-permute-start | bytes 92168 | tf_op jit(solution)/shard_map/ppermute | solution.py:324
  (9 other events, 59.6 us)

commit v6 on v5

--- a/solution.py
+++ b/solution.py
@@ -11,6 +11,7 @@
 BF = jnp.bfloat16
 F32 = jnp.float32
 MEMBERS = 8
+CHAIN = 3 * 10**10
 
 
 def mm(a, b):
@@ -49,12 +50,13 @@
     return jax.ShapeDtypeStruct(dims, dtype)
 
 
-def call(body, outs, args, scratch=(), flops=0, behind=(), remote=()):
+def call(body, outs, args, scratch=(), behind=()):
     size = sum(a.size * a.dtype.itemsize for a in args)
     smem = pl.BlockSpec(memory_space=pltpu.SMEM)
     vmem = pl.BlockSpec(memory_space=pltpu.VMEM)
     aside = pl.BlockSpec(memory_space=pl.ANY)
     count = len(args)
+    flops = CHAIN if body in (fine_forward, pool_add, deep_sides, deep_forward, deep_backward, pool_sum, fine_backward) else 0
 
     def kernel(*refs):
         body(*refs[:count], *refs[count + len(behind) :])
@@ -62,13 +64,10 @@
     return pl.pallas_call(
         kernel,
         out_shape=outs,
-        in_specs=[
-            smem if a.dtype == jnp.int32 else aside if i in remote else vmem for i, a in enumerate(args)
-        ]
-        + [aside] * len(behind),
+        in_specs=[smem if a.dtype == jnp.int32 else vmem for a in args] + [aside] * len(behind),
         out_specs=jax.tree.map(lambda _: vmem, outs),
         scratch_shapes=list(scratch),
-        compiler_params=pltpu.CompilerParams(vmem_limit_bytes=40 * 2**20),
+        compiler_params=pltpu.CompilerParams(vmem_limit_bytes=16 * 2**20),
         cost_estimate=pl.CostEstimate(flops=flops, bytes_accessed=size, transcendentals=0),
     )(*args, *behind)
 
@@ -90,13 +89,6 @@
     return jnp.where(source == lax.broadcasted_iota(jnp.int32, (cols, cols), 1), 1.0, 0.0).astype(BF)
 
 
-def fetch(source, target, sems):
-    copies = [pltpu.make_async_copy(source.at[t], target.at[t], sems.at[t]) for t in range(source.shape[0])]
-    for copy in copies:
-        copy.start()
-    return copies
-
-
 def fine_rows(x):
     pieces = x.shape[0]
     return [jnp.concatenate([x[k, r] for k in range(pieces)]) for r in range(2)]
@@ -117,8 +109,9 @@
         other[...] = down
 
 
-def fine_forward(at, x, weights, own, partner, other, w, sems):
-    copies = fetch(weights, w, sems)
+def fine_forward(at, mine, got1, got2, got3, w, x, own, partner, other):
+    for s, piece in enumerate((mine, got1, got2, got3)):
+        x[jnp.bitwise_and(at[4] - s, 3)] = piece[...]
     deep = own.shape[1]
     rows = fine_rows(x)
     u0, us, u1 = [], [], []
@@ -129,8 +122,6 @@
         u1.append(u[1].astype(BF))
         us.append((u[0] + u[1]).astype(BF))
     pair = [jnp.concatenate([u0[b], u1[b]]) for b in range(3)]
-    for copy in copies:
-        copy.wait()
     mine = sum(mm_t(w[3 + b], us[b]) for b in range(3))
     first = sum(mm_t(w[b], pair[b]) for b in range(3))
     last = sum(mm_t(w[6 + b], pair[b]) for b in range(3))
@@ -190,8 +181,7 @@
     out[...] = sum(v[...].astype(F32) for v in (own, got1, got2, got3)).astype(BF)
 
 
-def fine_backward(at, partner, mine, other, weights, out, rows, w, sems):
-    copies = fetch(weights, w, sems)
+def fine_backward(at, partner, mine, other, w, out, rows):
     before, after = side_rows(at, partner, other, rows)
     deep = mine.shape[1]
     turn = unit(deep)
@@ -201,8 +191,6 @@
     top = jnp.concatenate([here, after])
     low = jnp.concatenate([before, here])
     z = []
-    for copy in copies:
-        copy.wait()
     for b in range(3):
         both = mm(top, w[b]) + mm(low, w[6 + b])
         mid = mm(here, w[3 + b])
@@ -268,9 +256,9 @@
                 fine[t * size : (t + 1) * size, i * cols : (i + 1) * cols] = rows[a].astype(BF)
 
 
-def weight_part(at, own, partner, near, far, rest, table, order, out0, out1, out2, out3, grads, parts):
+def weight_part(at, own, partner, four, eight, table, order, out0, out1, out2, out3, grads, parts):
     cols = own.shape[1]
-    blocks = (own[...], partner[...], near[...], rest[0], far[0], rest[1], far[1], rest[2])
+    blocks = [own[...], partner[...]] + [four[i] for i in range(2)] + [eight[i] for i in range(4)]
     for r, block in enumerate(blocks):
         grads[jnp.bitwise_xor(at[1], r)] = block
     total = sum(mm_t(table[:, i * cols : (i + 1) * cols], grads[i]) for i in range(MEMBERS))
@@ -327,22 +315,18 @@
         other = lax.ppermute(to_other, "wide", [(i, i - 1 + 2 * (i % 2)) for i in range(1, wide - 1)])
         return swap(to_partner, 1), other
 
-    x = lax.all_to_all(jnp.broadcast_to(latent[None], (pieces,) + latent.shape), "narrow", 0, 0)
-    own, partner, other = call(
+    got = [across(latent, s) for s in (1, 2, 3)]
+    x, own, partner, other = call(
         fine_forward,
-        [shape((fine, deep), F32), shape((fine, deep)), shape((fine, deep))],
-        (at, x, w_fine),
-        [pltpu.VMEM(w_fine.shape, BF), pltpu.SemaphoreType.DMA((9,))],
-        flops=2 * 9 * deep * depth * (2 * cols + 2 * fine),
-        remote=(2,),
+        [shape((pieces,) + latent.shape), shape((fine, deep), F32), shape((fine, deep)), shape((fine, deep))],
+        (at, latent, *got, w_fine),
     )
     partner, other = pairs(partner, other)
     fine_slab = call(
         fine_slices,
         shape((MEMBERS, size, rows * cols)),
         (x, pick),
-        flops=2 * depth * depth * rows * cols,
-        behind=(own,),
+        behind=(partner,),
     )
     mine = call(pool_add, shape((fine, deep)), (own, partner, other), behind=(fine_slab,))
     fine_slab = lax.all_to_all(fine_slab, "wide", 0, 0, axis_index_groups=near)
@@ -351,52 +335,41 @@
         deep_sides,
         [shape((depth, deep)), shape((full, deep)), shape((full, deep))],
         (at, mine, *got, w_deep),
-        flops=2 * 6 * deep * depth * full,
         behind=(fine_slab,),
     )
     partner, other = pairs(partner, other)
-    deep_slab = call(
-        deep_slices, shape((MEMBERS, size, deep)), (pooled, pick), flops=2 * depth * depth * deep
-    )
     preact = call(
-        deep_own, shape((full, deep), F32), (pooled, w_deep), flops=2 * 3 * deep * depth * full, behind=(pooled,)
+        deep_own, shape((full, deep), F32), (pooled, w_deep), behind=(pooled,)
     )
     output, grad_pre = call(
         deep_forward,
         [shape((full, deep))] * 2,
         (preact, partner, other, upstream[0].T),
-        behind=(deep_slab,),
-    )
+    )
+    pre_partner, other = pairs(grad_pre, grad_pre)
+    deep_slab = call(deep_slices, shape((MEMBERS, size, deep)), (pooled, pick), behind=(pre_partner,))
     deep_slab = lax.all_to_all(deep_slab, "wide", 0, 0, axis_index_groups=near)
-    first, last = call(edges, [shape((size, cols + deep))] * 2, (fine_slab, deep_slab))
-    before = lax.ppermute(last, "wide", [(i, i + MEMBERS) for i in range(wide - MEMBERS)])
-    after = lax.ppermute(first, "wide", [(i + MEMBERS, i) for i in range(wide - MEMBERS)])
-
-    pre_partner, other = pairs(grad_pre, grad_pre)
-    pre_near = swap(grad_pre, 2)
+    pre_four = swap(jnp.stack([grad_pre, pre_partner]), 2)
+    pre_eight = swap(jnp.concatenate([grad_pre[None], pre_partner[None], pre_four]), 4)
     parts = call(
         deep_backward,
         [shape((fine, deep))] * 4,
         (at, pre_partner, grad_pre, other, w_deep),
         [pltpu.VMEM((2, full, deep), BF), pltpu.VMEM((depth, deep), BF)],
-        flops=2 * 9 * deep * depth * full,
-        behind=(pre_near, before, after),
-    )
-    pre_far = swap(jnp.stack([grad_pre, pre_near]), 4)
+    )
+    got = [across(parts[s], s) for s in (1, 2, 3)]
+    first, last = call(edges, [shape((size, cols + deep))] * 2, (fine_slab, deep_slab), behind=(got[0],))
+    before = lax.ppermute(last, "wide", [(i, i + MEMBERS) for i in range(wide - MEMBERS)])
+    after = lax.ppermute(first, "wide", [(i + MEMBERS, i) for i in range(wide - MEMBERS)])
     fine_table, deep_table = call(
         tables,
         [shape((9 * size, MEMBERS * deep))] * 2,
         (fine_slab, deep_slab, before, after),
-        flops=2 * 9 * size * 6 * deep * 2 * deep,
-        behind=(parts[0],),
-    )
-    got = [across(parts[s], s) for s in (1, 2, 3)]
-    grad_pool = call(pool_sum, shape((fine, deep)), (parts[0], *got), behind=(pre_far, deep_table))
+    )
+    grad_pool = call(pool_sum, shape((fine, deep)), (parts[0], *got))
     pool_partner, other = pairs(grad_pool, grad_pool)
-    pool_near = swap(grad_pool, 2)
-    pre_rest = swap(jnp.concatenate([pre_near[None], pre_far]), 1)
-    pool_far = swap(jnp.stack([grad_pool, pool_near]), 4)
-    pool_rest = swap(jnp.concatenate([pool_near[None], pool_far]), 1)
+    pool_four = swap(jnp.stack([grad_pool, pool_partner]), 2)
+    pool_eight = swap(jnp.concatenate([grad_pool[None], pool_partner[None], pool_four]), 4)
 
     def products(table, *grads):
         width = grads[0].shape[0]
@@ -405,8 +378,7 @@
             [shape((2, block, width))] * 4,
             (at, *grads, table, order),
             [pltpu.VMEM((MEMBERS, width, deep), BF), pltpu.VMEM((groups * block, width), BF)],
-            flops=2 * 9 * size * MEMBERS * deep * width,
-        )
+            )
 
     def owners(parts):
         width = parts[0].shape[2]
@@ -420,16 +392,14 @@
         total = call(weight_sum, shape((9, grain, width), F32), (keep, swap(send, 32)))
         return total.reshape(3, 3, grain, width)
 
-    deep_parts = products(deep_table, grad_pre, pre_partner, pre_near, pre_far, pre_rest)
-    fine_parts = products(fine_table, grad_pool, pool_partner, pool_near, pool_far, pool_rest)
+    deep_parts = products(deep_table, grad_pre, pre_partner, pre_four, pre_eight)
+    fine_parts = products(fine_table, grad_pool, pool_partner, pool_four, pool_eight)
     back = call(
         fine_backward,
         shape((pieces, rows, part, depth)),
         (at, pool_partner, grad_pool, other, w_fine),
-        [pltpu.VMEM((2, fine, deep), BF), pltpu.VMEM(w_fine.shape, BF), pltpu.SemaphoreType.DMA((9,))],
-        flops=2 * 18 * cols * depth * fine,
-        behind=(deep_parts[0], fine_parts[0]),
-        remote=(4,),
+        [pltpu.VMEM((2, fine, deep), BF)],
+        behind=(deep_parts[0],),
     )
     partial = lax.all_to_all(back, "narrow", 0, 0)
     grad_latent = jnp.sum(partial.astype(F32), axis=0).astype(BF)

time: 178 us -> 165 us (0.927)
  starting transfers between devices: 101 us -> 91.4 us
  Pallas kernels: 26.2 us -> 21.2 us
  waiting for transfers between devices: 40.1 us -> 37 us
  other arithmetic: 0.85 us -> 3.55 us
  local copies, waits for them, and re-layouts: 8 us -> 9.81 us
    all_to_all x1 -> x0, waiting for transfers between devices: 13.9 us -> none  [on_device(): lax.all_to_all(jnp.broadcast_to(latent[None], (pieces,) + latent.shape),...]
    ppermute x6 -> x9, waiting for transfers between devices: 6.04 us -> 17.7 us  [across(): lax.ppermute(v, 'narrow', [(i, (i + step) % pieces) for i in range(pieces)])]
    ppermute x12 -> x10, starting transfers between devices: 34.8 us -> 23.9 us  [swap(): return lax.ppermute(v, 'wide', [(i, i ^ bit) for i in range(wide)])]
    all_to_all x1 -> x0, starting transfers between devices: 6 us -> none  [on_device(): lax.all_to_all(jnp.broadcast_to(latent[None], (pieces,) + latent.shape),...]
    pallas_call x18, Pallas kernels: 26.2 us -> 21.2 us  [call(): pl.pallas_call(kernel, out_shape=outs, in_specs=[smem if a.dtype == jnp.i...]
    unnamed x16 -> x42, local copies, waits for them, and re-layouts: 5.95 us -> 9.73 us
    all_to_all x1, waiting for transfers between devices: 1.12 us -> 4.48 us  [on_device(): fine_slab = lax.all_to_all(fine_slab, 'wide', 0, 0, axis_index_groups=near)]
    ppermute x6, waiting for transfers between devices: 2.97 us -> 0.02 us  [owners(): lax.ppermute(parts[s], 'wide', [(i, i // 32 * 32 + (i // 8 + s) % 4 * 8 +...]
  transfers between devices with their start and end apart: 34 -> 34, of which waited for: 16 -> 15; matrix products, arithmetic and copies ran while one was open for 1% -> 2% of each run, Pallas kernels for 7% -> 9%
where the time goes in v6:
time: 165 us; the launch traced here: 164 us
  starting transfers between devices  91.4 us (55%)
  waiting for transfers between devices  37 us (22%)
  Pallas kernels  21.2 us (13%)
  local copies, waits for them, and re-layouts  9.81 us (6%)
  other arithmetic  3.55 us (2%)
    ppermute x6, starting transfers between devices, owners(): lax.ppermute(parts[s], 'wide', [(i, i // 32 * 32 + (i // 8 + s) % 4 * 8 +...  27.4 us
    ppermute x10, starting transfers between devices, swap(): return lax.ppermute(v, 'wide', [(i, i ^ bit) for i in range(wide)])  23.9 us
    pallas_call x18, Pallas kernels, call(): pl.pallas_call(kernel, out_shape=outs, in_specs=[smem if a.dtype == jnp.i...  21.2 us
    ppermute x9, waiting for transfers between devices, across(): lax.ppermute(v, 'narrow', [(i, (i + step) % pieces) for i in range(pieces)])  17.7 us
    ppermute x9, starting transfers between devices, across(): lax.ppermute(v, 'narrow', [(i, (i + step) % pieces) for i in range(pieces)])  12.3 us
    ppermute x10, waiting for transfers between devices, swap(): return lax.ppermute(v, 'wide', [(i, i ^ bit) for i in range(wide)])  11.8 us
    unnamed x42, local copies, waits for them, and re-layouts  9.73 us
    all_to_all x1, starting transfers between devices, on_device(): deep_slab = lax.all_to_all(deep_slab, 'wide', 0, 0, axis_index_groups=near)  8.82 us
  transfers between devices with their start and end apart: 34, of which 15 were waited for; matrix products, arithmetic and copies ran while one was open for 2% of the time, Pallas kernels for 9%

profile of v6, /device:TPU:32, one launch (start us, length us, event | category | flops | bytes accessed | tf_op | source)
XLA Modules:
  0.0 164.0 jit_solution(14776250581849840227)
XLA Ops:
  0.6 2.0 %collective-permute-start = (bf16[2,64,640]{2,1,0:T(8,128)(2,1)}, bf16[2,64,640]{2,1,0:T(8,128)(2,1)S(1)}, u32[]{:S(2)}, u32[]{:S(2)}) collective-permute-start(bf16[2,64,640]{2,1,0:T(8,128)(2,1)} %refs_1_.3), channel_id=1, source_target_pairs={{0,1},{1,2},{2,3},{3,0},{4,5},{5,6},{6,7},{7,4},{8,9},{9,10},{10,1... | collective-permute-start | bytes 491528 | tf_op jit(solution)/shard_map/ppermute | solution.py:309
  2.6 2.3 %collective-permute-start.1 = (bf16[2,64,640]{2,1,0:T(8,128)(2,1)}, bf16[2,64,640]{2,1,0:T(8,128)(2,1)S(1)}, u32[]{:S(2)}, u32[]{:S(2)}) collective-permute-start(bf16[2,64,640]{2,1,0:T(8,128)(2,1)} %refs_1_.3), channel_id=1, source_target_pairs={{0,2},{1,3},{2,0},{3,1},{4,6},{5,7},{6,4},{7,5},{8,10},{9,11},{10,... | collective-permute-start | bytes 491528 | tf_op jit(solution)/shard_map/ppermute | solution.py:309
  6.1 8.5 %collective-permute-done.refs_2_ = bf16[2,64,640]{2,1,0:T(8,128)(2,1)S(1)} collective-permute-done((bf16[2,64,640]{2,1,0:T(8,128)(2,1)}, bf16[2,64,640]{2,1,0:T(8,128)(2,1)S(1)}, u32[]{:S(2)}, u32[]{:S(2)}) %collective-permute-start) | collective-permute-done | bytes 163872 | tf_op jit(solution)/shard_map/ppermute | solution.py:309
  14.6 2.4 %collective-permute-done.1.refs_3_ = bf16[2,64,640]{2,1,0:T(8,128)(2,1)S(1)} collective-permute-done((bf16[2,64,640]{2,1,0:T(8,128)(2,1)}, bf16[2,64,640]{2,1,0:T(8,128)(2,1)S(1)}, u32[]{:S(2)}, u32[]{:S(2)}) %collective-permute-start.1) | collective-permute-done | bytes 163872 | tf_op jit(solution)/shard_map/ppermute | solution.py:309
  16.9 2.0 %collective-permute-done.2.refs_4_ = bf16[2,64,640]{2,1,0:T(8,128)(2,1)S(1)} collective-permute-done((bf16[2,64,640]{2,1,0:T(8,128)(2,1)}, bf16[2,64,640]{2,1,0:T(8,128)(2,1)S(1)}, u32[]{:S(2)}, u32[]{:S(2)}) %collective-permute-start.2) | collective-permute-done | bytes 163872 | tf_op jit(solution)/shard_map/ppermute | solution.py:309
  24.6 2.6 %shard_map.94.refs_3_ = bf16[8,80,512]{2,1,0:T(8,128)(2,1)} custom-call(bf16[4,2,64,640]{3,2,1,0:T(8,128)(2,1)S(1)} %get-tuple-element.36.refs_0_, bf16[640,640]{1,0:T(8,128)(2,1)S(1)} %copy-done.4, bf16[160,128]{1,0:T(8,128)(2,1)S(1)} %collective-permute-done.3.refs_2_.refs_1_), custom_call_target="tpu_custom_call" | custom-call | bytes 1474560 | tf_op jit(solution)/shard_map/pallas_call | solution.py:64
  27.2 6.0 %all-to-all-start = ((bf16[8,80,512]{2,1,0:T(8,128)(2,1)}), bf16[8,80,512]{2,1,0:T(8,128)(2,1)S(1)}, u32[]{:S(2)}, u32[]{:S(2)}) async-start(bf16[8,80,512]{2,1,0:T(8,128)(2,1)} %shard_map.94.refs_3_), calls=%async_computation | async-start | bytes 1310720 | tf_op jit(solution)/shard_map/all_to_all | solution.py:332
  34.6 1.9 %collective-permute-start.7 = (bf16[160,128]{1,0:T(8,128)(2,1)S(1)}, bf16[160,128]{1,0:T(8,128)(2,1)S(1)}, u32[]{:S(2)}, u32[]{:S(2)}) collective-permute-start(bf16[160,128]{1,0:T(8,128)(2,1)S(1)} %shard_map.95.refs_1_), channel_id=1, source_target_pairs={{0,3},{1,0},{2,1},{3,2},{4,7},{5,4},{6,5},{7,6},{8,11},{9,8},{10,9... | collective-permute-start | bytes 122888 | tf_op jit(solution)/shard_map/ppermute | solution.py:309
  40.4 4.5 %all-to-all-done.refs_6_.refs_0_ = bf16[8,80,512]{2,1,0:T(8,128)(2,1)S(1)} async-done(((bf16[8,80,512]{2,1,0:T(8,128)(2,1)}), bf16[8,80,512]{2,1,0:T(8,128)(2,1)S(1)}, u32[]{:S(2)}, u32[]{:S(2)}) %all-to-all-start) | async-done | bytes 655392 | tf_op jit(solution)/shard_map/all_to_all | solution.py:332
  44.9 2.0 %copy-done.1 = bf16[3,3,640,320]{2,3,1,0:T(8,128)(2,1)S(1)} copy-done((bf16[3,3,640,320]{2,3,1,0:T(8,128)(2,1)S(1)}, bf16[3,3,640,320]{2,3,1,0:T(8,128)(2,1)}, u32[]{:S(2)}) %copy-start.1) | copy-done | bytes 3686424
  50.7 4.7 %collective-permute-start.10 = (bf16[320,128]{1,0:T(8,128)(2,1)S(1)}, bf16[320,128]{1,0:T(8,128)(2,1)S(1)}, u32[]{:S(2)}, u32[]{:S(2)}) collective-permute-start(bf16[320,128]{1,0:T(8,128)(2,1)S(1)} %get-tuple-element.41.refs_2_.refs_1_), channel_id=1, source_target_pairs={{0,4},{4,0},{8,12},{12,8},{16,20},{20,16},{24,28},{28,24},{32,36},... | collective-permute-start | bytes 245768 | tf_op jit(solution)/shard_map/ppermute | solution.py:312
  57.4 8.8 %all-to-all-start.1 = ((bf16[8,80,128]{2,1,0:T(8,128)(2,1)}), bf16[8,80,128]{2,1,0:T(8,128)(2,1)S(1)}, u32[]{:S(2)}, u32[]{:S(2)}) async-start(bf16[8,80,128]{2,1,0:T(8,128)(2,1)} %shard_map.101), calls=%async_computation.1 | async-start | bytes 327680 | tf_op jit(solution)/shard_map/all_to_all | solution.py:351
  66.2 2.1 %collective-permute-start.17 = (bf16[2,320,128]{2,1,0:T(8,128)(2,1)S(1)}, bf16[2,320,128]{2,1,0:T(8,128)(2,1)S(1)}, u32[]{:S(2)}, u32[]{:S(2)}) collective-permute-start(bf16[2,320,128]{2,1,0:T(8,128)(2,1)S(1)} %pad_maximum_fusion.1), channel_id=1, source_target_pairs={{0,8},{4,12},{8,0},{12,4},{16,24},{20,28},{24,16},{28,20},{32,40},... | collective-permute-start | bytes 491528 | tf_op jit(solution)/shard_map/ppermute | solution.py:312
  68.3 2.0 %copy-done.3 = bf16[3,3,640,320]{2,3,1,0:T(8,128)(2,1)S(1)} copy-done((bf16[3,3,640,320]{2,3,1,0:T(8,128)(2,1)S(1)}, bf16[3,3,640,320]{2,3,1,0:T(8,128)(2,1)}, u32[]{:S(2)}) %copy-start.3) | copy-done | bytes 3686424
  70.4 1.9 %shard_map.99 = (bf16[160,128]{1,0:T(8,128)(2,1)S(1)}, bf16[160,128]{1,0:T(8,128)(2,1)S(1)}, bf16[160,128]{1,0:T(8,128)(2,1)S(1)}, bf16[160,128]{1,0:T(8,128)(2,1)S(1)}) custom-call(s32[5]{0:T(128)S(1)} %stack.41.refs_0_, bf16[320,128]{1,0:T(8,128)(2,1)S(1)} %collective-permute-done.10.refs_1_.refs_2_, ...), custom_call_target="tpu_custom_call" | custom-call | flops 30000001024 | bytes 3932180 | tf_op jit(solution)/shard_map/pallas_call | solution.py:64
  76.9 3.5 %collective-permute-start.19 = (bf16[80,384]{1,0:T(8,128)(2,1)S(1)}, bf16[80,384]{1,0:T(8,128)(2,1)S(1)}, u32[]{:S(2)}, u32[]{:S(2)}) collective-permute-start(bf16[80,384]{1,0:T(8,128)(2,1)S(1)} %get-tuple-element.46), channel_id=1, source_target_pairs={{0,32},{4,36},{8,40},{12,44},{16,48},{20,52},{24,56},{28,60},{32,6... | collective-permute-start | bytes 184328 | tf_op jit(solution)/shard_map/ppermute | solution.py:362
  81.8 2.8 %collective-permute-start.18 = (bf16[4,320,128]{2,1,0:T(8,128)(2,1)S(1)}, bf16[4,320,128]{2,1,0:T(8,128)(2,1)S(1)}, u32[]{:S(2)}, u32[]{:S(2)}) collective-permute-start(bf16[4,320,128]{2,1,0:T(8,128)(2,1)S(1)} %pad_maximum_fusion), channel_id=1, source_target_pairs={{0,16},{4,20},{8,24},{12,28},{16,0},{20,4},{24,8},{28,12},{32,48},... | collective-permute-start | bytes 983048 | tf_op jit(solution)/shard_map/ppermute | solution.py:312
  85.6 3.0 %collective-permute-done.20.refs_3_ = bf16[80,384]{1,0:T(8,128)(2,1)S(1)} collective-permute-done((bf16[80,384]{1,0:T(8,128)(2,1)S(1)}, bf16[80,384]{1,0:T(8,128)(2,1)S(1)}, u32[]{:S(2)}, u32[]{:S(2)}) %collective-permute-start.20) | collective-permute-done | bytes 61472 | tf_op jit(solution)/shard_map/ppermute | solution.py:363
  89.4 2.2 %collective-permute-done.18.refs_4_ = bf16[4,320,128]{2,1,0:T(8,128)(2,1)S(1)} collective-permute-done((bf16[4,320,128]{2,1,0:T(8,128)(2,1)S(1)}, bf16[4,320,128]{2,1,0:T(8,128)(2,1)S(1)}, u32[]{:S(2)}, u32[]{:S(2)}) %collective-permute-start.18) | collective-permute-done | bytes 327712 | tf_op jit(solution)/shard_map/ppermute | solution.py:312
  91.6 3.7 %shard_map.104 = (bf16[2,96,320]{2,1,0:T(8,128)(2,1)S(1)}, bf16[2,96,320]{2,1,0:T(8,128)(2,1)}, bf16[2,96,320]{2,1,0:T(8,128)(2,1)}, bf16[2,96,320]{2,1,0:T(8,128)(2,1)}) custom-call(s32[5]{0:T(128)S(1)} %copy-done.14, bf16[320,128]{1,0:T(8,128)(2,1)S(1)} %copy-done.6, bf16[320,128]{1,0:T(8,128)(2,1)S(1)} %collective-permute-done.10.refs_1_.refs_2_, ...), custom_call_target="tpu_custom_call" | custom-call | bytes 3235860 | tf_op jit(solution)/shard_map/pallas_call | solution.py:64
  95.2 3.0 %shard_map.105 = bf16[4,2,64,640]{3,2,1,0:T(8,128)(2,1)} custom-call(s32[5]{0:T(128)S(1)} %copy-done.14, bf16[160,128]{1,0:T(8,128)(2,1)S(1)} %collective-permute-done.15.refs_1_.refs_2_, bf16[160,128]{1,0:T(8,128)(2,1)S(1)} %shard_map.100.refs_2_.refs_1_, bf16[160,128]{1,0:T(8,128)(2,1)S(1)} %collective-permute-done.16.refs_3_, ...), custom_call_target="tpu_custom_call" | custom-call | flops 30000001024 | bytes 1966100 | tf_op jit(solution)/shard_map/pallas_call | solution.py:64
  98.9 5.3 %all-to-all-start.2 = ((bf16[4,2,64,640]{3,2,1,0:T(8,128)(2,1)}), bf16[4,2,64,640]{3,2,1,0:T(8,128)(2,1)}, u32[]{:S(2)}, u32[]{:S(2)}) async-start(bf16[4,2,64,640]{3,2,1,0:T(8,128)(2,1)} %shard_map.105), calls=%async_computation.2 | async-start | bytes 1310720 | tf_op jit(solution)/shard_map/all_to_all | solution.py:404
  105.1 4.4 %collective-permute-done.21.refs_3_ = bf16[2,160,128]{2,1,0:T(8,128)(2,1)S(1)} collective-permute-done((bf16[2,160,128]{2,1,0:T(8,128)(2,1)S(1)}, bf16[2,160,128]{2,1,0:T(8,128)(2,1)S(1)}, u32[]{:S(2)}, u32[]{:S(2)}) %collective-permute-start.21) | collective-permute-done | bytes 81952 | tf_op jit(solution)/shard_map/ppermute | solution.py:312
  110.4 2.8 %collective-permute-start.22 = (bf16[4,160,128]{2,1,0:T(8,128)(2,1)S(1)}, bf16[4,160,128]{2,1,0:T(8,128)(2,1)S(1)}, u32[]{:S(2)}, u32[]{:S(2)}) collective-permute-start(bf16[4,160,128]{2,1,0:T(8,128)(2,1)S(1)} %pad_maximum_fusion.2), channel_id=1, source_target_pairs={{0,16},{4,20},{8,24},{12,28},{16,0},{20,4},{24,8},{28,12},{32,48},... | collective-permute-start | bytes 491528 | tf_op jit(solution)/shard_map/ppermute | solution.py:312
  113.1 8.7 %collective-permute-start.27 = (bf16[2,96,320]{2,1,0:T(8,128)(2,1)}, bf16[2,96,320]{2,1,0:T(8,128)(2,1)S(1)}, u32[]{:S(2)}, u32[]{:S(2)}) collective-permute-start(bf16[2,96,320]{2,1,0:T(8,128)(2,1)} %get-tuple-element.57), channel_id=1, source_target_pairs={{0,32},{4,36},{8,40},{12,44},{16,48},{20,52},{24,56},{28,60},{32,6... | collective-permute-start | bytes 368648 | tf_op jit(solution)/shard_map/ppermute | solution.py:386
  121.8 12.3 %collective-permute-start.28 = (bf16[2,96,320]{2,1,0:T(8,128)(2,1)}, bf16[2,96,320]{2,1,0:T(8,128)(2,1)S(1)}, u32[]{:S(2)}, u32[]{:S(2)}) collective-permute-start(bf16[2,96,320]{2,1,0:T(8,128)(2,1)} %get-tuple-element.58), channel_id=1, source_target_pairs={{0,64},{4,68},{8,72},{12,76},{16,80},{20,84},{24,88},{28,92},{32,9... | collective-permute-start | bytes 368648 | tf_op jit(solution)/shard_map/ppermute | solution.py:386
  134.9 2.4 %shard_map.106 = (bf16[2,96,160]{2,1,0:T(8,128)(2,1)S(1)}, bf16[2,96,160]{2,1,0:T(8,128)(2,1)S(1)}, bf16[2,96,160]{2,1,0:T(8,128)(2,1)S(1)}, bf16[2,96,160]{2,1,0:T(8,128)(2,1)S(1)}) custom-call(s32[5]{0:T(128)S(1)} %copy-done.15, bf16[160,128]{1,0:T(8,128)(2,1)S(1)} %copy-done.10, bf16[160,128]{1,0:T(8,128)(2,1)S(1)} %copy-done.12, ...), custom_call_target="tpu_custom_call" | custom-call | bytes 2908180 | tf_op jit(solution)/shard_map/pallas_call | solution.py:64
  137.3 2.1 %collective-permute-start.23 = (bf16[2,96,160]{2,1,0:T(8,128)(2,1)S(1)}, bf16[2,96,160]{2,1,0:T(8,128)(2,1)S(1)}, u32[]{:S(2)}, u32[]{:S(2)}) collective-permute-start(bf16[2,96,160]{2,1,0:T(8,128)(2,1)S(1)} %get-tuple-element.52), channel_id=1, source_target_pairs={{0,32},{4,36},{8,40},{12,44},{16,48},{20,52},{24,56},{28,60},{32,6... | collective-permute-start | bytes 184328 | tf_op jit(solution)/shard_map/ppermute | solution.py:386
  139.4 4.4 %collective-permute-start.24 = (bf16[2,96,160]{2,1,0:T(8,128)(2,1)S(1)}, bf16[2,96,160]{2,1,0:T(8,128)(2,1)S(1)}, u32[]{:S(2)}, u32[]{:S(2)}) collective-permute-start(bf16[2,96,160]{2,1,0:T(8,128)(2,1)S(1)} %get-tuple-element.53), channel_id=1, source_target_pairs={{0,64},{4,68},{8,72},{12,76},{16,80},{20,84},{24,88},{28,92},{32,9... | collective-permute-start | bytes 184328 | tf_op jit(solution)/shard_map/ppermute | solution.py:386
  144.4 7.3 %collective-permute-start.30 = (bf16[96,320]{1,0:T(8,128)(2,1)S(1)}, bf16[96,320]{1,0:T(8,128)(2,1)S(1)}, u32[]{:S(2)}, u32[]{:S(2)}) collective-permute-start(bf16[96,320]{1,0:T(8,128)(2,1)S(1)} %get-tuple-element.61), channel_id=1, source_target_pairs={{0,128},{4,132},{8,136},{12,140},{16,144},{20,148},{24,152},{28,15... | collective-permute-start | bytes 184328 | tf_op jit(solution)/shard_map/ppermute | solution.py:312
  152.4 3.9 %collective-permute-start.26 = (bf16[96,160]{1,0:T(8,128)(2,1)S(1)}, bf16[96,160]{1,0:T(8,128)(2,1)S(1)}, u32[]{:S(2)}, u32[]{:S(2)}) collective-permute-start(bf16[96,160]{1,0:T(8,128)(2,1)S(1)} %get-tuple-element.56), channel_id=1, source_target_pairs={{0,128},{4,132},{8,136},{12,140},{16,144},{20,148},{24,152},{28,15... | collective-permute-start | bytes 92168 | tf_op jit(solution)/shard_map/ppermute | solution.py:312
  156.3 4.3 %collective-permute-done.26.refs_1_ = bf16[96,160]{1,0:T(8,128)(2,1)S(1)} collective-permute-done((bf16[96,160]{1,0:T(8,128)(2,1)S(1)}, bf16[96,160]{1,0:T(8,128)(2,1)S(1)}, u32[]{:S(2)}, u32[]{:S(2)}) %collective-permute-start.26) | collective-permute-done | bytes 30752 | tf_op jit(solution)/shard_map/ppermute | solution.py:312
  (102 shorter events, 33.3 us)
Async XLA Ops:
  0.6 13.9 %collective-permute-start = (bf16[2,64,640]{2,1,0:T(8,128)(2,1)}, bf16[2,64,640]{2,1,0:T(8,128)(2,1)S(1)}, u32[]{:S(2)}, u32[]{:S(2)}) collective-permute-start(bf16[2,64,640]{2,1,0:T(8,128)(2,1)} %refs_1_.3), channel_id=1, source_target_pairs={{0,1},{1,2},{2,3},{3,0},{4,5},{5,6},{6,7},{7,4},{8,9},{9,10},{10,1... | collective-permute-start | bytes 491528 | tf_op jit(solution)/shard_map/ppermute | solution.py:309
  2.6 14.3 %collective-permute-start.1 = (bf16[2,64,640]{2,1,0:T(8,128)(2,1)}, bf16[2,64,640]{2,1,0:T(8,128)(2,1)S(1)}, u32[]{:S(2)}, u32[]{:S(2)}) collective-permute-start(bf16[2,64,640]{2,1,0:T(8,128)(2,1)} %refs_1_.3), channel_id=1, source_target_pairs={{0,2},{1,3},{2,0},{3,1},{4,6},{5,7},{6,4},{7,5},{8,10},{9,11},{10,... | collective-permute-start | bytes 491528 | tf_op jit(solution)/shard_map/ppermute | solution.py:309
  4.9 14.0 %collective-permute-start.2 = (bf16[2,64,640]{2,1,0:T(8,128)(2,1)}, bf16[2,64,640]{2,1,0:T(8,128)(2,1)S(1)}, u32[]{:S(2)}, u32[]{:S(2)}) collective-permute-start(bf16[2,64,640]{2,1,0:T(8,128)(2,1)} %refs_1_.3), channel_id=1, source_target_pairs={{0,3},{1,0},{2,1},{3,2},{4,7},{5,4},{6,5},{7,6},{8,11},{9,8},{10,9... | collective-permute-start | bytes 491528 | tf_op jit(solution)/shard_map/ppermute | solution.py:309
  23.4 9.8 %collective-permute-start.4 = (bf16[160,128]{1,0:T(8,128)(2,1)S(1)}, bf16[160,128]{1,0:T(8,128)(2,1)S(1)}, u32[]{:S(2)}, u32[]{:S(2)}) collective-permute-start(bf16[160,128]{1,0:T(8,128)(2,1)S(1)} %get-tuple-element.35), channel_id=1, source_target_pairs={{4,8},{8,4},{12,16},{16,12},{20,24},{24,20},{28,32},{32,28},{36,40... | collective-permute-start | bytes 122888 | tf_op jit(solution)/shard_map/ppermute | solution.py:315
  27.2 17.7 %all-to-all-start = ((bf16[8,80,512]{2,1,0:T(8,128)(2,1)}), bf16[8,80,512]{2,1,0:T(8,128)(2,1)S(1)}, u32[]{:S(2)}, u32[]{:S(2)}) async-start(bf16[8,80,512]{2,1,0:T(8,128)(2,1)} %shard_map.94.refs_3_), calls=%async_computation | async-start | bytes 1310720 | tf_op jit(solution)/shard_map/all_to_all | solution.py:332
  33.2 4.1 %collective-permute-start.5 = (bf16[160,128]{1,0:T(8,128)(2,1)S(1)}, bf16[160,128]{1,0:T(8,128)(2,1)S(1)}, u32[]{:S(2)}, u32[]{:S(2)}) collective-permute-start(bf16[160,128]{1,0:T(8,128)(2,1)S(1)} %shard_map.95.refs_1_), channel_id=1, source_target_pairs={{0,1},{1,2},{2,3},{3,0},{4,5},{5,6},{6,7},{7,4},{8,9},{9,10},{10,1... | collective-permute-start | bytes 122888 | tf_op jit(solution)/shard_map/ppermute | solution.py:309
  33.3 5.5 %collective-permute-start.6 = (bf16[160,128]{1,0:T(8,128)(2,1)S(1)}, bf16[160,128]{1,0:T(8,128)(2,1)S(1)}, u32[]{:S(2)}, u32[]{:S(2)}) collective-permute-start(bf16[160,128]{1,0:T(8,128)(2,1)S(1)} %shard_map.95.refs_1_), channel_id=1, source_target_pairs={{0,2},{1,3},{2,0},{3,1},{4,6},{5,7},{6,4},{7,5},{8,10},{9,11},{10,... | collective-permute-start | bytes 122888 | tf_op jit(solution)/shard_map/ppermute | solution.py:309
  34.6 5.8 %collective-permute-start.7 = (bf16[160,128]{1,0:T(8,128)(2,1)S(1)}, bf16[160,128]{1,0:T(8,128)(2,1)S(1)}, u32[]{:S(2)}, u32[]{:S(2)}) collective-permute-start(bf16[160,128]{1,0:T(8,128)(2,1)S(1)} %shard_map.95.refs_1_), channel_id=1, source_target_pairs={{0,3},{1,0},{2,1},{3,2},{4,7},{5,4},{6,5},{7,6},{8,11},{9,8},{10,9... | collective-permute-start | bytes 122888 | tf_op jit(solution)/shard_map/ppermute | solution.py:309
  48.3 1.4 collective-permute-start.8
  50.7 5.6 %collective-permute-start.10 = (bf16[320,128]{1,0:T(8,128)(2,1)S(1)}, bf16[320,128]{1,0:T(8,128)(2,1)S(1)}, u32[]{:S(2)}, u32[]{:S(2)}) collective-permute-start(bf16[320,128]{1,0:T(8,128)(2,1)S(1)} %get-tuple-element.41.refs_2_.refs_1_), channel_id=1, source_target_pairs={{0,4},{4,0},{8,12},{12,8},{16,20},{20,16},{24,28},{28,24},{32,36},... | collective-permute-start | bytes 245768 | tf_op jit(solution)/shard_map/ppermute | solution.py:312
  55.4 13.0 %collective-permute-start.11 = (bf16[320,128]{1,0:T(8,128)(2,1)S(1)}, bf16[320,128]{1,0:T(8,128)(2,1)S(1)}, u32[]{:S(2)}, u32[]{:S(2)}) collective-permute-start(bf16[320,128]{1,0:T(8,128)(2,1)S(1)} %get-tuple-element.41.refs_2_.refs_1_), channel_id=1, source_target_pairs={{4,8},{8,4},{12,16},{16,12},{20,24},{24,20},{28,32},{32,28},{36,40... | collective-permute-start | bytes 245768 | tf_op jit(solution)/shard_map/ppermute | solution.py:315
  57.4 19.5 %all-to-all-start.1 = ((bf16[8,80,128]{2,1,0:T(8,128)(2,1)}), bf16[8,80,128]{2,1,0:T(8,128)(2,1)S(1)}, u32[]{:S(2)}, u32[]{:S(2)}) async-start(bf16[8,80,128]{2,1,0:T(8,128)(2,1)} %shard_map.101), calls=%async_computation.1 | async-start | bytes 327680 | tf_op jit(solution)/shard_map/all_to_all | solution.py:351
  66.2 15.5 %collective-permute-start.17 = (bf16[2,320,128]{2,1,0:T(8,128)(2,1)S(1)}, bf16[2,320,128]{2,1,0:T(8,128)(2,1)S(1)}, u32[]{:S(2)}, u32[]{:S(2)}) collective-permute-start(bf16[2,320,128]{2,1,0:T(8,128)(2,1)S(1)} %pad_maximum_fusion.1), channel_id=1, source_target_pairs={{0,8},{4,12},{8,0},{12,4},{16,24},{20,28},{24,16},{28,20},{32,40},... | collective-permute-start | bytes 491528 | tf_op jit(solution)/shard_map/ppermute | solution.py:312
  72.3 4.6 %collective-permute-start.12 = (bf16[160,128]{1,0:T(8,128)(2,1)S(1)}, bf16[160,128]{1,0:T(8,128)(2,1)S(1)}, u32[]{:S(2)}, u32[]{:S(2)}) collective-permute-start(bf16[160,128]{1,0:T(8,128)(2,1)S(1)} %get-tuple-element.43), channel_id=1, source_target_pairs={{0,1},{1,2},{2,3},{3,0},{4,5},{5,6},{6,7},{7,4},{8,9},{9,10},{10,1... | collective-permute-start | bytes 122888 | tf_op jit(solution)/shard_map/ppermute | solution.py:309
  72.6 12.0 %collective-permute-start.13 = (bf16[160,128]{1,0:T(8,128)(2,1)S(1)}, bf16[160,128]{1,0:T(8,128)(2,1)S(1)}, u32[]{:S(2)}, u32[]{:S(2)}) collective-permute-start(bf16[160,128]{1,0:T(8,128)(2,1)S(1)} %get-tuple-element.44), channel_id=1, source_target_pairs={{0,2},{1,3},{2,0},{3,1},{4,6},{5,7},{6,4},{7,5},{8,10},{9,11},{10,... | collective-permute-start | bytes 122888 | tf_op jit(solution)/shard_map/ppermute | solution.py:309
  74.0 10.6 %collective-permute-start.14 = (bf16[160,128]{1,0:T(8,128)(2,1)S(1)}, bf16[160,128]{1,0:T(8,128)(2,1)S(1)}, u32[]{:S(2)}, u32[]{:S(2)}) collective-permute-start(bf16[160,128]{1,0:T(8,128)(2,1)S(1)} %get-tuple-element.45), channel_id=1, source_target_pairs={{0,3},{1,0},{2,1},{3,2},{4,7},{5,4},{6,5},{7,6},{8,11},{9,8},{10,9... | collective-permute-start | bytes 122888 | tf_op jit(solution)/shard_map/ppermute | solution.py:309
  76.9 8.6 %collective-permute-start.19 = (bf16[80,384]{1,0:T(8,128)(2,1)S(1)}, bf16[80,384]{1,0:T(8,128)(2,1)S(1)}, u32[]{:S(2)}, u32[]{:S(2)}) collective-permute-start(bf16[80,384]{1,0:T(8,128)(2,1)S(1)} %get-tuple-element.46), channel_id=1, source_target_pairs={{0,32},{4,36},{8,40},{12,44},{16,48},{20,52},{24,56},{28,60},{32,6... | collective-permute-start | bytes 184328 | tf_op jit(solution)/shard_map/ppermute | solution.py:362
  80.4 8.1 %collective-permute-start.20 = (bf16[80,384]{1,0:T(8,128)(2,1)S(1)}, bf16[80,384]{1,0:T(8,128)(2,1)S(1)}, u32[]{:S(2)}, u32[]{:S(2)}) collective-permute-start(bf16[80,384]{1,0:T(8,128)(2,1)S(1)} %get-tuple-element.47), channel_id=1, source_target_pairs={{32,0},{36,4},{40,8},{44,12},{48,16},{52,20},{56,24},{60,28},{64,3... | collective-permute-start | bytes 184328 | tf_op jit(solution)/shard_map/ppermute | solution.py:363
  81.8 9.7 %collective-permute-start.18 = (bf16[4,320,128]{2,1,0:T(8,128)(2,1)S(1)}, bf16[4,320,128]{2,1,0:T(8,128)(2,1)S(1)}, u32[]{:S(2)}, u32[]{:S(2)}) collective-permute-start(bf16[4,320,128]{2,1,0:T(8,128)(2,1)S(1)} %pad_maximum_fusion), channel_id=1, source_target_pairs={{0,16},{4,20},{8,24},{12,28},{16,0},{20,4},{24,8},{28,12},{32,48},... | collective-permute-start | bytes 983048 | tf_op jit(solution)/shard_map/ppermute | solution.py:312
  84.7 10.6 %collective-permute-start.15 = (bf16[160,128]{1,0:T(8,128)(2,1)S(1)}, bf16[160,128]{1,0:T(8,128)(2,1)S(1)}, u32[]{:S(2)}, u32[]{:S(2)}) collective-permute-start(bf16[160,128]{1,0:T(8,128)(2,1)S(1)} %shard_map.100.refs_2_.refs_1_), channel_id=1, source_target_pairs={{0,4},{4,0},{8,12},{12,8},{16,20},{20,16},{24,28},{28,24},{32,36},... | collective-permute-start | bytes 122888 | tf_op jit(solution)/shard_map/ppermute | solution.py:312
  84.8 10.5 %collective-permute-start.16 = (bf16[160,128]{1,0:T(8,128)(2,1)S(1)}, bf16[160,128]{1,0:T(8,128)(2,1)S(1)}, u32[]{:S(2)}, u32[]{:S(2)}) collective-permute-start(bf16[160,128]{1,0:T(8,128)(2,1)S(1)} %shard_map.100.refs_2_.refs_1_), channel_id=1, source_target_pairs={{4,8},{8,4},{12,16},{16,12},{20,24},{24,20},{28,32},{32,28},{36,40... | collective-permute-start | bytes 122888 | tf_op jit(solution)/shard_map/ppermute | solution.py:315
  98.9 63.2 %all-to-all-start.2 = ((bf16[4,2,64,640]{3,2,1,0:T(8,128)(2,1)}), bf16[4,2,64,640]{3,2,1,0:T(8,128)(2,1)}, u32[]{:S(2)}, u32[]{:S(2)}) async-start(bf16[4,2,64,640]{3,2,1,0:T(8,128)(2,1)} %shard_map.105), calls=%async_computation.2 | async-start | bytes 1310720 | tf_op jit(solution)/shard_map/all_to_all | solution.py:404
  105.0 4.5 %collective-permute-start.21 = (bf16[2,160,128]{2,1,0:T(8,128)(2,1)S(1)}, bf16[2,160,128]{2,1,0:T(8,128)(2,1)S(1)}, u32[]{:S(2)}, u32[]{:S(2)}) collective-permute-start(bf16[2,160,128]{2,1,0:T(8,128)(2,1)S(1)} %pad_maximum_fusion.3), channel_id=1, source_target_pairs={{0,8},{4,12},{8,0},{12,4},{16,24},{20,28},{24,16},{28,20},{32,40},... | collective-permute-start | bytes 245768 | tf_op jit(solution)/shard_map/ppermute | solution.py:312
  110.4 23.7 %collective-permute-start.22 = (bf16[4,160,128]{2,1,0:T(8,128)(2,1)S(1)}, bf16[4,160,128]{2,1,0:T(8,128)(2,1)S(1)}, u32[]{:S(2)}, u32[]{:S(2)}) collective-permute-start(bf16[4,160,128]{2,1,0:T(8,128)(2,1)S(1)} %pad_maximum_fusion.2), channel_id=1, source_target_pairs={{0,16},{4,20},{8,24},{12,28},{16,0},{20,4},{24,8},{28,12},{32,48},... | collective-permute-start | bytes 491528 | tf_op jit(solution)/shard_map/ppermute | solution.py:312
  113.1 30.6 %collective-permute-start.27 = (bf16[2,96,320]{2,1,0:T(8,128)(2,1)}, bf16[2,96,320]{2,1,0:T(8,128)(2,1)S(1)}, u32[]{:S(2)}, u32[]{:S(2)}) collective-permute-start(bf16[2,96,320]{2,1,0:T(8,128)(2,1)} %get-tuple-element.57), channel_id=1, source_target_pairs={{0,32},{4,36},{8,40},{12,44},{16,48},{20,52},{24,56},{28,60},{32,6... | collective-permute-start | bytes 368648 | tf_op jit(solution)/shard_map/ppermute | solution.py:386
  121.8 22.0 %collective-permute-start.28 = (bf16[2,96,320]{2,1,0:T(8,128)(2,1)}, bf16[2,96,320]{2,1,0:T(8,128)(2,1)S(1)}, u32[]{:S(2)}, u32[]{:S(2)}) collective-permute-start(bf16[2,96,320]{2,1,0:T(8,128)(2,1)} %get-tuple-element.58), channel_id=1, source_target_pairs={{0,64},{4,68},{8,72},{12,76},{16,80},{20,84},{24,88},{28,92},{32,9... | collective-permute-start | bytes 368648 | tf_op jit(solution)/shard_map/ppermute | solution.py:386
  134.1 9.7 %collective-permute-start.29 = (bf16[2,96,320]{2,1,0:T(8,128)(2,1)}, bf16[2,96,320]{2,1,0:T(8,128)(2,1)S(1)}, u32[]{:S(2)}, u32[]{:S(2)}) collective-permute-start(bf16[2,96,320]{2,1,0:T(8,128)(2,1)} %get-tuple-element.59), channel_id=1, source_target_pairs={{0,96},{4,100},{8,104},{12,108},{16,112},{20,116},{24,120},{28,124... | collective-permute-start | bytes 368648 | tf_op jit(solution)/shard_map/ppermute | solution.py:386
  137.3 14.5 %collective-permute-start.23 = (bf16[2,96,160]{2,1,0:T(8,128)(2,1)S(1)}, bf16[2,96,160]{2,1,0:T(8,128)(2,1)S(1)}, u32[]{:S(2)}, u32[]{:S(2)}) collective-permute-start(bf16[2,96,160]{2,1,0:T(8,128)(2,1)S(1)} %get-tuple-element.52), channel_id=1, source_target_pairs={{0,32},{4,36},{8,40},{12,44},{16,48},{20,52},{24,56},{28,60},{32,6... | collective-permute-start | bytes 184328 | tf_op jit(solution)/shard_map/ppermute | solution.py:386
  139.4 12.4 %collective-permute-start.24 = (bf16[2,96,160]{2,1,0:T(8,128)(2,1)S(1)}, bf16[2,96,160]{2,1,0:T(8,128)(2,1)S(1)}, u32[]{:S(2)}, u32[]{:S(2)}) collective-permute-start(bf16[2,96,160]{2,1,0:T(8,128)(2,1)S(1)} %get-tuple-element.53), channel_id=1, source_target_pairs={{0,64},{4,68},{8,72},{12,76},{16,80},{20,84},{24,88},{28,92},{32,9... | collective-permute-start | bytes 184328 | tf_op jit(solution)/shard_map/ppermute | solution.py:386
  143.8 8.0 %collective-permute-start.25 = (bf16[2,96,160]{2,1,0:T(8,128)(2,1)S(1)}, bf16[2,96,160]{2,1,0:T(8,128)(2,1)S(1)}, u32[]{:S(2)}, u32[]{:S(2)}) collective-permute-start(bf16[2,96,160]{2,1,0:T(8,128)(2,1)S(1)} %get-tuple-element.54), channel_id=1, source_target_pairs={{0,96},{4,100},{8,104},{12,108},{16,112},{20,116},{24,120},{28,124... | collective-permute-start | bytes 184328 | tf_op jit(solution)/shard_map/ppermute | solution.py:386
  144.4 16.9 %collective-permute-start.30 = (bf16[96,320]{1,0:T(8,128)(2,1)S(1)}, bf16[96,320]{1,0:T(8,128)(2,1)S(1)}, u32[]{:S(2)}, u32[]{:S(2)}) collective-permute-start(bf16[96,320]{1,0:T(8,128)(2,1)S(1)} %get-tuple-element.61), channel_id=1, source_target_pairs={{0,128},{4,132},{8,136},{12,140},{16,144},{20,148},{24,152},{28,15... | collective-permute-start | bytes 184328 | tf_op jit(solution)/shard_map/ppermute | solution.py:312
  152.4 8.2 %collective-permute-start.26 = (bf16[96,160]{1,0:T(8,128)(2,1)S(1)}, bf16[96,160]{1,0:T(8,128)(2,1)S(1)}, u32[]{:S(2)}, u32[]{:S(2)}) collective-permute-start(bf16[96,160]{1,0:T(8,128)(2,1)S(1)} %get-tuple-element.56), channel_id=1, source_target_pairs={{0,128},{4,132},{8,136},{12,140},{16,144},{20,148},{24,152},{28,15... | collective-permute-start | bytes 92168 | tf_op jit(solution)/shard_map/ppermute | solution.py:312
  (22 other events, 200.8 us)

commit v7 on v6

--- a/solution.py
+++ b/solution.py
@@ -218,56 +218,96 @@
         out[j] = mm(pick[j * size : (j + 1) * size], pooled[...]).astype(BF)
 
 
-def edges(fine, deep, first, last):
-    cols = fine.shape[2] // 2
-    first[:, :cols] = fine[0, :, :cols]
-    first[:, cols:] = deep[0]
-    last[:, :cols] = fine[MEMBERS - 1, :, cols:]
-    last[:, cols:] = deep[MEMBERS - 1]
-
-
-def tables(fine_slab, deep_slab, before, after, fine, deep):
+def tables(fine_slab, deep_slab, even, late, deep):
     size = fine_slab.shape[1]
     cols = deep_slab.shape[2]
     wide = 2 * cols
-    blocks = [before[:, wide:]] + [deep_slab[i] for i in range(MEMBERS)] + [after[:, wide:]]
-    for i, block in enumerate(blocks):
+    for i in range(MEMBERS):
+        block = deep_slab[i]
         row = block.astype(F32)
-        turned = [moved(row, 1, 1).astype(BF), block, moved(row, -1, 1).astype(BF)]
-        for a in range(3):
-            home = i - a
-            if 0 <= home < MEMBERS:
-                for b in range(3):
-                    t = 3 * a + b
-                    deep[t * size : (t + 1) * size, home * cols : (home + 1) * cols] = turned[b]
+        turned = (moved(row, 1, 1).astype(BF), block, moved(row, -1, 1).astype(BF))
+        for b in range(3):
+            deep[b * size : (b + 1) * size, i * cols : (i + 1) * cols] = turned[b]
     slab = [fine_slab[i] for i in range(MEMBERS)]
-    evens = jnp.concatenate([row[:, :wide] for row in slab] + [after[:, :wide]])
-    odds = jnp.concatenate([before[:, :wide]] + [row[:, wide:] for row in slab])
-    for b in range(3):
-        box = column_box(wide, b)
-        even = mm_t(evens, box)
-        late = mm_t(odds, box)
-        even = [even[i * size : (i + 1) * size] for i in range(MEMBERS + 1)]
-        late = [late[i * size : (i + 1) * size] for i in range(MEMBERS + 1)]
-        for i in range(MEMBERS):
-            rows = (late[i] + even[i], even[i] + late[i + 1], late[i + 1] + even[i + 1])
-            for a in range(3):
-                t = 3 * a + b
-                fine[t * size : (t + 1) * size, i * cols : (i + 1) * cols] = rows[a].astype(BF)
-
-
-def weight_part(at, own, partner, four, eight, table, order, out0, out1, out2, out3, grads, parts):
-    cols = own.shape[1]
-    blocks = [own[...], partner[...]] + [four[i] for i in range(2)] + [eight[i] for i in range(4)]
-    for r, block in enumerate(blocks):
-        grads[jnp.bitwise_xor(at[1], r)] = block
-    total = sum(mm_t(table[:, i * cols : (i + 1) * cols], grads[i]) for i in range(MEMBERS))
-    parts[...] = mm(order[...], total.astype(BF)).astype(BF)
-    size = out0.shape[1]
-    for step, out in enumerate((out0, out1, out2, out3)):
+    for r, out in enumerate((even, late)):
+        stack = jnp.concatenate([row[:, r * wide : (r + 1) * wide] for row in slab])
+        for b in range(3):
+            u = mm_t(stack, column_box(wide, b)).astype(BF)
+            for i in range(MEMBERS):
+                out[b * size : (b + 1) * size, i * cols : (i + 1) * cols] = u[i * size : (i + 1) * size]
+
+
+def pack(own, partner, other, out):
+    for i, v in enumerate((own, partner, other)):
+        out[i] = v[...]
+
+
+def pack_more(at, first, near, out, edge):
+    for i in range(2):
+        out[i] = first[i]
+        out[2 + i] = near[i]
+    place = jnp.bitwise_and(at[1] // 2, 1)
+    kept = place == at[0]
+
+    @pl.when(kept)
+    def _():
+        out[4] = first[2]
+        edge[...] = first[2]
+
+    @pl.when(jnp.logical_not(kept))
+    def _():
+        out[4] = near[2]
+        edge[...] = near[2]
+
+
+def outer(at, edge, far, out):
+    kept = jnp.bitwise_and(at[1] // 4, 1) == at[0]
+
+    @pl.when(kept)
+    def _():
+        out[...] = edge[...]
+
+    @pl.when(jnp.logical_not(kept))
+    def _():
+        out[...] = far[4]
+
+
+def group_rows(at, four, far, edge, swapped, grads):
+    for r in range(4):
+        grads[jnp.bitwise_xor(at[1], r) + 1] = four[r]
+        grads[jnp.bitwise_xor(at[1], 4 + r) + 1] = far[r]
+    ends = (MEMBERS + 1) * at[0]
+    grads[ends] = edge[...]
+    grads[MEMBERS + 1 - ends] = swapped[...]
+
+
+def against(table, grads, step):
+    cols = grads.shape[2]
+    return sum(mm_t(table[:, i * cols : (i + 1) * cols], grads[i + 1 + step]) for i in range(MEMBERS))
+
+
+def to_owners(at, taps, order, outs, parts):
+    total = jnp.concatenate([tap.astype(BF) for tap in taps])
+    parts[...] = mm(order[...], total).astype(BF)
+    size = outs[0].shape[1]
+    for step, out in enumerate(outs):
         for half in range(2):
             place = (half * 4 + jnp.bitwise_and(at[2] + step, 3)) * size
             out[half] = parts[pl.ds(pl.multiple_of(place, 32), size)]
+
+
+def deep_part(at, four, far, edge, swapped, table, order, out0, out1, out2, out3, grads, parts):
+    group_rows(at, four, far, edge, swapped, grads)
+    taps = [against(table, grads, 1 - a) for a in range(3)]
+    to_owners(at, taps, order, (out0, out1, out2, out3), parts)
+
+
+def fine_part(at, four, far, edge, swapped, even, late, order, out0, out1, out2, out3, grads, parts):
+    group_rows(at, four, far, edge, swapped, grads)
+    even_here = against(even, grads, 0)
+    late_here = against(late, grads, 0)
+    taps = (even_here + against(late, grads, 1), even_here + late_here, late_here + against(even, grads, -1))
+    to_owners(at, taps, order, (out0, out1, out2, out3), parts)
 
 
 def weight_half(at, own, got1, got2, got3, keep, send):
@@ -305,6 +345,16 @@
     pick = jnp.asarray(channel_matrix(depth, groups), BF)
     order = jnp.asarray(owner_matrix(groups, grain, block), BF)
 
+    def group_gather(first, behind, later=()):
+        own = first[0]
+        near = swap(first, 2)
+        more, edge = call(
+            pack_more, [shape((5,) + own.shape), shape(own.shape)], (at, first, near), behind=behind
+        )
+        far = swap(more, 4)
+        edge = call(outer, shape(own.shape), (at, edge, far), behind=later)
+        return more, far, edge, swap(edge, 1)
+
     def across(v, step):
         return lax.ppermute(v, "narrow", [(i, (i + step) % pieces) for i in range(pieces)])
 
@@ -335,11 +385,10 @@
         deep_sides,
         [shape((depth, deep)), shape((full, deep)), shape((full, deep))],
         (at, mine, *got, w_deep),
-        behind=(fine_slab,),
     )
     partner, other = pairs(partner, other)
     preact = call(
-        deep_own, shape((full, deep), F32), (pooled, w_deep), behind=(pooled,)
+        deep_own, shape((full, deep), F32), (pooled, w_deep), behind=(fine_slab,)
     )
     output, grad_pre = call(
         deep_forward,
@@ -349,8 +398,7 @@
     pre_partner, other = pairs(grad_pre, grad_pre)
     deep_slab = call(deep_slices, shape((MEMBERS, size, deep)), (pooled, pick), behind=(pre_partner,))
     deep_slab = lax.all_to_all(deep_slab, "wide", 0, 0, axis_index_groups=near)
-    pre_four = swap(jnp.stack([grad_pre, pre_partner]), 2)
-    pre_eight = swap(jnp.concatenate([grad_pre[None], pre_partner[None], pre_four]), 4)
+    pre_first = call(pack, shape((3, full, deep)), (grad_pre, pre_partner, other))
     parts = call(
         deep_backward,
         [shape((fine, deep))] * 4,
@@ -358,29 +406,25 @@
         [pltpu.VMEM((2, full, deep), BF), pltpu.VMEM((depth, deep), BF)],
     )
     got = [across(parts[s], s) for s in (1, 2, 3)]
-    first, last = call(edges, [shape((size, cols + deep))] * 2, (fine_slab, deep_slab), behind=(got[0],))
-    before = lax.ppermute(last, "wide", [(i, i + MEMBERS) for i in range(wide - MEMBERS)])
-    after = lax.ppermute(first, "wide", [(i + MEMBERS, i) for i in range(wide - MEMBERS)])
-    fine_table, deep_table = call(
-        tables,
-        [shape((9 * size, MEMBERS * deep))] * 2,
-        (fine_slab, deep_slab, before, after),
+    even_table, late_table, deep_table = call(
+        tables, [shape((3 * size, MEMBERS * deep))] * 3, (fine_slab, deep_slab)
     )
     grad_pool = call(pool_sum, shape((fine, deep)), (parts[0], *got))
     pool_partner, other = pairs(grad_pool, grad_pool)
-    pool_four = swap(jnp.stack([grad_pool, pool_partner]), 2)
-    pool_eight = swap(jnp.concatenate([grad_pool[None], pool_partner[None], pool_four]), 4)
-
-    def products(table, *grads):
-        width = grads[0].shape[0]
+    pre_rows = group_gather(pre_first, (got[0],))
+    pool_first = call(pack, shape((3, fine, deep)), (grad_pool, pool_partner, other))
+
+    def products(body, tables, rows, behind=()):
+        width = rows[0].shape[1]
         return call(
-            weight_part,
+            body,
             [shape((2, block, width))] * 4,
-            (at, *grads, table, order),
-            [pltpu.VMEM((MEMBERS, width, deep), BF), pltpu.VMEM((groups * block, width), BF)],
-            )
-
-    def owners(parts):
+            (at, *rows, *tables, order),
+            [pltpu.VMEM((MEMBERS + 2, width, deep), BF), pltpu.VMEM((groups * block, width), BF)],
+            behind=behind,
+        )
+
+    def owners(parts, behind=()):
         width = parts[0].shape[2]
         got = [
             lax.ppermute(
@@ -389,23 +433,24 @@
             for s in (1, 2, 3)
         ]
         keep, send = call(weight_half, [shape((block, width), F32), shape((block, width))], (at, parts[0], *got))
-        total = call(weight_sum, shape((9, grain, width), F32), (keep, swap(send, 32)))
+        total = call(weight_sum, shape((9, grain, width), F32), (keep, swap(send, 32)), behind=behind)
         return total.reshape(3, 3, grain, width)
 
-    deep_parts = products(deep_table, grad_pre, pre_partner, pre_four, pre_eight)
-    fine_parts = products(fine_table, grad_pool, pool_partner, pool_four, pool_eight)
     back = call(
         fine_backward,
         shape((pieces, rows, part, depth)),
         (at, pool_partner, grad_pool, other, w_fine),
         [pltpu.VMEM((2, fine, deep), BF)],
-        behind=(deep_parts[0],),
-    )
+        behind=(pre_rows[2], deep_table),
+    )
+    pool_rows = group_gather(pool_first, (back,))
+    deep_parts = products(deep_part, (deep_table,), pre_rows, (back,))
+    fine_parts = products(fine_part, (even_table, late_table), pool_rows)
     partial = lax.all_to_all(back, "narrow", 0, 0)
     grad_latent = jnp.sum(partial.astype(F32), axis=0).astype(BF)
 
     grad_deep = owners(deep_parts)
-    grad_fine = owners(fine_parts)
+    grad_fine = owners(fine_parts, (grad_latent, grad_deep))
     return output.T[None], grad_latent, grad_fine, grad_deep
 
 

time: 165 us -> 161 us (0.976)
  starting transfers between devices: 91.4 us -> 78.4 us
  waiting for transfers between devices: 37 us -> 42.6 us
  local copies, waits for them, and re-layouts: 9.81 us -> 14.1 us
  other arithmetic: 3.55 us -> 1.19 us
    ppermute x10 -> x12, waiting for transfers between devices: 11.8 us -> 20 us  [swap(): return lax.ppermute(v, 'wide', [(i, i ^ bit) for i in range(wide)])]
    ppermute x10 -> x12, starting transfers between devices: 23.9 us -> 18.1 us  [swap(): return lax.ppermute(v, 'wide', [(i, i ^ bit) for i in range(wide)])]
    ppermute x9, waiting for transfers between devices: 17.7 us -> 12.8 us  [across(): lax.ppermute(v, 'narrow', [(i, (i + step) % pieces) for i in range(pieces)])]
    ppermute x2 -> x0, starting transfers between devices: 4.78 us -> none  [the longest x1 3.48 us: on_device(): lax.ppermute(last, 'wide', [(i, i + MEMBERS) for i in range(wide - MEMBER...]
    all_to_all x1, starting transfers between devices: 8.82 us -> 4.41 us  [on_device(): deep_slab = lax.all_to_all(deep_slab, 'wide', 0, 0, axis_index_groups=near)]
    unnamed x42 -> x40, local copies, waits for them, and re-layouts: 9.73 us -> 14.1 us
    all_to_all x1, waiting for transfers between devices: 4.48 us -> 7.51 us  [on_device(): fine_slab = lax.all_to_all(fine_slab, 'wide', 0, 0, axis_index_groups=near)]
    ppermute x2 -> x0, waiting for transfers between devices: 2.98 us -> none  [the longest x1 2.98 us: on_device(): lax.ppermute(first, 'wide', [(i + MEMBERS, i) for i in range(wide - MEMBE...]
  transfers between devices with their start and end apart: 34 -> 34, of which waited for: 15 -> 14; matrix products, arithmetic and copies ran while one was open for 2% -> 1% of each run, Pallas kernels for 9% -> 11%
where the time goes in v7:
time: 161 us; the launch traced here: 160 us
  starting transfers between devices  78.4 us (49%)
  waiting for transfers between devices  42.6 us (26%)
  Pallas kernels  22.5 us (14%)
  local copies, waits for them, and re-layouts  14.1 us (9%)
    ppermute x6, starting transfers between devices, owners(): lax.ppermute(parts[s], 'wide', [(i, i // 32 * 32 + (i // 8 + s) % 4 * 8 +...  27.9 us
    pallas_call x23, Pallas kernels, call(): pl.pallas_call(kernel, out_shape=outs, in_specs=[smem if a.dtype == jnp.i...  22.5 us
    ppermute x12, waiting for transfers between devices, swap(): return lax.ppermute(v, 'wide', [(i, i ^ bit) for i in range(wide)])  20 us
    ppermute x12, starting transfers between devices, swap(): return lax.ppermute(v, 'wide', [(i, i ^ bit) for i in range(wide)])  18.1 us
    unnamed x40, local copies, waits for them, and re-layouts  14.1 us
    ppermute x9, waiting for transfers between devices, across(): lax.ppermute(v, 'narrow', [(i, (i + step) % pieces) for i in range(pieces)])  12.8 us
    ppermute x9, starting transfers between devices, across(): lax.ppermute(v, 'narrow', [(i, (i + step) % pieces) for i in range(pieces)])  12.7 us
    all_to_all x1, waiting for transfers between devices, on_device(): fine_slab = lax.all_to_all(fine_slab, 'wide', 0, 0, axis_index_groups=near)  7.51 us
  transfers between devices with their start and end apart: 34, of which 14 were waited for; matrix products, arithmetic and copies ran while one was open for 1% of the time, Pallas kernels for 11%

profile of v7, /device:TPU:32, one launch (start us, length us, event | category | flops | bytes accessed | tf_op | source)
XLA Modules:
  0.0 159.8 jit_solution(10068803989786105687)
XLA Ops:
  0.6 2.0 %collective-permute-start = (bf16[2,64,640]{2,1,0:T(8,128)(2,1)}, bf16[2,64,640]{2,1,0:T(8,128)(2,1)S(1)}, u32[]{:S(2)}, u32[]{:S(2)}) collective-permute-start(bf16[2,64,640]{2,1,0:T(8,128)(2,1)} %refs_1_.3), channel_id=1, source_target_pairs={{0,1},{1,2},{2,3},{3,0},{4,5},{5,6},{6,7},{7,4},{8,9},{9,10},{10,1... | collective-permute-start | bytes 491528 | tf_op jit(solution)/shard_map/ppermute | solution.py:359
  2.6 2.3 %collective-permute-start.1 = (bf16[2,64,640]{2,1,0:T(8,128)(2,1)}, bf16[2,64,640]{2,1,0:T(8,128)(2,1)S(1)}, u32[]{:S(2)}, u32[]{:S(2)}) collective-permute-start(bf16[2,64,640]{2,1,0:T(8,128)(2,1)} %refs_1_.3), channel_id=1, source_target_pairs={{0,2},{1,3},{2,0},{3,1},{4,6},{5,7},{6,4},{7,5},{8,10},{9,11},{10,... | collective-permute-start | bytes 491528 | tf_op jit(solution)/shard_map/ppermute | solution.py:359
  6.1 8.5 %collective-permute-done.refs_2_ = bf16[2,64,640]{2,1,0:T(8,128)(2,1)S(1)} collective-permute-done((bf16[2,64,640]{2,1,0:T(8,128)(2,1)}, bf16[2,64,640]{2,1,0:T(8,128)(2,1)S(1)}, u32[]{:S(2)}, u32[]{:S(2)}) %collective-permute-start) | collective-permute-done | bytes 163872 | tf_op jit(solution)/shard_map/ppermute | solution.py:359
  14.6 2.4 %collective-permute-done.1.refs_3_ = bf16[2,64,640]{2,1,0:T(8,128)(2,1)S(1)} collective-permute-done((bf16[2,64,640]{2,1,0:T(8,128)(2,1)}, bf16[2,64,640]{2,1,0:T(8,128)(2,1)S(1)}, u32[]{:S(2)}, u32[]{:S(2)}) %collective-permute-start.1) | collective-permute-done | bytes 163872 | tf_op jit(solution)/shard_map/ppermute | solution.py:359
  16.9 2.0 %collective-permute-done.2.refs_4_ = bf16[2,64,640]{2,1,0:T(8,128)(2,1)S(1)} collective-permute-done((bf16[2,64,640]{2,1,0:T(8,128)(2,1)}, bf16[2,64,640]{2,1,0:T(8,128)(2,1)S(1)}, u32[]{:S(2)}, u32[]{:S(2)}) %collective-permute-start.2) | collective-permute-done | bytes 163872 | tf_op jit(solution)/shard_map/ppermute | solution.py:359
  21.3 1.9 %shard_map.93 = (bf16[4,2,64,640]{3,2,1,0:T(8,128)(2,1)S(1)}, f32[160,128]{1,0:T(8,128)S(1)}, bf16[160,128]{1,0:T(8,128)(2,1)S(1)}, bf16[160,128]{1,0:T(8,128)(2,1)S(1)}) custom-call(s32[5]{0:T(128)S(1)} %stack.23.refs_0_, bf16[2,64,640]{2,1,0:T(8,128)(2,1)S(1)} %copy-done.17, bf16[2,64,640]{2,1,0:T(8,128)(2,1)S(1)} %collective-permute-done.refs_2_, ...), custom_call_target="tpu_custom_call" | custom-call | flops 30000001024 | bytes 2498580 | tf_op jit(solution)/shard_map/pallas_call | solution.py:64
  24.6 2.6 %shard_map.94.refs_3_ = bf16[8,80,512]{2,1,0:T(8,128)(2,1)} custom-call(bf16[4,2,64,640]{3,2,1,0:T(8,128)(2,1)S(1)} %get-tuple-element.39.refs_0_, bf16[640,640]{1,0:T(8,128)(2,1)S(1)} %copy-done.4, bf16[160,128]{1,0:T(8,128)(2,1)S(1)} %collective-permute-done.3.refs_2_.refs_1_), custom_call_target="tpu_custom_call" | custom-call | bytes 1474560 | tf_op jit(solution)/shard_map/pallas_call | solution.py:64
  28.7 1.9 %collective-permute-start.7 = (bf16[160,128]{1,0:T(8,128)(2,1)S(1)}, bf16[160,128]{1,0:T(8,128)(2,1)S(1)}, u32[]{:S(2)}, u32[]{:S(2)}) collective-permute-start(bf16[160,128]{1,0:T(8,128)(2,1)S(1)} %shard_map.95.refs_1_), channel_id=1, source_target_pairs={{0,3},{1,0},{2,1},{3,2},{4,7},{5,4},{6,5},{7,6},{8,11},{9,8},{10,9... | collective-permute-start | bytes 122888 | tf_op jit(solution)/shard_map/ppermute | solution.py:359
  30.6 6.9 %all-to-all-start = ((bf16[8,80,512]{2,1,0:T(8,128)(2,1)}), bf16[8,80,512]{2,1,0:T(8,128)(2,1)S(1)}, u32[]{:S(2)}, u32[]{:S(2)}) async-start(bf16[8,80,512]{2,1,0:T(8,128)(2,1)} %shard_map.94.refs_3_), calls=%async_computation | async-start | bytes 1310720 | tf_op jit(solution)/shard_map/all_to_all | solution.py:382
  37.6 2.0 %copy-done.1 = bf16[3,3,640,320]{2,3,1,0:T(8,128)(2,1)S(1)} copy-done((bf16[3,3,640,320]{2,3,1,0:T(8,128)(2,1)S(1)}, bf16[3,3,640,320]{2,3,1,0:T(8,128)(2,1)}, u32[]{:S(2)}) %copy-start.1) | copy-done | bytes 3686424
  42.2 7.5 %all-to-all-done.refs_2_.refs_0_ = bf16[8,80,512]{2,1,0:T(8,128)(2,1)S(1)} async-done(((bf16[8,80,512]{2,1,0:T(8,128)(2,1)}), bf16[8,80,512]{2,1,0:T(8,128)(2,1)S(1)}, u32[]{:S(2)}, u32[]{:S(2)}) %all-to-all-start) | async-done | bytes 655392 | tf_op jit(solution)/shard_map/all_to_all | solution.py:382
  49.7 2.0 %copy-done.2 = bf16[3,3,640,320]{2,3,1,0:T(8,128)(2,1)S(1)} copy-done((bf16[3,3,640,320]{2,3,1,0:T(8,128)(2,1)S(1)}, bf16[3,3,640,320]{2,3,1,0:T(8,128)(2,1)}, u32[]{:S(2)}) %copy-start.2) | copy-done | bytes 3686424
  54.7 5.0 %collective-permute-start.17 = (bf16[3,320,128]{2,1,0:T(8,128)(2,1)S(1)}, bf16[3,320,128]{2,1,0:T(8,128)(2,1)S(1)}, u32[]{:S(2)}, u32[]{:S(2)}) collective-permute-start(bf16[3,320,128]{2,1,0:T(8,128)(2,1)S(1)} %shard_map.101.refs_1_), channel_id=1, source_target_pairs={{0,8},{4,12},{8,0},{12,4},{16,24},{20,28},{24,16},{28,20},{32,40},... | collective-permute-start | bytes 737288 | tf_op jit(solution)/shard_map/ppermute | solution.py:362
  59.6 1.9 %shard_map.99 = (bf16[160,128]{1,0:T(8,128)(2,1)S(1)}, bf16[160,128]{1,0:T(8,128)(2,1)S(1)}, bf16[160,128]{1,0:T(8,128)(2,1)S(1)}, bf16[160,128]{1,0:T(8,128)(2,1)S(1)}) custom-call(s32[5]{0:T(128)S(1)} %stack.23.refs_0_, bf16[320,128]{1,0:T(8,128)(2,1)S(1)} %collective-permute-done.10.refs_1_.refs_2_, ...), custom_call_target="tpu_custom_call" | custom-call | flops 30000001024 | bytes 3932180 | tf_op jit(solution)/shard_map/pallas_call | solution.py:64
  62.1 3.4 %collective-permute-start.13 = (bf16[160,128]{1,0:T(8,128)(2,1)S(1)}, bf16[160,128]{1,0:T(8,128)(2,1)S(1)}, u32[]{:S(2)}, u32[]{:S(2)}) collective-permute-start(bf16[160,128]{1,0:T(8,128)(2,1)S(1)} %get-tuple-element.47), channel_id=1, source_target_pairs={{0,2},{1,3},{2,0},{3,1},{4,6},{5,7},{6,4},{7,5},{8,10},{9,11},{10,... | collective-permute-start | bytes 122888 | tf_op jit(solution)/shard_map/ppermute | solution.py:359
  66.5 4.4 %all-to-all-start.1 = ((bf16[8,80,128]{2,1,0:T(8,128)(2,1)}), bf16[8,80,128]{2,1,0:T(8,128)(2,1)S(1)}, u32[]{:S(2)}, u32[]{:S(2)}) async-start(bf16[8,80,128]{2,1,0:T(8,128)(2,1)} %shard_map.104), calls=%async_computation.1 | async-start | bytes 327680 | tf_op jit(solution)/shard_map/all_to_all | solution.py:400
  71.6 3.6 %collective-permute-start.18 = (bf16[5,320,128]{2,1,0:T(8,128)(2,1)S(1)}, bf16[5,320,128]{2,1,0:T(8,128)(2,1)S(1)}, u32[]{:S(2)}, u32[]{:S(2)}) collective-permute-start(bf16[5,320,128]{2,1,0:T(8,128)(2,1)S(1)} %get-tuple-element.50.refs_1_), channel_id=1, source_target_pairs={{0,16},{4,20},{8,24},{12,28},{16,0},{20,4},{24,8},{28,12},{32,48},... | collective-permute-start | bytes 1228808 | tf_op jit(solution)/shard_map/ppermute | solution.py:362
  76.0 1.9 %all-to-all-done.1.refs_1_ = bf16[8,80,128]{2,1,0:T(8,128)(2,1)S(1)} async-done(((bf16[8,80,128]{2,1,0:T(8,128)(2,1)}), bf16[8,80,128]{2,1,0:T(8,128)(2,1)S(1)}, u32[]{:S(2)}, u32[]{:S(2)}) %all-to-all-start.1) | async-done | bytes 163872 | tf_op jit(solution)/shard_map/all_to_all | solution.py:400
  78.6 8.0 %collective-permute-done.18.refs_2_ = bf16[5,320,128]{2,1,0:T(8,128)(2,1)S(1)} collective-permute-done((bf16[5,320,128]{2,1,0:T(8,128)(2,1)S(1)}, bf16[5,320,128]{2,1,0:T(8,128)(2,1)S(1)}, u32[]{:S(2)}, u32[]{:S(2)}) %collective-permute-start.18) | collective-permute-done | bytes 409632 | tf_op jit(solution)/shard_map/ppermute | solution.py:362
  88.8 3.0 %shard_map.106.refs_3_.refs_7_ = bf16[4,2,64,640]{3,2,1,0:T(8,128)(2,1)} custom-call(s32[5]{0:T(128)S(1)} %copy-done.7, bf16[160,128]{1,0:T(8,128)(2,1)S(1)} %collective-permute-done.15.refs_1_, bf16[160,128]{1,0:T(8,128)(2,1)S(1)} %shard_map.100.refs_2_.refs_0_, bf16[160,128]{1,0:T(8,128)(2,1)S(1)} %collective-permute-done.16.refs_3_.refs_2_, ...), custom_call_target="tpu_custom_call" | custom-call | flops 30000001024 | bytes 1966100 | tf_op jit(solution)/shard_map/pallas_call | solution.py:64
  93.0 5.7 %all-to-all-start.2 = ((bf16[4,2,64,640]{3,2,1,0:T(8,128)(2,1)}), bf16[4,2,64,640]{3,2,1,0:T(8,128)(2,1)}, u32[]{:S(2)}, u32[]{:S(2)}) async-start(bf16[4,2,64,640]{3,2,1,0:T(8,128)(2,1)} %shard_map.106.refs_3_.refs_7_), calls=%async_computation.2 | async-start | bytes 1310720 | tf_op jit(solution)/shard_map/all_to_all | solution.py:449
  101.4 4.6 %collective-permute-done.19.refs_2_ = bf16[3,160,128]{2,1,0:T(8,128)(2,1)S(1)} collective-permute-done((bf16[3,160,128]{2,1,0:T(8,128)(2,1)S(1)}, bf16[3,160,128]{2,1,0:T(8,128)(2,1)S(1)}, u32[]{:S(2)}, u32[]{:S(2)}) %collective-permute-start.19) | collective-permute-done | bytes 122912 | tf_op jit(solution)/shard_map/ppermute | solution.py:362
  107.2 2.6 %collective-permute-start.20 = (bf16[5,160,128]{2,1,0:T(8,128)(2,1)S(1)}, bf16[5,160,128]{2,1,0:T(8,128)(2,1)S(1)}, u32[]{:S(2)}, u32[]{:S(2)}) collective-permute-start(bf16[5,160,128]{2,1,0:T(8,128)(2,1)S(1)} %get-tuple-element.52.refs_1_), channel_id=1, source_target_pairs={{0,16},{4,20},{8,24},{12,28},{16,0},{20,4},{24,8},{28,12},{32,48},... | collective-permute-start | bytes 614408 | tf_op jit(solution)/shard_map/ppermute | solution.py:362
  111.1 2.9 %shard_map.112 = (bf16[2,96,320]{2,1,0:T(8,128)(2,1)S(1)}, bf16[2,96,320]{2,1,0:T(8,128)(2,1)S(1)}, bf16[2,96,320]{2,1,0:T(8,128)(2,1)S(1)}, bf16[2,96,320]{2,1,0:T(8,128)(2,1)S(1)}) custom-call(s32[5]{0:T(128)S(1)} %copy-done.8, bf16[5,320,128]{2,1,0:T(8,128)(2,1)S(1)} %get-tuple-element.50.refs_1_, ...), custom_call_target="tpu_custom_call" | custom-call | bytes 2580500 | tf_op jit(solution)/shard_map/pallas_call | solution.py:64
  114.0 4.3 %collective-permute-start.27 = (bf16[2,96,320]{2,1,0:T(8,128)(2,1)S(1)}, bf16[2,96,320]{2,1,0:T(8,128)(2,1)S(1)}, u32[]{:S(2)}, u32[]{:S(2)}) collective-permute-start(bf16[2,96,320]{2,1,0:T(8,128)(2,1)S(1)} %get-tuple-element.63), channel_id=1, source_target_pairs={{0,32},{4,36},{8,40},{12,44},{16,48},{20,52},{24,56},{28,60},{32,6... | collective-permute-start | bytes 368648 | tf_op jit(solution)/shard_map/ppermute | solution.py:430
  118.3 18.5 %collective-permute-start.28 = (bf16[2,96,320]{2,1,0:T(8,128)(2,1)S(1)}, bf16[2,96,320]{2,1,0:T(8,128)(2,1)S(1)}, u32[]{:S(2)}, u32[]{:S(2)}) collective-permute-start(bf16[2,96,320]{2,1,0:T(8,128)(2,1)S(1)} %get-tuple-element.64), channel_id=1, source_target_pairs={{0,64},{4,68},{8,72},{12,76},{16,80},{20,84},{24,88},{28,92},{32,9... | collective-permute-start | bytes 368648 | tf_op jit(solution)/shard_map/ppermute | solution.py:430
  138.7 2.2 %shard_map.110 = (bf16[2,96,160]{2,1,0:T(8,128)(2,1)S(1)}, bf16[2,96,160]{2,1,0:T(8,128)(2,1)S(1)}, bf16[2,96,160]{2,1,0:T(8,128)(2,1)S(1)}, bf16[2,96,160]{2,1,0:T(8,128)(2,1)S(1)}) custom-call(s32[5]{0:T(128)S(1)} %copy-done.8, bf16[5,160,128]{2,1,0:T(8,128)(2,1)S(1)} %get-tuple-element.52.refs_1_, ...), custom_call_target="tpu_custom_call" | custom-call | bytes 2580500 | tf_op jit(solution)/shard_map/pallas_call | solution.py:64
  140.9 2.3 %collective-permute-start.22 = (bf16[2,96,160]{2,1,0:T(8,128)(2,1)S(1)}, bf16[2,96,160]{2,1,0:T(8,128)(2,1)S(1)}, u32[]{:S(2)}, u32[]{:S(2)}) collective-permute-start(bf16[2,96,160]{2,1,0:T(8,128)(2,1)S(1)} %get-tuple-element.57), channel_id=1, source_target_pairs={{0,32},{4,36},{8,40},{12,44},{16,48},{20,52},{24,56},{28,60},{32,6... | collective-permute-start | bytes 184328 | tf_op jit(solution)/shard_map/ppermute | solution.py:430
  143.2 2.8 %collective-permute-start.24 = (bf16[2,96,160]{2,1,0:T(8,128)(2,1)S(1)}, bf16[2,96,160]{2,1,0:T(8,128)(2,1)S(1)}, u32[]{:S(2)}, u32[]{:S(2)}) collective-permute-start(bf16[2,96,160]{2,1,0:T(8,128)(2,1)S(1)} %get-tuple-element.59), channel_id=1, source_target_pairs={{0,96},{4,100},{8,104},{12,108},{16,112},{20,116},{24,120},{28,124... | collective-permute-start | bytes 184328 | tf_op jit(solution)/shard_map/ppermute | solution.py:430
  146.6 2.9 %collective-permute-start.30 = (bf16[96,320]{1,0:T(8,128)(2,1)S(1)}, bf16[96,320]{1,0:T(8,128)(2,1)S(1)}, u32[]{:S(2)}, u32[]{:S(2)}) collective-permute-start(bf16[96,320]{1,0:T(8,128)(2,1)S(1)} %get-tuple-element.67), channel_id=1, source_target_pairs={{0,128},{4,132},{8,136},{12,140},{16,144},{20,148},{24,152},{28,15... | collective-permute-start | bytes 184328 | tf_op jit(solution)/shard_map/ppermute | solution.py:362
  150.5 2.8 %collective-permute-start.25 = (bf16[96,160]{1,0:T(8,128)(2,1)S(1)}, bf16[96,160]{1,0:T(8,128)(2,1)S(1)}, u32[]{:S(2)}, u32[]{:S(2)}) collective-permute-start(bf16[96,160]{1,0:T(8,128)(2,1)S(1)} %get-tuple-element.61), channel_id=1, source_target_pairs={{0,128},{4,132},{8,136},{12,140},{16,144},{20,148},{24,152},{28,15... | collective-permute-start | bytes 92168 | tf_op jit(solution)/shard_map/ppermute | solution.py:362
  153.3 1.9 %collective-permute-done.30.refs_1_ = bf16[96,320]{1,0:T(8,128)(2,1)S(1)} collective-permute-done((bf16[96,320]{1,0:T(8,128)(2,1)S(1)}, bf16[96,320]{1,0:T(8,128)(2,1)S(1)}, u32[]{:S(2)}, u32[]{:S(2)}) %collective-permute-start.30) | collective-permute-done | bytes 61472 | tf_op jit(solution)/shard_map/ppermute | solution.py:362
  (101 shorter events, 32.0 us)
Async XLA Ops:
  0.6 13.9 %collective-permute-start = (bf16[2,64,640]{2,1,0:T(8,128)(2,1)}, bf16[2,64,640]{2,1,0:T(8,128)(2,1)S(1)}, u32[]{:S(2)}, u32[]{:S(2)}) collective-permute-start(bf16[2,64,640]{2,1,0:T(8,128)(2,1)} %refs_1_.3), channel_id=1, source_target_pairs={{0,1},{1,2},{2,3},{3,0},{4,5},{5,6},{6,7},{7,4},{8,9},{9,10},{10,1... | collective-permute-start | bytes 491528 | tf_op jit(solution)/shard_map/ppermute | solution.py:359
  2.6 14.3 %collective-permute-start.1 = (bf16[2,64,640]{2,1,0:T(8,128)(2,1)}, bf16[2,64,640]{2,1,0:T(8,128)(2,1)S(1)}, u32[]{:S(2)}, u32[]{:S(2)}) collective-permute-start(bf16[2,64,640]{2,1,0:T(8,128)(2,1)} %refs_1_.3), channel_id=1, source_target_pairs={{0,2},{1,3},{2,0},{3,1},{4,6},{5,7},{6,4},{7,5},{8,10},{9,11},{10,... | collective-permute-start | bytes 491528 | tf_op jit(solution)/shard_map/ppermute | solution.py:359
  4.9 14.0 %collective-permute-start.2 = (bf16[2,64,640]{2,1,0:T(8,128)(2,1)}, bf16[2,64,640]{2,1,0:T(8,128)(2,1)S(1)}, u32[]{:S(2)}, u32[]{:S(2)}) collective-permute-start(bf16[2,64,640]{2,1,0:T(8,128)(2,1)} %refs_1_.3), channel_id=1, source_target_pairs={{0,3},{1,0},{2,1},{3,2},{4,7},{5,4},{6,5},{7,6},{8,11},{9,8},{10,9... | collective-permute-start | bytes 491528 | tf_op jit(solution)/shard_map/ppermute | solution.py:359
  23.3 1.3 collective-permute-start.3
  23.4 3.8 %collective-permute-start.4 = (bf16[160,128]{1,0:T(8,128)(2,1)S(1)}, bf16[160,128]{1,0:T(8,128)(2,1)S(1)}, u32[]{:S(2)}, u32[]{:S(2)}) collective-permute-start(bf16[160,128]{1,0:T(8,128)(2,1)S(1)} %get-tuple-element.38), channel_id=1, source_target_pairs={{4,8},{8,4},{12,16},{16,12},{20,24},{24,20},{28,32},{32,28},{36,40... | collective-permute-start | bytes 122888 | tf_op jit(solution)/shard_map/ppermute | solution.py:365
  27.2 10.3 %collective-permute-start.5 = (bf16[160,128]{1,0:T(8,128)(2,1)S(1)}, bf16[160,128]{1,0:T(8,128)(2,1)S(1)}, u32[]{:S(2)}, u32[]{:S(2)}) collective-permute-start(bf16[160,128]{1,0:T(8,128)(2,1)S(1)} %shard_map.95.refs_1_), channel_id=1, source_target_pairs={{0,1},{1,2},{2,3},{3,0},{4,5},{5,6},{6,7},{7,4},{8,9},{9,10},{10,1... | collective-permute-start | bytes 122888 | tf_op jit(solution)/shard_map/ppermute | solution.py:359
  27.3 10.2 %collective-permute-start.6 = (bf16[160,128]{1,0:T(8,128)(2,1)S(1)}, bf16[160,128]{1,0:T(8,128)(2,1)S(1)}, u32[]{:S(2)}, u32[]{:S(2)}) collective-permute-start(bf16[160,128]{1,0:T(8,128)(2,1)S(1)} %shard_map.95.refs_1_), channel_id=1, source_target_pairs={{0,2},{1,3},{2,0},{3,1},{4,6},{5,7},{6,4},{7,5},{8,10},{9,11},{10,... | collective-permute-start | bytes 122888 | tf_op jit(solution)/shard_map/ppermute | solution.py:359
  28.7 8.8 %collective-permute-start.7 = (bf16[160,128]{1,0:T(8,128)(2,1)S(1)}, bf16[160,128]{1,0:T(8,128)(2,1)S(1)}, u32[]{:S(2)}, u32[]{:S(2)}) collective-permute-start(bf16[160,128]{1,0:T(8,128)(2,1)S(1)} %shard_map.95.refs_1_), channel_id=1, source_target_pairs={{0,3},{1,0},{2,1},{3,2},{4,7},{5,4},{6,5},{7,6},{8,11},{9,8},{10,9... | collective-permute-start | bytes 122888 | tf_op jit(solution)/shard_map/ppermute | solution.py:359
  30.6 19.1 %all-to-all-start = ((bf16[8,80,512]{2,1,0:T(8,128)(2,1)}), bf16[8,80,512]{2,1,0:T(8,128)(2,1)S(1)}, u32[]{:S(2)}, u32[]{:S(2)}) async-start(bf16[8,80,512]{2,1,0:T(8,128)(2,1)} %shard_map.94.refs_3_), calls=%async_computation | async-start | bytes 1310720 | tf_op jit(solution)/shard_map/all_to_all | solution.py:382
  41.0 11.3 %collective-permute-start.8 = (bf16[320,128]{1,0:T(8,128)(2,1)S(1)}, bf16[320,128]{1,0:T(8,128)(2,1)S(1)}, u32[]{:S(2)}, u32[]{:S(2)}) collective-permute-start(bf16[320,128]{1,0:T(8,128)(2,1)S(1)} %get-tuple-element.41), channel_id=1, source_target_pairs={{0,4},{4,0},{8,12},{12,8},{16,20},{20,16},{24,28},{28,24},{32,36},... | collective-permute-start | bytes 245768 | tf_op jit(solution)/shard_map/ppermute | solution.py:362
  41.6 10.7 %collective-permute-start.9 = (bf16[320,128]{1,0:T(8,128)(2,1)S(1)}, bf16[320,128]{1,0:T(8,128)(2,1)S(1)}, u32[]{:S(2)}, u32[]{:S(2)}) collective-permute-start(bf16[320,128]{1,0:T(8,128)(2,1)S(1)} %get-tuple-element.42), channel_id=1, source_target_pairs={{4,8},{8,4},{12,16},{16,12},{20,24},{24,20},{28,32},{32,28},{36,40... | collective-permute-start | bytes 245768 | tf_op jit(solution)/shard_map/ppermute | solution.py:365
  53.4 1.3 collective-permute-start.11
  54.7 16.3 %collective-permute-start.17 = (bf16[3,320,128]{2,1,0:T(8,128)(2,1)S(1)}, bf16[3,320,128]{2,1,0:T(8,128)(2,1)S(1)}, u32[]{:S(2)}, u32[]{:S(2)}) collective-permute-start(bf16[3,320,128]{2,1,0:T(8,128)(2,1)S(1)} %shard_map.101.refs_1_), channel_id=1, source_target_pairs={{0,8},{4,12},{8,0},{12,4},{16,24},{20,28},{24,16},{28,20},{32,40},... | collective-permute-start | bytes 737288 | tf_op jit(solution)/shard_map/ppermute | solution.py:362
  61.6 9.4 %collective-permute-start.12 = (bf16[160,128]{1,0:T(8,128)(2,1)S(1)}, bf16[160,128]{1,0:T(8,128)(2,1)S(1)}, u32[]{:S(2)}, u32[]{:S(2)}) collective-permute-start(bf16[160,128]{1,0:T(8,128)(2,1)S(1)} %get-tuple-element.46), channel_id=1, source_target_pairs={{0,1},{1,2},{2,3},{3,0},{4,5},{5,6},{6,7},{7,4},{8,9},{9,10},{10,1... | collective-permute-start | bytes 122888 | tf_op jit(solution)/shard_map/ppermute | solution.py:359
  62.1 13.1 %collective-permute-start.13 = (bf16[160,128]{1,0:T(8,128)(2,1)S(1)}, bf16[160,128]{1,0:T(8,128)(2,1)S(1)}, u32[]{:S(2)}, u32[]{:S(2)}) collective-permute-start(bf16[160,128]{1,0:T(8,128)(2,1)S(1)} %get-tuple-element.47), channel_id=1, source_target_pairs={{0,2},{1,3},{2,0},{3,1},{4,6},{5,7},{6,4},{7,5},{8,10},{9,11},{10,... | collective-permute-start | bytes 122888 | tf_op jit(solution)/shard_map/ppermute | solution.py:359
  65.5 9.7 %collective-permute-start.14 = (bf16[160,128]{1,0:T(8,128)(2,1)S(1)}, bf16[160,128]{1,0:T(8,128)(2,1)S(1)}, u32[]{:S(2)}, u32[]{:S(2)}) collective-permute-start(bf16[160,128]{1,0:T(8,128)(2,1)S(1)} %get-tuple-element.48), channel_id=1, source_target_pairs={{0,3},{1,0},{2,1},{3,2},{4,7},{5,4},{6,5},{7,6},{8,11},{9,8},{10,9... | collective-permute-start | bytes 122888 | tf_op jit(solution)/shard_map/ppermute | solution.py:359
  66.5 11.4 %all-to-all-start.1 = ((bf16[8,80,128]{2,1,0:T(8,128)(2,1)}), bf16[8,80,128]{2,1,0:T(8,128)(2,1)S(1)}, u32[]{:S(2)}, u32[]{:S(2)}) async-start(bf16[8,80,128]{2,1,0:T(8,128)(2,1)} %shard_map.104), calls=%async_computation.1 | async-start | bytes 327680 | tf_op jit(solution)/shard_map/all_to_all | solution.py:400
  71.6 15.1 %collective-permute-start.18 = (bf16[5,320,128]{2,1,0:T(8,128)(2,1)S(1)}, bf16[5,320,128]{2,1,0:T(8,128)(2,1)S(1)}, u32[]{:S(2)}, u32[]{:S(2)}) collective-permute-start(bf16[5,320,128]{2,1,0:T(8,128)(2,1)S(1)} %get-tuple-element.50.refs_1_), channel_id=1, source_target_pairs={{0,16},{4,20},{8,24},{12,28},{16,0},{20,4},{24,8},{28,12},{32,48},... | collective-permute-start | bytes 1228808 | tf_op jit(solution)/shard_map/ppermute | solution.py:362
  75.2 12.0 %collective-permute-start.15 = (bf16[160,128]{1,0:T(8,128)(2,1)S(1)}, bf16[160,128]{1,0:T(8,128)(2,1)S(1)}, u32[]{:S(2)}, u32[]{:S(2)}) collective-permute-start(bf16[160,128]{1,0:T(8,128)(2,1)S(1)} %shard_map.100.refs_2_.refs_0_), channel_id=1, source_target_pairs={{0,4},{4,0},{8,12},{12,8},{16,20},{20,16},{24,28},{28,24},{32,36},... | collective-permute-start | bytes 122888 | tf_op jit(solution)/shard_map/ppermute | solution.py:362
  75.3 11.9 %collective-permute-start.16 = (bf16[160,128]{1,0:T(8,128)(2,1)S(1)}, bf16[160,128]{1,0:T(8,128)(2,1)S(1)}, u32[]{:S(2)}, u32[]{:S(2)}) collective-permute-start(bf16[160,128]{1,0:T(8,128)(2,1)S(1)} %shard_map.100.refs_2_.refs_0_), channel_id=1, source_target_pairs={{4,8},{8,4},{12,16},{16,12},{20,24},{24,20},{28,32},{32,28},{36,40... | collective-permute-start | bytes 122888 | tf_op jit(solution)/shard_map/ppermute | solution.py:365
  93.0 63.0 %all-to-all-start.2 = ((bf16[4,2,64,640]{3,2,1,0:T(8,128)(2,1)}), bf16[4,2,64,640]{3,2,1,0:T(8,128)(2,1)}, u32[]{:S(2)}, u32[]{:S(2)}) async-start(bf16[4,2,64,640]{3,2,1,0:T(8,128)(2,1)} %shard_map.106.refs_3_.refs_7_), calls=%async_computation.2 | async-start | bytes 1310720 | tf_op jit(solution)/shard_map/all_to_all | solution.py:449
  101.1 5.0 %collective-permute-start.19 = (bf16[3,160,128]{2,1,0:T(8,128)(2,1)S(1)}, bf16[3,160,128]{2,1,0:T(8,128)(2,1)S(1)}, u32[]{:S(2)}, u32[]{:S(2)}) collective-permute-start(bf16[3,160,128]{2,1,0:T(8,128)(2,1)S(1)} %shard_map.107.refs_1_), channel_id=1, source_target_pairs={{0,8},{4,12},{8,0},{12,4},{16,24},{20,28},{24,16},{28,20},{32,40},... | collective-permute-start | bytes 368648 | tf_op jit(solution)/shard_map/ppermute | solution.py:362
  107.2 29.6 %collective-permute-start.20 = (bf16[5,160,128]{2,1,0:T(8,128)(2,1)S(1)}, bf16[5,160,128]{2,1,0:T(8,128)(2,1)S(1)}, u32[]{:S(2)}, u32[]{:S(2)}) collective-permute-start(bf16[5,160,128]{2,1,0:T(8,128)(2,1)S(1)} %get-tuple-element.52.refs_1_), channel_id=1, source_target_pairs={{0,16},{4,20},{8,24},{12,28},{16,0},{20,4},{24,8},{28,12},{32,48},... | collective-permute-start | bytes 614408 | tf_op jit(solution)/shard_map/ppermute | solution.py:362
  114.0 29.2 %collective-permute-start.27 = (bf16[2,96,320]{2,1,0:T(8,128)(2,1)S(1)}, bf16[2,96,320]{2,1,0:T(8,128)(2,1)S(1)}, u32[]{:S(2)}, u32[]{:S(2)}) collective-permute-start(bf16[2,96,320]{2,1,0:T(8,128)(2,1)S(1)} %get-tuple-element.63), channel_id=1, source_target_pairs={{0,32},{4,36},{8,40},{12,44},{16,48},{20,52},{24,56},{28,60},{32,6... | collective-permute-start | bytes 368648 | tf_op jit(solution)/shard_map/ppermute | solution.py:430
  118.3 27.7 %collective-permute-start.28 = (bf16[2,96,320]{2,1,0:T(8,128)(2,1)S(1)}, bf16[2,96,320]{2,1,0:T(8,128)(2,1)S(1)}, u32[]{:S(2)}, u32[]{:S(2)}) collective-permute-start(bf16[2,96,320]{2,1,0:T(8,128)(2,1)S(1)} %get-tuple-element.64), channel_id=1, source_target_pairs={{0,64},{4,68},{8,72},{12,76},{16,80},{20,84},{24,88},{28,92},{32,9... | collective-permute-start | bytes 368648 | tf_op jit(solution)/shard_map/ppermute | solution.py:430
  136.8 9.2 %collective-permute-start.29 = (bf16[2,96,320]{2,1,0:T(8,128)(2,1)S(1)}, bf16[2,96,320]{2,1,0:T(8,128)(2,1)S(1)}, u32[]{:S(2)}, u32[]{:S(2)}) collective-permute-start(bf16[2,96,320]{2,1,0:T(8,128)(2,1)S(1)} %get-tuple-element.65), channel_id=1, source_target_pairs={{0,96},{4,100},{8,104},{12,108},{16,112},{20,116},{24,120},{28,124... | collective-permute-start | bytes 368648 | tf_op jit(solution)/shard_map/ppermute | solution.py:430
  137.4 1.3 collective-permute-start.21
  140.9 8.7 %collective-permute-start.22 = (bf16[2,96,160]{2,1,0:T(8,128)(2,1)S(1)}, bf16[2,96,160]{2,1,0:T(8,128)(2,1)S(1)}, u32[]{:S(2)}, u32[]{:S(2)}) collective-permute-start(bf16[2,96,160]{2,1,0:T(8,128)(2,1)S(1)} %get-tuple-element.57), channel_id=1, source_target_pairs={{0,32},{4,36},{8,40},{12,44},{16,48},{20,52},{24,56},{28,60},{32,6... | collective-permute-start | bytes 184328 | tf_op jit(solution)/shard_map/ppermute | solution.py:430
  143.2 6.4 %collective-permute-start.23 = (bf16[2,96,160]{2,1,0:T(8,128)(2,1)S(1)}, bf16[2,96,160]{2,1,0:T(8,128)(2,1)S(1)}, u32[]{:S(2)}, u32[]{:S(2)}) collective-permute-start(bf16[2,96,160]{2,1,0:T(8,128)(2,1)S(1)} %get-tuple-element.58), channel_id=1, source_target_pairs={{0,64},{4,68},{8,72},{12,76},{16,80},{20,84},{24,88},{28,92},{32,9... | collective-permute-start | bytes 184328 | tf_op jit(solution)/shard_map/ppermute | solution.py:430
  143.2 6.7 %collective-permute-start.24 = (bf16[2,96,160]{2,1,0:T(8,128)(2,1)S(1)}, bf16[2,96,160]{2,1,0:T(8,128)(2,1)S(1)}, u32[]{:S(2)}, u32[]{:S(2)}) collective-permute-start(bf16[2,96,160]{2,1,0:T(8,128)(2,1)S(1)} %get-tuple-element.59), channel_id=1, source_target_pairs={{0,96},{4,100},{8,104},{12,108},{16,112},{20,116},{24,120},{28,124... | collective-permute-start | bytes 184328 | tf_op jit(solution)/shard_map/ppermute | solution.py:430
  146.6 8.7 %collective-permute-start.30 = (bf16[96,320]{1,0:T(8,128)(2,1)S(1)}, bf16[96,320]{1,0:T(8,128)(2,1)S(1)}, u32[]{:S(2)}, u32[]{:S(2)}) collective-permute-start(bf16[96,320]{1,0:T(8,128)(2,1)S(1)} %get-tuple-element.67), channel_id=1, source_target_pairs={{0,128},{4,132},{8,136},{12,140},{16,144},{20,148},{24,152},{28,15... | collective-permute-start | bytes 184328 | tf_op jit(solution)/shard_map/ppermute | solution.py:362
  150.5 8.6 %collective-permute-start.25 = (bf16[96,160]{1,0:T(8,128)(2,1)S(1)}, bf16[96,160]{1,0:T(8,128)(2,1)S(1)}, u32[]{:S(2)}, u32[]{:S(2)}) collective-permute-start(bf16[96,160]{1,0:T(8,128)(2,1)S(1)} %get-tuple-element.61), channel_id=1, source_target_pairs={{0,128},{4,132},{8,136},{12,140},{16,144},{20,148},{24,152},{28,15... | collective-permute-start | bytes 92168 | tf_op jit(solution)/shard_map/ppermute | solution.py:362
  (21 other events, 134.9 us)

commit v8 on v7

--- a/solution.py
+++ b/solution.py
@@ -186,8 +186,6 @@
     deep = mine.shape[1]
     turn = unit(deep)
     before, here, after = [mm_t(turn, row).astype(BF) for row in (before, mine[...], after)]
-    weave = interleave(2 * deep)
-    pieces, _, part, _ = out.shape
     top = jnp.concatenate([here, after])
     low = jnp.concatenate([before, here])
     z = []
@@ -198,8 +196,15 @@
     for r in range(2):
         even = z[1][r] + z[0][r] + moved(z[2][r], 1, 0)
         late = z[1][r] + moved(z[0][r], -1, 0) + z[2][r]
-        y = jnp.concatenate([(0.25 * even).astype(BF), (0.25 * late).astype(BF)])
-        y = mm(weave, y).astype(BF)
+        out[r, :deep] = (0.25 * even).astype(BF)
+        out[r, deep:] = (0.25 * late).astype(BF)
+
+
+def weave(sides, out):
+    pieces, rows, part, _ = out.shape
+    order = interleave(sides.shape[1])
+    for r in range(rows):
+        y = mm(order, sides[r]).astype(BF)
         for k in range(pieces):
             out[k, r] = y[k * part : (k + 1) * part]
 
@@ -387,6 +392,7 @@
         (at, mine, *got, w_deep),
     )
     partner, other = pairs(partner, other)
+    deep_slab = call(deep_slices, shape((MEMBERS, size, deep)), (pooled, pick), behind=(partner,))
     preact = call(
         deep_own, shape((full, deep), F32), (pooled, w_deep), behind=(fine_slab,)
     )
@@ -394,16 +400,17 @@
         deep_forward,
         [shape((full, deep))] * 2,
         (preact, partner, other, upstream[0].T),
-    )
+        behind=(deep_slab,),
+    )
+    deep_slab = lax.all_to_all(deep_slab, "wide", 0, 0, axis_index_groups=near)
     pre_partner, other = pairs(grad_pre, grad_pre)
-    deep_slab = call(deep_slices, shape((MEMBERS, size, deep)), (pooled, pick), behind=(pre_partner,))
-    deep_slab = lax.all_to_all(deep_slab, "wide", 0, 0, axis_index_groups=near)
     pre_first = call(pack, shape((3, full, deep)), (grad_pre, pre_partner, other))
     parts = call(
         deep_backward,
         [shape((fine, deep))] * 4,
         (at, pre_partner, grad_pre, other, w_deep),
         [pltpu.VMEM((2, full, deep), BF), pltpu.VMEM((depth, deep), BF)],
+        behind=(deep_slab,),
     )
     got = [across(parts[s], s) for s in (1, 2, 3)]
     even_table, late_table, deep_table = call(
@@ -412,7 +419,7 @@
     grad_pool = call(pool_sum, shape((fine, deep)), (parts[0], *got))
     pool_partner, other = pairs(grad_pool, grad_pool)
     pre_rows = group_gather(pre_first, (got[0],))
-    pool_first = call(pack, shape((3, fine, deep)), (grad_pool, pool_partner, other))
+    pool_first = call(pack, shape((3, fine, deep)), (grad_pool, pool_partner, other), behind=(deep_table, pre_rows[2]))
 
     def products(body, tables, rows, behind=()):
         width = rows[0].shape[1]
@@ -436,16 +443,17 @@
         total = call(weight_sum, shape((9, grain, width), F32), (keep, swap(send, 32)), behind=behind)
         return total.reshape(3, 3, grain, width)
 
-    back = call(
+    deep_parts = products(deep_part, (deep_table,), pre_rows)
+    pool_rows = group_gather(pool_first, (deep_parts[0],))
+    sides = call(
         fine_backward,
-        shape((pieces, rows, part, depth)),
+        shape((rows, cols, depth)),
         (at, pool_partner, grad_pool, other, w_fine),
         [pltpu.VMEM((2, fine, deep), BF)],
-        behind=(pre_rows[2], deep_table),
-    )
-    pool_rows = group_gather(pool_first, (back,))
-    deep_parts = products(deep_part, (deep_table,), pre_rows, (back,))
+        behind=(pool_rows[0],),
+    )
     fine_parts = products(fine_part, (even_table, late_table), pool_rows)
+    back = call(weave, shape((pieces, rows, part, depth)), (sides,), behind=(pool_rows[2],))
     partial = lax.all_to_all(back, "narrow", 0, 0)
     grad_latent = jnp.sum(partial.astype(F32), axis=0).astype(BF)
 

time: 161 us -> 154 us (0.957)
  waiting for transfers between devices: 42.6 us -> 37.9 us
  local copies, waits for them, and re-layouts: 14.1 us -> 10.5 us
    ppermute x6, starting transfers between devices: 27.9 us -> 22 us  [owners(): lax.ppermute(parts[s], 'wide', [(i, i // 32 * 32 + (i // 8 + s) % 4 * 8 +...]
    ppermute x12, starting transfers between devices: 18.1 us -> 22.9 us  [swap(): return lax.ppermute(v, 'wide', [(i, i ^ bit) for i in range(wide)])]
    unnamed x40 -> x22, local copies, waits for them, and re-layouts: 14.1 us -> 10.4 us
    all_to_all x1, waiting for transfers between devices: 1.9 us -> 0.01 us  [on_device(): deep_slab = lax.all_to_all(deep_slab, 'wide', 0, 0, axis_index_groups=near)]
    pallas_call x23 -> x24, Pallas kernels: 22.5 us -> 22.6 us  [call(): pl.pallas_call(kernel, out_shape=outs, in_specs=[smem if a.dtype == jnp.i...]
  transfers between devices with their start and end apart: 34 -> 34, of which waited for: 14 -> 13; matrix products, arithmetic and copies ran while one was open for 1% -> 1% of each run, Pallas kernels for 11% -> 12%
where the time goes in v8:
time: 154 us; the launch traced here: 153 us
  starting transfers between devices  79.5 us (52%)
  waiting for transfers between devices  37.9 us (25%)
  Pallas kernels  22.6 us (15%)
  local copies, waits for them, and re-layouts  10.5 us (7%)
    ppermute x12, starting transfers between devices, swap(): return lax.ppermute(v, 'wide', [(i, i ^ bit) for i in range(wide)])  22.9 us
    pallas_call x24, Pallas kernels, call(): pl.pallas_call(kernel, out_shape=outs, in_specs=[smem if a.dtype == jnp.i...  22.6 us
    ppermute x6, starting transfers between devices, owners(): lax.ppermute(parts[s], 'wide', [(i, i // 32 * 32 + (i // 8 + s) % 4 * 8 +...  22 us
    ppermute x12, waiting for transfers between devices, swap(): return lax.ppermute(v, 'wide', [(i, i ^ bit) for i in range(wide)])  19.7 us
    ppermute x9, starting transfers between devices, across(): lax.ppermute(v, 'narrow', [(i, (i + step) % pieces) for i in range(pieces)])  14 us
    ppermute x9, waiting for transfers between devices, across(): lax.ppermute(v, 'narrow', [(i, (i + step) % pieces) for i in range(pieces)])  12 us
    unnamed x22, local copies, waits for them, and re-layouts  10.4 us
    all_to_all x1, starting transfers between devices, on_device(): partial = lax.all_to_all(back, 'narrow', 0, 0)  7.19 us
  transfers between devices with their start and end apart: 34, of which 13 were waited for; matrix products, arithmetic and copies ran while one was open for 1% of the time, Pallas kernels for 12%

profile of v8, /device:TPU:32, one launch (start us, length us, event | category | flops | bytes accessed | tf_op | source)
XLA Modules:
  0.0 152.5 jit_solution(17706938864136121729)
XLA Ops:
  0.6 3.4 %collective-permute-start.1 = (bf16[2,64,640]{2,1,0:T(8,128)(2,1)}, bf16[2,64,640]{2,1,0:T(8,128)(2,1)S(1)}, u32[]{:S(2)}, u32[]{:S(2)}) collective-permute-start(bf16[2,64,640]{2,1,0:T(8,128)(2,1)} %refs_1_.3), channel_id=1, source_target_pairs={{0,2},{1,3},{2,0},{3,1},{4,6},{5,7},{6,4},{7,5},{8,10},{9,11},{10,... | collective-permute-start | bytes 491528 | tf_op jit(solution)/shard_map/ppermute | solution.py:364
  4.0 2.0 %collective-permute-start.2 = (bf16[2,64,640]{2,1,0:T(8,128)(2,1)}, bf16[2,64,640]{2,1,0:T(8,128)(2,1)S(1)}, u32[]{:S(2)}, u32[]{:S(2)}) collective-permute-start(bf16[2,64,640]{2,1,0:T(8,128)(2,1)} %refs_1_.3), channel_id=1, source_target_pairs={{0,3},{1,0},{2,1},{3,2},{4,7},{5,4},{6,5},{7,6},{8,11},{9,8},{10,9... | collective-permute-start | bytes 491528 | tf_op jit(solution)/shard_map/ppermute | solution.py:364
  6.1 5.7 %collective-permute-done.1.refs_3_ = bf16[2,64,640]{2,1,0:T(8,128)(2,1)S(1)} collective-permute-done((bf16[2,64,640]{2,1,0:T(8,128)(2,1)}, bf16[2,64,640]{2,1,0:T(8,128)(2,1)S(1)}, u32[]{:S(2)}, u32[]{:S(2)}) %collective-permute-start.1) | collective-permute-done | bytes 163872 | tf_op jit(solution)/shard_map/ppermute | solution.py:364
  11.8 6.1 %collective-permute-done.refs_2_ = bf16[2,64,640]{2,1,0:T(8,128)(2,1)S(1)} collective-permute-done((bf16[2,64,640]{2,1,0:T(8,128)(2,1)}, bf16[2,64,640]{2,1,0:T(8,128)(2,1)S(1)}, u32[]{:S(2)}, u32[]{:S(2)}) %collective-permute-start) | collective-permute-done | bytes 163872 | tf_op jit(solution)/shard_map/ppermute | solution.py:364
  20.3 1.9 %shard_map.93 = (bf16[4,2,64,640]{3,2,1,0:T(8,128)(2,1)S(1)}, f32[160,128]{1,0:T(8,128)S(1)}, bf16[160,128]{1,0:T(8,128)(2,1)S(1)}, bf16[160,128]{1,0:T(8,128)(2,1)S(1)}) custom-call(s32[5]{0:T(128)S(1)} %stack.23.refs_0_, bf16[2,64,640]{2,1,0:T(8,128)(2,1)S(1)} %copy-done.8, bf16[2,64,640]{2,1,0:T(8,128)(2,1)S(1)} %collective-permute-done.refs_2_, ...), custom_call_target="tpu_custom_call" | custom-call | flops 30000001024 | bytes 2498580 | tf_op jit(solution)/shard_map/pallas_call | solution.py:64
  23.5 2.6 %shard_map.94.refs_3_ = bf16[8,80,512]{2,1,0:T(8,128)(2,1)} custom-call(bf16[4,2,64,640]{3,2,1,0:T(8,128)(2,1)S(1)} %get-tuple-element.39.refs_0_, bf16[640,640]{1,0:T(8,128)(2,1)S(1)} %copy-done.4, bf16[160,128]{1,0:T(8,128)(2,1)S(1)} %collective-permute-done.3.refs_2_.refs_1_), custom_call_target="tpu_custom_call" | custom-call | bytes 1474560 | tf_op jit(solution)/shard_map/pallas_call | solution.py:64
  26.2 3.8 %collective-permute-start.6 = (bf16[160,128]{1,0:T(8,128)(2,1)S(1)}, bf16[160,128]{1,0:T(8,128)(2,1)S(1)}, u32[]{:S(2)}, u32[]{:S(2)}) collective-permute-start(bf16[160,128]{1,0:T(8,128)(2,1)S(1)} %shard_map.95.refs_1_), channel_id=1, source_target_pairs={{0,2},{1,3},{2,0},{3,1},{4,6},{5,7},{6,4},{7,5},{8,10},{9,11},{10,... | collective-permute-start | bytes 122888 | tf_op jit(solution)/shard_map/ppermute | solution.py:364
  30.1 7.2 %all-to-all-start = ((bf16[8,80,512]{2,1,0:T(8,128)(2,1)}), bf16[8,80,512]{2,1,0:T(8,128)(2,1)S(1)}, u32[]{:S(2)}, u32[]{:S(2)}) async-start(bf16[8,80,512]{2,1,0:T(8,128)(2,1)} %shard_map.94.refs_3_), calls=%async_computation | async-start | bytes 1310720 | tf_op jit(solution)/shard_map/all_to_all | solution.py:387
  37.3 2.0 %copy-done.1 = bf16[3,3,640,320]{2,3,1,0:T(8,128)(2,1)S(1)} copy-done((bf16[3,3,640,320]{2,3,1,0:T(8,128)(2,1)S(1)}, bf16[3,3,640,320]{2,3,1,0:T(8,128)(2,1)}, u32[]{:S(2)}) %copy-start.1) | copy-done | bytes 3686424
  43.3 6.2 %all-to-all-done.refs_2_.refs_0_ = bf16[8,80,512]{2,1,0:T(8,128)(2,1)S(1)} async-done(((bf16[8,80,512]{2,1,0:T(8,128)(2,1)}), bf16[8,80,512]{2,1,0:T(8,128)(2,1)S(1)}, u32[]{:S(2)}, u32[]{:S(2)}) %all-to-all-start) | async-done | bytes 655392 | tf_op jit(solution)/shard_map/all_to_all | solution.py:387
  49.5 3.4 %all-to-all-start.1 = ((bf16[8,80,128]{2,1,0:T(8,128)(2,1)}), bf16[8,80,128]{2,1,0:T(8,128)(2,1)S(1)}, u32[]{:S(2)}, u32[]{:S(2)}) async-start(bf16[8,80,128]{2,1,0:T(8,128)(2,1)} %shard_map.98.refs_4_), calls=%async_computation.1 | async-start | bytes 327680 | tf_op jit(solution)/shard_map/all_to_all | solution.py:405
  52.9 2.0 %copy-done.2 = bf16[3,3,640,320]{2,3,1,0:T(8,128)(2,1)S(1)} copy-done((bf16[3,3,640,320]{2,3,1,0:T(8,128)(2,1)S(1)}, bf16[3,3,640,320]{2,3,1,0:T(8,128)(2,1)}, u32[]{:S(2)}) %copy-start.2) | copy-done | bytes 3686424
  57.1 3.4 %collective-permute-start.10 = (bf16[320,128]{1,0:T(8,128)(2,1)S(1)}, bf16[320,128]{1,0:T(8,128)(2,1)S(1)}, u32[]{:S(2)}, u32[]{:S(2)}) collective-permute-start(bf16[320,128]{1,0:T(8,128)(2,1)S(1)} %get-tuple-element.44.refs_2_.refs_0_), channel_id=1, source_target_pairs={{0,4},{4,0},{8,12},{12,8},{16,20},{20,16},{24,28},{28,24},{32,36},... | collective-permute-start | bytes 245768 | tf_op jit(solution)/shard_map/ppermute | solution.py:367
  61.4 2.8 %collective-permute-start.17 = (bf16[3,320,128]{2,1,0:T(8,128)(2,1)S(1)}, bf16[3,320,128]{2,1,0:T(8,128)(2,1)S(1)}, u32[]{:S(2)}, u32[]{:S(2)}) collective-permute-start(bf16[3,320,128]{2,1,0:T(8,128)(2,1)S(1)} %shard_map.103.refs_1_), channel_id=1, source_target_pairs={{0,8},{4,12},{8,0},{12,4},{16,24},{20,28},{24,16},{28,20},{32,40},... | collective-permute-start | bytes 737288 | tf_op jit(solution)/shard_map/ppermute | solution.py:367
  64.3 2.0 %copy-done.3 = bf16[3,3,640,320]{2,3,1,0:T(8,128)(2,1)S(1)} copy-done((bf16[3,3,640,320]{2,3,1,0:T(8,128)(2,1)S(1)}, bf16[3,3,640,320]{2,3,1,0:T(8,128)(2,1)}, u32[]{:S(2)}) %copy-start.3) | copy-done | bytes 3686424
  66.3 1.9 %shard_map.100 = (bf16[160,128]{1,0:T(8,128)(2,1)S(1)}, bf16[160,128]{1,0:T(8,128)(2,1)S(1)}, bf16[160,128]{1,0:T(8,128)(2,1)S(1)}, bf16[160,128]{1,0:T(8,128)(2,1)S(1)}) custom-call(s32[5]{0:T(128)S(1)} %stack.23.refs_0_, bf16[320,128]{1,0:T(8,128)(2,1)S(1)} %collective-permute-done.10.refs_1_, bf16[320,128]{1,0:T(8,128)(2,1)S(1)} %get-tuple-element.44.refs_2_.refs_0_, ...), custom_call_target="tpu_custom_call" | custom-call | flops 30000001024 | bytes 3932180 | tf_op jit(solution)/shard_map/pallas_call | solution.py:64
  69.1 3.5 %collective-permute-start.13 = (bf16[160,128]{1,0:T(8,128)(2,1)S(1)}, bf16[160,128]{1,0:T(8,128)(2,1)S(1)}, u32[]{:S(2)}, u32[]{:S(2)}) collective-permute-start(bf16[160,128]{1,0:T(8,128)(2,1)S(1)} %get-tuple-element.47), channel_id=1, source_target_pairs={{0,2},{1,3},{2,0},{3,1},{4,6},{5,7},{6,4},{7,5},{8,10},{9,11},{10,... | collective-permute-start | bytes 122888 | tf_op jit(solution)/shard_map/ppermute | solution.py:364
  73.6 2.8 %collective-permute-start.18 = (bf16[5,320,128]{2,1,0:T(8,128)(2,1)S(1)}, bf16[5,320,128]{2,1,0:T(8,128)(2,1)S(1)}, u32[]{:S(2)}, u32[]{:S(2)}) collective-permute-start(bf16[5,320,128]{2,1,0:T(8,128)(2,1)S(1)} %get-tuple-element.51.refs_1_), channel_id=1, source_target_pairs={{0,16},{4,20},{8,24},{12,28},{16,0},{20,4},{24,8},{28,12},{32,48},... | collective-permute-start | bytes 1228808 | tf_op jit(solution)/shard_map/ppermute | solution.py:367
  77.5 2.0 %collective-permute-start.15 = (bf16[160,128]{1,0:T(8,128)(2,1)S(1)}, bf16[160,128]{1,0:T(8,128)(2,1)S(1)}, u32[]{:S(2)}, u32[]{:S(2)}) collective-permute-start(bf16[160,128]{1,0:T(8,128)(2,1)S(1)} %shard_map.101.refs_0_.refs_2_), channel_id=1, source_target_pairs={{0,4},{4,0},{8,12},{12,8},{16,20},{20,16},{24,28},{28,24},{32,36},... | collective-permute-start | bytes 122888 | tf_op jit(solution)/shard_map/ppermute | solution.py:367
  80.2 7.3 %collective-permute-done.18.refs_2_ = bf16[5,320,128]{2,1,0:T(8,128)(2,1)S(1)} collective-permute-done((bf16[5,320,128]{2,1,0:T(8,128)(2,1)S(1)}, bf16[5,320,128]{2,1,0:T(8,128)(2,1)S(1)}, u32[]{:S(2)}, u32[]{:S(2)}) %collective-permute-start.18) | collective-permute-done | bytes 409632 | tf_op jit(solution)/shard_map/ppermute | solution.py:367
  90.6 2.9 %shard_map.107 = (bf16[2,96,320]{2,1,0:T(8,128)(2,1)S(1)}, bf16[2,96,320]{2,1,0:T(8,128)(2,1)S(1)}, bf16[2,96,320]{2,1,0:T(8,128)(2,1)S(1)}, bf16[2,96,320]{2,1,0:T(8,128)(2,1)S(1)}) custom-call(s32[5]{0:T(128)S(1)} %stack.23.refs_0_, bf16[5,320,128]{2,1,0:T(8,128)(2,1)S(1)} %get-tuple-element.51.refs_1_, ...), custom_call_target="tpu_custom_call" | custom-call | bytes 2580500 | tf_op jit(solution)/shard_map/pallas_call | solution.py:64
  94.1 2.8 %collective-permute-start.21 = (bf16[5,160,128]{2,1,0:T(8,128)(2,1)S(1)}, bf16[5,160,128]{2,1,0:T(8,128)(2,1)S(1)}, u32[]{:S(2)}, u32[]{:S(2)}) collective-permute-start(bf16[5,160,128]{2,1,0:T(8,128)(2,1)S(1)} %get-tuple-element.53.refs_5_.refs_1_), channel_id=1, source_target_pairs={{0,16},{4,20},{8,24},{12,28},{16,0},{20,4},{24,8},{28,12},{32,48},... | collective-permute-start | bytes 614408 | tf_op jit(solution)/shard_map/ppermute | solution.py:367
  98.7 4.1 %collective-permute-done.21.refs_2_ = bf16[5,160,128]{2,1,0:T(8,128)(2,1)S(1)} collective-permute-done((bf16[5,160,128]{2,1,0:T(8,128)(2,1)S(1)}, bf16[5,160,128]{2,1,0:T(8,128)(2,1)S(1)}, u32[]{:S(2)}, u32[]{:S(2)}) %collective-permute-start.21) | collective-permute-done | bytes 204832 | tf_op jit(solution)/shard_map/ppermute | solution.py:367
  104.6 7.2 %all-to-all-start.2 = ((bf16[4,2,64,640]{3,2,1,0:T(8,128)(2,1)}), bf16[4,2,64,640]{3,2,1,0:T(8,128)(2,1)}, u32[]{:S(2)}, u32[]{:S(2)}) async-start(bf16[4,2,64,640]{3,2,1,0:T(8,128)(2,1)} %shard_map.111), calls=%async_computation.2 | async-start | bytes 1310720 | tf_op jit(solution)/shard_map/all_to_all | solution.py:457
  111.8 4.7 %collective-permute-start.27 = (bf16[2,96,320]{2,1,0:T(8,128)(2,1)S(1)}, bf16[2,96,320]{2,1,0:T(8,128)(2,1)S(1)}, u32[]{:S(2)}, u32[]{:S(2)}) collective-permute-start(bf16[2,96,320]{2,1,0:T(8,128)(2,1)S(1)} %get-tuple-element.63), channel_id=1, source_target_pairs={{0,32},{4,36},{8,40},{12,44},{16,48},{20,52},{24,56},{28,60},{32,6... | collective-permute-start | bytes 368648 | tf_op jit(solution)/shard_map/ppermute | solution.py:437
  116.5 12.3 %collective-permute-start.28 = (bf16[2,96,320]{2,1,0:T(8,128)(2,1)S(1)}, bf16[2,96,320]{2,1,0:T(8,128)(2,1)S(1)}, u32[]{:S(2)}, u32[]{:S(2)}) collective-permute-start(bf16[2,96,320]{2,1,0:T(8,128)(2,1)S(1)} %get-tuple-element.64), channel_id=1, source_target_pairs={{0,64},{4,68},{8,72},{12,76},{16,80},{20,84},{24,88},{28,92},{32,9... | collective-permute-start | bytes 368648 | tf_op jit(solution)/shard_map/ppermute | solution.py:437
  130.0 2.2 %shard_map.112 = (bf16[2,96,160]{2,1,0:T(8,128)(2,1)S(1)}, bf16[2,96,160]{2,1,0:T(8,128)(2,1)S(1)}, bf16[2,96,160]{2,1,0:T(8,128)(2,1)S(1)}, bf16[2,96,160]{2,1,0:T(8,128)(2,1)S(1)}) custom-call(s32[5]{0:T(128)S(1)} %stack.23.refs_0_, bf16[5,160,128]{2,1,0:T(8,128)(2,1)S(1)} %get-tuple-element.53.refs_5_.refs_1_, ...), custom_call_target="tpu_custom_call" | custom-call | bytes 2580500 | tf_op jit(solution)/shard_map/pallas_call | solution.py:64
  132.2 2.3 %collective-permute-start.23 = (bf16[2,96,160]{2,1,0:T(8,128)(2,1)S(1)}, bf16[2,96,160]{2,1,0:T(8,128)(2,1)S(1)}, u32[]{:S(2)}, u32[]{:S(2)}) collective-permute-start(bf16[2,96,160]{2,1,0:T(8,128)(2,1)S(1)} %get-tuple-element.58), channel_id=1, source_target_pairs={{0,32},{4,36},{8,40},{12,44},{16,48},{20,52},{24,56},{28,60},{32,6... | collective-permute-start | bytes 184328 | tf_op jit(solution)/shard_map/ppermute | solution.py:437
  134.5 2.8 %collective-permute-start.25 = (bf16[2,96,160]{2,1,0:T(8,128)(2,1)S(1)}, bf16[2,96,160]{2,1,0:T(8,128)(2,1)S(1)}, u32[]{:S(2)}, u32[]{:S(2)}) collective-permute-start(bf16[2,96,160]{2,1,0:T(8,128)(2,1)S(1)} %get-tuple-element.60), channel_id=1, source_target_pairs={{0,96},{4,100},{8,104},{12,108},{16,112},{20,116},{24,120},{28,124... | collective-permute-start | bytes 184328 | tf_op jit(solution)/shard_map/ppermute | solution.py:437
  137.9 4.7 %collective-permute-start.30 = (bf16[96,320]{1,0:T(8,128)(2,1)S(1)}, bf16[96,320]{1,0:T(8,128)(2,1)S(1)}, u32[]{:S(2)}, u32[]{:S(2)}) collective-permute-start(bf16[96,320]{1,0:T(8,128)(2,1)S(1)} %get-tuple-element.67), channel_id=1, source_target_pairs={{0,128},{4,132},{8,136},{12,140},{16,144},{20,148},{24,152},{28,15... | collective-permute-start | bytes 184328 | tf_op jit(solution)/shard_map/ppermute | solution.py:367
  143.2 2.6 %collective-permute-start.26 = (bf16[96,160]{1,0:T(8,128)(2,1)S(1)}, bf16[96,160]{1,0:T(8,128)(2,1)S(1)}, u32[]{:S(2)}, u32[]{:S(2)}) collective-permute-start(bf16[96,160]{1,0:T(8,128)(2,1)S(1)} %get-tuple-element.62), channel_id=1, source_target_pairs={{0,128},{4,132},{8,136},{12,140},{16,144},{20,148},{24,152},{28,15... | collective-permute-start | bytes 92168 | tf_op jit(solution)/shard_map/ppermute | solution.py:367
  149.1 2.7 %collective-permute-done.26.refs_1_ = bf16[96,160]{1,0:T(8,128)(2,1)S(1)} collective-permute-done((bf16[96,160]{1,0:T(8,128)(2,1)S(1)}, bf16[96,160]{1,0:T(8,128)(2,1)S(1)}, u32[]{:S(2)}, u32[]{:S(2)}) %collective-permute-start.26) | collective-permute-done | bytes 30752 | tf_op jit(solution)/shard_map/ppermute | solution.py:367
  (84 shorter events, 28.5 us)
Async XLA Ops:
  0.6 11.1 %collective-permute-start.1 = (bf16[2,64,640]{2,1,0:T(8,128)(2,1)}, bf16[2,64,640]{2,1,0:T(8,128)(2,1)S(1)}, u32[]{:S(2)}, u32[]{:S(2)}) collective-permute-start(bf16[2,64,640]{2,1,0:T(8,128)(2,1)} %refs_1_.3), channel_id=1, source_target_pairs={{0,2},{1,3},{2,0},{3,1},{4,6},{5,7},{6,4},{7,5},{8,10},{9,11},{10,... | collective-permute-start | bytes 491528 | tf_op jit(solution)/shard_map/ppermute | solution.py:364
  4.0 13.9 %collective-permute-start = (bf16[2,64,640]{2,1,0:T(8,128)(2,1)}, bf16[2,64,640]{2,1,0:T(8,128)(2,1)S(1)}, u32[]{:S(2)}, u32[]{:S(2)}) collective-permute-start(bf16[2,64,640]{2,1,0:T(8,128)(2,1)} %refs_1_.3), channel_id=1, source_target_pairs={{0,1},{1,2},{2,3},{3,0},{4,5},{5,6},{6,7},{7,4},{8,9},{9,10},{10,1... | collective-permute-start | bytes 491528 | tf_op jit(solution)/shard_map/ppermute | solution.py:364
  4.0 13.8 %collective-permute-start.2 = (bf16[2,64,640]{2,1,0:T(8,128)(2,1)}, bf16[2,64,640]{2,1,0:T(8,128)(2,1)S(1)}, u32[]{:S(2)}, u32[]{:S(2)}) collective-permute-start(bf16[2,64,640]{2,1,0:T(8,128)(2,1)} %refs_1_.3), channel_id=1, source_target_pairs={{0,3},{1,0},{2,1},{3,2},{4,7},{5,4},{6,5},{7,6},{8,11},{9,8},{10,9... | collective-permute-start | bytes 491528 | tf_op jit(solution)/shard_map/ppermute | solution.py:364
  22.2 1.3 collective-permute-start.3
  22.3 3.8 %collective-permute-start.4 = (bf16[160,128]{1,0:T(8,128)(2,1)S(1)}, bf16[160,128]{1,0:T(8,128)(2,1)S(1)}, u32[]{:S(2)}, u32[]{:S(2)}) collective-permute-start(bf16[160,128]{1,0:T(8,128)(2,1)S(1)} %get-tuple-element.38), channel_id=1, source_target_pairs={{4,8},{8,4},{12,16},{16,12},{20,24},{24,20},{28,32},{32,28},{36,40... | collective-permute-start | bytes 122888 | tf_op jit(solution)/shard_map/ppermute | solution.py:370
  26.1 11.1 %collective-permute-start.7 = (bf16[160,128]{1,0:T(8,128)(2,1)S(1)}, bf16[160,128]{1,0:T(8,128)(2,1)S(1)}, u32[]{:S(2)}, u32[]{:S(2)}) collective-permute-start(bf16[160,128]{1,0:T(8,128)(2,1)S(1)} %shard_map.95.refs_1_), channel_id=1, source_target_pairs={{0,3},{1,0},{2,1},{3,2},{4,7},{5,4},{6,5},{7,6},{8,11},{9,8},{10,9... | collective-permute-start | bytes 122888 | tf_op jit(solution)/shard_map/ppermute | solution.py:364
  26.2 11.0 %collective-permute-start.6 = (bf16[160,128]{1,0:T(8,128)(2,1)S(1)}, bf16[160,128]{1,0:T(8,128)(2,1)S(1)}, u32[]{:S(2)}, u32[]{:S(2)}) collective-permute-start(bf16[160,128]{1,0:T(8,128)(2,1)S(1)} %shard_map.95.refs_1_), channel_id=1, source_target_pairs={{0,2},{1,3},{2,0},{3,1},{4,6},{5,7},{6,4},{7,5},{8,10},{9,11},{10,... | collective-permute-start | bytes 122888 | tf_op jit(solution)/shard_map/ppermute | solution.py:364
  30.1 7.2 %collective-permute-start.5 = (bf16[160,128]{1,0:T(8,128)(2,1)S(1)}, bf16[160,128]{1,0:T(8,128)(2,1)S(1)}, u32[]{:S(2)}, u32[]{:S(2)}) collective-permute-start(bf16[160,128]{1,0:T(8,128)(2,1)S(1)} %shard_map.95.refs_1_), channel_id=1, source_target_pairs={{0,1},{1,2},{2,3},{3,0},{4,5},{5,6},{6,7},{7,4},{8,9},{9,10},{10,1... | collective-permute-start | bytes 122888 | tf_op jit(solution)/shard_map/ppermute | solution.py:364
  30.1 19.4 %all-to-all-start = ((bf16[8,80,512]{2,1,0:T(8,128)(2,1)}), bf16[8,80,512]{2,1,0:T(8,128)(2,1)S(1)}, u32[]{:S(2)}, u32[]{:S(2)}) async-start(bf16[8,80,512]{2,1,0:T(8,128)(2,1)} %shard_map.94.refs_3_), calls=%async_computation | async-start | bytes 1310720 | tf_op jit(solution)/shard_map/all_to_all | solution.py:387
  40.7 1.5 collective-permute-start.8
  41.3 14.1 %collective-permute-start.9 = (bf16[320,128]{1,0:T(8,128)(2,1)S(1)}, bf16[320,128]{1,0:T(8,128)(2,1)S(1)}, u32[]{:S(2)}, u32[]{:S(2)}) collective-permute-start(bf16[320,128]{1,0:T(8,128)(2,1)S(1)} %get-tuple-element.42), channel_id=1, source_target_pairs={{4,8},{8,4},{12,16},{16,12},{20,24},{24,20},{28,32},{32,28},{36,40... | collective-permute-start | bytes 245768 | tf_op jit(solution)/shard_map/ppermute | solution.py:370
  49.5 14.8 %all-to-all-start.1 = ((bf16[8,80,128]{2,1,0:T(8,128)(2,1)}), bf16[8,80,128]{2,1,0:T(8,128)(2,1)S(1)}, u32[]{:S(2)}, u32[]{:S(2)}) async-start(bf16[8,80,128]{2,1,0:T(8,128)(2,1)} %shard_map.98.refs_4_), calls=%async_computation.1 | async-start | bytes 327680 | tf_op jit(solution)/shard_map/all_to_all | solution.py:405
  56.5 4.0 %collective-permute-start.11 = (bf16[320,128]{1,0:T(8,128)(2,1)S(1)}, bf16[320,128]{1,0:T(8,128)(2,1)S(1)}, u32[]{:S(2)}, u32[]{:S(2)}) collective-permute-start(bf16[320,128]{1,0:T(8,128)(2,1)S(1)} %get-tuple-element.44.refs_2_.refs_0_), channel_id=1, source_target_pairs={{4,8},{8,4},{12,16},{16,12},{20,24},{24,20},{28,32},{32,28},{36,40... | collective-permute-start | bytes 245768 | tf_op jit(solution)/shard_map/ppermute | solution.py:370
  57.1 4.3 %collective-permute-start.10 = (bf16[320,128]{1,0:T(8,128)(2,1)S(1)}, bf16[320,128]{1,0:T(8,128)(2,1)S(1)}, u32[]{:S(2)}, u32[]{:S(2)}) collective-permute-start(bf16[320,128]{1,0:T(8,128)(2,1)S(1)} %get-tuple-element.44.refs_2_.refs_0_), channel_id=1, source_target_pairs={{0,4},{4,0},{8,12},{12,8},{16,20},{20,16},{24,28},{28,24},{32,36},... | collective-permute-start | bytes 245768 | tf_op jit(solution)/shard_map/ppermute | solution.py:367
  61.4 11.6 %collective-permute-start.17 = (bf16[3,320,128]{2,1,0:T(8,128)(2,1)S(1)}, bf16[3,320,128]{2,1,0:T(8,128)(2,1)S(1)}, u32[]{:S(2)}, u32[]{:S(2)}) collective-permute-start(bf16[3,320,128]{2,1,0:T(8,128)(2,1)S(1)} %shard_map.103.refs_1_), channel_id=1, source_target_pairs={{0,8},{4,12},{8,0},{12,4},{16,24},{20,28},{24,16},{28,20},{32,40},... | collective-permute-start | bytes 737288 | tf_op jit(solution)/shard_map/ppermute | solution.py:367
  68.3 4.7 %collective-permute-start.12 = (bf16[160,128]{1,0:T(8,128)(2,1)S(1)}, bf16[160,128]{1,0:T(8,128)(2,1)S(1)}, u32[]{:S(2)}, u32[]{:S(2)}) collective-permute-start(bf16[160,128]{1,0:T(8,128)(2,1)S(1)} %get-tuple-element.46), channel_id=1, source_target_pairs={{0,1},{1,2},{2,3},{3,0},{4,5},{5,6},{6,7},{7,4},{8,9},{9,10},{10,1... | collective-permute-start | bytes 122888 | tf_op jit(solution)/shard_map/ppermute | solution.py:364
  69.1 7.3 %collective-permute-start.13 = (bf16[160,128]{1,0:T(8,128)(2,1)S(1)}, bf16[160,128]{1,0:T(8,128)(2,1)S(1)}, u32[]{:S(2)}, u32[]{:S(2)}) collective-permute-start(bf16[160,128]{1,0:T(8,128)(2,1)S(1)} %get-tuple-element.47), channel_id=1, source_target_pairs={{0,2},{1,3},{2,0},{3,1},{4,6},{5,7},{6,4},{7,5},{8,10},{9,11},{10,... | collective-permute-start | bytes 122888 | tf_op jit(solution)/shard_map/ppermute | solution.py:364
  72.6 4.0 %collective-permute-start.14 = (bf16[160,128]{1,0:T(8,128)(2,1)S(1)}, bf16[160,128]{1,0:T(8,128)(2,1)S(1)}, u32[]{:S(2)}, u32[]{:S(2)}) collective-permute-start(bf16[160,128]{1,0:T(8,128)(2,1)S(1)} %get-tuple-element.48), channel_id=1, source_target_pairs={{0,3},{1,0},{2,1},{3,2},{4,7},{5,4},{6,5},{7,6},{8,11},{9,8},{10,9... | collective-permute-start | bytes 122888 | tf_op jit(solution)/shard_map/ppermute | solution.py:364
  73.6 13.8 %collective-permute-start.18 = (bf16[5,320,128]{2,1,0:T(8,128)(2,1)S(1)}, bf16[5,320,128]{2,1,0:T(8,128)(2,1)S(1)}, u32[]{:S(2)}, u32[]{:S(2)}) collective-permute-start(bf16[5,320,128]{2,1,0:T(8,128)(2,1)S(1)} %get-tuple-element.51.refs_1_), channel_id=1, source_target_pairs={{0,16},{4,20},{8,24},{12,28},{16,0},{20,4},{24,8},{28,12},{32,48},... | collective-permute-start | bytes 1228808 | tf_op jit(solution)/shard_map/ppermute | solution.py:367
  76.7 11.4 %collective-permute-start.16 = (bf16[160,128]{1,0:T(8,128)(2,1)S(1)}, bf16[160,128]{1,0:T(8,128)(2,1)S(1)}, u32[]{:S(2)}, u32[]{:S(2)}) collective-permute-start(bf16[160,128]{1,0:T(8,128)(2,1)S(1)} %shard_map.101.refs_0_.refs_2_), channel_id=1, source_target_pairs={{4,8},{8,4},{12,16},{16,12},{20,24},{24,20},{28,32},{32,28},{36,40... | collective-permute-start | bytes 122888 | tf_op jit(solution)/shard_map/ppermute | solution.py:370
  77.5 10.6 %collective-permute-start.15 = (bf16[160,128]{1,0:T(8,128)(2,1)S(1)}, bf16[160,128]{1,0:T(8,128)(2,1)S(1)}, u32[]{:S(2)}, u32[]{:S(2)}) collective-permute-start(bf16[160,128]{1,0:T(8,128)(2,1)S(1)} %shard_map.101.refs_0_.refs_2_), channel_id=1, source_target_pairs={{0,4},{4,0},{8,12},{12,8},{16,20},{20,16},{24,28},{28,24},{32,36},... | collective-permute-start | bytes 122888 | tf_op jit(solution)/shard_map/ppermute | solution.py:367
  88.1 5.5 %collective-permute-start.19 = (bf16[3,160,128]{2,1,0:T(8,128)(2,1)S(1)}, bf16[3,160,128]{2,1,0:T(8,128)(2,1)S(1)}, u32[]{:S(2)}, u32[]{:S(2)}) collective-permute-start(bf16[3,160,128]{2,1,0:T(8,128)(2,1)S(1)} %shard_map.106.refs_1_), channel_id=1, source_target_pairs={{0,8},{4,12},{8,0},{12,4},{16,24},{20,28},{24,16},{28,20},{32,40},... | collective-permute-start | bytes 368648 | tf_op jit(solution)/shard_map/ppermute | solution.py:367
  94.1 8.7 %collective-permute-start.21 = (bf16[5,160,128]{2,1,0:T(8,128)(2,1)S(1)}, bf16[5,160,128]{2,1,0:T(8,128)(2,1)S(1)}, u32[]{:S(2)}, u32[]{:S(2)}) collective-permute-start(bf16[5,160,128]{2,1,0:T(8,128)(2,1)S(1)} %get-tuple-element.53.refs_5_.refs_1_), channel_id=1, source_target_pairs={{0,16},{4,20},{8,24},{12,28},{16,0},{20,4},{24,8},{28,12},{32,48},... | collective-permute-start | bytes 614408 | tf_op jit(solution)/shard_map/ppermute | solution.py:367
  104.6 43.3 %all-to-all-start.2 = ((bf16[4,2,64,640]{3,2,1,0:T(8,128)(2,1)}), bf16[4,2,64,640]{3,2,1,0:T(8,128)(2,1)}, u32[]{:S(2)}, u32[]{:S(2)}) async-start(bf16[4,2,64,640]{3,2,1,0:T(8,128)(2,1)} %shard_map.111), calls=%async_computation.2 | async-start | bytes 1310720 | tf_op jit(solution)/shard_map/all_to_all | solution.py:457
  111.8 22.7 %collective-permute-start.27 = (bf16[2,96,320]{2,1,0:T(8,128)(2,1)S(1)}, bf16[2,96,320]{2,1,0:T(8,128)(2,1)S(1)}, u32[]{:S(2)}, u32[]{:S(2)}) collective-permute-start(bf16[2,96,320]{2,1,0:T(8,128)(2,1)S(1)} %get-tuple-element.63), channel_id=1, source_target_pairs={{0,32},{4,36},{8,40},{12,44},{16,48},{20,52},{24,56},{28,60},{32,6... | collective-permute-start | bytes 368648 | tf_op jit(solution)/shard_map/ppermute | solution.py:437
  116.5 20.8 %collective-permute-start.28 = (bf16[2,96,320]{2,1,0:T(8,128)(2,1)S(1)}, bf16[2,96,320]{2,1,0:T(8,128)(2,1)S(1)}, u32[]{:S(2)}, u32[]{:S(2)}) collective-permute-start(bf16[2,96,320]{2,1,0:T(8,128)(2,1)S(1)} %get-tuple-element.64), channel_id=1, source_target_pairs={{0,64},{4,68},{8,72},{12,76},{16,80},{20,84},{24,88},{28,92},{32,9... | collective-permute-start | bytes 368648 | tf_op jit(solution)/shard_map/ppermute | solution.py:437
  128.7 8.5 %collective-permute-start.29 = (bf16[2,96,320]{2,1,0:T(8,128)(2,1)S(1)}, bf16[2,96,320]{2,1,0:T(8,128)(2,1)S(1)}, u32[]{:S(2)}, u32[]{:S(2)}) collective-permute-start(bf16[2,96,320]{2,1,0:T(8,128)(2,1)S(1)} %get-tuple-element.65), channel_id=1, source_target_pairs={{0,96},{4,100},{8,104},{12,108},{16,112},{20,116},{24,120},{28,124... | collective-permute-start | bytes 368648 | tf_op jit(solution)/shard_map/ppermute | solution.py:437
  132.2 10.4 %collective-permute-start.23 = (bf16[2,96,160]{2,1,0:T(8,128)(2,1)S(1)}, bf16[2,96,160]{2,1,0:T(8,128)(2,1)S(1)}, u32[]{:S(2)}, u32[]{:S(2)}) collective-permute-start(bf16[2,96,160]{2,1,0:T(8,128)(2,1)S(1)} %get-tuple-element.58), channel_id=1, source_target_pairs={{0,32},{4,36},{8,40},{12,44},{16,48},{20,52},{24,56},{28,60},{32,6... | collective-permute-start | bytes 184328 | tf_op jit(solution)/shard_map/ppermute | solution.py:437
  134.5 8.1 %collective-permute-start.24 = (bf16[2,96,160]{2,1,0:T(8,128)(2,1)S(1)}, bf16[2,96,160]{2,1,0:T(8,128)(2,1)S(1)}, u32[]{:S(2)}, u32[]{:S(2)}) collective-permute-start(bf16[2,96,160]{2,1,0:T(8,128)(2,1)S(1)} %get-tuple-element.59), channel_id=1, source_target_pairs={{0,64},{4,68},{8,72},{12,76},{16,80},{20,84},{24,88},{28,92},{32,9... | collective-permute-start | bytes 184328 | tf_op jit(solution)/shard_map/ppermute | solution.py:437
  134.5 8.1 %collective-permute-start.25 = (bf16[2,96,160]{2,1,0:T(8,128)(2,1)S(1)}, bf16[2,96,160]{2,1,0:T(8,128)(2,1)S(1)}, u32[]{:S(2)}, u32[]{:S(2)}) collective-permute-start(bf16[2,96,160]{2,1,0:T(8,128)(2,1)S(1)} %get-tuple-element.60), channel_id=1, source_target_pairs={{0,96},{4,100},{8,104},{12,108},{16,112},{20,116},{24,120},{28,124... | collective-permute-start | bytes 184328 | tf_op jit(solution)/shard_map/ppermute | solution.py:437
  137.9 9.2 %collective-permute-start.30 = (bf16[96,320]{1,0:T(8,128)(2,1)S(1)}, bf16[96,320]{1,0:T(8,128)(2,1)S(1)}, u32[]{:S(2)}, u32[]{:S(2)}) collective-permute-start(bf16[96,320]{1,0:T(8,128)(2,1)S(1)} %get-tuple-element.67), channel_id=1, source_target_pairs={{0,128},{4,132},{8,136},{12,140},{16,144},{20,148},{24,152},{28,15... | collective-permute-start | bytes 184328 | tf_op jit(solution)/shard_map/ppermute | solution.py:367
  143.2 8.6 %collective-permute-start.26 = (bf16[96,160]{1,0:T(8,128)(2,1)S(1)}, bf16[96,160]{1,0:T(8,128)(2,1)S(1)}, u32[]{:S(2)}, u32[]{:S(2)}) collective-permute-start(bf16[96,160]{1,0:T(8,128)(2,1)S(1)} %get-tuple-element.62), channel_id=1, source_target_pairs={{0,128},{4,132},{8,136},{12,140},{16,144},{20,148},{24,152},{28,15... | collective-permute-start | bytes 92168 | tf_op jit(solution)/shard_map/ppermute | solution.py:367
  (12 other events, 41.4 us)

commit v9 on v8

--- a/solution.py
+++ b/solution.py
@@ -56,7 +56,7 @@
     vmem = pl.BlockSpec(memory_space=pltpu.VMEM)
     aside = pl.BlockSpec(memory_space=pl.ANY)
     count = len(args)
-    flops = CHAIN if body in (fine_forward, pool_add, deep_sides, deep_forward, deep_backward, pool_sum, fine_backward) else 0
+    flops = CHAIN if body in (fine_forward, pool_add, deep_forward, deep_backward, pool_sum, fine_backward) else 0
 
     def kernel(*refs):
         body(*refs[:count], *refs[count + len(behind) :])
@@ -87,6 +87,10 @@
     place = lax.broadcasted_iota(jnp.int32, (cols, cols), 0)
     source = place // 2 + (place % 2) * (cols // 2)
     return jnp.where(source == lax.broadcasted_iota(jnp.int32, (cols, cols), 1), 1.0, 0.0).astype(BF)
+
+
+def warm(x, w, out):
+    out[...] = w[0, :16, :128] + x[0, :16, :128]
 
 
 def fine_rows(x):
@@ -375,6 +379,7 @@
         fine_forward,
         [shape((pieces,) + latent.shape), shape((fine, deep), F32), shape((fine, deep)), shape((fine, deep))],
         (at, latent, *got, w_fine),
+        behind=(call(warm, shape((16, 128)), (latent, w_fine)),),
     )
     partner, other = pairs(partner, other)
     fine_slab = call(
@@ -392,7 +397,6 @@
         (at, mine, *got, w_deep),
     )
     partner, other = pairs(partner, other)
-    deep_slab = call(deep_slices, shape((MEMBERS, size, deep)), (pooled, pick), behind=(partner,))
     preact = call(
         deep_own, shape((full, deep), F32), (pooled, w_deep), behind=(fine_slab,)
     )
@@ -400,26 +404,41 @@
         deep_forward,
         [shape((full, deep))] * 2,
         (preact, partner, other, upstream[0].T),
-        behind=(deep_slab,),
-    )
+    )
+    pre_partner, other = pairs(grad_pre, grad_pre)
+    deep_slab = call(deep_slices, shape((MEMBERS, size, deep)), (pooled, pick), behind=(pre_partner,))
     deep_slab = lax.all_to_all(deep_slab, "wide", 0, 0, axis_index_groups=near)
-    pre_partner, other = pairs(grad_pre, grad_pre)
     pre_first = call(pack, shape((3, full, deep)), (grad_pre, pre_partner, other))
     parts = call(
         deep_backward,
         [shape((fine, deep))] * 4,
         (at, pre_partner, grad_pre, other, w_deep),
         [pltpu.VMEM((2, full, deep), BF), pltpu.VMEM((depth, deep), BF)],
-        behind=(deep_slab,),
     )
     got = [across(parts[s], s) for s in (1, 2, 3)]
     even_table, late_table, deep_table = call(
         tables, [shape((3 * size, MEMBERS * deep))] * 3, (fine_slab, deep_slab)
     )
-    grad_pool = call(pool_sum, shape((fine, deep)), (parts[0], *got))
+    grad_pool = call(pool_sum, shape((fine, deep)), (parts[0], *got), behind=(deep_slab,))
     pool_partner, other = pairs(grad_pool, grad_pool)
     pre_rows = group_gather(pre_first, (got[0],))
     pool_first = call(pack, shape((3, fine, deep)), (grad_pool, pool_partner, other), behind=(deep_table, pre_rows[2]))
+
+    def halves(parts):
+        width = parts[0].shape[2]
+        got = [
+            lax.ppermute(
+                parts[s], "wide", [(i, i // 32 * 32 + (i // 8 + s) % 4 * 8 + i % 8) for i in range(wide)]
+            )
+            for s in (1, 2, 3)
+        ]
+        return call(weight_half, [shape((block, width), F32), shape((block, width))], (at, parts[0], *got))
+
+    def owners(half, behind=()):
+        keep, send = half
+        width = keep.shape[1]
+        total = call(weight_sum, shape((9, grain, width), F32), (keep, swap(send, 32)), behind=behind)
+        return total.reshape(3, 3, grain, width)
 
     def products(body, tables, rows, behind=()):
         width = rows[0].shape[1]
@@ -431,34 +450,23 @@
             behind=behind,
         )
 
-    def owners(parts, behind=()):
-        width = parts[0].shape[2]
-        got = [
-            lax.ppermute(
-                parts[s], "wide", [(i, i // 32 * 32 + (i // 8 + s) % 4 * 8 + i % 8) for i in range(wide)]
-            )
-            for s in (1, 2, 3)
-        ]
-        keep, send = call(weight_half, [shape((block, width), F32), shape((block, width))], (at, parts[0], *got))
-        total = call(weight_sum, shape((9, grain, width), F32), (keep, swap(send, 32)), behind=behind)
-        return total.reshape(3, 3, grain, width)
-
-    deep_parts = products(deep_part, (deep_table,), pre_rows)
-    pool_rows = group_gather(pool_first, (deep_parts[0],))
     sides = call(
         fine_backward,
         shape((rows, cols, depth)),
         (at, pool_partner, grad_pool, other, w_fine),
         [pltpu.VMEM((2, fine, deep), BF)],
-        behind=(pool_rows[0],),
-    )
+        behind=(pool_first,),
+    )
+    pool_rows = group_gather(pool_first, (sides,))
+    deep_parts = products(deep_part, (deep_table,), pre_rows, (pool_rows[0],))
     fine_parts = products(fine_part, (even_table, late_table), pool_rows)
-    back = call(weave, shape((pieces, rows, part, depth)), (sides,), behind=(pool_rows[2],))
+    deep_half = halves(deep_parts)
+    back = call(weave, shape((pieces, rows, part, depth)), (sides,), behind=(pool_rows[2], deep_half[0]))
     partial = lax.all_to_all(back, "narrow", 0, 0)
     grad_latent = jnp.sum(partial.astype(F32), axis=0).astype(BF)
 
-    grad_deep = owners(deep_parts)
-    grad_fine = owners(fine_parts, (grad_latent, grad_deep))
+    grad_deep = owners(deep_half)
+    grad_fine = owners(halves(fine_parts), (grad_latent, grad_deep))
     return output.T[None], grad_latent, grad_fine, grad_deep
 
 

time: 154 us -> 166 us (1.078)
  local copies, waits for them, and re-layouts: 10.5 us -> 24.8 us
  waiting for transfers between devices: 37.9 us -> 29.4 us
  starting transfers between devices: 79.5 us -> 83.8 us
  Pallas kernels: 22.6 us -> 24.8 us
    unnamed x22 -> x76, local copies, waits for them, and re-layouts: 10.4 us -> 24.7 us
    ppermute x12, waiting for transfers between devices: 19.7 us -> 8.69 us  [swap(): return lax.ppermute(v, 'wide', [(i, i ^ bit) for i in range(wide)])]
    ppermute x6, waiting for transfers between devices: 0.02 us -> 8.84 us  [halves(): lax.ppermute(parts[s], 'wide', [(i, i // 32 * 32 + (i // 8 + s) % 4 * 8 +...]
    all_to_all x1, waiting for transfers between devices: 6.16 us -> 0.45 us  [on_device(): fine_slab = lax.all_to_all(fine_slab, 'wide', 0, 0, axis_index_groups=near)]
    all_to_all x1, starting transfers between devices: 3.38 us -> 8.04 us  [on_device(): deep_slab = lax.all_to_all(deep_slab, 'wide', 0, 0, axis_index_groups=near)]
    pallas_call x24 -> x25, Pallas kernels: 22.6 us -> 24.8 us  [call(): pl.pallas_call(kernel, out_shape=outs, in_specs=[smem if a.dtype == jnp.i...]
    ppermute x12, starting transfers between devices: 22.9 us -> 21.2 us  [swap(): return lax.ppermute(v, 'wide', [(i, i ^ bit) for i in range(wide)])]
  transfers between devices with their start and end apart: 34 -> 34, of which waited for: 13 -> 16; matrix products, arithmetic and copies ran while one was open for 1% -> 1% of each run, Pallas kernels for 12% -> 12%
where the time goes in v9:
time: 166 us; the launch traced here: 165 us
  starting transfers between devices  83.8 us (50%)
  waiting for transfers between devices  29.4 us (18%)
  local copies, waits for them, and re-layouts  24.8 us (15%)
  Pallas kernels  24.8 us (15%)
    pallas_call x25, Pallas kernels, call(): pl.pallas_call(kernel, out_shape=outs, in_specs=[smem if a.dtype == jnp.i...  24.8 us
    unnamed x76, local copies, waits for them, and re-layouts  24.7 us
    ppermute x6, starting transfers between devices, halves(): lax.ppermute(parts[s], 'wide', [(i, i // 32 * 32 + (i // 8 + s) % 4 * 8 +...  21.8 us
    ppermute x12, starting transfers between devices, swap(): return lax.ppermute(v, 'wide', [(i, i ^ bit) for i in range(wide)])  21.2 us
    ppermute x9, starting transfers between devices, across(): lax.ppermute(v, 'narrow', [(i, (i + step) % pieces) for i in range(pieces)])  15.1 us
    ppermute x9, waiting for transfers between devices, across(): lax.ppermute(v, 'narrow', [(i, (i + step) % pieces) for i in range(pieces)])  11.4 us
    ppermute x6, waiting for transfers between devices, halves(): lax.ppermute(parts[s], 'wide', [(i, i // 32 * 32 + (i // 8 + s) % 4 * 8 +...  8.84 us
    ppermute x12, waiting for transfers between devices, swap(): return lax.ppermute(v, 'wide', [(i, i ^ bit) for i in range(wide)])  8.69 us
  transfers between devices with their start and end apart: 34, of which 16 were waited for; matrix products, arithmetic and copies ran while one was open for 1% of the time, Pallas kernels for 12%

profile of v9, /device:TPU:32, one launch (start us, length us, event | category | flops | bytes accessed | tf_op | source)
XLA Modules:
  0.0 165.0 jit_solution(17349275874425751077)
XLA Ops:
  0.6 1.9 %collective-permute-start.2 = (bf16[2,64,640]{2,1,0:T(8,128)(2,1)}, bf16[2,64,640]{2,1,0:T(8,128)(2,1)S(1)}, u32[]{:S(2)}, u32[]{:S(2)}) collective-permute-start(bf16[2,64,640]{2,1,0:T(8,128)(2,1)} %refs_1_.3), channel_id=1, source_target_pairs={{0,3},{1,0},{2,1},{3,2},{4,7},{5,4},{6,5},{7,6},{8,11},{9,8},{10,9... | collective-permute-start | bytes 491528 | tf_op jit(solution)/shard_map/ppermute | solution.py:368
  4.1 2.8 %collective-permute-start = (bf16[2,64,640]{2,1,0:T(8,128)(2,1)}, bf16[2,64,640]{2,1,0:T(8,128)(2,1)S(1)}, u32[]{:S(2)}, u32[]{:S(2)}) collective-permute-start(bf16[2,64,640]{2,1,0:T(8,128)(2,1)} %refs_1_.3), channel_id=1, source_target_pairs={{0,1},{1,2},{2,3},{3,0},{4,5},{5,6},{6,7},{7,4},{8,9},{9,10},{10,1... | collective-permute-start | bytes 491528 | tf_op jit(solution)/shard_map/ppermute | solution.py:368
  10.1 5.7 %collective-permute-done.1.refs_3_ = bf16[2,64,640]{2,1,0:T(8,128)(2,1)S(1)} collective-permute-done((bf16[2,64,640]{2,1,0:T(8,128)(2,1)}, bf16[2,64,640]{2,1,0:T(8,128)(2,1)S(1)}, u32[]{:S(2)}, u32[]{:S(2)}) %collective-permute-start.1) | collective-permute-done | bytes 163872 | tf_op jit(solution)/shard_map/ppermute | solution.py:368
  16.5 1.9 %collective-permute-done.refs_2_ = bf16[2,64,640]{2,1,0:T(8,128)(2,1)S(1)} collective-permute-done((bf16[2,64,640]{2,1,0:T(8,128)(2,1)}, bf16[2,64,640]{2,1,0:T(8,128)(2,1)S(1)}, u32[]{:S(2)}, u32[]{:S(2)}) %collective-permute-start) | collective-permute-done | bytes 163872 | tf_op jit(solution)/shard_map/ppermute | solution.py:368
  21.8 1.9 %shard_map.94 = (bf16[4,2,64,640]{3,2,1,0:T(8,128)(2,1)S(1)}, f32[160,128]{1,0:T(8,128)S(1)}, bf16[160,128]{1,0:T(8,128)(2,1)S(1)}, bf16[160,128]{1,0:T(8,128)(2,1)S(1)}) custom-call(s32[5]{0:T(128)S(1)} %stack.23.refs_0_, bf16[2,64,640]{2,1,0:T(8,128)(2,1)S(1)} %copy-done.19, bf16[2,64,640]{2,1,0:T(8,128)(2,1)S(1)} %copy-done.27, ...), custom_call_target="tpu_custom_call" | custom-call | flops 30000001024 | bytes 2498580 | tf_op jit(solution)/shard_map/pallas_call | solution.py:64
  25.6 2.6 %shard_map.95.refs_3_ = bf16[8,80,512]{2,1,0:T(8,128)(2,1)} custom-call(bf16[4,2,64,640]{3,2,1,0:T(8,128)(2,1)S(1)} %get-tuple-element.39.refs_0_, bf16[640,640]{1,0:T(8,128)(2,1)S(1)} %copy-done.4, bf16[160,128]{1,0:T(8,128)(2,1)S(1)} %collective-permute-done.3.refs_2_.refs_1_), custom_call_target="tpu_custom_call" | custom-call | bytes 1474560 | tf_op jit(solution)/shard_map/pallas_call | solution.py:64
  28.3 6.1 %all-to-all-start = ((bf16[8,80,512]{2,1,0:T(8,128)(2,1)}), bf16[8,80,512]{2,1,0:T(8,128)(2,1)S(1)}, u32[]{:S(2)}, u32[]{:S(2)}) async-start(bf16[8,80,512]{2,1,0:T(8,128)(2,1)} %shard_map.95.refs_3_), calls=%async_computation | async-start | bytes 1310720 | tf_op jit(solution)/shard_map/all_to_all | solution.py:392
  35.9 2.4 %collective-permute-start.6 = (bf16[160,128]{1,0:T(8,128)(2,1)S(1)}, bf16[160,128]{1,0:T(8,128)(2,1)S(1)}, u32[]{:S(2)}, u32[]{:S(2)}) collective-permute-start(bf16[160,128]{1,0:T(8,128)(2,1)S(1)} %shard_map.96.refs_1_), channel_id=1, source_target_pairs={{0,2},{1,3},{2,0},{3,1},{4,6},{5,7},{6,4},{7,5},{8,10},{9,11},{10,... | collective-permute-start | bytes 122888 | tf_op jit(solution)/shard_map/ppermute | solution.py:368
  42.3 2.0 %shard_map.97 = (bf16[640,128]{1,0:T(8,128)(2,1)S(1)}, bf16[320,128]{1,0:T(8,128)(2,1)}, bf16[320,128]{1,0:T(8,128)(2,1)}) custom-call(s32[5]{0:T(128)S(1)} %stack.23.refs_0_, bf16[160,128]{1,0:T(8,128)(2,1)S(1)} %shard_map.96.refs_1_, bf16[160,128]{1,0:T(8,128)(2,1)S(1)} %collective-permute-done.5.refs_2_, ...), custom_call_target="tpu_custom_call" | custom-call | bytes 3850260 | tf_op jit(solution)/shard_map/pallas_call | solution.py:64
  46.1 2.0 %copy-done.1 = bf16[3,3,640,320]{2,3,1,0:T(8,128)(2,1)S(1)} copy-done((bf16[3,3,640,320]{2,3,1,0:T(8,128)(2,1)S(1)}, bf16[3,3,640,320]{2,3,1,0:T(8,128)(2,1)}, u32[]{:S(2)}) %copy-start.1) | copy-done | bytes 3686424
  50.7 2.3 %collective-permute-start.10 = (bf16[320,128]{1,0:T(8,128)(2,1)}, bf16[320,128]{1,0:T(8,128)(2,1)S(1)}, u32[]{:S(2)}, u32[]{:S(2)}) collective-permute-start(bf16[320,128]{1,0:T(8,128)(2,1)} %get-tuple-element.44.refs_2_.refs_0_), channel_id=1, source_target_pairs={{0,4},{4,0},{8,12},{12,8},{16,20},{20,16},{24,28},{28,24},{32,36},... | collective-permute-start | bytes 245768 | tf_op jit(solution)/shard_map/ppermute | solution.py:371
  56.0 8.0 %all-to-all-start.1 = ((bf16[8,80,128]{2,1,0:T(8,128)(2,1)}), bf16[8,80,128]{2,1,0:T(8,128)(2,1)S(1)}, u32[]{:S(2)}, u32[]{:S(2)}) async-start(bf16[8,80,128]{2,1,0:T(8,128)(2,1)} %copy-done.9), calls=%async_computation.1 | async-start | bytes 327680 | tf_op jit(solution)/shard_map/all_to_all | solution.py:410
  65.9 2.1 %collective-permute-start.17 = (bf16[3,320,128]{2,1,0:T(8,128)(2,1)S(1)}, bf16[3,320,128]{2,1,0:T(8,128)(2,1)S(1)}, u32[]{:S(2)}, u32[]{:S(2)}) collective-permute-start(bf16[3,320,128]{2,1,0:T(8,128)(2,1)S(1)} %shard_map.104.refs_1_), channel_id=1, source_target_pairs={{0,8},{4,12},{8,0},{12,4},{16,24},{20,28},{24,16},{28,20},{32,40},... | collective-permute-start | bytes 737288 | tf_op jit(solution)/shard_map/ppermute | solution.py:371
  68.0 2.0 %copy-done.2 = bf16[3,3,640,320]{2,3,1,0:T(8,128)(2,1)S(1)} copy-done((bf16[3,3,640,320]{2,3,1,0:T(8,128)(2,1)S(1)}, bf16[3,3,640,320]{2,3,1,0:T(8,128)(2,1)}, u32[]{:S(2)}) %copy-start.2) | copy-done | bytes 3686424
  70.9 2.3 %shard_map.100 = (bf16[160,128]{1,0:T(8,128)(2,1)S(1)}, bf16[160,128]{1,0:T(8,128)(2,1)S(1)}, bf16[160,128]{1,0:T(8,128)(2,1)S(1)}, bf16[160,128]{1,0:T(8,128)(2,1)S(1)}) custom-call(s32[5]{0:T(128)S(1)} %stack.23.refs_0_, bf16[320,128]{1,0:T(8,128)(2,1)S(1)} %copy-done.17, bf16[320,128]{1,0:T(8,128)(2,1)} %get-tuple-element.44.refs_2_.refs_0_, ...), custom_call_target="tpu_custom_call" | custom-call | flops 30000001024 | bytes 3932180 | tf_op jit(solution)/shard_map/pallas_call | solution.py:64
  74.6 3.1 %collective-permute-start.13 = (bf16[160,128]{1,0:T(8,128)(2,1)S(1)}, bf16[160,128]{1,0:T(8,128)(2,1)S(1)}, u32[]{:S(2)}, u32[]{:S(2)}) collective-permute-start(bf16[160,128]{1,0:T(8,128)(2,1)S(1)} %get-tuple-element.47), channel_id=1, source_target_pairs={{0,2},{1,3},{2,0},{3,1},{4,6},{5,7},{6,4},{7,5},{8,10},{9,11},{10,... | collective-permute-start | bytes 122888 | tf_op jit(solution)/shard_map/ppermute | solution.py:368
  79.2 2.7 %collective-permute-start.18 = (bf16[5,320,128]{2,1,0:T(8,128)(2,1)S(1)}, bf16[5,320,128]{2,1,0:T(8,128)(2,1)S(1)}, u32[]{:S(2)}, u32[]{:S(2)}) collective-permute-start(bf16[5,320,128]{2,1,0:T(8,128)(2,1)S(1)} %get-tuple-element.51.refs_1_), channel_id=1, source_target_pairs={{0,16},{4,20},{8,24},{12,28},{16,0},{20,4},{24,8},{28,12},{32,48},... | collective-permute-start | bytes 1228808 | tf_op jit(solution)/shard_map/ppermute | solution.py:371
  86.1 1.7 %collective-permute-start.15 = (bf16[160,128]{1,0:T(8,128)(2,1)S(1)}, bf16[160,128]{1,0:T(8,128)(2,1)S(1)}, u32[]{:S(2)}, u32[]{:S(2)}) collective-permute-start(bf16[160,128]{1,0:T(8,128)(2,1)S(1)} %shard_map.102.refs_0_.refs_2_), channel_id=1, source_target_pairs={{0,4},{4,0},{8,12},{12,8},{16,20},{20,16},{24,28},{28,24},{32,36},... | collective-permute-start | bytes 122888 | tf_op jit(solution)/shard_map/ppermute | solution.py:371
  92.7 1.8 %shard_map.108.refs_3_.refs_0_ = bf16[2,256,640]{2,1,0:T(8,128)(2,1)S(1)} custom-call(s32[5]{0:T(128)S(1)} %stack.23.refs_0_, bf16[160,128]{1,0:T(8,128)(2,1)S(1)} %collective-permute-done.15.refs_1_, bf16[160,128]{1,0:T(8,128)(2,1)S(1)} %shard_map.102.refs_0_.refs_2_, bf16[160,128]{1,0:T(8,128)(2,1)S(1)} %collective-permute-done.16.refs_2_.refs_3_, ...), custom_call_target="tpu_custom_call" | custom-call | flops 30000001024 | bytes 1966100 | tf_op jit(solution)/shard_map/pallas_call | solution.py:64
  94.5 3.3 %collective-permute-done.19.refs_2_ = bf16[3,160,128]{2,1,0:T(8,128)(2,1)S(1)} collective-permute-done((bf16[3,160,128]{2,1,0:T(8,128)(2,1)S(1)}, bf16[3,160,128]{2,1,0:T(8,128)(2,1)S(1)}, u32[]{:S(2)}, u32[]{:S(2)}) %collective-permute-start.19) | collective-permute-done | bytes 122912 | tf_op jit(solution)/shard_map/ppermute | solution.py:371
  98.3 3.5 %collective-permute-start.20 = (bf16[5,160,128]{2,1,0:T(8,128)(2,1)S(1)}, bf16[5,160,128]{2,1,0:T(8,128)(2,1)S(1)}, u32[]{:S(2)}, u32[]{:S(2)}) collective-permute-start(bf16[5,160,128]{2,1,0:T(8,128)(2,1)S(1)} %get-tuple-element.53.refs_7_.refs_1_), channel_id=1, source_target_pairs={{0,16},{4,20},{8,24},{12,28},{16,0},{20,4},{24,8},{28,12},{32,48},... | collective-permute-start | bytes 614408 | tf_op jit(solution)/shard_map/ppermute | solution.py:371
  101.9 2.9 %shard_map.111 = (bf16[2,96,320]{2,1,0:T(8,128)(2,1)S(1)}, bf16[2,96,320]{2,1,0:T(8,128)(2,1)S(1)}, bf16[2,96,320]{2,1,0:T(8,128)(2,1)S(1)}, bf16[2,96,320]{2,1,0:T(8,128)(2,1)S(1)}) custom-call(s32[5]{0:T(128)S(1)} %stack.23.refs_0_, bf16[5,320,128]{2,1,0:T(8,128)(2,1)S(1)} %get-tuple-element.51.refs_1_, bf16[5,320,128]{2,1,0:T(8,128)(2,1)S(1)} %copy-done.8, ...), custom_call_target="tpu_custom_call" | custom-call | bytes 2580500 | tf_op jit(solution)/shard_map/pallas_call | solution.py:64
  104.8 2.6 %collective-permute-start.22 = (bf16[2,96,320]{2,1,0:T(8,128)(2,1)S(1)}, bf16[2,96,320]{2,1,0:T(8,128)(2,1)S(1)}, u32[]{:S(2)}, u32[]{:S(2)}) collective-permute-start(bf16[2,96,320]{2,1,0:T(8,128)(2,1)S(1)} %get-tuple-element.55), channel_id=1, source_target_pairs={{0,32},{4,36},{8,40},{12,44},{16,48},{20,52},{24,56},{28,60},{32,6... | collective-permute-start | bytes 368648 | tf_op jit(solution)/shard_map/ppermute | solution.py:430
  107.4 15.5 %collective-permute-start.23 = (bf16[2,96,320]{2,1,0:T(8,128)(2,1)S(1)}, bf16[2,96,320]{2,1,0:T(8,128)(2,1)S(1)}, u32[]{:S(2)}, u32[]{:S(2)}) collective-permute-start(bf16[2,96,320]{2,1,0:T(8,128)(2,1)S(1)} %get-tuple-element.56), channel_id=1, source_target_pairs={{0,64},{4,68},{8,72},{12,76},{16,80},{20,84},{24,88},{28,92},{32,9... | collective-permute-start | bytes 368648 | tf_op jit(solution)/shard_map/ppermute | solution.py:430
  122.9 3.0 %collective-permute-done.22.refs_2_ = bf16[2,96,320]{2,1,0:T(8,128)(2,1)S(1)} collective-permute-done((bf16[2,96,320]{2,1,0:T(8,128)(2,1)S(1)}, bf16[2,96,320]{2,1,0:T(8,128)(2,1)S(1)}, u32[]{:S(2)}, u32[]{:S(2)}) %collective-permute-start.22) | collective-permute-done | bytes 122912 | tf_op jit(solution)/shard_map/ppermute | solution.py:430
  125.9 4.8 %collective-permute-done.23.refs_3_ = bf16[2,96,320]{2,1,0:T(8,128)(2,1)S(1)} collective-permute-done((bf16[2,96,320]{2,1,0:T(8,128)(2,1)S(1)}, bf16[2,96,320]{2,1,0:T(8,128)(2,1)S(1)}, u32[]{:S(2)}, u32[]{:S(2)}) %collective-permute-start.23) | collective-permute-done | bytes 122912 | tf_op jit(solution)/shard_map/ppermute | solution.py:430
  133.1 7.5 %all-to-all-start.2 = ((bf16[4,2,64,640]{3,2,1,0:T(8,128)(2,1)}), bf16[4,2,64,640]{3,2,1,0:T(8,128)(2,1)}, u32[]{:S(2)}, u32[]{:S(2)}) async-start(bf16[4,2,64,640]{3,2,1,0:T(8,128)(2,1)} %shard_map.113), calls=%async_computation.2 | async-start | bytes 1310720 | tf_op jit(solution)/shard_map/all_to_all | solution.py:465
  143.9 2.2 %shard_map.114 = (bf16[2,96,160]{2,1,0:T(8,128)(2,1)S(1)}, bf16[2,96,160]{2,1,0:T(8,128)(2,1)S(1)}, bf16[2,96,160]{2,1,0:T(8,128)(2,1)S(1)}, bf16[2,96,160]{2,1,0:T(8,128)(2,1)S(1)}) custom-call(s32[5]{0:T(128)S(1)} %stack.23.refs_0_, bf16[5,160,128]{2,1,0:T(8,128)(2,1)S(1)} %get-tuple-element.53.refs_7_.refs_1_, ...), custom_call_target="tpu_custom_call" | custom-call | bytes 2580500 | tf_op jit(solution)/shard_map/pallas_call | solution.py:64
  146.2 3.6 %collective-permute-start.27 = (bf16[2,96,160]{2,1,0:T(8,128)(2,1)S(1)}, bf16[2,96,160]{2,1,0:T(8,128)(2,1)S(1)}, u32[]{:S(2)}, u32[]{:S(2)}) collective-permute-start(bf16[2,96,160]{2,1,0:T(8,128)(2,1)S(1)} %get-tuple-element.63), channel_id=1, source_target_pairs={{0,64},{4,68},{8,72},{12,76},{16,80},{20,84},{24,88},{28,92},{32,9... | collective-permute-start | bytes 184328 | tf_op jit(solution)/shard_map/ppermute | solution.py:430
  149.8 4.1 %collective-permute-start.30 = (bf16[96,320]{1,0:T(8,128)(2,1)S(1)}, bf16[96,320]{1,0:T(8,128)(2,1)S(1)}, u32[]{:S(2)}, u32[]{:S(2)}) collective-permute-start(bf16[96,320]{1,0:T(8,128)(2,1)S(1)} %get-tuple-element.67), channel_id=1, source_target_pairs={{0,128},{4,132},{8,136},{12,140},{16,144},{20,148},{24,152},{28,15... | collective-permute-start | bytes 184328 | tf_op jit(solution)/shard_map/ppermute | solution.py:371
  155.6 4.0 %collective-permute-start.29 = (bf16[96,160]{1,0:T(8,128)(2,1)S(1)}, bf16[96,160]{1,0:T(8,128)(2,1)S(1)}, u32[]{:S(2)}, u32[]{:S(2)}) collective-permute-start(bf16[96,160]{1,0:T(8,128)(2,1)S(1)} %get-tuple-element.66), channel_id=1, source_target_pairs={{0,128},{4,132},{8,136},{12,140},{16,144},{20,148},{24,152},{28,15... | collective-permute-start | bytes 92168 | tf_op jit(solution)/shard_map/ppermute | solution.py:371
  161.6 2.7 %collective-permute-done.29.refs_1_ = bf16[96,160]{1,0:T(8,128)(2,1)S(1)} collective-permute-done((bf16[96,160]{1,0:T(8,128)(2,1)S(1)}, bf16[96,160]{1,0:T(8,128)(2,1)S(1)}, u32[]{:S(2)}, u32[]{:S(2)}) %collective-permute-start.29) | collective-permute-done | bytes 30752 | tf_op jit(solution)/shard_map/ppermute | solution.py:371
  (139 shorter events, 48.7 us)
Async XLA Ops:
  0.6 8.8 %collective-permute-start.2 = (bf16[2,64,640]{2,1,0:T(8,128)(2,1)}, bf16[2,64,640]{2,1,0:T(8,128)(2,1)S(1)}, u32[]{:S(2)}, u32[]{:S(2)}) collective-permute-start(bf16[2,64,640]{2,1,0:T(8,128)(2,1)} %refs_1_.3), channel_id=1, source_target_pairs={{0,3},{1,0},{2,1},{3,2},{4,7},{5,4},{6,5},{7,6},{8,11},{9,8},{10,9... | collective-permute-start | bytes 491528 | tf_op jit(solution)/shard_map/ppermute | solution.py:368
  2.6 13.3 %collective-permute-start.1 = (bf16[2,64,640]{2,1,0:T(8,128)(2,1)}, bf16[2,64,640]{2,1,0:T(8,128)(2,1)S(1)}, u32[]{:S(2)}, u32[]{:S(2)}) collective-permute-start(bf16[2,64,640]{2,1,0:T(8,128)(2,1)} %refs_1_.3), channel_id=1, source_target_pairs={{0,2},{1,3},{2,0},{3,1},{4,6},{5,7},{6,4},{7,5},{8,10},{9,11},{10,... | collective-permute-start | bytes 491528 | tf_op jit(solution)/shard_map/ppermute | solution.py:368
  4.1 14.3 %collective-permute-start = (bf16[2,64,640]{2,1,0:T(8,128)(2,1)}, bf16[2,64,640]{2,1,0:T(8,128)(2,1)S(1)}, u32[]{:S(2)}, u32[]{:S(2)}) collective-permute-start(bf16[2,64,640]{2,1,0:T(8,128)(2,1)} %refs_1_.3), channel_id=1, source_target_pairs={{0,1},{1,2},{2,3},{3,0},{4,5},{5,6},{6,7},{7,4},{8,9},{9,10},{10,1... | collective-permute-start | bytes 491528 | tf_op jit(solution)/shard_map/ppermute | solution.py:368
  24.4 9.9 %collective-permute-start.4 = (bf16[160,128]{1,0:T(8,128)(2,1)S(1)}, bf16[160,128]{1,0:T(8,128)(2,1)S(1)}, u32[]{:S(2)}, u32[]{:S(2)}) collective-permute-start(bf16[160,128]{1,0:T(8,128)(2,1)S(1)} %get-tuple-element.38), channel_id=1, source_target_pairs={{4,8},{8,4},{12,16},{16,12},{20,24},{24,20},{28,32},{32,28},{36,40... | collective-permute-start | bytes 122888 | tf_op jit(solution)/shard_map/ppermute | solution.py:374
  28.3 17.8 %all-to-all-start = ((bf16[8,80,512]{2,1,0:T(8,128)(2,1)}), bf16[8,80,512]{2,1,0:T(8,128)(2,1)S(1)}, u32[]{:S(2)}, u32[]{:S(2)}) async-start(bf16[8,80,512]{2,1,0:T(8,128)(2,1)} %shard_map.95.refs_3_), calls=%async_computation | async-start | bytes 1310720 | tf_op jit(solution)/shard_map/all_to_all | solution.py:392
  34.4 5.1 %collective-permute-start.7 = (bf16[160,128]{1,0:T(8,128)(2,1)S(1)}, bf16[160,128]{1,0:T(8,128)(2,1)S(1)}, u32[]{:S(2)}, u32[]{:S(2)}) collective-permute-start(bf16[160,128]{1,0:T(8,128)(2,1)S(1)} %shard_map.96.refs_1_), channel_id=1, source_target_pairs={{0,3},{1,0},{2,1},{3,2},{4,7},{5,4},{6,5},{7,6},{8,11},{9,8},{10,9... | collective-permute-start | bytes 122888 | tf_op jit(solution)/shard_map/ppermute | solution.py:368
  35.9 5.2 %collective-permute-start.6 = (bf16[160,128]{1,0:T(8,128)(2,1)S(1)}, bf16[160,128]{1,0:T(8,128)(2,1)S(1)}, u32[]{:S(2)}, u32[]{:S(2)}) collective-permute-start(bf16[160,128]{1,0:T(8,128)(2,1)S(1)} %shard_map.96.refs_1_), channel_id=1, source_target_pairs={{0,2},{1,3},{2,0},{3,1},{4,6},{5,7},{6,4},{7,5},{8,10},{9,11},{10,... | collective-permute-start | bytes 122888 | tf_op jit(solution)/shard_map/ppermute | solution.py:368
  38.3 4.0 %collective-permute-start.5 = (bf16[160,128]{1,0:T(8,128)(2,1)S(1)}, bf16[160,128]{1,0:T(8,128)(2,1)S(1)}, u32[]{:S(2)}, u32[]{:S(2)}) collective-permute-start(bf16[160,128]{1,0:T(8,128)(2,1)S(1)} %shard_map.96.refs_1_), channel_id=1, source_target_pairs={{0,1},{1,2},{2,3},{3,0},{4,5},{5,6},{6,7},{7,4},{8,9},{9,10},{10,1... | collective-permute-start | bytes 122888 | tf_op jit(solution)/shard_map/ppermute | solution.py:368
  44.4 4.3 %collective-permute-start.8 = (bf16[320,128]{1,0:T(8,128)(2,1)}, bf16[320,128]{1,0:T(8,128)(2,1)}, u32[]{:S(2)}, u32[]{:S(2)}) collective-permute-start(bf16[320,128]{1,0:T(8,128)(2,1)} %get-tuple-element.41), channel_id=1, source_target_pairs={{0,4},{4,0},{8,12},{12,8},{16,20},{20,16},{24,28},{28,24},{32,36},... | collective-permute-start | bytes 245768 | tf_op jit(solution)/shard_map/ppermute | solution.py:371
  44.4 4.3 %collective-permute-start.9 = (bf16[320,128]{1,0:T(8,128)(2,1)}, bf16[320,128]{1,0:T(8,128)(2,1)}, u32[]{:S(2)}, u32[]{:S(2)}) collective-permute-start(bf16[320,128]{1,0:T(8,128)(2,1)} %get-tuple-element.42), channel_id=1, source_target_pairs={{4,8},{8,4},{12,16},{16,12},{20,24},{24,20},{28,32},{32,28},{36,40... | collective-permute-start | bytes 245768 | tf_op jit(solution)/shard_map/ppermute | solution.py:374
  50.7 3.6 %collective-permute-start.10 = (bf16[320,128]{1,0:T(8,128)(2,1)}, bf16[320,128]{1,0:T(8,128)(2,1)S(1)}, u32[]{:S(2)}, u32[]{:S(2)}) collective-permute-start(bf16[320,128]{1,0:T(8,128)(2,1)} %get-tuple-element.44.refs_2_.refs_0_), channel_id=1, source_target_pairs={{0,4},{4,0},{8,12},{12,8},{16,20},{20,16},{24,28},{28,24},{32,36},... | collective-permute-start | bytes 245768 | tf_op jit(solution)/shard_map/ppermute | solution.py:371
  53.0 11.1 %collective-permute-start.11 = (bf16[320,128]{1,0:T(8,128)(2,1)}, bf16[320,128]{1,0:T(8,128)(2,1)}, u32[]{:S(2)}, u32[]{:S(2)}) collective-permute-start(bf16[320,128]{1,0:T(8,128)(2,1)} %get-tuple-element.44.refs_2_.refs_0_), channel_id=1, source_target_pairs={{4,8},{8,4},{12,16},{16,12},{20,24},{24,20},{28,32},{32,28},{36,40... | collective-permute-start | bytes 245768 | tf_op jit(solution)/shard_map/ppermute | solution.py:374
  56.0 27.1 %all-to-all-start.1 = ((bf16[8,80,128]{2,1,0:T(8,128)(2,1)}), bf16[8,80,128]{2,1,0:T(8,128)(2,1)S(1)}, u32[]{:S(2)}, u32[]{:S(2)}) async-start(bf16[8,80,128]{2,1,0:T(8,128)(2,1)} %copy-done.9), calls=%async_computation.1 | async-start | bytes 327680 | tf_op jit(solution)/shard_map/all_to_all | solution.py:410
  65.9 12.0 %collective-permute-start.17 = (bf16[3,320,128]{2,1,0:T(8,128)(2,1)S(1)}, bf16[3,320,128]{2,1,0:T(8,128)(2,1)S(1)}, u32[]{:S(2)}, u32[]{:S(2)}) collective-permute-start(bf16[3,320,128]{2,1,0:T(8,128)(2,1)S(1)} %shard_map.104.refs_1_), channel_id=1, source_target_pairs={{0,8},{4,12},{8,0},{12,4},{16,24},{20,28},{24,16},{28,20},{32,40},... | collective-permute-start | bytes 737288 | tf_op jit(solution)/shard_map/ppermute | solution.py:371
  73.3 4.7 %collective-permute-start.12 = (bf16[160,128]{1,0:T(8,128)(2,1)S(1)}, bf16[160,128]{1,0:T(8,128)(2,1)S(1)}, u32[]{:S(2)}, u32[]{:S(2)}) collective-permute-start(bf16[160,128]{1,0:T(8,128)(2,1)S(1)} %get-tuple-element.46), channel_id=1, source_target_pairs={{0,1},{1,2},{2,3},{3,0},{4,5},{5,6},{6,7},{7,4},{8,9},{9,10},{10,1... | collective-permute-start | bytes 122888 | tf_op jit(solution)/shard_map/ppermute | solution.py:368
  74.6 7.2 %collective-permute-start.13 = (bf16[160,128]{1,0:T(8,128)(2,1)S(1)}, bf16[160,128]{1,0:T(8,128)(2,1)S(1)}, u32[]{:S(2)}, u32[]{:S(2)}) collective-permute-start(bf16[160,128]{1,0:T(8,128)(2,1)S(1)} %get-tuple-element.47), channel_id=1, source_target_pairs={{0,2},{1,3},{2,0},{3,1},{4,6},{5,7},{6,4},{7,5},{8,10},{9,11},{10,... | collective-permute-start | bytes 122888 | tf_op jit(solution)/shard_map/ppermute | solution.py:368
  77.8 4.7 %collective-permute-start.14 = (bf16[160,128]{1,0:T(8,128)(2,1)S(1)}, bf16[160,128]{1,0:T(8,128)(2,1)S(1)}, u32[]{:S(2)}, u32[]{:S(2)}) collective-permute-start(bf16[160,128]{1,0:T(8,128)(2,1)S(1)} %get-tuple-element.48), channel_id=1, source_target_pairs={{0,3},{1,0},{2,1},{3,2},{4,7},{5,4},{6,5},{7,6},{8,11},{9,8},{10,9... | collective-permute-start | bytes 122888 | tf_op jit(solution)/shard_map/ppermute | solution.py:368
  79.2 12.0 %collective-permute-start.18 = (bf16[5,320,128]{2,1,0:T(8,128)(2,1)S(1)}, bf16[5,320,128]{2,1,0:T(8,128)(2,1)S(1)}, u32[]{:S(2)}, u32[]{:S(2)}) collective-permute-start(bf16[5,320,128]{2,1,0:T(8,128)(2,1)S(1)} %get-tuple-element.51.refs_1_), channel_id=1, source_target_pairs={{0,16},{4,20},{8,24},{12,28},{16,0},{20,4},{24,8},{28,12},{32,48},... | collective-permute-start | bytes 1228808 | tf_op jit(solution)/shard_map/ppermute | solution.py:371
  85.4 6.4 %collective-permute-start.16 = (bf16[160,128]{1,0:T(8,128)(2,1)S(1)}, bf16[160,128]{1,0:T(8,128)(2,1)S(1)}, u32[]{:S(2)}, u32[]{:S(2)}) collective-permute-start(bf16[160,128]{1,0:T(8,128)(2,1)S(1)} %shard_map.102.refs_0_.refs_2_), channel_id=1, source_target_pairs={{4,8},{8,4},{12,16},{16,12},{20,24},{24,20},{28,32},{32,28},{36,40... | collective-permute-start | bytes 122888 | tf_op jit(solution)/shard_map/ppermute | solution.py:374
  86.1 5.8 %collective-permute-start.15 = (bf16[160,128]{1,0:T(8,128)(2,1)S(1)}, bf16[160,128]{1,0:T(8,128)(2,1)S(1)}, u32[]{:S(2)}, u32[]{:S(2)}) collective-permute-start(bf16[160,128]{1,0:T(8,128)(2,1)S(1)} %shard_map.102.refs_0_.refs_2_), channel_id=1, source_target_pairs={{0,4},{4,0},{8,12},{12,8},{16,20},{20,16},{24,28},{28,24},{32,36},... | collective-permute-start | bytes 122888 | tf_op jit(solution)/shard_map/ppermute | solution.py:371
  91.8 10.1 %collective-permute-start.21 = (bf16[320,128]{1,0:T(8,128)(2,1)S(1)}, bf16[320,128]{1,0:T(8,128)(2,1)S(1)}, u32[]{:S(2)}, u32[]{:S(2)}) collective-permute-start(bf16[320,128]{1,0:T(8,128)(2,1)S(1)} %shard_map.106.refs_4_.refs_3_), channel_id=1, source_target_pairs={{0,4},{4,0},{8,12},{12,8},{16,20},{20,16},{24,28},{28,24},{32,36},... | collective-permute-start | bytes 245768 | tf_op jit(solution)/shard_map/ppermute | solution.py:371
  92.0 5.7 %collective-permute-start.19 = (bf16[3,160,128]{2,1,0:T(8,128)(2,1)S(1)}, bf16[3,160,128]{2,1,0:T(8,128)(2,1)S(1)}, u32[]{:S(2)}, u32[]{:S(2)}) collective-permute-start(bf16[3,160,128]{2,1,0:T(8,128)(2,1)S(1)} %shard_map.107.refs_5_.refs_1_), channel_id=1, source_target_pairs={{0,8},{4,12},{8,0},{12,4},{16,24},{20,28},{24,16},{28,20},{32,40},... | collective-permute-start | bytes 368648 | tf_op jit(solution)/shard_map/ppermute | solution.py:371
  98.3 33.0 %collective-permute-start.20 = (bf16[5,160,128]{2,1,0:T(8,128)(2,1)S(1)}, bf16[5,160,128]{2,1,0:T(8,128)(2,1)S(1)}, u32[]{:S(2)}, u32[]{:S(2)}) collective-permute-start(bf16[5,160,128]{2,1,0:T(8,128)(2,1)S(1)} %get-tuple-element.53.refs_7_.refs_1_), channel_id=1, source_target_pairs={{0,16},{4,20},{8,24},{12,28},{16,0},{20,4},{24,8},{28,12},{32,48},... | collective-permute-start | bytes 614408 | tf_op jit(solution)/shard_map/ppermute | solution.py:371
  104.8 21.1 %collective-permute-start.22 = (bf16[2,96,320]{2,1,0:T(8,128)(2,1)S(1)}, bf16[2,96,320]{2,1,0:T(8,128)(2,1)S(1)}, u32[]{:S(2)}, u32[]{:S(2)}) collective-permute-start(bf16[2,96,320]{2,1,0:T(8,128)(2,1)S(1)} %get-tuple-element.55), channel_id=1, source_target_pairs={{0,32},{4,36},{8,40},{12,44},{16,48},{20,52},{24,56},{28,60},{32,6... | collective-permute-start | bytes 368648 | tf_op jit(solution)/shard_map/ppermute | solution.py:430
  107.4 23.3 %collective-permute-start.23 = (bf16[2,96,320]{2,1,0:T(8,128)(2,1)S(1)}, bf16[2,96,320]{2,1,0:T(8,128)(2,1)S(1)}, u32[]{:S(2)}, u32[]{:S(2)}) collective-permute-start(bf16[2,96,320]{2,1,0:T(8,128)(2,1)S(1)} %get-tuple-element.56), channel_id=1, source_target_pairs={{0,64},{4,68},{8,72},{12,76},{16,80},{20,84},{24,88},{28,92},{32,9... | collective-permute-start | bytes 368648 | tf_op jit(solution)/shard_map/ppermute | solution.py:430
  122.9 7.8 %collective-permute-start.24 = (bf16[2,96,320]{2,1,0:T(8,128)(2,1)S(1)}, bf16[2,96,320]{2,1,0:T(8,128)(2,1)S(1)}, u32[]{:S(2)}, u32[]{:S(2)}) collective-permute-start(bf16[2,96,320]{2,1,0:T(8,128)(2,1)S(1)} %get-tuple-element.57), channel_id=1, source_target_pairs={{0,96},{4,100},{8,104},{12,108},{16,112},{20,116},{24,120},{28,124... | collective-permute-start | bytes 368648 | tf_op jit(solution)/shard_map/ppermute | solution.py:430
  133.1 27.3 %all-to-all-start.2 = ((bf16[4,2,64,640]{3,2,1,0:T(8,128)(2,1)}), bf16[4,2,64,640]{3,2,1,0:T(8,128)(2,1)}, u32[]{:S(2)}, u32[]{:S(2)}) async-start(bf16[4,2,64,640]{3,2,1,0:T(8,128)(2,1)} %shard_map.113), calls=%async_computation.2 | async-start | bytes 1310720 | tf_op jit(solution)/shard_map/all_to_all | solution.py:465
  146.1 7.8 %collective-permute-start.26 = (bf16[2,96,160]{2,1,0:T(8,128)(2,1)S(1)}, bf16[2,96,160]{2,1,0:T(8,128)(2,1)S(1)}, u32[]{:S(2)}, u32[]{:S(2)}) collective-permute-start(bf16[2,96,160]{2,1,0:T(8,128)(2,1)S(1)} %get-tuple-element.62), channel_id=1, source_target_pairs={{0,32},{4,36},{8,40},{12,44},{16,48},{20,52},{24,56},{28,60},{32,6... | collective-permute-start | bytes 184328 | tf_op jit(solution)/shard_map/ppermute | solution.py:430
  146.2 8.6 %collective-permute-start.27 = (bf16[2,96,160]{2,1,0:T(8,128)(2,1)S(1)}, bf16[2,96,160]{2,1,0:T(8,128)(2,1)S(1)}, u32[]{:S(2)}, u32[]{:S(2)}) collective-permute-start(bf16[2,96,160]{2,1,0:T(8,128)(2,1)S(1)} %get-tuple-element.63), channel_id=1, source_target_pairs={{0,64},{4,68},{8,72},{12,76},{16,80},{20,84},{24,88},{28,92},{32,9... | collective-permute-start | bytes 184328 | tf_op jit(solution)/shard_map/ppermute | solution.py:430
  149.8 5.2 %collective-permute-start.28 = (bf16[2,96,160]{2,1,0:T(8,128)(2,1)S(1)}, bf16[2,96,160]{2,1,0:T(8,128)(2,1)S(1)}, u32[]{:S(2)}, u32[]{:S(2)}) collective-permute-start(bf16[2,96,160]{2,1,0:T(8,128)(2,1)S(1)} %get-tuple-element.64), channel_id=1, source_target_pairs={{0,96},{4,100},{8,104},{12,108},{16,112},{20,116},{24,120},{28,124... | collective-permute-start | bytes 184328 | tf_op jit(solution)/shard_map/ppermute | solution.py:430
  149.8 9.8 %collective-permute-start.30 = (bf16[96,320]{1,0:T(8,128)(2,1)S(1)}, bf16[96,320]{1,0:T(8,128)(2,1)S(1)}, u32[]{:S(2)}, u32[]{:S(2)}) collective-permute-start(bf16[96,320]{1,0:T(8,128)(2,1)S(1)} %get-tuple-element.67), channel_id=1, source_target_pairs={{0,128},{4,132},{8,136},{12,140},{16,144},{20,148},{24,152},{28,15... | collective-permute-start | bytes 184328 | tf_op jit(solution)/shard_map/ppermute | solution.py:371
  155.6 8.7 %collective-permute-start.29 = (bf16[96,160]{1,0:T(8,128)(2,1)S(1)}, bf16[96,160]{1,0:T(8,128)(2,1)S(1)}, u32[]{:S(2)}, u32[]{:S(2)}) collective-permute-start(bf16[96,160]{1,0:T(8,128)(2,1)S(1)} %get-tuple-element.66), channel_id=1, source_target_pairs={{0,128},{4,132},{8,136},{12,140},{16,144},{20,148},{24,152},{28,15... | collective-permute-start | bytes 92168 | tf_op jit(solution)/shard_map/ppermute | solution.py:371
  (39 other events, 118.2 us)

commit v10 on v9

--- a/solution.py
+++ b/solution.py
@@ -87,10 +87,6 @@
     place = lax.broadcasted_iota(jnp.int32, (cols, cols), 0)
     source = place // 2 + (place % 2) * (cols // 2)
     return jnp.where(source == lax.broadcasted_iota(jnp.int32, (cols, cols), 1), 1.0, 0.0).astype(BF)
-
-
-def warm(x, w, out):
-    out[...] = w[0, :16, :128] + x[0, :16, :128]
 
 
 def fine_rows(x):
@@ -379,7 +375,6 @@
         fine_forward,
         [shape((pieces,) + latent.shape), shape((fine, deep), F32), shape((fine, deep)), shape((fine, deep))],
         (at, latent, *got, w_fine),
-        behind=(call(warm, shape((16, 128)), (latent, w_fine)),),
     )
     partner, other = pairs(partner, other)
     fine_slab = call(

time: 166 us -> 155 us (0.934)
  local copies, waits for them, and re-layouts: 24.8 us -> 8.47 us
  waiting for transfers between devices: 29.4 us -> 43.4 us
  starting transfers between devices: 83.8 us -> 76.6 us
  Pallas kernels: 24.8 us -> 22.6 us
    unnamed x76 -> x22, local copies, waits for them, and re-layouts: 24.7 us -> 8.38 us
    ppermute x12, waiting for transfers between devices: 8.69 us -> 15.6 us  [swap(): return lax.ppermute(v, 'wide', [(i, i ^ bit) for i in range(wide)])]
    ppermute x9, waiting for transfers between devices: 11.4 us -> 17.3 us  [across(): lax.ppermute(v, 'narrow', [(i, (i + step) % pieces) for i in range(pieces)])]
    ppermute x12, starting transfers between devices: 21.2 us -> 18.1 us  [swap(): return lax.ppermute(v, 'wide', [(i, i ^ bit) for i in range(wide)])]
    pallas_call x25 -> x24, Pallas kernels: 24.8 us -> 22.6 us  [call(): pl.pallas_call(kernel, out_shape=outs, in_specs=[smem if a.dtype == jnp.i...]
  transfers between devices with their start and end apart: 34 -> 34, of which waited for: 16 -> 17; matrix products, arithmetic and copies ran while one was open for 1% -> 1% of each run, Pallas kernels for 12% -> 12%
where the time goes in v10:
time: 155 us; the launch traced here: 153 us
  starting transfers between devices  76.6 us (49%)
  waiting for transfers between devices  43.4 us (28%)
  Pallas kernels  22.6 us (15%)
  local copies, waits for them, and re-layouts  8.47 us (5%)
    pallas_call x24, Pallas kernels, call(): pl.pallas_call(kernel, out_shape=outs, in_specs=[smem if a.dtype == jnp.i...  22.6 us
    ppermute x6, starting transfers between devices, halves(): lax.ppermute(parts[s], 'wide', [(i, i // 32 * 32 + (i // 8 + s) % 4 * 8 +...  21.9 us
    ppermute x12, starting transfers between devices, swap(): return lax.ppermute(v, 'wide', [(i, i ^ bit) for i in range(wide)])  18.1 us
    ppermute x9, waiting for transfers between devices, across(): lax.ppermute(v, 'narrow', [(i, (i + step) % pieces) for i in range(pieces)])  17.3 us
    ppermute x12, waiting for transfers between devices, swap(): return lax.ppermute(v, 'wide', [(i, i ^ bit) for i in range(wide)])  15.6 us
    ppermute x9, starting transfers between devices, across(): lax.ppermute(v, 'narrow', [(i, (i + step) % pieces) for i in range(pieces)])  13.8 us
    ppermute x6, waiting for transfers between devices, halves(): lax.ppermute(parts[s], 'wide', [(i, i // 32 * 32 + (i // 8 + s) % 4 * 8 +...  8.92 us
    unnamed x22, local copies, waits for them, and re-layouts  8.38 us
  transfers between devices with their start and end apart: 34, of which 17 were waited for; matrix products, arithmetic and copies ran while one was open for 1% of the time, Pallas kernels for 12%

profile of v10, /device:TPU:32, one launch (start us, length us, event | category | flops | bytes accessed | tf_op | source)
XLA Modules:
  0.0 153.3 jit_solution(16862384811349033396)
XLA Ops:
  0.6 3.4 %collective-permute-start.1 = (bf16[2,64,640]{2,1,0:T(8,128)(2,1)}, bf16[2,64,640]{2,1,0:T(8,128)(2,1)S(1)}, u32[]{:S(2)}, u32[]{:S(2)}) collective-permute-start(bf16[2,64,640]{2,1,0:T(8,128)(2,1)} %refs_1_.3), channel_id=1, source_target_pairs={{0,2},{1,3},{2,0},{3,1},{4,6},{5,7},{6,4},{7,5},{8,10},{9,11},{10,... | collective-permute-start | bytes 491528 | tf_op jit(solution)/shard_map/ppermute | solution.py:364
  4.0 2.0 %collective-permute-start.2 = (bf16[2,64,640]{2,1,0:T(8,128)(2,1)}, bf16[2,64,640]{2,1,0:T(8,128)(2,1)S(1)}, u32[]{:S(2)}, u32[]{:S(2)}) collective-permute-start(bf16[2,64,640]{2,1,0:T(8,128)(2,1)} %refs_1_.3), channel_id=1, source_target_pairs={{0,3},{1,0},{2,1},{3,2},{4,7},{5,4},{6,5},{7,6},{8,11},{9,8},{10,9... | collective-permute-start | bytes 491528 | tf_op jit(solution)/shard_map/ppermute | solution.py:364
  6.1 5.7 %collective-permute-done.1.refs_3_ = bf16[2,64,640]{2,1,0:T(8,128)(2,1)S(1)} collective-permute-done((bf16[2,64,640]{2,1,0:T(8,128)(2,1)}, bf16[2,64,640]{2,1,0:T(8,128)(2,1)S(1)}, u32[]{:S(2)}, u32[]{:S(2)}) %collective-permute-start.1) | collective-permute-done | bytes 163872 | tf_op jit(solution)/shard_map/ppermute | solution.py:364
  11.8 6.1 %collective-permute-done.refs_2_ = bf16[2,64,640]{2,1,0:T(8,128)(2,1)S(1)} collective-permute-done((bf16[2,64,640]{2,1,0:T(8,128)(2,1)}, bf16[2,64,640]{2,1,0:T(8,128)(2,1)S(1)}, u32[]{:S(2)}, u32[]{:S(2)}) %collective-permute-start) | collective-permute-done | bytes 163872 | tf_op jit(solution)/shard_map/ppermute | solution.py:364
  20.3 1.9 %shard_map.93 = (bf16[4,2,64,640]{3,2,1,0:T(8,128)(2,1)S(1)}, f32[160,128]{1,0:T(8,128)S(1)}, bf16[160,128]{1,0:T(8,128)(2,1)S(1)}, bf16[160,128]{1,0:T(8,128)(2,1)S(1)}) custom-call(s32[5]{0:T(128)S(1)} %stack.23.refs_0_, bf16[2,64,640]{2,1,0:T(8,128)(2,1)S(1)} %copy-done.8, bf16[2,64,640]{2,1,0:T(8,128)(2,1)S(1)} %collective-permute-done.refs_2_, ...), custom_call_target="tpu_custom_call" | custom-call | flops 30000001024 | bytes 2498580 | tf_op jit(solution)/shard_map/pallas_call | solution.py:64
  23.5 2.6 %shard_map.94.refs_3_ = bf16[8,80,512]{2,1,0:T(8,128)(2,1)} custom-call(bf16[4,2,64,640]{3,2,1,0:T(8,128)(2,1)S(1)} %get-tuple-element.39.refs_0_, bf16[640,640]{1,0:T(8,128)(2,1)S(1)} %copy-done.4, bf16[160,128]{1,0:T(8,128)(2,1)S(1)} %collective-permute-done.3.refs_2_.refs_1_), custom_call_target="tpu_custom_call" | custom-call | bytes 1474560 | tf_op jit(solution)/shard_map/pallas_call | solution.py:64
  26.1 6.0 %all-to-all-start = ((bf16[8,80,512]{2,1,0:T(8,128)(2,1)}), bf16[8,80,512]{2,1,0:T(8,128)(2,1)S(1)}, u32[]{:S(2)}, u32[]{:S(2)}) async-start(bf16[8,80,512]{2,1,0:T(8,128)(2,1)} %shard_map.94.refs_3_), calls=%async_computation | async-start | bytes 1310720 | tf_op jit(solution)/shard_map/all_to_all | solution.py:387
  32.2 3.8 %collective-permute-start.6 = (bf16[160,128]{1,0:T(8,128)(2,1)S(1)}, bf16[160,128]{1,0:T(8,128)(2,1)S(1)}, u32[]{:S(2)}, u32[]{:S(2)}) collective-permute-start(bf16[160,128]{1,0:T(8,128)(2,1)S(1)} %shard_map.95.refs_1_), channel_id=1, source_target_pairs={{0,2},{1,3},{2,0},{3,1},{4,6},{5,7},{6,4},{7,5},{8,10},{9,11},{10,... | collective-permute-start | bytes 122888 | tf_op jit(solution)/shard_map/ppermute | solution.py:364
  42.2 1.6 %all-to-all-done.refs_2_.refs_0_ = bf16[8,80,512]{2,1,0:T(8,128)(2,1)S(1)} async-done(((bf16[8,80,512]{2,1,0:T(8,128)(2,1)}), bf16[8,80,512]{2,1,0:T(8,128)(2,1)S(1)}, u32[]{:S(2)}, u32[]{:S(2)}) %all-to-all-start) | async-done | bytes 655392 | tf_op jit(solution)/shard_map/all_to_all | solution.py:387
  43.9 2.0 %copy-done.1 = bf16[3,3,640,320]{2,3,1,0:T(8,128)(2,1)S(1)} copy-done((bf16[3,3,640,320]{2,3,1,0:T(8,128)(2,1)S(1)}, bf16[3,3,640,320]{2,3,1,0:T(8,128)(2,1)}, u32[]{:S(2)}) %copy-start.1) | copy-done | bytes 3686424
  47.5 1.8 %collective-permute-start.10 = (bf16[320,128]{1,0:T(8,128)(2,1)S(1)}, bf16[320,128]{1,0:T(8,128)(2,1)S(1)}, u32[]{:S(2)}, u32[]{:S(2)}) collective-permute-start(bf16[320,128]{1,0:T(8,128)(2,1)S(1)} %get-tuple-element.44.refs_2_.refs_0_), channel_id=1, source_target_pairs={{0,4},{4,0},{8,12},{12,8},{16,20},{20,16},{24,28},{28,24},{32,36},... | collective-permute-start | bytes 245768 | tf_op jit(solution)/shard_map/ppermute | solution.py:367
  51.2 8.2 %all-to-all-start.1 = ((bf16[8,80,128]{2,1,0:T(8,128)(2,1)}), bf16[8,80,128]{2,1,0:T(8,128)(2,1)S(1)}, u32[]{:S(2)}, u32[]{:S(2)}) async-start(bf16[8,80,128]{2,1,0:T(8,128)(2,1)} %shard_map.100), calls=%async_computation.1 | async-start | bytes 327680 | tf_op jit(solution)/shard_map/all_to_all | solution.py:405
  59.5 2.1 %collective-permute-start.17 = (bf16[3,320,128]{2,1,0:T(8,128)(2,1)S(1)}, bf16[3,320,128]{2,1,0:T(8,128)(2,1)S(1)}, u32[]{:S(2)}, u32[]{:S(2)}) collective-permute-start(bf16[3,320,128]{2,1,0:T(8,128)(2,1)S(1)} %shard_map.103.refs_1_), channel_id=1, source_target_pairs={{0,8},{4,12},{8,0},{12,4},{16,24},{20,28},{24,16},{28,20},{32,40},... | collective-permute-start | bytes 737288 | tf_op jit(solution)/shard_map/ppermute | solution.py:367
  61.6 2.0 %copy-done.2 = bf16[3,3,640,320]{2,3,1,0:T(8,128)(2,1)S(1)} copy-done((bf16[3,3,640,320]{2,3,1,0:T(8,128)(2,1)S(1)}, bf16[3,3,640,320]{2,3,1,0:T(8,128)(2,1)}, u32[]{:S(2)}) %copy-start.2) | copy-done | bytes 3686424
  63.6 1.9 %shard_map.99 = (bf16[160,128]{1,0:T(8,128)(2,1)S(1)}, bf16[160,128]{1,0:T(8,128)(2,1)S(1)}, bf16[160,128]{1,0:T(8,128)(2,1)S(1)}, bf16[160,128]{1,0:T(8,128)(2,1)S(1)}) custom-call(s32[5]{0:T(128)S(1)} %stack.23.refs_0_, bf16[320,128]{1,0:T(8,128)(2,1)S(1)} %collective-permute-done.10.refs_1_.refs_2_, ...), custom_call_target="tpu_custom_call" | custom-call | flops 30000001024 | bytes 3932180 | tf_op jit(solution)/shard_map/pallas_call | solution.py:64
  66.9 3.1 %collective-permute-start.13 = (bf16[160,128]{1,0:T(8,128)(2,1)S(1)}, bf16[160,128]{1,0:T(8,128)(2,1)S(1)}, u32[]{:S(2)}, u32[]{:S(2)}) collective-permute-start(bf16[160,128]{1,0:T(8,128)(2,1)S(1)} %get-tuple-element.47), channel_id=1, source_target_pairs={{0,2},{1,3},{2,0},{3,1},{4,6},{5,7},{6,4},{7,5},{8,10},{9,11},{10,... | collective-permute-start | bytes 122888 | tf_op jit(solution)/shard_map/ppermute | solution.py:364
  70.8 2.8 %collective-permute-start.18 = (bf16[5,320,128]{2,1,0:T(8,128)(2,1)S(1)}, bf16[5,320,128]{2,1,0:T(8,128)(2,1)S(1)}, u32[]{:S(2)}, u32[]{:S(2)}) collective-permute-start(bf16[5,320,128]{2,1,0:T(8,128)(2,1)S(1)} %get-tuple-element.51.refs_1_), channel_id=1, source_target_pairs={{0,16},{4,20},{8,24},{12,28},{16,0},{20,4},{24,8},{28,12},{32,48},... | collective-permute-start | bytes 1228808 | tf_op jit(solution)/shard_map/ppermute | solution.py:367
  77.1 6.4 %collective-permute-done.18.refs_2_ = bf16[5,320,128]{2,1,0:T(8,128)(2,1)S(1)} collective-permute-done((bf16[5,320,128]{2,1,0:T(8,128)(2,1)S(1)}, bf16[5,320,128]{2,1,0:T(8,128)(2,1)S(1)}, u32[]{:S(2)}, u32[]{:S(2)}) %collective-permute-start.18) | collective-permute-done | bytes 409632 | tf_op jit(solution)/shard_map/ppermute | solution.py:367
  84.3 1.8 %shard_map.107.refs_3_.refs_0_ = bf16[2,256,640]{2,1,0:T(8,128)(2,1)S(1)} custom-call(s32[5]{0:T(128)S(1)} %stack.23.refs_0_, bf16[160,128]{1,0:T(8,128)(2,1)S(1)} %collective-permute-done.15.refs_1_, bf16[160,128]{1,0:T(8,128)(2,1)S(1)} %shard_map.101.refs_0_.refs_2_, bf16[160,128]{1,0:T(8,128)(2,1)S(1)} %collective-permute-done.16.refs_2_.refs_3_, ...), custom_call_target="tpu_custom_call" | custom-call | flops 30000001024 | bytes 1966100 | tf_op jit(solution)/shard_map/pallas_call | solution.py:64
  86.1 3.9 %collective-permute-done.19.refs_2_ = bf16[3,160,128]{2,1,0:T(8,128)(2,1)S(1)} collective-permute-done((bf16[3,160,128]{2,1,0:T(8,128)(2,1)S(1)}, bf16[3,160,128]{2,1,0:T(8,128)(2,1)S(1)}, u32[]{:S(2)}, u32[]{:S(2)}) %collective-permute-start.19) | collective-permute-done | bytes 122912 | tf_op jit(solution)/shard_map/ppermute | solution.py:367
  90.6 2.7 %collective-permute-start.20 = (bf16[5,160,128]{2,1,0:T(8,128)(2,1)S(1)}, bf16[5,160,128]{2,1,0:T(8,128)(2,1)S(1)}, u32[]{:S(2)}, u32[]{:S(2)}) collective-permute-start(bf16[5,160,128]{2,1,0:T(8,128)(2,1)S(1)} %get-tuple-element.53.refs_7_.refs_1_), channel_id=1, source_target_pairs={{0,16},{4,20},{8,24},{12,28},{16,0},{20,4},{24,8},{28,12},{32,48},... | collective-permute-start | bytes 614408 | tf_op jit(solution)/shard_map/ppermute | solution.py:367
  93.3 2.9 %shard_map.110 = (bf16[2,96,320]{2,1,0:T(8,128)(2,1)S(1)}, bf16[2,96,320]{2,1,0:T(8,128)(2,1)S(1)}, bf16[2,96,320]{2,1,0:T(8,128)(2,1)S(1)}, bf16[2,96,320]{2,1,0:T(8,128)(2,1)S(1)}) custom-call(s32[5]{0:T(128)S(1)} %stack.23.refs_0_, bf16[5,320,128]{2,1,0:T(8,128)(2,1)S(1)} %get-tuple-element.51.refs_1_, ...), custom_call_target="tpu_custom_call" | custom-call | bytes 2580500 | tf_op jit(solution)/shard_map/pallas_call | solution.py:64
  96.2 2.9 %collective-permute-start.22 = (bf16[2,96,320]{2,1,0:T(8,128)(2,1)S(1)}, bf16[2,96,320]{2,1,0:T(8,128)(2,1)S(1)}, u32[]{:S(2)}, u32[]{:S(2)}) collective-permute-start(bf16[2,96,320]{2,1,0:T(8,128)(2,1)S(1)} %get-tuple-element.55), channel_id=1, source_target_pairs={{0,32},{4,36},{8,40},{12,44},{16,48},{20,52},{24,56},{28,60},{32,6... | collective-permute-start | bytes 368648 | tf_op jit(solution)/shard_map/ppermute | solution.py:425
  99.1 14.4 %collective-permute-start.23 = (bf16[2,96,320]{2,1,0:T(8,128)(2,1)S(1)}, bf16[2,96,320]{2,1,0:T(8,128)(2,1)S(1)}, u32[]{:S(2)}, u32[]{:S(2)}) collective-permute-start(bf16[2,96,320]{2,1,0:T(8,128)(2,1)S(1)} %get-tuple-element.56), channel_id=1, source_target_pairs={{0,64},{4,68},{8,72},{12,76},{16,80},{20,84},{24,88},{28,92},{32,9... | collective-permute-start | bytes 368648 | tf_op jit(solution)/shard_map/ppermute | solution.py:425
  113.6 2.9 %collective-permute-done.22.refs_2_ = bf16[2,96,320]{2,1,0:T(8,128)(2,1)S(1)} collective-permute-done((bf16[2,96,320]{2,1,0:T(8,128)(2,1)S(1)}, bf16[2,96,320]{2,1,0:T(8,128)(2,1)S(1)}, u32[]{:S(2)}, u32[]{:S(2)}) %collective-permute-start.22) | collective-permute-done | bytes 122912 | tf_op jit(solution)/shard_map/ppermute | solution.py:425
  116.5 4.9 %collective-permute-done.23.refs_3_ = bf16[2,96,320]{2,1,0:T(8,128)(2,1)S(1)} collective-permute-done((bf16[2,96,320]{2,1,0:T(8,128)(2,1)S(1)}, bf16[2,96,320]{2,1,0:T(8,128)(2,1)S(1)}, u32[]{:S(2)}, u32[]{:S(2)}) %collective-permute-start.23) | collective-permute-done | bytes 122912 | tf_op jit(solution)/shard_map/ppermute | solution.py:425
  123.8 5.9 %all-to-all-start.2 = ((bf16[4,2,64,640]{3,2,1,0:T(8,128)(2,1)}), bf16[4,2,64,640]{3,2,1,0:T(8,128)(2,1)}, u32[]{:S(2)}, u32[]{:S(2)}) async-start(bf16[4,2,64,640]{3,2,1,0:T(8,128)(2,1)} %shard_map.112), calls=%async_computation.2 | async-start | bytes 1310720 | tf_op jit(solution)/shard_map/all_to_all | solution.py:460
  130.9 2.2 %shard_map.113 = (bf16[2,96,160]{2,1,0:T(8,128)(2,1)S(1)}, bf16[2,96,160]{2,1,0:T(8,128)(2,1)S(1)}, bf16[2,96,160]{2,1,0:T(8,128)(2,1)S(1)}, bf16[2,96,160]{2,1,0:T(8,128)(2,1)S(1)}) custom-call(s32[5]{0:T(128)S(1)} %stack.23.refs_0_, bf16[5,160,128]{2,1,0:T(8,128)(2,1)S(1)} %get-tuple-element.53.refs_7_.refs_1_, ...), custom_call_target="tpu_custom_call" | custom-call | bytes 2580500 | tf_op jit(solution)/shard_map/pallas_call | solution.py:64
  134.7 3.0 %collective-permute-start.27 = (bf16[2,96,160]{2,1,0:T(8,128)(2,1)S(1)}, bf16[2,96,160]{2,1,0:T(8,128)(2,1)S(1)}, u32[]{:S(2)}, u32[]{:S(2)}) collective-permute-start(bf16[2,96,160]{2,1,0:T(8,128)(2,1)S(1)} %get-tuple-element.63), channel_id=1, source_target_pairs={{0,64},{4,68},{8,72},{12,76},{16,80},{20,84},{24,88},{28,92},{32,9... | collective-permute-start | bytes 184328 | tf_op jit(solution)/shard_map/ppermute | solution.py:425
  137.7 3.9 %collective-permute-start.30 = (bf16[96,320]{1,0:T(8,128)(2,1)S(1)}, bf16[96,320]{1,0:T(8,128)(2,1)S(1)}, u32[]{:S(2)}, u32[]{:S(2)}) collective-permute-start(bf16[96,320]{1,0:T(8,128)(2,1)S(1)} %get-tuple-element.67), channel_id=1, source_target_pairs={{0,128},{4,132},{8,136},{12,140},{16,144},{20,148},{24,152},{28,15... | collective-permute-start | bytes 184328 | tf_op jit(solution)/shard_map/ppermute | solution.py:367
  143.2 4.0 %collective-permute-start.29 = (bf16[96,160]{1,0:T(8,128)(2,1)S(1)}, bf16[96,160]{1,0:T(8,128)(2,1)S(1)}, u32[]{:S(2)}, u32[]{:S(2)}) collective-permute-start(bf16[96,160]{1,0:T(8,128)(2,1)S(1)} %get-tuple-element.66), channel_id=1, source_target_pairs={{0,128},{4,132},{8,136},{12,140},{16,144},{20,148},{24,152},{28,15... | collective-permute-start | bytes 92168 | tf_op jit(solution)/shard_map/ppermute | solution.py:367
  149.2 3.3 %collective-permute-done.29.refs_1_ = bf16[96,160]{1,0:T(8,128)(2,1)S(1)} collective-permute-done((bf16[96,160]{1,0:T(8,128)(2,1)S(1)}, bf16[96,160]{1,0:T(8,128)(2,1)S(1)}, u32[]{:S(2)}, u32[]{:S(2)}) %collective-permute-start.29) | collective-permute-done | bytes 30752 | tf_op jit(solution)/shard_map/ppermute | solution.py:367
  (84 shorter events, 30.2 us)
Async XLA Ops:
  0.6 11.1 %collective-permute-start.1 = (bf16[2,64,640]{2,1,0:T(8,128)(2,1)}, bf16[2,64,640]{2,1,0:T(8,128)(2,1)S(1)}, u32[]{:S(2)}, u32[]{:S(2)}) collective-permute-start(bf16[2,64,640]{2,1,0:T(8,128)(2,1)} %refs_1_.3), channel_id=1, source_target_pairs={{0,2},{1,3},{2,0},{3,1},{4,6},{5,7},{6,4},{7,5},{8,10},{9,11},{10,... | collective-permute-start | bytes 491528 | tf_op jit(solution)/shard_map/ppermute | solution.py:364
  4.0 13.9 %collective-permute-start = (bf16[2,64,640]{2,1,0:T(8,128)(2,1)}, bf16[2,64,640]{2,1,0:T(8,128)(2,1)S(1)}, u32[]{:S(2)}, u32[]{:S(2)}) collective-permute-start(bf16[2,64,640]{2,1,0:T(8,128)(2,1)} %refs_1_.3), channel_id=1, source_target_pairs={{0,1},{1,2},{2,3},{3,0},{4,5},{5,6},{6,7},{7,4},{8,9},{9,10},{10,1... | collective-permute-start | bytes 491528 | tf_op jit(solution)/shard_map/ppermute | solution.py:364
  4.0 13.8 %collective-permute-start.2 = (bf16[2,64,640]{2,1,0:T(8,128)(2,1)}, bf16[2,64,640]{2,1,0:T(8,128)(2,1)S(1)}, u32[]{:S(2)}, u32[]{:S(2)}) collective-permute-start(bf16[2,64,640]{2,1,0:T(8,128)(2,1)} %refs_1_.3), channel_id=1, source_target_pairs={{0,3},{1,0},{2,1},{3,2},{4,7},{5,4},{6,5},{7,6},{8,11},{9,8},{10,9... | collective-permute-start | bytes 491528 | tf_op jit(solution)/shard_map/ppermute | solution.py:364
  22.3 9.8 %collective-permute-start.4 = (bf16[160,128]{1,0:T(8,128)(2,1)S(1)}, bf16[160,128]{1,0:T(8,128)(2,1)S(1)}, u32[]{:S(2)}, u32[]{:S(2)}) collective-permute-start(bf16[160,128]{1,0:T(8,128)(2,1)S(1)} %get-tuple-element.38), channel_id=1, source_target_pairs={{4,8},{8,4},{12,16},{16,12},{20,24},{24,20},{28,32},{32,28},{36,40... | collective-permute-start | bytes 122888 | tf_op jit(solution)/shard_map/ppermute | solution.py:370
  26.1 17.7 %all-to-all-start = ((bf16[8,80,512]{2,1,0:T(8,128)(2,1)}), bf16[8,80,512]{2,1,0:T(8,128)(2,1)S(1)}, u32[]{:S(2)}, u32[]{:S(2)}) async-start(bf16[8,80,512]{2,1,0:T(8,128)(2,1)} %shard_map.94.refs_3_), calls=%async_computation | async-start | bytes 1310720 | tf_op jit(solution)/shard_map/all_to_all | solution.py:387
  32.2 5.3 %collective-permute-start.7 = (bf16[160,128]{1,0:T(8,128)(2,1)S(1)}, bf16[160,128]{1,0:T(8,128)(2,1)S(1)}, u32[]{:S(2)}, u32[]{:S(2)}) collective-permute-start(bf16[160,128]{1,0:T(8,128)(2,1)S(1)} %shard_map.95.refs_1_), channel_id=1, source_target_pairs={{0,3},{1,0},{2,1},{3,2},{4,7},{5,4},{6,5},{7,6},{8,11},{9,8},{10,9... | collective-permute-start | bytes 122888 | tf_op jit(solution)/shard_map/ppermute | solution.py:364
  32.2 6.6 %collective-permute-start.6 = (bf16[160,128]{1,0:T(8,128)(2,1)S(1)}, bf16[160,128]{1,0:T(8,128)(2,1)S(1)}, u32[]{:S(2)}, u32[]{:S(2)}) collective-permute-start(bf16[160,128]{1,0:T(8,128)(2,1)S(1)} %shard_map.95.refs_1_), channel_id=1, source_target_pairs={{0,2},{1,3},{2,0},{3,1},{4,6},{5,7},{6,4},{7,5},{8,10},{9,11},{10,... | collective-permute-start | bytes 122888 | tf_op jit(solution)/shard_map/ppermute | solution.py:364
  36.1 4.0 %collective-permute-start.5 = (bf16[160,128]{1,0:T(8,128)(2,1)S(1)}, bf16[160,128]{1,0:T(8,128)(2,1)S(1)}, u32[]{:S(2)}, u32[]{:S(2)}) collective-permute-start(bf16[160,128]{1,0:T(8,128)(2,1)S(1)} %shard_map.95.refs_1_), channel_id=1, source_target_pairs={{0,1},{1,2},{2,3},{3,0},{4,5},{5,6},{6,7},{7,4},{8,9},{9,10},{10,1... | collective-permute-start | bytes 122888 | tf_op jit(solution)/shard_map/ppermute | solution.py:364
  41.5 4.9 %collective-permute-start.8 = (bf16[320,128]{1,0:T(8,128)(2,1)S(1)}, bf16[320,128]{1,0:T(8,128)(2,1)S(1)}, u32[]{:S(2)}, u32[]{:S(2)}) collective-permute-start(bf16[320,128]{1,0:T(8,128)(2,1)S(1)} %get-tuple-element.41), channel_id=1, source_target_pairs={{0,4},{4,0},{8,12},{12,8},{16,20},{20,16},{24,28},{28,24},{32,36},... | collective-permute-start | bytes 245768 | tf_op jit(solution)/shard_map/ppermute | solution.py:367
  41.6 4.8 %collective-permute-start.9 = (bf16[320,128]{1,0:T(8,128)(2,1)S(1)}, bf16[320,128]{1,0:T(8,128)(2,1)S(1)}, u32[]{:S(2)}, u32[]{:S(2)}) collective-permute-start(bf16[320,128]{1,0:T(8,128)(2,1)S(1)} %get-tuple-element.42), channel_id=1, source_target_pairs={{4,8},{8,4},{12,16},{16,12},{20,24},{24,20},{28,32},{32,28},{36,40... | collective-permute-start | bytes 245768 | tf_op jit(solution)/shard_map/ppermute | solution.py:370
  47.5 2.7 %collective-permute-start.10 = (bf16[320,128]{1,0:T(8,128)(2,1)S(1)}, bf16[320,128]{1,0:T(8,128)(2,1)S(1)}, u32[]{:S(2)}, u32[]{:S(2)}) collective-permute-start(bf16[320,128]{1,0:T(8,128)(2,1)S(1)} %get-tuple-element.44.refs_2_.refs_0_), channel_id=1, source_target_pairs={{0,4},{4,0},{8,12},{12,8},{16,20},{20,16},{24,28},{28,24},{32,36},... | collective-permute-start | bytes 245768 | tf_op jit(solution)/shard_map/ppermute | solution.py:367
  49.2 10.2 %collective-permute-start.11 = (bf16[320,128]{1,0:T(8,128)(2,1)S(1)}, bf16[320,128]{1,0:T(8,128)(2,1)S(1)}, u32[]{:S(2)}, u32[]{:S(2)}) collective-permute-start(bf16[320,128]{1,0:T(8,128)(2,1)S(1)} %get-tuple-element.44.refs_2_.refs_0_), channel_id=1, source_target_pairs={{4,8},{8,4},{12,16},{16,12},{20,24},{24,20},{28,32},{32,28},{36,40... | collective-permute-start | bytes 245768 | tf_op jit(solution)/shard_map/ppermute | solution.py:370
  51.2 23.7 %all-to-all-start.1 = ((bf16[8,80,128]{2,1,0:T(8,128)(2,1)}), bf16[8,80,128]{2,1,0:T(8,128)(2,1)S(1)}, u32[]{:S(2)}, u32[]{:S(2)}) async-start(bf16[8,80,128]{2,1,0:T(8,128)(2,1)} %shard_map.100), calls=%async_computation.1 | async-start | bytes 327680 | tf_op jit(solution)/shard_map/all_to_all | solution.py:405
  59.5 10.8 %collective-permute-start.17 = (bf16[3,320,128]{2,1,0:T(8,128)(2,1)S(1)}, bf16[3,320,128]{2,1,0:T(8,128)(2,1)S(1)}, u32[]{:S(2)}, u32[]{:S(2)}) collective-permute-start(bf16[3,320,128]{2,1,0:T(8,128)(2,1)S(1)} %shard_map.103.refs_1_), channel_id=1, source_target_pairs={{0,8},{4,12},{8,0},{12,4},{16,24},{20,28},{24,16},{28,20},{32,40},... | collective-permute-start | bytes 737288 | tf_op jit(solution)/shard_map/ppermute | solution.py:367
  65.6 4.7 %collective-permute-start.12 = (bf16[160,128]{1,0:T(8,128)(2,1)S(1)}, bf16[160,128]{1,0:T(8,128)(2,1)S(1)}, u32[]{:S(2)}, u32[]{:S(2)}) collective-permute-start(bf16[160,128]{1,0:T(8,128)(2,1)S(1)} %get-tuple-element.46), channel_id=1, source_target_pairs={{0,1},{1,2},{2,3},{3,0},{4,5},{5,6},{6,7},{7,4},{8,9},{9,10},{10,1... | collective-permute-start | bytes 122888 | tf_op jit(solution)/shard_map/ppermute | solution.py:364
  66.9 6.6 %collective-permute-start.13 = (bf16[160,128]{1,0:T(8,128)(2,1)S(1)}, bf16[160,128]{1,0:T(8,128)(2,1)S(1)}, u32[]{:S(2)}, u32[]{:S(2)}) collective-permute-start(bf16[160,128]{1,0:T(8,128)(2,1)S(1)} %get-tuple-element.47), channel_id=1, source_target_pairs={{0,2},{1,3},{2,0},{3,1},{4,6},{5,7},{6,4},{7,5},{8,10},{9,11},{10,... | collective-permute-start | bytes 122888 | tf_op jit(solution)/shard_map/ppermute | solution.py:364
  70.1 4.9 %collective-permute-start.14 = (bf16[160,128]{1,0:T(8,128)(2,1)S(1)}, bf16[160,128]{1,0:T(8,128)(2,1)S(1)}, u32[]{:S(2)}, u32[]{:S(2)}) collective-permute-start(bf16[160,128]{1,0:T(8,128)(2,1)S(1)} %get-tuple-element.48), channel_id=1, source_target_pairs={{0,3},{1,0},{2,1},{3,2},{4,7},{5,4},{6,5},{7,6},{8,11},{9,8},{10,9... | collective-permute-start | bytes 122888 | tf_op jit(solution)/shard_map/ppermute | solution.py:364
  70.8 12.7 %collective-permute-start.18 = (bf16[5,320,128]{2,1,0:T(8,128)(2,1)S(1)}, bf16[5,320,128]{2,1,0:T(8,128)(2,1)S(1)}, u32[]{:S(2)}, u32[]{:S(2)}) collective-permute-start(bf16[5,320,128]{2,1,0:T(8,128)(2,1)S(1)} %get-tuple-element.51.refs_1_), channel_id=1, source_target_pairs={{0,16},{4,20},{8,24},{12,28},{16,0},{20,4},{24,8},{28,12},{32,48},... | collective-permute-start | bytes 1228808 | tf_op jit(solution)/shard_map/ppermute | solution.py:367
  75.0 9.2 %collective-permute-start.16 = (bf16[160,128]{1,0:T(8,128)(2,1)S(1)}, bf16[160,128]{1,0:T(8,128)(2,1)S(1)}, u32[]{:S(2)}, u32[]{:S(2)}) collective-permute-start(bf16[160,128]{1,0:T(8,128)(2,1)S(1)} %shard_map.101.refs_0_.refs_2_), channel_id=1, source_target_pairs={{4,8},{8,4},{12,16},{16,12},{20,24},{24,20},{28,32},{32,28},{36,40... | collective-permute-start | bytes 122888 | tf_op jit(solution)/shard_map/ppermute | solution.py:370
  75.8 8.4 %collective-permute-start.15 = (bf16[160,128]{1,0:T(8,128)(2,1)S(1)}, bf16[160,128]{1,0:T(8,128)(2,1)S(1)}, u32[]{:S(2)}, u32[]{:S(2)}) collective-permute-start(bf16[160,128]{1,0:T(8,128)(2,1)S(1)} %shard_map.101.refs_0_.refs_2_), channel_id=1, source_target_pairs={{0,4},{4,0},{8,12},{12,8},{16,20},{20,16},{24,28},{28,24},{32,36},... | collective-permute-start | bytes 122888 | tf_op jit(solution)/shard_map/ppermute | solution.py:367
  84.1 9.2 %collective-permute-start.21 = (bf16[320,128]{1,0:T(8,128)(2,1)S(1)}, bf16[320,128]{1,0:T(8,128)(2,1)S(1)}, u32[]{:S(2)}, u32[]{:S(2)}) collective-permute-start(bf16[320,128]{1,0:T(8,128)(2,1)S(1)} %shard_map.105.refs_4_.refs_3_), channel_id=1, source_target_pairs={{0,4},{4,0},{8,12},{12,8},{16,20},{20,16},{24,28},{28,24},{32,36},... | collective-permute-start | bytes 245768 | tf_op jit(solution)/shard_map/ppermute | solution.py:367
  84.2 5.8 %collective-permute-start.19 = (bf16[3,160,128]{2,1,0:T(8,128)(2,1)S(1)}, bf16[3,160,128]{2,1,0:T(8,128)(2,1)S(1)}, u32[]{:S(2)}, u32[]{:S(2)}) collective-permute-start(bf16[3,160,128]{2,1,0:T(8,128)(2,1)S(1)} %shard_map.106.refs_5_.refs_1_), channel_id=1, source_target_pairs={{0,8},{4,12},{8,0},{12,4},{16,24},{20,28},{24,16},{28,20},{32,40},... | collective-permute-start | bytes 368648 | tf_op jit(solution)/shard_map/ppermute | solution.py:367
  90.6 31.5 %collective-permute-start.20 = (bf16[5,160,128]{2,1,0:T(8,128)(2,1)S(1)}, bf16[5,160,128]{2,1,0:T(8,128)(2,1)S(1)}, u32[]{:S(2)}, u32[]{:S(2)}) collective-permute-start(bf16[5,160,128]{2,1,0:T(8,128)(2,1)S(1)} %get-tuple-element.53.refs_7_.refs_1_), channel_id=1, source_target_pairs={{0,16},{4,20},{8,24},{12,28},{16,0},{20,4},{24,8},{28,12},{32,48},... | collective-permute-start | bytes 614408 | tf_op jit(solution)/shard_map/ppermute | solution.py:367
  96.2 20.3 %collective-permute-start.22 = (bf16[2,96,320]{2,1,0:T(8,128)(2,1)S(1)}, bf16[2,96,320]{2,1,0:T(8,128)(2,1)S(1)}, u32[]{:S(2)}, u32[]{:S(2)}) collective-permute-start(bf16[2,96,320]{2,1,0:T(8,128)(2,1)S(1)} %get-tuple-element.55), channel_id=1, source_target_pairs={{0,32},{4,36},{8,40},{12,44},{16,48},{20,52},{24,56},{28,60},{32,6... | collective-permute-start | bytes 368648 | tf_op jit(solution)/shard_map/ppermute | solution.py:425
  99.1 22.3 %collective-permute-start.23 = (bf16[2,96,320]{2,1,0:T(8,128)(2,1)S(1)}, bf16[2,96,320]{2,1,0:T(8,128)(2,1)S(1)}, u32[]{:S(2)}, u32[]{:S(2)}) collective-permute-start(bf16[2,96,320]{2,1,0:T(8,128)(2,1)S(1)} %get-tuple-element.56), channel_id=1, source_target_pairs={{0,64},{4,68},{8,72},{12,76},{16,80},{20,84},{24,88},{28,92},{32,9... | collective-permute-start | bytes 368648 | tf_op jit(solution)/shard_map/ppermute | solution.py:425
  113.6 7.8 %collective-permute-start.24 = (bf16[2,96,320]{2,1,0:T(8,128)(2,1)S(1)}, bf16[2,96,320]{2,1,0:T(8,128)(2,1)S(1)}, u32[]{:S(2)}, u32[]{:S(2)}) collective-permute-start(bf16[2,96,320]{2,1,0:T(8,128)(2,1)S(1)} %get-tuple-element.57), channel_id=1, source_target_pairs={{0,96},{4,100},{8,104},{12,108},{16,112},{20,116},{24,120},{28,124... | collective-permute-start | bytes 368648 | tf_op jit(solution)/shard_map/ppermute | solution.py:425
  123.8 24.1 %all-to-all-start.2 = ((bf16[4,2,64,640]{3,2,1,0:T(8,128)(2,1)}), bf16[4,2,64,640]{3,2,1,0:T(8,128)(2,1)}, u32[]{:S(2)}, u32[]{:S(2)}) async-start(bf16[4,2,64,640]{3,2,1,0:T(8,128)(2,1)} %shard_map.112), calls=%async_computation.2 | async-start | bytes 1310720 | tf_op jit(solution)/shard_map/all_to_all | solution.py:460
  133.2 8.4 %collective-permute-start.26 = (bf16[2,96,160]{2,1,0:T(8,128)(2,1)S(1)}, bf16[2,96,160]{2,1,0:T(8,128)(2,1)S(1)}, u32[]{:S(2)}, u32[]{:S(2)}) collective-permute-start(bf16[2,96,160]{2,1,0:T(8,128)(2,1)S(1)} %get-tuple-element.62), channel_id=1, source_target_pairs={{0,32},{4,36},{8,40},{12,44},{16,48},{20,52},{24,56},{28,60},{32,6... | collective-permute-start | bytes 184328 | tf_op jit(solution)/shard_map/ppermute | solution.py:425
  134.7 7.9 %collective-permute-start.27 = (bf16[2,96,160]{2,1,0:T(8,128)(2,1)S(1)}, bf16[2,96,160]{2,1,0:T(8,128)(2,1)S(1)}, u32[]{:S(2)}, u32[]{:S(2)}) collective-permute-start(bf16[2,96,160]{2,1,0:T(8,128)(2,1)S(1)} %get-tuple-element.63), channel_id=1, source_target_pairs={{0,64},{4,68},{8,72},{12,76},{16,80},{20,84},{24,88},{28,92},{32,9... | collective-permute-start | bytes 184328 | tf_op jit(solution)/shard_map/ppermute | solution.py:425
  137.7 4.9 %collective-permute-start.28 = (bf16[2,96,160]{2,1,0:T(8,128)(2,1)S(1)}, bf16[2,96,160]{2,1,0:T(8,128)(2,1)S(1)}, u32[]{:S(2)}, u32[]{:S(2)}) collective-permute-start(bf16[2,96,160]{2,1,0:T(8,128)(2,1)S(1)} %get-tuple-element.64), channel_id=1, source_target_pairs={{0,96},{4,100},{8,104},{12,108},{16,112},{20,116},{24,120},{28,124... | collective-permute-start | bytes 184328 | tf_op jit(solution)/shard_map/ppermute | solution.py:425
  137.7 9.5 %collective-permute-start.30 = (bf16[96,320]{1,0:T(8,128)(2,1)S(1)}, bf16[96,320]{1,0:T(8,128)(2,1)S(1)}, u32[]{:S(2)}, u32[]{:S(2)}) collective-permute-start(bf16[96,320]{1,0:T(8,128)(2,1)S(1)} %get-tuple-element.67), channel_id=1, source_target_pairs={{0,128},{4,132},{8,136},{12,140},{16,144},{20,148},{24,152},{28,15... | collective-permute-start | bytes 184328 | tf_op jit(solution)/shard_map/ppermute | solution.py:367
  143.2 9.3 %collective-permute-start.29 = (bf16[96,160]{1,0:T(8,128)(2,1)S(1)}, bf16[96,160]{1,0:T(8,128)(2,1)S(1)}, u32[]{:S(2)}, u32[]{:S(2)}) collective-permute-start(bf16[96,160]{1,0:T(8,128)(2,1)S(1)} %get-tuple-element.66), channel_id=1, source_target_pairs={{0,128},{4,132},{8,136},{12,140},{16,144},{20,148},{24,152},{28,15... | collective-permute-start | bytes 92168 | tf_op jit(solution)/shard_map/ppermute | solution.py:367
  (12 other events, 43.6 us)

commit v11 on v10

--- a/solution.py
+++ b/solution.py
@@ -277,10 +277,18 @@
         out[...] = far[4]
 
 
-def group_rows(at, four, far, edge, swapped, grads):
-    for r in range(4):
-        grads[jnp.bitwise_xor(at[1], r) + 1] = four[r]
-        grads[jnp.bitwise_xor(at[1], 4 + r) + 1] = far[r]
+def outer_direct(at, own, near, far, both, out):
+    source = jnp.bitwise_xor(at[1] // 2, 3 * at[0])
+    for i, rows in enumerate((own, near, far, both)):
+
+        @pl.when(source == i)
+        def _(rows=rows):
+            out[...] = rows[2]
+
+
+def group_rows(at, rows, edge, swapped, grads):
+    for r, row in enumerate(rows):
+        grads[jnp.bitwise_xor(at[1], r) + 1] = row[...]
     ends = (MEMBERS + 1) * at[0]
     grads[ends] = edge[...]
     grads[MEMBERS + 1 - ends] = swapped[...]
@@ -302,13 +310,15 @@
 
 
 def deep_part(at, four, far, edge, swapped, table, order, out0, out1, out2, out3, grads, parts):
-    group_rows(at, four, far, edge, swapped, grads)
+    rows = [four.at[r] for r in range(4)] + [far.at[r] for r in range(4)]
+    group_rows(at, rows, edge, swapped, grads)
     taps = [against(table, grads, 1 - a) for a in range(3)]
     to_owners(at, taps, order, (out0, out1, out2, out3), parts)
 
 
-def fine_part(at, four, far, edge, swapped, even, late, order, out0, out1, out2, out3, grads, parts):
-    group_rows(at, four, far, edge, swapped, grads)
+def fine_part(at, own, near, far, both, edge, swapped, even, late, order, out0, out1, out2, out3, grads, parts):
+    rows = [rows.at[r] for rows in (own, near, far, both) for r in range(2)]
+    group_rows(at, rows, edge, swapped, grads)
     even_here = against(even, grads, 0)
     late_here = against(late, grads, 0)
     taps = (even_here + against(late, grads, 1), even_here + late_here, late_here + against(even, grads, -1))
@@ -436,7 +446,7 @@
         return total.reshape(3, 3, grain, width)
 
     def products(body, tables, rows, behind=()):
-        width = rows[0].shape[1]
+        width = rows[-1].shape[0]
         return call(
             body,
             [shape((2, block, width))] * 4,
@@ -452,11 +462,13 @@
         [pltpu.VMEM((2, fine, deep), BF)],
         behind=(pool_first,),
     )
-    pool_rows = group_gather(pool_first, (sides,))
-    deep_parts = products(deep_part, (deep_table,), pre_rows, (pool_rows[0],))
+    deep_parts = products(deep_part, (deep_table,), pre_rows, (pool_first,))
+    pool_rows = [pool_first] + [swap(pool_first, bit) for bit in (2, 4, 6)]
+    pool_edge = call(outer_direct, shape((fine, deep)), (at, *pool_rows), behind=(sides, deep_parts[0]))
+    pool_rows += [pool_edge, swap(pool_edge, 1)]
     fine_parts = products(fine_part, (even_table, late_table), pool_rows)
     deep_half = halves(deep_parts)
-    back = call(weave, shape((pieces, rows, part, depth)), (sides,), behind=(pool_rows[2], deep_half[0]))
+    back = call(weave, shape((pieces, rows, part, depth)), (sides,), behind=(pool_edge,))
     partial = lax.all_to_all(back, "narrow", 0, 0)
     grad_latent = jnp.sum(partial.astype(F32), axis=0).astype(BF)
 

time: 155 us -> 153 us (0.987)
  waiting for transfers between devices: 43.4 us -> 36 us
  starting transfers between devices: 76.6 us -> 83.2 us
    ppermute x6, waiting for transfers between devices: 8.92 us -> 0.02 us  [halves(): lax.ppermute(parts[s], 'wide', [(i, i // 32 * 32 + (i // 8 + s) % 4 * 8 +...]
    ppermute x12 -> x13, starting transfers between devices: 18.1 us -> 23.3 us  [swap(): return lax.ppermute(v, 'wide', [(i, i ^ bit) for i in range(wide)])]
    ppermute x6, starting transfers between devices: 21.9 us -> 23.9 us  [halves(): lax.ppermute(parts[s], 'wide', [(i, i // 32 * 32 + (i // 8 + s) % 4 * 8 +...]
    ppermute x12 -> x13, waiting for transfers between devices: 15.6 us -> 17 us  [swap(): return lax.ppermute(v, 'wide', [(i, i ^ bit) for i in range(wide)])]
    unnamed x22 -> x30, local copies, waits for them, and re-layouts: 8.38 us -> 9.05 us
    pallas_call x24 -> x23, Pallas kernels: 22.6 us -> 22 us  [call(): pl.pallas_call(kernel, out_shape=outs, in_specs=[smem if a.dtype == jnp.i...]
  transfers between devices with their start and end apart: 34 -> 35, of which waited for: 17 -> 15; matrix products, arithmetic and copies ran while one was open for 1% -> 1% of each run, Pallas kernels for 12% -> 12%
where the time goes in v11:
time: 153 us; the launch traced here: 152 us
  starting transfers between devices  83.2 us (54%)
  waiting for transfers between devices  36 us (24%)
  Pallas kernels  22 us (14%)
  local copies, waits for them, and re-layouts  9.13 us (6%)
    ppermute x6, starting transfers between devices, halves(): lax.ppermute(parts[s], 'wide', [(i, i // 32 * 32 + (i // 8 + s) % 4 * 8 +...  23.9 us
    ppermute x13, starting transfers between devices, swap(): return lax.ppermute(v, 'wide', [(i, i ^ bit) for i in range(wide)])  23.3 us
    pallas_call x23, Pallas kernels, call(): pl.pallas_call(kernel, out_shape=outs, in_specs=[smem if a.dtype == jnp.i...  22 us
    ppermute x13, waiting for transfers between devices, swap(): return lax.ppermute(v, 'wide', [(i, i ^ bit) for i in range(wide)])  17 us
    ppermute x9, waiting for transfers between devices, across(): lax.ppermute(v, 'narrow', [(i, (i + step) % pieces) for i in range(pieces)])  16.7 us
    ppermute x9, starting transfers between devices, across(): lax.ppermute(v, 'narrow', [(i, (i + step) % pieces) for i in range(pieces)])  13.5 us
    unnamed x30, local copies, waits for them, and re-layouts  9.05 us
    all_to_all x1, starting transfers between devices, on_device(): deep_slab = lax.all_to_all(deep_slab, 'wide', 0, 0, axis_index_groups=near)  7.31 us
  transfers between devices with their start and end apart: 35, of which 15 were waited for; matrix products, arithmetic and copies ran while one was open for 1% of the time, Pallas kernels for 12%

profile of v11, /device:TPU:32, one launch (start us, length us, event | category | flops | bytes accessed | tf_op | source)
XLA Modules:
  0.0 152.4 jit_solution(735503209351716668)
XLA Ops:
  0.6 2.0 %collective-permute-start = (bf16[2,64,640]{2,1,0:T(8,128)(2,1)}, bf16[2,64,640]{2,1,0:T(8,128)(2,1)S(1)}, u32[]{:S(2)}, u32[]{:S(2)}) collective-permute-start(bf16[2,64,640]{2,1,0:T(8,128)(2,1)} %refs_1_.3), channel_id=1, source_target_pairs={{0,1},{1,2},{2,3},{3,0},{4,5},{5,6},{6,7},{7,4},{8,9},{9,10},{10,1... | collective-permute-start | bytes 491528 | tf_op jit(solution)/shard_map/ppermute | solution.py:374
  2.6 2.3 %collective-permute-start.1 = (bf16[2,64,640]{2,1,0:T(8,128)(2,1)}, bf16[2,64,640]{2,1,0:T(8,128)(2,1)S(1)}, u32[]{:S(2)}, u32[]{:S(2)}) collective-permute-start(bf16[2,64,640]{2,1,0:T(8,128)(2,1)} %refs_1_.3), channel_id=1, source_target_pairs={{0,2},{1,3},{2,0},{3,1},{4,6},{5,7},{6,4},{7,5},{8,10},{9,11},{10,... | collective-permute-start | bytes 491528 | tf_op jit(solution)/shard_map/ppermute | solution.py:374
  6.1 8.5 %collective-permute-done.refs_2_ = bf16[2,64,640]{2,1,0:T(8,128)(2,1)S(1)} collective-permute-done((bf16[2,64,640]{2,1,0:T(8,128)(2,1)}, bf16[2,64,640]{2,1,0:T(8,128)(2,1)S(1)}, u32[]{:S(2)}, u32[]{:S(2)}) %collective-permute-start) | collective-permute-done | bytes 163872 | tf_op jit(solution)/shard_map/ppermute | solution.py:374
  14.6 2.4 %collective-permute-done.1.refs_3_ = bf16[2,64,640]{2,1,0:T(8,128)(2,1)S(1)} collective-permute-done((bf16[2,64,640]{2,1,0:T(8,128)(2,1)}, bf16[2,64,640]{2,1,0:T(8,128)(2,1)S(1)}, u32[]{:S(2)}, u32[]{:S(2)}) %collective-permute-start.1) | collective-permute-done | bytes 163872 | tf_op jit(solution)/shard_map/ppermute | solution.py:374
  16.9 2.0 %collective-permute-done.2.refs_4_ = bf16[2,64,640]{2,1,0:T(8,128)(2,1)S(1)} collective-permute-done((bf16[2,64,640]{2,1,0:T(8,128)(2,1)}, bf16[2,64,640]{2,1,0:T(8,128)(2,1)S(1)}, u32[]{:S(2)}, u32[]{:S(2)}) %collective-permute-start.2) | collective-permute-done | bytes 163872 | tf_op jit(solution)/shard_map/ppermute | solution.py:374
  21.3 1.9 %shard_map.93 = (bf16[4,2,64,640]{3,2,1,0:T(8,128)(2,1)S(1)}, f32[160,128]{1,0:T(8,128)S(1)}, bf16[160,128]{1,0:T(8,128)(2,1)S(1)}, bf16[160,128]{1,0:T(8,128)(2,1)S(1)}) custom-call(s32[5]{0:T(128)S(1)} %stack.23.refs_0_, bf16[2,64,640]{2,1,0:T(8,128)(2,1)S(1)} %copy-done.10, bf16[2,64,640]{2,1,0:T(8,128)(2,1)S(1)} %collective-permute-done.refs_2_, ...), custom_call_target="tpu_custom_call" | custom-call | flops 30000001024 | bytes 2498580 | tf_op jit(solution)/shard_map/pallas_call | solution.py:64
  24.6 2.6 %shard_map.94.refs_3_ = bf16[8,80,512]{2,1,0:T(8,128)(2,1)} custom-call(bf16[4,2,64,640]{3,2,1,0:T(8,128)(2,1)S(1)} %get-tuple-element.37.refs_0_, bf16[640,640]{1,0:T(8,128)(2,1)S(1)} %copy-done.4, bf16[160,128]{1,0:T(8,128)(2,1)S(1)} %collective-permute-done.3.refs_2_.refs_1_), custom_call_target="tpu_custom_call" | custom-call | bytes 1474560 | tf_op jit(solution)/shard_map/pallas_call | solution.py:64
  27.2 6.0 %all-to-all-start = ((bf16[8,80,512]{2,1,0:T(8,128)(2,1)}), bf16[8,80,512]{2,1,0:T(8,128)(2,1)S(1)}, u32[]{:S(2)}, u32[]{:S(2)}) async-start(bf16[8,80,512]{2,1,0:T(8,128)(2,1)} %shard_map.94.refs_3_), calls=%async_computation | async-start | bytes 1310720 | tf_op jit(solution)/shard_map/all_to_all | solution.py:397
  34.7 1.9 %collective-permute-start.7 = (bf16[160,128]{1,0:T(8,128)(2,1)S(1)}, bf16[160,128]{1,0:T(8,128)(2,1)S(1)}, u32[]{:S(2)}, u32[]{:S(2)}) collective-permute-start(bf16[160,128]{1,0:T(8,128)(2,1)S(1)} %shard_map.95.refs_1_), channel_id=1, source_target_pairs={{0,3},{1,0},{2,1},{3,2},{4,7},{5,4},{6,5},{7,6},{8,11},{9,8},{10,9... | collective-permute-start | bytes 122888 | tf_op jit(solution)/shard_map/ppermute | solution.py:374
  38.8 1.7 %collective-permute-done.7.refs_4_ = bf16[160,128]{1,0:T(8,128)(2,1)S(1)} collective-permute-done((bf16[160,128]{1,0:T(8,128)(2,1)S(1)}, bf16[160,128]{1,0:T(8,128)(2,1)S(1)}, u32[]{:S(2)}, u32[]{:S(2)}) %collective-permute-start.7) | collective-permute-done | bytes 40992 | tf_op jit(solution)/shard_map/ppermute | solution.py:374
  42.6 2.3 %all-to-all-done.refs_2_.refs_0_ = bf16[8,80,512]{2,1,0:T(8,128)(2,1)S(1)} async-done(((bf16[8,80,512]{2,1,0:T(8,128)(2,1)}), bf16[8,80,512]{2,1,0:T(8,128)(2,1)S(1)}, u32[]{:S(2)}, u32[]{:S(2)}) %all-to-all-start) | async-done | bytes 655392 | tf_op jit(solution)/shard_map/all_to_all | solution.py:397
  44.9 2.0 %copy-done.1 = bf16[3,3,640,320]{2,3,1,0:T(8,128)(2,1)S(1)} copy-done((bf16[3,3,640,320]{2,3,1,0:T(8,128)(2,1)S(1)}, bf16[3,3,640,320]{2,3,1,0:T(8,128)(2,1)}, u32[]{:S(2)}) %copy-start.1) | copy-done | bytes 3686424
  49.8 6.3 %collective-permute-start.17 = (bf16[3,320,128]{2,1,0:T(8,128)(2,1)S(1)}, bf16[3,320,128]{2,1,0:T(8,128)(2,1)S(1)}, u32[]{:S(2)}, u32[]{:S(2)}) collective-permute-start(bf16[3,320,128]{2,1,0:T(8,128)(2,1)S(1)} %shard_map.103.refs_1_), channel_id=1, source_target_pairs={{0,8},{4,12},{8,0},{12,4},{16,24},{20,28},{24,16},{28,20},{32,40},... | collective-permute-start | bytes 737288 | tf_op jit(solution)/shard_map/ppermute | solution.py:377
  57.2 7.3 %all-to-all-start.1 = ((bf16[8,80,128]{2,1,0:T(8,128)(2,1)}), bf16[8,80,128]{2,1,0:T(8,128)(2,1)S(1)}, u32[]{:S(2)}, u32[]{:S(2)}) async-start(bf16[8,80,128]{2,1,0:T(8,128)(2,1)} %shard_map.100), calls=%async_computation.1 | async-start | bytes 327680 | tf_op jit(solution)/shard_map/all_to_all | solution.py:415
  64.5 2.0 %copy-done.2 = bf16[3,3,640,320]{2,3,1,0:T(8,128)(2,1)S(1)} copy-done((bf16[3,3,640,320]{2,3,1,0:T(8,128)(2,1)S(1)}, bf16[3,3,640,320]{2,3,1,0:T(8,128)(2,1)}, u32[]{:S(2)}) %copy-start.2) | copy-done | bytes 3686424
  66.6 1.9 %shard_map.99 = (bf16[160,128]{1,0:T(8,128)(2,1)S(1)}, bf16[160,128]{1,0:T(8,128)(2,1)S(1)}, bf16[160,128]{1,0:T(8,128)(2,1)S(1)}, bf16[160,128]{1,0:T(8,128)(2,1)S(1)}) custom-call(s32[5]{0:T(128)S(1)} %stack.23.refs_0_, bf16[320,128]{1,0:T(8,128)(2,1)S(1)} %collective-permute-done.10.refs_1_.refs_2_, ...), custom_call_target="tpu_custom_call" | custom-call | flops 30000001024 | bytes 3932180 | tf_op jit(solution)/shard_map/pallas_call | solution.py:64
  69.9 2.4 %collective-permute-start.13 = (bf16[160,128]{1,0:T(8,128)(2,1)S(1)}, bf16[160,128]{1,0:T(8,128)(2,1)S(1)}, u32[]{:S(2)}, u32[]{:S(2)}) collective-permute-start(bf16[160,128]{1,0:T(8,128)(2,1)S(1)} %get-tuple-element.45), channel_id=1, source_target_pairs={{0,2},{1,3},{2,0},{3,1},{4,6},{5,7},{6,4},{7,5},{8,10},{9,11},{10,... | collective-permute-start | bytes 122888 | tf_op jit(solution)/shard_map/ppermute | solution.py:374
  73.9 3.6 %collective-permute-start.18 = (bf16[5,320,128]{2,1,0:T(8,128)(2,1)S(1)}, bf16[5,320,128]{2,1,0:T(8,128)(2,1)S(1)}, u32[]{:S(2)}, u32[]{:S(2)}) collective-permute-start(bf16[5,320,128]{2,1,0:T(8,128)(2,1)S(1)} %get-tuple-element.49.refs_1_), channel_id=1, source_target_pairs={{0,16},{4,20},{8,24},{12,28},{16,0},{20,4},{24,8},{28,12},{32,48},... | collective-permute-start | bytes 1228808 | tf_op jit(solution)/shard_map/ppermute | solution.py:377
  79.2 7.9 %collective-permute-done.18.refs_2_ = bf16[5,320,128]{2,1,0:T(8,128)(2,1)S(1)} collective-permute-done((bf16[5,320,128]{2,1,0:T(8,128)(2,1)S(1)}, bf16[5,320,128]{2,1,0:T(8,128)(2,1)S(1)}, u32[]{:S(2)}, u32[]{:S(2)}) %collective-permute-start.18) | collective-permute-done | bytes 409632 | tf_op jit(solution)/shard_map/ppermute | solution.py:377
  89.1 2.6 %collective-permute-start.20 = (bf16[3,160,128]{2,1,0:T(8,128)(2,1)S(1)}, bf16[3,160,128]{2,1,0:T(8,128)(2,1)S(1)}, u32[]{:S(2)}, u32[]{:S(2)}) collective-permute-start(bf16[3,160,128]{2,1,0:T(8,128)(2,1)S(1)} %shard_map.106.refs_5_.refs_7_.refs_1_), channel_id=1, source_target_pairs={{0,16},{4,20},{8,24},{12,28},{16,0},{20,4},{24,8},{28,12},{32,48},... | collective-permute-start | bytes 368648 | tf_op jit(solution)/shard_map/ppermute | solution.py:377
  92.6 1.8 %shard_map.107.refs_5_.refs_0_ = bf16[2,256,640]{2,1,0:T(8,128)(2,1)S(1)} custom-call(s32[5]{0:T(128)S(1)} %stack.23.refs_0_, bf16[160,128]{1,0:T(8,128)(2,1)S(1)} %collective-permute-done.15.refs_1_, bf16[160,128]{1,0:T(8,128)(2,1)S(1)} %shard_map.101.refs_0_.refs_2_, bf16[160,128]{1,0:T(8,128)(2,1)S(1)} %collective-permute-done.16.refs_2_.refs_3_, ...), custom_call_target="tpu_custom_call" | custom-call | flops 30000001024 | bytes 1966100 | tf_op jit(solution)/shard_map/pallas_call | solution.py:64
  94.4 2.9 %shard_map.108 = (bf16[2,96,320]{2,1,0:T(8,128)(2,1)S(1)}, bf16[2,96,320]{2,1,0:T(8,128)(2,1)S(1)}, bf16[2,96,320]{2,1,0:T(8,128)(2,1)S(1)}, bf16[2,96,320]{2,1,0:T(8,128)(2,1)S(1)}) custom-call(s32[5]{0:T(128)S(1)} %stack.23.refs_0_, bf16[5,320,128]{2,1,0:T(8,128)(2,1)S(1)} %copy-done.7, bf16[5,320,128]{2,1,0:T(8,128)(2,1)S(1)} %collective-permute-done.18.refs_2_, ...), custom_call_target="tpu_custom_call" | custom-call | bytes 2580500 | tf_op jit(solution)/shard_map/pallas_call | solution.py:64
  98.0 3.0 %collective-permute-done.21.refs_4_ = bf16[3,160,128]{2,1,0:T(8,128)(2,1)S(1)} collective-permute-done((bf16[3,160,128]{2,1,0:T(8,128)(2,1)S(1)}, bf16[3,160,128]{2,1,0:T(8,128)(2,1)S(1)}, u32[]{:S(2)}, u32[]{:S(2)}) %collective-permute-start.21) | collective-permute-done | bytes 122912 | tf_op jit(solution)/shard_map/ppermute | solution.py:377
  102.9 6.4 %all-to-all-start.2 = ((bf16[4,2,64,640]{3,2,1,0:T(8,128)(2,1)}), bf16[4,2,64,640]{3,2,1,0:T(8,128)(2,1)}, u32[]{:S(2)}, u32[]{:S(2)}) async-start(bf16[4,2,64,640]{3,2,1,0:T(8,128)(2,1)} %shard_map.110), calls=%async_computation.2 | async-start | bytes 1310720 | tf_op jit(solution)/shard_map/all_to_all | solution.py:472
  109.3 2.5 %collective-permute-start.28 = (bf16[2,96,320]{2,1,0:T(8,128)(2,1)S(1)}, bf16[2,96,320]{2,1,0:T(8,128)(2,1)S(1)}, u32[]{:S(2)}, u32[]{:S(2)}) collective-permute-start(bf16[2,96,320]{2,1,0:T(8,128)(2,1)S(1)} %copy-done.12), channel_id=1, source_target_pairs={{0,32},{4,36},{8,40},{12,44},{16,48},{20,52},{24,56},{28,60},{32,6... | collective-permute-start | bytes 368648 | tf_op jit(solution)/shard_map/ppermute | solution.py:435
  111.8 16.5 %collective-permute-start.29 = (bf16[2,96,320]{2,1,0:T(8,128)(2,1)S(1)}, bf16[2,96,320]{2,1,0:T(8,128)(2,1)S(1)}, u32[]{:S(2)}, u32[]{:S(2)}) collective-permute-start(bf16[2,96,320]{2,1,0:T(8,128)(2,1)S(1)} %get-tuple-element.60), channel_id=1, source_target_pairs={{0,64},{4,68},{8,72},{12,76},{16,80},{20,84},{24,88},{28,92},{32,9... | collective-permute-start | bytes 368648 | tf_op jit(solution)/shard_map/ppermute | solution.py:435
  129.6 2.2 %shard_map.111 = (bf16[2,96,160]{2,1,0:T(8,128)(2,1)S(1)}, bf16[2,96,160]{2,1,0:T(8,128)(2,1)S(1)}, bf16[2,96,160]{2,1,0:T(8,128)(2,1)S(1)}, bf16[2,96,160]{2,1,0:T(8,128)(2,1)S(1)}) custom-call(s32[5]{0:T(128)S(1)} %stack.23.refs_0_, bf16[3,160,128]{2,1,0:T(8,128)(2,1)S(1)} %shard_map.106.refs_5_.refs_7_.refs_1_, ...), custom_call_target="tpu_custom_call" | custom-call | bytes 2662420 | tf_op jit(solution)/shard_map/pallas_call | solution.py:64
  131.8 2.1 %collective-permute-start.24 = (bf16[2,96,160]{2,1,0:T(8,128)(2,1)S(1)}, bf16[2,96,160]{2,1,0:T(8,128)(2,1)S(1)}, u32[]{:S(2)}, u32[]{:S(2)}) collective-permute-start(bf16[2,96,160]{2,1,0:T(8,128)(2,1)S(1)} %get-tuple-element.54), channel_id=1, source_target_pairs={{0,32},{4,36},{8,40},{12,44},{16,48},{20,52},{24,56},{28,60},{32,6... | collective-permute-start | bytes 184328 | tf_op jit(solution)/shard_map/ppermute | solution.py:435
  133.9 2.8 %collective-permute-start.26 = (bf16[2,96,160]{2,1,0:T(8,128)(2,1)S(1)}, bf16[2,96,160]{2,1,0:T(8,128)(2,1)S(1)}, u32[]{:S(2)}, u32[]{:S(2)}) collective-permute-start(bf16[2,96,160]{2,1,0:T(8,128)(2,1)S(1)} %get-tuple-element.56), channel_id=1, source_target_pairs={{0,96},{4,100},{8,104},{12,108},{16,112},{20,116},{24,120},{28,124... | collective-permute-start | bytes 184328 | tf_op jit(solution)/shard_map/ppermute | solution.py:435
  137.3 5.3 %collective-permute-start.31 = (bf16[96,320]{1,0:T(8,128)(2,1)S(1)}, bf16[96,320]{1,0:T(8,128)(2,1)S(1)}, u32[]{:S(2)}, u32[]{:S(2)}) collective-permute-start(bf16[96,320]{1,0:T(8,128)(2,1)S(1)} %get-tuple-element.63), channel_id=1, source_target_pairs={{0,128},{4,132},{8,136},{12,140},{16,144},{20,148},{24,152},{28,15... | collective-permute-start | bytes 184328 | tf_op jit(solution)/shard_map/ppermute | solution.py:377
  143.2 2.6 %collective-permute-start.27 = (bf16[96,160]{1,0:T(8,128)(2,1)S(1)}, bf16[96,160]{1,0:T(8,128)(2,1)S(1)}, u32[]{:S(2)}, u32[]{:S(2)}) collective-permute-start(bf16[96,160]{1,0:T(8,128)(2,1)S(1)} %get-tuple-element.58), channel_id=1, source_target_pairs={{0,128},{4,132},{8,136},{12,140},{16,144},{20,148},{24,152},{28,15... | collective-permute-start | bytes 92168 | tf_op jit(solution)/shard_map/ppermute | solution.py:377
  148.4 3.3 %collective-permute-done.27.refs_1_ = bf16[96,160]{1,0:T(8,128)(2,1)S(1)} collective-permute-done((bf16[96,160]{1,0:T(8,128)(2,1)S(1)}, bf16[96,160]{1,0:T(8,128)(2,1)S(1)}, u32[]{:S(2)}, u32[]{:S(2)}) %collective-permute-start.27) | collective-permute-done | bytes 30752 | tf_op jit(solution)/shard_map/ppermute | solution.py:377
  (93 shorter events, 30.5 us)
Async XLA Ops:
  0.6 13.9 %collective-permute-start = (bf16[2,64,640]{2,1,0:T(8,128)(2,1)}, bf16[2,64,640]{2,1,0:T(8,128)(2,1)S(1)}, u32[]{:S(2)}, u32[]{:S(2)}) collective-permute-start(bf16[2,64,640]{2,1,0:T(8,128)(2,1)} %refs_1_.3), channel_id=1, source_target_pairs={{0,1},{1,2},{2,3},{3,0},{4,5},{5,6},{6,7},{7,4},{8,9},{9,10},{10,1... | collective-permute-start | bytes 491528 | tf_op jit(solution)/shard_map/ppermute | solution.py:374
  2.6 14.3 %collective-permute-start.1 = (bf16[2,64,640]{2,1,0:T(8,128)(2,1)}, bf16[2,64,640]{2,1,0:T(8,128)(2,1)S(1)}, u32[]{:S(2)}, u32[]{:S(2)}) collective-permute-start(bf16[2,64,640]{2,1,0:T(8,128)(2,1)} %refs_1_.3), channel_id=1, source_target_pairs={{0,2},{1,3},{2,0},{3,1},{4,6},{5,7},{6,4},{7,5},{8,10},{9,11},{10,... | collective-permute-start | bytes 491528 | tf_op jit(solution)/shard_map/ppermute | solution.py:374
  4.9 14.0 %collective-permute-start.2 = (bf16[2,64,640]{2,1,0:T(8,128)(2,1)}, bf16[2,64,640]{2,1,0:T(8,128)(2,1)S(1)}, u32[]{:S(2)}, u32[]{:S(2)}) collective-permute-start(bf16[2,64,640]{2,1,0:T(8,128)(2,1)} %refs_1_.3), channel_id=1, source_target_pairs={{0,3},{1,0},{2,1},{3,2},{4,7},{5,4},{6,5},{7,6},{8,11},{9,8},{10,9... | collective-permute-start | bytes 491528 | tf_op jit(solution)/shard_map/ppermute | solution.py:374
  23.3 1.3 collective-permute-start.3
  23.4 9.8 %collective-permute-start.4 = (bf16[160,128]{1,0:T(8,128)(2,1)S(1)}, bf16[160,128]{1,0:T(8,128)(2,1)S(1)}, u32[]{:S(2)}, u32[]{:S(2)}) collective-permute-start(bf16[160,128]{1,0:T(8,128)(2,1)S(1)} %get-tuple-element.36), channel_id=1, source_target_pairs={{4,8},{8,4},{12,16},{16,12},{20,24},{24,20},{28,32},{32,28},{36,40... | collective-permute-start | bytes 122888 | tf_op jit(solution)/shard_map/ppermute | solution.py:380
  27.2 17.7 %all-to-all-start = ((bf16[8,80,512]{2,1,0:T(8,128)(2,1)}), bf16[8,80,512]{2,1,0:T(8,128)(2,1)S(1)}, u32[]{:S(2)}, u32[]{:S(2)}) async-start(bf16[8,80,512]{2,1,0:T(8,128)(2,1)} %shard_map.94.refs_3_), calls=%async_computation | async-start | bytes 1310720 | tf_op jit(solution)/shard_map/all_to_all | solution.py:397
  33.2 4.1 %collective-permute-start.5 = (bf16[160,128]{1,0:T(8,128)(2,1)S(1)}, bf16[160,128]{1,0:T(8,128)(2,1)S(1)}, u32[]{:S(2)}, u32[]{:S(2)}) collective-permute-start(bf16[160,128]{1,0:T(8,128)(2,1)S(1)} %shard_map.95.refs_1_), channel_id=1, source_target_pairs={{0,1},{1,2},{2,3},{3,0},{4,5},{5,6},{6,7},{7,4},{8,9},{9,10},{10,1... | collective-permute-start | bytes 122888 | tf_op jit(solution)/shard_map/ppermute | solution.py:374
  33.3 5.5 %collective-permute-start.6 = (bf16[160,128]{1,0:T(8,128)(2,1)S(1)}, bf16[160,128]{1,0:T(8,128)(2,1)S(1)}, u32[]{:S(2)}, u32[]{:S(2)}) collective-permute-start(bf16[160,128]{1,0:T(8,128)(2,1)S(1)} %shard_map.95.refs_1_), channel_id=1, source_target_pairs={{0,2},{1,3},{2,0},{3,1},{4,6},{5,7},{6,4},{7,5},{8,10},{9,11},{10,... | collective-permute-start | bytes 122888 | tf_op jit(solution)/shard_map/ppermute | solution.py:374
  34.7 5.8 %collective-permute-start.7 = (bf16[160,128]{1,0:T(8,128)(2,1)S(1)}, bf16[160,128]{1,0:T(8,128)(2,1)S(1)}, u32[]{:S(2)}, u32[]{:S(2)}) collective-permute-start(bf16[160,128]{1,0:T(8,128)(2,1)S(1)} %shard_map.95.refs_1_), channel_id=1, source_target_pairs={{0,3},{1,0},{2,1},{3,2},{4,7},{5,4},{6,5},{7,6},{8,11},{9,8},{10,9... | collective-permute-start | bytes 122888 | tf_op jit(solution)/shard_map/ppermute | solution.py:374
  41.8 5.6 %collective-permute-start.8 = (bf16[320,128]{1,0:T(8,128)(2,1)S(1)}, bf16[320,128]{1,0:T(8,128)(2,1)S(1)}, u32[]{:S(2)}, u32[]{:S(2)}) collective-permute-start(bf16[320,128]{1,0:T(8,128)(2,1)S(1)} %get-tuple-element.39), channel_id=1, source_target_pairs={{0,4},{4,0},{8,12},{12,8},{16,20},{20,16},{24,28},{28,24},{32,36},... | collective-permute-start | bytes 245768 | tf_op jit(solution)/shard_map/ppermute | solution.py:377
  42.0 5.5 %collective-permute-start.9 = (bf16[320,128]{1,0:T(8,128)(2,1)S(1)}, bf16[320,128]{1,0:T(8,128)(2,1)S(1)}, u32[]{:S(2)}, u32[]{:S(2)}) collective-permute-start(bf16[320,128]{1,0:T(8,128)(2,1)S(1)} %get-tuple-element.40), channel_id=1, source_target_pairs={{4,8},{8,4},{12,16},{16,12},{20,24},{24,20},{28,32},{32,28},{36,40... | collective-permute-start | bytes 245768 | tf_op jit(solution)/shard_map/ppermute | solution.py:380
  49.8 23.4 %collective-permute-start.17 = (bf16[3,320,128]{2,1,0:T(8,128)(2,1)S(1)}, bf16[3,320,128]{2,1,0:T(8,128)(2,1)S(1)}, u32[]{:S(2)}, u32[]{:S(2)}) collective-permute-start(bf16[3,320,128]{2,1,0:T(8,128)(2,1)S(1)} %shard_map.103.refs_1_), channel_id=1, source_target_pairs={{0,8},{4,12},{8,0},{12,4},{16,24},{20,28},{24,16},{28,20},{32,40},... | collective-permute-start | bytes 737288 | tf_op jit(solution)/shard_map/ppermute | solution.py:377
  57.2 20.3 %all-to-all-start.1 = ((bf16[8,80,128]{2,1,0:T(8,128)(2,1)}), bf16[8,80,128]{2,1,0:T(8,128)(2,1)S(1)}, u32[]{:S(2)}, u32[]{:S(2)}) async-start(bf16[8,80,128]{2,1,0:T(8,128)(2,1)} %shard_map.100), calls=%async_computation.1 | async-start | bytes 327680 | tf_op jit(solution)/shard_map/all_to_all | solution.py:415
  68.5 4.7 %collective-permute-start.12 = (bf16[160,128]{1,0:T(8,128)(2,1)S(1)}, bf16[160,128]{1,0:T(8,128)(2,1)S(1)}, u32[]{:S(2)}, u32[]{:S(2)}) collective-permute-start(bf16[160,128]{1,0:T(8,128)(2,1)S(1)} %get-tuple-element.44), channel_id=1, source_target_pairs={{0,1},{1,2},{2,3},{3,0},{4,5},{5,6},{6,7},{7,4},{8,9},{9,10},{10,1... | collective-permute-start | bytes 122888 | tf_op jit(solution)/shard_map/ppermute | solution.py:374
  69.9 7.6 %collective-permute-start.13 = (bf16[160,128]{1,0:T(8,128)(2,1)S(1)}, bf16[160,128]{1,0:T(8,128)(2,1)S(1)}, u32[]{:S(2)}, u32[]{:S(2)}) collective-permute-start(bf16[160,128]{1,0:T(8,128)(2,1)S(1)} %get-tuple-element.45), channel_id=1, source_target_pairs={{0,2},{1,3},{2,0},{3,1},{4,6},{5,7},{6,4},{7,5},{8,10},{9,11},{10,... | collective-permute-start | bytes 122888 | tf_op jit(solution)/shard_map/ppermute | solution.py:374
  72.3 5.2 %collective-permute-start.14 = (bf16[160,128]{1,0:T(8,128)(2,1)S(1)}, bf16[160,128]{1,0:T(8,128)(2,1)S(1)}, u32[]{:S(2)}, u32[]{:S(2)}) collective-permute-start(bf16[160,128]{1,0:T(8,128)(2,1)S(1)} %get-tuple-element.46), channel_id=1, source_target_pairs={{0,3},{1,0},{2,1},{3,2},{4,7},{5,4},{6,5},{7,6},{8,11},{9,8},{10,9... | collective-permute-start | bytes 122888 | tf_op jit(solution)/shard_map/ppermute | solution.py:374
  73.9 13.2 %collective-permute-start.18 = (bf16[5,320,128]{2,1,0:T(8,128)(2,1)S(1)}, bf16[5,320,128]{2,1,0:T(8,128)(2,1)S(1)}, u32[]{:S(2)}, u32[]{:S(2)}) collective-permute-start(bf16[5,320,128]{2,1,0:T(8,128)(2,1)S(1)} %get-tuple-element.49.refs_1_), channel_id=1, source_target_pairs={{0,16},{4,20},{8,24},{12,28},{16,0},{20,4},{24,8},{28,12},{32,48},... | collective-permute-start | bytes 1228808 | tf_op jit(solution)/shard_map/ppermute | solution.py:377
  77.6 10.2 %collective-permute-start.15 = (bf16[160,128]{1,0:T(8,128)(2,1)S(1)}, bf16[160,128]{1,0:T(8,128)(2,1)S(1)}, u32[]{:S(2)}, u32[]{:S(2)}) collective-permute-start(bf16[160,128]{1,0:T(8,128)(2,1)S(1)} %shard_map.101.refs_0_.refs_2_), channel_id=1, source_target_pairs={{0,4},{4,0},{8,12},{12,8},{16,20},{20,16},{24,28},{28,24},{32,36},... | collective-permute-start | bytes 122888 | tf_op jit(solution)/shard_map/ppermute | solution.py:377
  77.7 10.1 %collective-permute-start.16 = (bf16[160,128]{1,0:T(8,128)(2,1)S(1)}, bf16[160,128]{1,0:T(8,128)(2,1)S(1)}, u32[]{:S(2)}, u32[]{:S(2)}) collective-permute-start(bf16[160,128]{1,0:T(8,128)(2,1)S(1)} %shard_map.101.refs_0_.refs_2_), channel_id=1, source_target_pairs={{4,8},{8,4},{12,16},{16,12},{20,24},{24,20},{28,32},{32,28},{36,40... | collective-permute-start | bytes 122888 | tf_op jit(solution)/shard_map/ppermute | solution.py:380
  87.6 6.7 %collective-permute-start.22 = (bf16[320,128]{1,0:T(8,128)(2,1)S(1)}, bf16[320,128]{1,0:T(8,128)(2,1)S(1)}, u32[]{:S(2)}, u32[]{:S(2)}) collective-permute-start(bf16[320,128]{1,0:T(8,128)(2,1)S(1)} %shard_map.105.refs_4_.refs_3_), channel_id=1, source_target_pairs={{0,4},{4,0},{8,12},{12,8},{16,20},{20,16},{24,28},{28,24},{32,36},... | collective-permute-start | bytes 245768 | tf_op jit(solution)/shard_map/ppermute | solution.py:377
  87.8 10.2 %collective-permute-start.19 = (bf16[3,160,128]{2,1,0:T(8,128)(2,1)S(1)}, bf16[3,160,128]{2,1,0:T(8,128)(2,1)S(1)}, u32[]{:S(2)}, u32[]{:S(2)}) collective-permute-start(bf16[3,160,128]{2,1,0:T(8,128)(2,1)S(1)} %shard_map.106.refs_5_.refs_7_.refs_1_), channel_id=1, source_target_pairs={{0,8},{4,12},{8,0},{12,4},{16,24},{20,28},{24,16},{28,20},{32,40},... | collective-permute-start | bytes 368648 | tf_op jit(solution)/shard_map/ppermute | solution.py:377
  89.1 9.0 %collective-permute-start.20 = (bf16[3,160,128]{2,1,0:T(8,128)(2,1)S(1)}, bf16[3,160,128]{2,1,0:T(8,128)(2,1)S(1)}, u32[]{:S(2)}, u32[]{:S(2)}) collective-permute-start(bf16[3,160,128]{2,1,0:T(8,128)(2,1)S(1)} %shard_map.106.refs_5_.refs_7_.refs_1_), channel_id=1, source_target_pairs={{0,16},{4,20},{8,24},{12,28},{16,0},{20,4},{24,8},{28,12},{32,48},... | collective-permute-start | bytes 368648 | tf_op jit(solution)/shard_map/ppermute | solution.py:377
  91.7 9.4 %collective-permute-start.21 = (bf16[3,160,128]{2,1,0:T(8,128)(2,1)S(1)}, bf16[3,160,128]{2,1,0:T(8,128)(2,1)S(1)}, u32[]{:S(2)}, u32[]{:S(2)}) collective-permute-start(bf16[3,160,128]{2,1,0:T(8,128)(2,1)S(1)} %shard_map.106.refs_5_.refs_7_.refs_1_), channel_id=1, source_target_pairs={{0,24},{4,28},{8,16},{12,20},{16,8},{20,12},{24,0},{28,4},{32,56},... | collective-permute-start | bytes 368648 | tf_op jit(solution)/shard_map/ppermute | solution.py:377
  102.9 44.3 %all-to-all-start.2 = ((bf16[4,2,64,640]{3,2,1,0:T(8,128)(2,1)}), bf16[4,2,64,640]{3,2,1,0:T(8,128)(2,1)}, u32[]{:S(2)}, u32[]{:S(2)}) async-start(bf16[4,2,64,640]{3,2,1,0:T(8,128)(2,1)} %shard_map.110), calls=%async_computation.2 | async-start | bytes 1310720 | tf_op jit(solution)/shard_map/all_to_all | solution.py:472
  109.3 24.6 %collective-permute-start.28 = (bf16[2,96,320]{2,1,0:T(8,128)(2,1)S(1)}, bf16[2,96,320]{2,1,0:T(8,128)(2,1)S(1)}, u32[]{:S(2)}, u32[]{:S(2)}) collective-permute-start(bf16[2,96,320]{2,1,0:T(8,128)(2,1)S(1)} %copy-done.12), channel_id=1, source_target_pairs={{0,32},{4,36},{8,40},{12,44},{16,48},{20,52},{24,56},{28,60},{32,6... | collective-permute-start | bytes 368648 | tf_op jit(solution)/shard_map/ppermute | solution.py:435
  111.8 24.9 %collective-permute-start.29 = (bf16[2,96,320]{2,1,0:T(8,128)(2,1)S(1)}, bf16[2,96,320]{2,1,0:T(8,128)(2,1)S(1)}, u32[]{:S(2)}, u32[]{:S(2)}) collective-permute-start(bf16[2,96,320]{2,1,0:T(8,128)(2,1)S(1)} %get-tuple-element.60), channel_id=1, source_target_pairs={{0,64},{4,68},{8,72},{12,76},{16,80},{20,84},{24,88},{28,92},{32,9... | collective-permute-start | bytes 368648 | tf_op jit(solution)/shard_map/ppermute | solution.py:435
  128.3 8.3 %collective-permute-start.30 = (bf16[2,96,320]{2,1,0:T(8,128)(2,1)S(1)}, bf16[2,96,320]{2,1,0:T(8,128)(2,1)S(1)}, u32[]{:S(2)}, u32[]{:S(2)}) collective-permute-start(bf16[2,96,320]{2,1,0:T(8,128)(2,1)S(1)} %get-tuple-element.61), channel_id=1, source_target_pairs={{0,96},{4,100},{8,104},{12,108},{16,112},{20,116},{24,120},{28,124... | collective-permute-start | bytes 368648 | tf_op jit(solution)/shard_map/ppermute | solution.py:435
  131.8 10.8 %collective-permute-start.24 = (bf16[2,96,160]{2,1,0:T(8,128)(2,1)S(1)}, bf16[2,96,160]{2,1,0:T(8,128)(2,1)S(1)}, u32[]{:S(2)}, u32[]{:S(2)}) collective-permute-start(bf16[2,96,160]{2,1,0:T(8,128)(2,1)S(1)} %get-tuple-element.54), channel_id=1, source_target_pairs={{0,32},{4,36},{8,40},{12,44},{16,48},{20,52},{24,56},{28,60},{32,6... | collective-permute-start | bytes 184328 | tf_op jit(solution)/shard_map/ppermute | solution.py:435
  133.9 8.7 %collective-permute-start.25 = (bf16[2,96,160]{2,1,0:T(8,128)(2,1)S(1)}, bf16[2,96,160]{2,1,0:T(8,128)(2,1)S(1)}, u32[]{:S(2)}, u32[]{:S(2)}) collective-permute-start(bf16[2,96,160]{2,1,0:T(8,128)(2,1)S(1)} %get-tuple-element.55), channel_id=1, source_target_pairs={{0,64},{4,68},{8,72},{12,76},{16,80},{20,84},{24,88},{28,92},{32,9... | collective-permute-start | bytes 184328 | tf_op jit(solution)/shard_map/ppermute | solution.py:435
  133.9 8.7 %collective-permute-start.26 = (bf16[2,96,160]{2,1,0:T(8,128)(2,1)S(1)}, bf16[2,96,160]{2,1,0:T(8,128)(2,1)S(1)}, u32[]{:S(2)}, u32[]{:S(2)}) collective-permute-start(bf16[2,96,160]{2,1,0:T(8,128)(2,1)S(1)} %get-tuple-element.56), channel_id=1, source_target_pairs={{0,96},{4,100},{8,104},{12,108},{16,112},{20,116},{24,120},{28,124... | collective-permute-start | bytes 184328 | tf_op jit(solution)/shard_map/ppermute | solution.py:435
  137.3 9.1 %collective-permute-start.31 = (bf16[96,320]{1,0:T(8,128)(2,1)S(1)}, bf16[96,320]{1,0:T(8,128)(2,1)S(1)}, u32[]{:S(2)}, u32[]{:S(2)}) collective-permute-start(bf16[96,320]{1,0:T(8,128)(2,1)S(1)} %get-tuple-element.63), channel_id=1, source_target_pairs={{0,128},{4,132},{8,136},{12,140},{16,144},{20,148},{24,152},{28,15... | collective-permute-start | bytes 184328 | tf_op jit(solution)/shard_map/ppermute | solution.py:377
  143.2 8.5 %collective-permute-start.27 = (bf16[96,160]{1,0:T(8,128)(2,1)S(1)}, bf16[96,160]{1,0:T(8,128)(2,1)S(1)}, u32[]{:S(2)}, u32[]{:S(2)}) collective-permute-start(bf16[96,160]{1,0:T(8,128)(2,1)S(1)} %get-tuple-element.58), channel_id=1, source_target_pairs={{0,128},{4,132},{8,136},{12,140},{16,144},{20,148},{24,152},{28,15... | collective-permute-start | bytes 92168 | tf_op jit(solution)/shard_map/ppermute | solution.py:377
  (17 other events, 66.2 us)

commit v12 on v11

--- a/solution.py
+++ b/solution.py
@@ -411,9 +411,9 @@
         (preact, partner, other, upstream[0].T),
     )
     pre_partner, other = pairs(grad_pre, grad_pre)
-    deep_slab = call(deep_slices, shape((MEMBERS, size, deep)), (pooled, pick), behind=(pre_partner,))
-    deep_slab = lax.all_to_all(deep_slab, "wide", 0, 0, axis_index_groups=near)
-    pre_first = call(pack, shape((3, full, deep)), (grad_pre, pre_partner, other))
+    deep_pre = call(deep_slices, shape((MEMBERS, size, deep)), (pooled, pick), behind=(pre_partner,))
+    deep_slab = lax.all_to_all(deep_pre, "wide", 0, 0, axis_index_groups=near)
+    pre_first = call(pack, shape((3, full, deep)), (grad_pre, pre_partner, other), behind=(deep_pre,))
     parts = call(
         deep_backward,
         [shape((fine, deep))] * 4,

time: 153 us -> 148 us (0.967)
  starting transfers between devices: 83.2 us -> 78 us
    ppermute x13, starting transfers between devices: 23.3 us -> 17.3 us  [swap(): return lax.ppermute(v, 'wide', [(i, i ^ bit) for i in range(wide)])]
where the time goes in v12:
time: 148 us; the launch traced here: 147 us
  starting transfers between devices  78 us (53%)
  waiting for transfers between devices  35.8 us (24%)
  Pallas kernels  22 us (15%)
  local copies, waits for them, and re-layouts  9.13 us (6%)
    ppermute x6, starting transfers between devices, halves(): lax.ppermute(parts[s], 'wide', [(i, i // 32 * 32 + (i // 8 + s) % 4 * 8 +...  24.1 us
    pallas_call x23, Pallas kernels, call(): pl.pallas_call(kernel, out_shape=outs, in_specs=[smem if a.dtype == jnp.i...  22 us
    ppermute x13, starting transfers between devices, swap(): return lax.ppermute(v, 'wide', [(i, i ^ bit) for i in range(wide)])  17.3 us
    ppermute x13, waiting for transfers between devices, swap(): return lax.ppermute(v, 'wide', [(i, i ^ bit) for i in range(wide)])  16.8 us
    ppermute x9, waiting for transfers between devices, across(): lax.ppermute(v, 'narrow', [(i, (i + step) % pieces) for i in range(pieces)])  16.7 us
    ppermute x9, starting transfers between devices, across(): lax.ppermute(v, 'narrow', [(i, (i + step) % pieces) for i in range(pieces)])  13.3 us
    unnamed x30, local copies, waits for them, and re-layouts  9.05 us
    all_to_all x1, starting transfers between devices, on_device(): deep_slab = lax.all_to_all(deep_pre, 'wide', 0, 0, axis_index_groups=near)  8.36 us
  transfers between devices with their start and end apart: 35, of which 15 were waited for; matrix products, arithmetic and copies ran while one was open for 1% of the time, Pallas kernels for 12%

profile of v12, /device:TPU:32, one launch (start us, length us, event | category | flops | bytes accessed | tf_op | source)
XLA Modules:
  0.0 147.1 jit_solution(14889645858099106573)
XLA Ops:
  0.6 2.0 %collective-permute-start = (bf16[2,64,640]{2,1,0:T(8,128)(2,1)}, bf16[2,64,640]{2,1,0:T(8,128)(2,1)S(1)}, u32[]{:S(2)}, u32[]{:S(2)}) collective-permute-start(bf16[2,64,640]{2,1,0:T(8,128)(2,1)} %refs_1_.3), channel_id=1, source_target_pairs={{0,1},{1,2},{2,3},{3,0},{4,5},{5,6},{6,7},{7,4},{8,9},{9,10},{10,1... | collective-permute-start | bytes 491528 | tf_op jit(solution)/shard_map/ppermute | solution.py:374
  2.6 2.3 %collective-permute-start.1 = (bf16[2,64,640]{2,1,0:T(8,128)(2,1)}, bf16[2,64,640]{2,1,0:T(8,128)(2,1)S(1)}, u32[]{:S(2)}, u32[]{:S(2)}) collective-permute-start(bf16[2,64,640]{2,1,0:T(8,128)(2,1)} %refs_1_.3), channel_id=1, source_target_pairs={{0,2},{1,3},{2,0},{3,1},{4,6},{5,7},{6,4},{7,5},{8,10},{9,11},{10,... | collective-permute-start | bytes 491528 | tf_op jit(solution)/shard_map/ppermute | solution.py:374
  6.1 8.5 %collective-permute-done.refs_2_ = bf16[2,64,640]{2,1,0:T(8,128)(2,1)S(1)} collective-permute-done((bf16[2,64,640]{2,1,0:T(8,128)(2,1)}, bf16[2,64,640]{2,1,0:T(8,128)(2,1)S(1)}, u32[]{:S(2)}, u32[]{:S(2)}) %collective-permute-start) | collective-permute-done | bytes 163872 | tf_op jit(solution)/shard_map/ppermute | solution.py:374
  14.6 2.4 %collective-permute-done.1.refs_3_ = bf16[2,64,640]{2,1,0:T(8,128)(2,1)S(1)} collective-permute-done((bf16[2,64,640]{2,1,0:T(8,128)(2,1)}, bf16[2,64,640]{2,1,0:T(8,128)(2,1)S(1)}, u32[]{:S(2)}, u32[]{:S(2)}) %collective-permute-start.1) | collective-permute-done | bytes 163872 | tf_op jit(solution)/shard_map/ppermute | solution.py:374
  16.9 2.0 %collective-permute-done.2.refs_4_ = bf16[2,64,640]{2,1,0:T(8,128)(2,1)S(1)} collective-permute-done((bf16[2,64,640]{2,1,0:T(8,128)(2,1)}, bf16[2,64,640]{2,1,0:T(8,128)(2,1)S(1)}, u32[]{:S(2)}, u32[]{:S(2)}) %collective-permute-start.2) | collective-permute-done | bytes 163872 | tf_op jit(solution)/shard_map/ppermute | solution.py:374
  21.3 1.9 %shard_map.93 = (bf16[4,2,64,640]{3,2,1,0:T(8,128)(2,1)S(1)}, f32[160,128]{1,0:T(8,128)S(1)}, bf16[160,128]{1,0:T(8,128)(2,1)S(1)}, bf16[160,128]{1,0:T(8,128)(2,1)S(1)}) custom-call(s32[5]{0:T(128)S(1)} %stack.23.refs_0_, bf16[2,64,640]{2,1,0:T(8,128)(2,1)S(1)} %copy-done.10, bf16[2,64,640]{2,1,0:T(8,128)(2,1)S(1)} %collective-permute-done.refs_2_, ...), custom_call_target="tpu_custom_call" | custom-call | flops 30000001024 | bytes 2498580 | tf_op jit(solution)/shard_map/pallas_call | solution.py:64
  24.6 2.6 %shard_map.94.refs_3_ = bf16[8,80,512]{2,1,0:T(8,128)(2,1)} custom-call(bf16[4,2,64,640]{3,2,1,0:T(8,128)(2,1)S(1)} %get-tuple-element.37.refs_0_, bf16[640,640]{1,0:T(8,128)(2,1)S(1)} %copy-done.4, bf16[160,128]{1,0:T(8,128)(2,1)S(1)} %collective-permute-done.3.refs_2_.refs_1_), custom_call_target="tpu_custom_call" | custom-call | bytes 1474560 | tf_op jit(solution)/shard_map/pallas_call | solution.py:64
  27.2 6.0 %all-to-all-start = ((bf16[8,80,512]{2,1,0:T(8,128)(2,1)}), bf16[8,80,512]{2,1,0:T(8,128)(2,1)S(1)}, u32[]{:S(2)}, u32[]{:S(2)}) async-start(bf16[8,80,512]{2,1,0:T(8,128)(2,1)} %shard_map.94.refs_3_), calls=%async_computation | async-start | bytes 1310720 | tf_op jit(solution)/shard_map/all_to_all | solution.py:397
  34.7 1.9 %collective-permute-start.7 = (bf16[160,128]{1,0:T(8,128)(2,1)S(1)}, bf16[160,128]{1,0:T(8,128)(2,1)S(1)}, u32[]{:S(2)}, u32[]{:S(2)}) collective-permute-start(bf16[160,128]{1,0:T(8,128)(2,1)S(1)} %shard_map.95.refs_1_), channel_id=1, source_target_pairs={{0,3},{1,0},{2,1},{3,2},{4,7},{5,4},{6,5},{7,6},{8,11},{9,8},{10,9... | collective-permute-start | bytes 122888 | tf_op jit(solution)/shard_map/ppermute | solution.py:374
  38.8 1.7 %collective-permute-done.7.refs_4_ = bf16[160,128]{1,0:T(8,128)(2,1)S(1)} collective-permute-done((bf16[160,128]{1,0:T(8,128)(2,1)S(1)}, bf16[160,128]{1,0:T(8,128)(2,1)S(1)}, u32[]{:S(2)}, u32[]{:S(2)}) %collective-permute-start.7) | collective-permute-done | bytes 40992 | tf_op jit(solution)/shard_map/ppermute | solution.py:374
  42.6 2.3 %all-to-all-done.refs_2_.refs_0_ = bf16[8,80,512]{2,1,0:T(8,128)(2,1)S(1)} async-done(((bf16[8,80,512]{2,1,0:T(8,128)(2,1)}), bf16[8,80,512]{2,1,0:T(8,128)(2,1)S(1)}, u32[]{:S(2)}, u32[]{:S(2)}) %all-to-all-start) | async-done | bytes 655392 | tf_op jit(solution)/shard_map/all_to_all | solution.py:397
  44.9 2.0 %copy-done.1 = bf16[3,3,640,320]{2,3,1,0:T(8,128)(2,1)S(1)} copy-done((bf16[3,3,640,320]{2,3,1,0:T(8,128)(2,1)S(1)}, bf16[3,3,640,320]{2,3,1,0:T(8,128)(2,1)}, u32[]{:S(2)}) %copy-start.1) | copy-done | bytes 3686424
  50.9 8.4 %all-to-all-start.1 = ((bf16[8,80,128]{2,1,0:T(8,128)(2,1)}), bf16[8,80,128]{2,1,0:T(8,128)(2,1)S(1)}, u32[]{:S(2)}, u32[]{:S(2)}) async-start(bf16[8,80,128]{2,1,0:T(8,128)(2,1)} %shard_map.100.refs_3_), calls=%async_computation.1 | async-start | bytes 327680 | tf_op jit(solution)/shard_map/all_to_all | solution.py:415
  59.3 2.1 %collective-permute-start.17 = (bf16[3,320,128]{2,1,0:T(8,128)(2,1)S(1)}, bf16[3,320,128]{2,1,0:T(8,128)(2,1)S(1)}, u32[]{:S(2)}, u32[]{:S(2)}) collective-permute-start(bf16[3,320,128]{2,1,0:T(8,128)(2,1)S(1)} %shard_map.103.refs_1_), channel_id=1, source_target_pairs={{0,8},{4,12},{8,0},{12,4},{16,24},{20,28},{24,16},{28,20},{32,40},... | collective-permute-start | bytes 737288 | tf_op jit(solution)/shard_map/ppermute | solution.py:377
  61.4 2.0 %copy-done.2 = bf16[3,3,640,320]{2,3,1,0:T(8,128)(2,1)S(1)} copy-done((bf16[3,3,640,320]{2,3,1,0:T(8,128)(2,1)S(1)}, bf16[3,3,640,320]{2,3,1,0:T(8,128)(2,1)}, u32[]{:S(2)}) %copy-start.2) | copy-done | bytes 3686424
  63.4 1.9 %shard_map.99 = (bf16[160,128]{1,0:T(8,128)(2,1)S(1)}, bf16[160,128]{1,0:T(8,128)(2,1)S(1)}, bf16[160,128]{1,0:T(8,128)(2,1)S(1)}, bf16[160,128]{1,0:T(8,128)(2,1)S(1)}) custom-call(s32[5]{0:T(128)S(1)} %stack.23.refs_0_, bf16[320,128]{1,0:T(8,128)(2,1)S(1)} %collective-permute-done.10.refs_1_.refs_2_, ...), custom_call_target="tpu_custom_call" | custom-call | flops 30000001024 | bytes 3932180 | tf_op jit(solution)/shard_map/pallas_call | solution.py:64
  66.5 2.5 %collective-permute-start.13 = (bf16[160,128]{1,0:T(8,128)(2,1)S(1)}, bf16[160,128]{1,0:T(8,128)(2,1)S(1)}, u32[]{:S(2)}, u32[]{:S(2)}) collective-permute-start(bf16[160,128]{1,0:T(8,128)(2,1)S(1)} %get-tuple-element.45), channel_id=1, source_target_pairs={{0,2},{1,3},{2,0},{3,1},{4,6},{5,7},{6,4},{7,5},{8,10},{9,11},{10,... | collective-permute-start | bytes 122888 | tf_op jit(solution)/shard_map/ppermute | solution.py:374
  70.5 2.8 %collective-permute-start.18 = (bf16[5,320,128]{2,1,0:T(8,128)(2,1)S(1)}, bf16[5,320,128]{2,1,0:T(8,128)(2,1)S(1)}, u32[]{:S(2)}, u32[]{:S(2)}) collective-permute-start(bf16[5,320,128]{2,1,0:T(8,128)(2,1)S(1)} %get-tuple-element.49.refs_1_), channel_id=1, source_target_pairs={{0,16},{4,20},{8,24},{12,28},{16,0},{20,4},{24,8},{28,12},{32,48},... | collective-permute-start | bytes 1228808 | tf_op jit(solution)/shard_map/ppermute | solution.py:377
  75.0 8.3 %collective-permute-done.18.refs_2_ = bf16[5,320,128]{2,1,0:T(8,128)(2,1)S(1)} collective-permute-done((bf16[5,320,128]{2,1,0:T(8,128)(2,1)S(1)}, bf16[5,320,128]{2,1,0:T(8,128)(2,1)S(1)}, u32[]{:S(2)}, u32[]{:S(2)}) %collective-permute-start.18) | collective-permute-done | bytes 409632 | tf_op jit(solution)/shard_map/ppermute | solution.py:377
  84.1 3.9 %collective-permute-start.20 = (bf16[3,160,128]{2,1,0:T(8,128)(2,1)S(1)}, bf16[3,160,128]{2,1,0:T(8,128)(2,1)S(1)}, u32[]{:S(2)}, u32[]{:S(2)}) collective-permute-start(bf16[3,160,128]{2,1,0:T(8,128)(2,1)S(1)} %shard_map.106.refs_5_.refs_7_.refs_1_), channel_id=1, source_target_pairs={{0,16},{4,20},{8,24},{12,28},{16,0},{20,4},{24,8},{28,12},{32,48},... | collective-permute-start | bytes 368648 | tf_op jit(solution)/shard_map/ppermute | solution.py:377
  88.8 1.8 %shard_map.107.refs_5_.refs_0_ = bf16[2,256,640]{2,1,0:T(8,128)(2,1)S(1)} custom-call(s32[5]{0:T(128)S(1)} %stack.23.refs_0_, bf16[160,128]{1,0:T(8,128)(2,1)S(1)} %collective-permute-done.15.refs_1_, bf16[160,128]{1,0:T(8,128)(2,1)S(1)} %shard_map.101.refs_0_.refs_2_, bf16[160,128]{1,0:T(8,128)(2,1)S(1)} %collective-permute-done.16.refs_2_.refs_3_, ...), custom_call_target="tpu_custom_call" | custom-call | flops 30000001024 | bytes 1966100 | tf_op jit(solution)/shard_map/pallas_call | solution.py:64
  90.6 2.9 %shard_map.108 = (bf16[2,96,320]{2,1,0:T(8,128)(2,1)S(1)}, bf16[2,96,320]{2,1,0:T(8,128)(2,1)S(1)}, bf16[2,96,320]{2,1,0:T(8,128)(2,1)S(1)}, bf16[2,96,320]{2,1,0:T(8,128)(2,1)S(1)}) custom-call(s32[5]{0:T(128)S(1)} %stack.23.refs_0_, bf16[5,320,128]{2,1,0:T(8,128)(2,1)S(1)} %copy-done.7, bf16[5,320,128]{2,1,0:T(8,128)(2,1)S(1)} %collective-permute-done.18.refs_2_, ...), custom_call_target="tpu_custom_call" | custom-call | bytes 2580500 | tf_op jit(solution)/shard_map/pallas_call | solution.py:64
  94.3 2.3 %collective-permute-done.21.refs_4_ = bf16[3,160,128]{2,1,0:T(8,128)(2,1)S(1)} collective-permute-done((bf16[3,160,128]{2,1,0:T(8,128)(2,1)S(1)}, bf16[3,160,128]{2,1,0:T(8,128)(2,1)S(1)}, u32[]{:S(2)}, u32[]{:S(2)}) %collective-permute-start.21) | collective-permute-done | bytes 122912 | tf_op jit(solution)/shard_map/ppermute | solution.py:377
  98.5 6.3 %all-to-all-start.2 = ((bf16[4,2,64,640]{3,2,1,0:T(8,128)(2,1)}), bf16[4,2,64,640]{3,2,1,0:T(8,128)(2,1)}, u32[]{:S(2)}, u32[]{:S(2)}) async-start(bf16[4,2,64,640]{3,2,1,0:T(8,128)(2,1)} %shard_map.110), calls=%async_computation.2 | async-start | bytes 1310720 | tf_op jit(solution)/shard_map/all_to_all | solution.py:472
  106.3 17.7 %collective-permute-start.29 = (bf16[2,96,320]{2,1,0:T(8,128)(2,1)S(1)}, bf16[2,96,320]{2,1,0:T(8,128)(2,1)S(1)}, u32[]{:S(2)}, u32[]{:S(2)}) collective-permute-start(bf16[2,96,320]{2,1,0:T(8,128)(2,1)S(1)} %get-tuple-element.60), channel_id=1, source_target_pairs={{0,64},{4,68},{8,72},{12,76},{16,80},{20,84},{24,88},{28,92},{32,9... | collective-permute-start | bytes 368648 | tf_op jit(solution)/shard_map/ppermute | solution.py:435
  125.2 2.2 %shard_map.111 = (bf16[2,96,160]{2,1,0:T(8,128)(2,1)S(1)}, bf16[2,96,160]{2,1,0:T(8,128)(2,1)S(1)}, bf16[2,96,160]{2,1,0:T(8,128)(2,1)S(1)}, bf16[2,96,160]{2,1,0:T(8,128)(2,1)S(1)}) custom-call(s32[5]{0:T(128)S(1)} %stack.23.refs_0_, bf16[3,160,128]{2,1,0:T(8,128)(2,1)S(1)} %shard_map.106.refs_5_.refs_7_.refs_1_, ...), custom_call_target="tpu_custom_call" | custom-call | bytes 2662420 | tf_op jit(solution)/shard_map/pallas_call | solution.py:64
  127.5 2.1 %collective-permute-start.24 = (bf16[2,96,160]{2,1,0:T(8,128)(2,1)S(1)}, bf16[2,96,160]{2,1,0:T(8,128)(2,1)S(1)}, u32[]{:S(2)}, u32[]{:S(2)}) collective-permute-start(bf16[2,96,160]{2,1,0:T(8,128)(2,1)S(1)} %get-tuple-element.54), channel_id=1, source_target_pairs={{0,32},{4,36},{8,40},{12,44},{16,48},{20,52},{24,56},{28,60},{32,6... | collective-permute-start | bytes 184328 | tf_op jit(solution)/shard_map/ppermute | solution.py:435
  129.6 2.8 %collective-permute-start.26 = (bf16[2,96,160]{2,1,0:T(8,128)(2,1)S(1)}, bf16[2,96,160]{2,1,0:T(8,128)(2,1)S(1)}, u32[]{:S(2)}, u32[]{:S(2)}) collective-permute-start(bf16[2,96,160]{2,1,0:T(8,128)(2,1)S(1)} %get-tuple-element.56), channel_id=1, source_target_pairs={{0,96},{4,100},{8,104},{12,108},{16,112},{20,116},{24,120},{28,124... | collective-permute-start | bytes 184328 | tf_op jit(solution)/shard_map/ppermute | solution.py:435
  133.0 4.3 %collective-permute-start.31 = (bf16[96,320]{1,0:T(8,128)(2,1)S(1)}, bf16[96,320]{1,0:T(8,128)(2,1)S(1)}, u32[]{:S(2)}, u32[]{:S(2)}) collective-permute-start(bf16[96,320]{1,0:T(8,128)(2,1)S(1)} %get-tuple-element.63), channel_id=1, source_target_pairs={{0,128},{4,132},{8,136},{12,140},{16,144},{20,148},{24,152},{28,15... | collective-permute-start | bytes 184328 | tf_op jit(solution)/shard_map/ppermute | solution.py:377
  137.9 2.5 %collective-permute-start.27 = (bf16[96,160]{1,0:T(8,128)(2,1)S(1)}, bf16[96,160]{1,0:T(8,128)(2,1)S(1)}, u32[]{:S(2)}, u32[]{:S(2)}) collective-permute-start(bf16[96,160]{1,0:T(8,128)(2,1)S(1)} %get-tuple-element.58), channel_id=1, source_target_pairs={{0,128},{4,132},{8,136},{12,140},{16,144},{20,148},{24,152},{28,15... | collective-permute-start | bytes 92168 | tf_op jit(solution)/shard_map/ppermute | solution.py:377
  140.4 1.8 %collective-permute-done.31.refs_1_ = bf16[96,320]{1,0:T(8,128)(2,1)S(1)} collective-permute-done((bf16[96,320]{1,0:T(8,128)(2,1)S(1)}, bf16[96,320]{1,0:T(8,128)(2,1)S(1)}, u32[]{:S(2)}, u32[]{:S(2)}) %collective-permute-start.31) | collective-permute-done | bytes 61472 | tf_op jit(solution)/shard_map/ppermute | solution.py:377
  144.2 2.2 %collective-permute-done.27.refs_1_ = bf16[96,160]{1,0:T(8,128)(2,1)S(1)} collective-permute-done((bf16[96,160]{1,0:T(8,128)(2,1)S(1)}, bf16[96,160]{1,0:T(8,128)(2,1)S(1)}, u32[]{:S(2)}, u32[]{:S(2)}) %collective-permute-start.27) | collective-permute-done | bytes 30752 | tf_op jit(solution)/shard_map/ppermute | solution.py:377
  (93 shorter events, 29.8 us)
Async XLA Ops:
  0.6 13.9 %collective-permute-start = (bf16[2,64,640]{2,1,0:T(8,128)(2,1)}, bf16[2,64,640]{2,1,0:T(8,128)(2,1)S(1)}, u32[]{:S(2)}, u32[]{:S(2)}) collective-permute-start(bf16[2,64,640]{2,1,0:T(8,128)(2,1)} %refs_1_.3), channel_id=1, source_target_pairs={{0,1},{1,2},{2,3},{3,0},{4,5},{5,6},{6,7},{7,4},{8,9},{9,10},{10,1... | collective-permute-start | bytes 491528 | tf_op jit(solution)/shard_map/ppermute | solution.py:374
  2.6 14.3 %collective-permute-start.1 = (bf16[2,64,640]{2,1,0:T(8,128)(2,1)}, bf16[2,64,640]{2,1,0:T(8,128)(2,1)S(1)}, u32[]{:S(2)}, u32[]{:S(2)}) collective-permute-start(bf16[2,64,640]{2,1,0:T(8,128)(2,1)} %refs_1_.3), channel_id=1, source_target_pairs={{0,2},{1,3},{2,0},{3,1},{4,6},{5,7},{6,4},{7,5},{8,10},{9,11},{10,... | collective-permute-start | bytes 491528 | tf_op jit(solution)/shard_map/ppermute | solution.py:374
  4.9 14.0 %collective-permute-start.2 = (bf16[2,64,640]{2,1,0:T(8,128)(2,1)}, bf16[2,64,640]{2,1,0:T(8,128)(2,1)S(1)}, u32[]{:S(2)}, u32[]{:S(2)}) collective-permute-start(bf16[2,64,640]{2,1,0:T(8,128)(2,1)} %refs_1_.3), channel_id=1, source_target_pairs={{0,3},{1,0},{2,1},{3,2},{4,7},{5,4},{6,5},{7,6},{8,11},{9,8},{10,9... | collective-permute-start | bytes 491528 | tf_op jit(solution)/shard_map/ppermute | solution.py:374
  23.4 9.8 %collective-permute-start.4 = (bf16[160,128]{1,0:T(8,128)(2,1)S(1)}, bf16[160,128]{1,0:T(8,128)(2,1)S(1)}, u32[]{:S(2)}, u32[]{:S(2)}) collective-permute-start(bf16[160,128]{1,0:T(8,128)(2,1)S(1)} %get-tuple-element.36), channel_id=1, source_target_pairs={{4,8},{8,4},{12,16},{16,12},{20,24},{24,20},{28,32},{32,28},{36,40... | collective-permute-start | bytes 122888 | tf_op jit(solution)/shard_map/ppermute | solution.py:380
  27.2 17.7 %all-to-all-start = ((bf16[8,80,512]{2,1,0:T(8,128)(2,1)}), bf16[8,80,512]{2,1,0:T(8,128)(2,1)S(1)}, u32[]{:S(2)}, u32[]{:S(2)}) async-start(bf16[8,80,512]{2,1,0:T(8,128)(2,1)} %shard_map.94.refs_3_), calls=%async_computation | async-start | bytes 1310720 | tf_op jit(solution)/shard_map/all_to_all | solution.py:397
  33.2 4.1 %collective-permute-start.5 = (bf16[160,128]{1,0:T(8,128)(2,1)S(1)}, bf16[160,128]{1,0:T(8,128)(2,1)S(1)}, u32[]{:S(2)}, u32[]{:S(2)}) collective-permute-start(bf16[160,128]{1,0:T(8,128)(2,1)S(1)} %shard_map.95.refs_1_), channel_id=1, source_target_pairs={{0,1},{1,2},{2,3},{3,0},{4,5},{5,6},{6,7},{7,4},{8,9},{9,10},{10,1... | collective-permute-start | bytes 122888 | tf_op jit(solution)/shard_map/ppermute | solution.py:374
  33.3 5.5 %collective-permute-start.6 = (bf16[160,128]{1,0:T(8,128)(2,1)S(1)}, bf16[160,128]{1,0:T(8,128)(2,1)S(1)}, u32[]{:S(2)}, u32[]{:S(2)}) collective-permute-start(bf16[160,128]{1,0:T(8,128)(2,1)S(1)} %shard_map.95.refs_1_), channel_id=1, source_target_pairs={{0,2},{1,3},{2,0},{3,1},{4,6},{5,7},{6,4},{7,5},{8,10},{9,11},{10,... | collective-permute-start | bytes 122888 | tf_op jit(solution)/shard_map/ppermute | solution.py:374
  34.7 5.8 %collective-permute-start.7 = (bf16[160,128]{1,0:T(8,128)(2,1)S(1)}, bf16[160,128]{1,0:T(8,128)(2,1)S(1)}, u32[]{:S(2)}, u32[]{:S(2)}) collective-permute-start(bf16[160,128]{1,0:T(8,128)(2,1)S(1)} %shard_map.95.refs_1_), channel_id=1, source_target_pairs={{0,3},{1,0},{2,1},{3,2},{4,7},{5,4},{6,5},{7,6},{8,11},{9,8},{10,9... | collective-permute-start | bytes 122888 | tf_op jit(solution)/shard_map/ppermute | solution.py:374
  41.8 5.6 %collective-permute-start.8 = (bf16[320,128]{1,0:T(8,128)(2,1)S(1)}, bf16[320,128]{1,0:T(8,128)(2,1)S(1)}, u32[]{:S(2)}, u32[]{:S(2)}) collective-permute-start(bf16[320,128]{1,0:T(8,128)(2,1)S(1)} %get-tuple-element.39), channel_id=1, source_target_pairs={{0,4},{4,0},{8,12},{12,8},{16,20},{20,16},{24,28},{28,24},{32,36},... | collective-permute-start | bytes 245768 | tf_op jit(solution)/shard_map/ppermute | solution.py:377
  42.0 5.5 %collective-permute-start.9 = (bf16[320,128]{1,0:T(8,128)(2,1)S(1)}, bf16[320,128]{1,0:T(8,128)(2,1)S(1)}, u32[]{:S(2)}, u32[]{:S(2)}) collective-permute-start(bf16[320,128]{1,0:T(8,128)(2,1)S(1)} %get-tuple-element.40), channel_id=1, source_target_pairs={{4,8},{8,4},{12,16},{16,12},{20,24},{24,20},{28,32},{32,28},{36,40... | collective-permute-start | bytes 245768 | tf_op jit(solution)/shard_map/ppermute | solution.py:380
  48.9 10.4 %collective-permute-start.11 = (bf16[320,128]{1,0:T(8,128)(2,1)S(1)}, bf16[320,128]{1,0:T(8,128)(2,1)S(1)}, u32[]{:S(2)}, u32[]{:S(2)}) collective-permute-start(bf16[320,128]{1,0:T(8,128)(2,1)S(1)} %get-tuple-element.42.refs_2_.refs_0_), channel_id=1, source_target_pairs={{4,8},{8,4},{12,16},{16,12},{20,24},{24,20},{28,32},{32,28},{36,40... | collective-permute-start | bytes 245768 | tf_op jit(solution)/shard_map/ppermute | solution.py:380
  50.9 22.4 %all-to-all-start.1 = ((bf16[8,80,128]{2,1,0:T(8,128)(2,1)}), bf16[8,80,128]{2,1,0:T(8,128)(2,1)S(1)}, u32[]{:S(2)}, u32[]{:S(2)}) async-start(bf16[8,80,128]{2,1,0:T(8,128)(2,1)} %shard_map.100.refs_3_), calls=%async_computation.1 | async-start | bytes 327680 | tf_op jit(solution)/shard_map/all_to_all | solution.py:415
  59.3 10.6 %collective-permute-start.17 = (bf16[3,320,128]{2,1,0:T(8,128)(2,1)S(1)}, bf16[3,320,128]{2,1,0:T(8,128)(2,1)S(1)}, u32[]{:S(2)}, u32[]{:S(2)}) collective-permute-start(bf16[3,320,128]{2,1,0:T(8,128)(2,1)S(1)} %shard_map.103.refs_1_), channel_id=1, source_target_pairs={{0,8},{4,12},{8,0},{12,4},{16,24},{20,28},{24,16},{28,20},{32,40},... | collective-permute-start | bytes 737288 | tf_op jit(solution)/shard_map/ppermute | solution.py:377
  65.4 4.5 %collective-permute-start.12 = (bf16[160,128]{1,0:T(8,128)(2,1)S(1)}, bf16[160,128]{1,0:T(8,128)(2,1)S(1)}, u32[]{:S(2)}, u32[]{:S(2)}) collective-permute-start(bf16[160,128]{1,0:T(8,128)(2,1)S(1)} %get-tuple-element.44), channel_id=1, source_target_pairs={{0,1},{1,2},{2,3},{3,0},{4,5},{5,6},{6,7},{7,4},{8,9},{9,10},{10,1... | collective-permute-start | bytes 122888 | tf_op jit(solution)/shard_map/ppermute | solution.py:374
  66.5 6.7 %collective-permute-start.13 = (bf16[160,128]{1,0:T(8,128)(2,1)S(1)}, bf16[160,128]{1,0:T(8,128)(2,1)S(1)}, u32[]{:S(2)}, u32[]{:S(2)}) collective-permute-start(bf16[160,128]{1,0:T(8,128)(2,1)S(1)} %get-tuple-element.45), channel_id=1, source_target_pairs={{0,2},{1,3},{2,0},{3,1},{4,6},{5,7},{6,4},{7,5},{8,10},{9,11},{10,... | collective-permute-start | bytes 122888 | tf_op jit(solution)/shard_map/ppermute | solution.py:374
  69.0 4.3 %collective-permute-start.14 = (bf16[160,128]{1,0:T(8,128)(2,1)S(1)}, bf16[160,128]{1,0:T(8,128)(2,1)S(1)}, u32[]{:S(2)}, u32[]{:S(2)}) collective-permute-start(bf16[160,128]{1,0:T(8,128)(2,1)S(1)} %get-tuple-element.46), channel_id=1, source_target_pairs={{0,3},{1,0},{2,1},{3,2},{4,7},{5,4},{6,5},{7,6},{8,11},{9,8},{10,9... | collective-permute-start | bytes 122888 | tf_op jit(solution)/shard_map/ppermute | solution.py:374
  70.5 12.7 %collective-permute-start.18 = (bf16[5,320,128]{2,1,0:T(8,128)(2,1)S(1)}, bf16[5,320,128]{2,1,0:T(8,128)(2,1)S(1)}, u32[]{:S(2)}, u32[]{:S(2)}) collective-permute-start(bf16[5,320,128]{2,1,0:T(8,128)(2,1)S(1)} %get-tuple-element.49.refs_1_), channel_id=1, source_target_pairs={{0,16},{4,20},{8,24},{12,28},{16,0},{20,4},{24,8},{28,12},{32,48},... | collective-permute-start | bytes 1228808 | tf_op jit(solution)/shard_map/ppermute | solution.py:377
  73.3 10.6 %collective-permute-start.15 = (bf16[160,128]{1,0:T(8,128)(2,1)S(1)}, bf16[160,128]{1,0:T(8,128)(2,1)S(1)}, u32[]{:S(2)}, u32[]{:S(2)}) collective-permute-start(bf16[160,128]{1,0:T(8,128)(2,1)S(1)} %shard_map.101.refs_0_.refs_2_), channel_id=1, source_target_pairs={{0,4},{4,0},{8,12},{12,8},{16,20},{20,16},{24,28},{28,24},{32,36},... | collective-permute-start | bytes 122888 | tf_op jit(solution)/shard_map/ppermute | solution.py:377
  73.4 10.5 %collective-permute-start.16 = (bf16[160,128]{1,0:T(8,128)(2,1)S(1)}, bf16[160,128]{1,0:T(8,128)(2,1)S(1)}, u32[]{:S(2)}, u32[]{:S(2)}) collective-permute-start(bf16[160,128]{1,0:T(8,128)(2,1)S(1)} %shard_map.101.refs_0_.refs_2_), channel_id=1, source_target_pairs={{4,8},{8,4},{12,16},{16,12},{20,24},{24,20},{28,32},{32,28},{36,40... | collective-permute-start | bytes 122888 | tf_op jit(solution)/shard_map/ppermute | solution.py:380
  83.8 6.7 %collective-permute-start.22 = (bf16[320,128]{1,0:T(8,128)(2,1)S(1)}, bf16[320,128]{1,0:T(8,128)(2,1)S(1)}, u32[]{:S(2)}, u32[]{:S(2)}) collective-permute-start(bf16[320,128]{1,0:T(8,128)(2,1)S(1)} %shard_map.105.refs_4_.refs_3_), channel_id=1, source_target_pairs={{0,4},{4,0},{8,12},{12,8},{16,20},{20,16},{24,28},{28,24},{32,36},... | collective-permute-start | bytes 245768 | tf_op jit(solution)/shard_map/ppermute | solution.py:377
  84.0 10.2 %collective-permute-start.19 = (bf16[3,160,128]{2,1,0:T(8,128)(2,1)S(1)}, bf16[3,160,128]{2,1,0:T(8,128)(2,1)S(1)}, u32[]{:S(2)}, u32[]{:S(2)}) collective-permute-start(bf16[3,160,128]{2,1,0:T(8,128)(2,1)S(1)} %shard_map.106.refs_5_.refs_7_.refs_1_), channel_id=1, source_target_pairs={{0,8},{4,12},{8,0},{12,4},{16,24},{20,28},{24,16},{28,20},{32,40},... | collective-permute-start | bytes 368648 | tf_op jit(solution)/shard_map/ppermute | solution.py:377
  84.1 10.3 %collective-permute-start.20 = (bf16[3,160,128]{2,1,0:T(8,128)(2,1)S(1)}, bf16[3,160,128]{2,1,0:T(8,128)(2,1)S(1)}, u32[]{:S(2)}, u32[]{:S(2)}) collective-permute-start(bf16[3,160,128]{2,1,0:T(8,128)(2,1)S(1)} %shard_map.106.refs_5_.refs_7_.refs_1_), channel_id=1, source_target_pairs={{0,16},{4,20},{8,24},{12,28},{16,0},{20,4},{24,8},{28,12},{32,48},... | collective-permute-start | bytes 368648 | tf_op jit(solution)/shard_map/ppermute | solution.py:377
  87.9 8.8 %collective-permute-start.21 = (bf16[3,160,128]{2,1,0:T(8,128)(2,1)S(1)}, bf16[3,160,128]{2,1,0:T(8,128)(2,1)S(1)}, u32[]{:S(2)}, u32[]{:S(2)}) collective-permute-start(bf16[3,160,128]{2,1,0:T(8,128)(2,1)S(1)} %shard_map.106.refs_5_.refs_7_.refs_1_), channel_id=1, source_target_pairs={{0,24},{4,28},{8,16},{12,20},{16,8},{20,12},{24,0},{28,4},{32,56},... | collective-permute-start | bytes 368648 | tf_op jit(solution)/shard_map/ppermute | solution.py:377
  98.5 44.5 %all-to-all-start.2 = ((bf16[4,2,64,640]{3,2,1,0:T(8,128)(2,1)}), bf16[4,2,64,640]{3,2,1,0:T(8,128)(2,1)}, u32[]{:S(2)}, u32[]{:S(2)}) async-start(bf16[4,2,64,640]{3,2,1,0:T(8,128)(2,1)} %shard_map.110), calls=%async_computation.2 | async-start | bytes 1310720 | tf_op jit(solution)/shard_map/all_to_all | solution.py:472
  104.8 24.8 %collective-permute-start.28 = (bf16[2,96,320]{2,1,0:T(8,128)(2,1)S(1)}, bf16[2,96,320]{2,1,0:T(8,128)(2,1)S(1)}, u32[]{:S(2)}, u32[]{:S(2)}) collective-permute-start(bf16[2,96,320]{2,1,0:T(8,128)(2,1)S(1)} %copy-done.12), channel_id=1, source_target_pairs={{0,32},{4,36},{8,40},{12,44},{16,48},{20,52},{24,56},{28,60},{32,6... | collective-permute-start | bytes 368648 | tf_op jit(solution)/shard_map/ppermute | solution.py:435
  106.3 26.1 %collective-permute-start.29 = (bf16[2,96,320]{2,1,0:T(8,128)(2,1)S(1)}, bf16[2,96,320]{2,1,0:T(8,128)(2,1)S(1)}, u32[]{:S(2)}, u32[]{:S(2)}) collective-permute-start(bf16[2,96,320]{2,1,0:T(8,128)(2,1)S(1)} %get-tuple-element.60), channel_id=1, source_target_pairs={{0,64},{4,68},{8,72},{12,76},{16,80},{20,84},{24,88},{28,92},{32,9... | collective-permute-start | bytes 368648 | tf_op jit(solution)/shard_map/ppermute | solution.py:435
  124.0 8.3 %collective-permute-start.30 = (bf16[2,96,320]{2,1,0:T(8,128)(2,1)S(1)}, bf16[2,96,320]{2,1,0:T(8,128)(2,1)S(1)}, u32[]{:S(2)}, u32[]{:S(2)}) collective-permute-start(bf16[2,96,320]{2,1,0:T(8,128)(2,1)S(1)} %get-tuple-element.61), channel_id=1, source_target_pairs={{0,96},{4,100},{8,104},{12,108},{16,112},{20,116},{24,120},{28,124... | collective-permute-start | bytes 368648 | tf_op jit(solution)/shard_map/ppermute | solution.py:435
  127.5 9.8 %collective-permute-start.24 = (bf16[2,96,160]{2,1,0:T(8,128)(2,1)S(1)}, bf16[2,96,160]{2,1,0:T(8,128)(2,1)S(1)}, u32[]{:S(2)}, u32[]{:S(2)}) collective-permute-start(bf16[2,96,160]{2,1,0:T(8,128)(2,1)S(1)} %get-tuple-element.54), channel_id=1, source_target_pairs={{0,32},{4,36},{8,40},{12,44},{16,48},{20,52},{24,56},{28,60},{32,6... | collective-permute-start | bytes 184328 | tf_op jit(solution)/shard_map/ppermute | solution.py:435
  129.6 7.7 %collective-permute-start.25 = (bf16[2,96,160]{2,1,0:T(8,128)(2,1)S(1)}, bf16[2,96,160]{2,1,0:T(8,128)(2,1)S(1)}, u32[]{:S(2)}, u32[]{:S(2)}) collective-permute-start(bf16[2,96,160]{2,1,0:T(8,128)(2,1)S(1)} %get-tuple-element.55), channel_id=1, source_target_pairs={{0,64},{4,68},{8,72},{12,76},{16,80},{20,84},{24,88},{28,92},{32,9... | collective-permute-start | bytes 184328 | tf_op jit(solution)/shard_map/ppermute | solution.py:435
  129.6 7.7 %collective-permute-start.26 = (bf16[2,96,160]{2,1,0:T(8,128)(2,1)S(1)}, bf16[2,96,160]{2,1,0:T(8,128)(2,1)S(1)}, u32[]{:S(2)}, u32[]{:S(2)}) collective-permute-start(bf16[2,96,160]{2,1,0:T(8,128)(2,1)S(1)} %get-tuple-element.56), channel_id=1, source_target_pairs={{0,96},{4,100},{8,104},{12,108},{16,112},{20,116},{24,120},{28,124... | collective-permute-start | bytes 184328 | tf_op jit(solution)/shard_map/ppermute | solution.py:435
  133.0 9.2 %collective-permute-start.31 = (bf16[96,320]{1,0:T(8,128)(2,1)S(1)}, bf16[96,320]{1,0:T(8,128)(2,1)S(1)}, u32[]{:S(2)}, u32[]{:S(2)}) collective-permute-start(bf16[96,320]{1,0:T(8,128)(2,1)S(1)} %get-tuple-element.63), channel_id=1, source_target_pairs={{0,128},{4,132},{8,136},{12,140},{16,144},{20,148},{24,152},{28,15... | collective-permute-start | bytes 184328 | tf_op jit(solution)/shard_map/ppermute | solution.py:377
  137.9 8.5 %collective-permute-start.27 = (bf16[96,160]{1,0:T(8,128)(2,1)S(1)}, bf16[96,160]{1,0:T(8,128)(2,1)S(1)}, u32[]{:S(2)}, u32[]{:S(2)}) collective-permute-start(bf16[96,160]{1,0:T(8,128)(2,1)S(1)} %get-tuple-element.58), channel_id=1, source_target_pairs={{0,128},{4,132},{8,136},{12,140},{16,144},{20,148},{24,152},{28,15... | collective-permute-start | bytes 92168 | tf_op jit(solution)/shard_map/ppermute | solution.py:377
  (17 other events, 64.9 us)

commit v13 on v12

--- a/solution.py
+++ b/solution.py
@@ -56,7 +56,7 @@
     vmem = pl.BlockSpec(memory_space=pltpu.VMEM)
     aside = pl.BlockSpec(memory_space=pl.ANY)
     count = len(args)
-    flops = CHAIN if body in (fine_forward, pool_add, deep_forward, deep_backward, pool_sum, fine_backward) else 0
+    flops = CHAIN if body in (fine_forward, pool_add, deep_forward, deep_backward, pool_sum, fine_backward) else CHAIN // 3 if body is tables else 0
 
     def kernel(*refs):
         body(*refs[:count], *refs[count + len(behind) :])
@@ -427,7 +427,6 @@
     grad_pool = call(pool_sum, shape((fine, deep)), (parts[0], *got), behind=(deep_slab,))
     pool_partner, other = pairs(grad_pool, grad_pool)
     pre_rows = group_gather(pre_first, (got[0],))
-    pool_first = call(pack, shape((3, fine, deep)), (grad_pool, pool_partner, other), behind=(deep_table, pre_rows[2]))
 
     def halves(parts):
         width = parts[0].shape[2]
@@ -455,6 +454,8 @@
             behind=behind,
         )
 
+    deep_parts = products(deep_part, (deep_table,), pre_rows)
+    pool_first = call(pack, shape((3, fine, deep)), (grad_pool, pool_partner, other), behind=(deep_parts[0],))
     sides = call(
         fine_backward,
         shape((rows, cols, depth)),
@@ -462,7 +463,6 @@
         [pltpu.VMEM((2, fine, deep), BF)],
         behind=(pool_first,),
     )
-    deep_parts = products(deep_part, (deep_table,), pre_rows, (pool_first,))
     pool_rows = [pool_first] + [swap(pool_first, bit) for bit in (2, 4, 6)]
     pool_edge = call(outer_direct, shape((fine, deep)), (at, *pool_rows), behind=(sides, deep_parts[0]))
     pool_rows += [pool_edge, swap(pool_edge, 1)]

time: 148 us -> 151 us (1.020)
  waiting for transfers between devices: 35.8 us -> 40.6 us
  starting transfers between devices: 78 us -> 75.9 us
    ppermute x13, waiting for transfers between devices: 16.8 us -> 21 us  [swap(): return lax.ppermute(v, 'wide', [(i, i ^ bit) for i in range(wide)])]
    unnamed x30 -> x26, local copies, waits for them, and re-layouts: 9.05 us -> 8.39 us
  transfers between devices with their start and end apart: 35 -> 35, of which waited for: 15 -> 18; matrix products, arithmetic and copies ran while one was open for 1% -> 1% of each run, Pallas kernels for 12% -> 12%
where the time goes in v13:
time: 151 us; the launch traced here: 150 us
  starting transfers between devices  75.9 us (50%)
  waiting for transfers between devices  40.6 us (27%)
  Pallas kernels  22.7 us (15%)
  local copies, waits for them, and re-layouts  8.47 us (6%)
    ppermute x6, starting transfers between devices, halves(): lax.ppermute(parts[s], 'wide', [(i, i // 32 * 32 + (i // 8 + s) % 4 * 8 +...  23.5 us
    pallas_call x23, Pallas kernels, call(): pl.pallas_call(kernel, out_shape=outs, in_specs=[smem if a.dtype == jnp.i...  22.7 us
    ppermute x13, waiting for transfers between devices, swap(): return lax.ppermute(v, 'wide', [(i, i ^ bit) for i in range(wide)])  21 us
    ppermute x9, waiting for transfers between devices, across(): lax.ppermute(v, 'narrow', [(i, (i + step) % pieces) for i in range(pieces)])  16.7 us
    ppermute x13, starting transfers between devices, swap(): return lax.ppermute(v, 'wide', [(i, i ^ bit) for i in range(wide)])  15.8 us
    ppermute x9, starting transfers between devices, across(): lax.ppermute(v, 'narrow', [(i, (i + step) % pieces) for i in range(pieces)])  13.3 us
    unnamed x26, local copies, waits for them, and re-layouts  8.39 us
    all_to_all x1, starting transfers between devices, on_device(): deep_slab = lax.all_to_all(deep_pre, 'wide', 0, 0, axis_index_groups=near)  8.36 us
  transfers between devices with their start and end apart: 35, of which 18 were waited for; matrix products, arithmetic and copies ran while one was open for 1% of the time, Pallas kernels for 12%

profile of v13, /device:TPU:32, one launch (start us, length us, event | category | flops | bytes accessed | tf_op | source)
XLA Modules:
  0.0 149.8 jit_solution(12533219195066511701)
XLA Ops:
  0.6 2.0 %collective-permute-start = (bf16[2,64,640]{2,1,0:T(8,128)(2,1)}, bf16[2,64,640]{2,1,0:T(8,128)(2,1)S(1)}, u32[]{:S(2)}, u32[]{:S(2)}) collective-permute-start(bf16[2,64,640]{2,1,0:T(8,128)(2,1)} %refs_1_.3), channel_id=1, source_target_pairs={{0,1},{1,2},{2,3},{3,0},{4,5},{5,6},{6,7},{7,4},{8,9},{9,10},{10,1... | collective-permute-start | bytes 491528 | tf_op jit(solution)/shard_map/ppermute | solution.py:374
  2.6 2.3 %collective-permute-start.1 = (bf16[2,64,640]{2,1,0:T(8,128)(2,1)}, bf16[2,64,640]{2,1,0:T(8,128)(2,1)S(1)}, u32[]{:S(2)}, u32[]{:S(2)}) collective-permute-start(bf16[2,64,640]{2,1,0:T(8,128)(2,1)} %refs_1_.3), channel_id=1, source_target_pairs={{0,2},{1,3},{2,0},{3,1},{4,6},{5,7},{6,4},{7,5},{8,10},{9,11},{10,... | collective-permute-start | bytes 491528 | tf_op jit(solution)/shard_map/ppermute | solution.py:374
  6.1 8.5 %collective-permute-done.refs_2_ = bf16[2,64,640]{2,1,0:T(8,128)(2,1)S(1)} collective-permute-done((bf16[2,64,640]{2,1,0:T(8,128)(2,1)}, bf16[2,64,640]{2,1,0:T(8,128)(2,1)S(1)}, u32[]{:S(2)}, u32[]{:S(2)}) %collective-permute-start) | collective-permute-done | bytes 163872 | tf_op jit(solution)/shard_map/ppermute | solution.py:374
  14.6 2.4 %collective-permute-done.1.refs_3_ = bf16[2,64,640]{2,1,0:T(8,128)(2,1)S(1)} collective-permute-done((bf16[2,64,640]{2,1,0:T(8,128)(2,1)}, bf16[2,64,640]{2,1,0:T(8,128)(2,1)S(1)}, u32[]{:S(2)}, u32[]{:S(2)}) %collective-permute-start.1) | collective-permute-done | bytes 163872 | tf_op jit(solution)/shard_map/ppermute | solution.py:374
  16.9 2.0 %collective-permute-done.2.refs_4_ = bf16[2,64,640]{2,1,0:T(8,128)(2,1)S(1)} collective-permute-done((bf16[2,64,640]{2,1,0:T(8,128)(2,1)}, bf16[2,64,640]{2,1,0:T(8,128)(2,1)S(1)}, u32[]{:S(2)}, u32[]{:S(2)}) %collective-permute-start.2) | collective-permute-done | bytes 163872 | tf_op jit(solution)/shard_map/ppermute | solution.py:374
  21.3 1.9 %shard_map.93 = (bf16[4,2,64,640]{3,2,1,0:T(8,128)(2,1)S(1)}, f32[160,128]{1,0:T(8,128)S(1)}, bf16[160,128]{1,0:T(8,128)(2,1)S(1)}, bf16[160,128]{1,0:T(8,128)(2,1)S(1)}) custom-call(s32[5]{0:T(128)S(1)} %stack.23.refs_0_, bf16[2,64,640]{2,1,0:T(8,128)(2,1)S(1)} %copy-done.10, bf16[2,64,640]{2,1,0:T(8,128)(2,1)S(1)} %collective-permute-done.refs_2_, ...), custom_call_target="tpu_custom_call" | custom-call | flops 30000001024 | bytes 2498580 | tf_op jit(solution)/shard_map/pallas_call | solution.py:64
  24.6 2.6 %shard_map.94.refs_3_ = bf16[8,80,512]{2,1,0:T(8,128)(2,1)} custom-call(bf16[4,2,64,640]{3,2,1,0:T(8,128)(2,1)S(1)} %get-tuple-element.37.refs_0_, bf16[640,640]{1,0:T(8,128)(2,1)S(1)} %copy-done.4, bf16[160,128]{1,0:T(8,128)(2,1)S(1)} %collective-permute-done.3.refs_2_.refs_1_), custom_call_target="tpu_custom_call" | custom-call | bytes 1474560 | tf_op jit(solution)/shard_map/pallas_call | solution.py:64
  27.2 6.0 %all-to-all-start = ((bf16[8,80,512]{2,1,0:T(8,128)(2,1)}), bf16[8,80,512]{2,1,0:T(8,128)(2,1)S(1)}, u32[]{:S(2)}, u32[]{:S(2)}) async-start(bf16[8,80,512]{2,1,0:T(8,128)(2,1)} %shard_map.94.refs_3_), calls=%async_computation | async-start | bytes 1310720 | tf_op jit(solution)/shard_map/all_to_all | solution.py:397
  34.7 1.9 %collective-permute-start.7 = (bf16[160,128]{1,0:T(8,128)(2,1)S(1)}, bf16[160,128]{1,0:T(8,128)(2,1)S(1)}, u32[]{:S(2)}, u32[]{:S(2)}) collective-permute-start(bf16[160,128]{1,0:T(8,128)(2,1)S(1)} %shard_map.95.refs_1_), channel_id=1, source_target_pairs={{0,3},{1,0},{2,1},{3,2},{4,7},{5,4},{6,5},{7,6},{8,11},{9,8},{10,9... | collective-permute-start | bytes 122888 | tf_op jit(solution)/shard_map/ppermute | solution.py:374
  42.6 2.3 %all-to-all-done.refs_2_.refs_0_ = bf16[8,80,512]{2,1,0:T(8,128)(2,1)S(1)} async-done(((bf16[8,80,512]{2,1,0:T(8,128)(2,1)}), bf16[8,80,512]{2,1,0:T(8,128)(2,1)S(1)}, u32[]{:S(2)}, u32[]{:S(2)}) %all-to-all-start) | async-done | bytes 655392 | tf_op jit(solution)/shard_map/all_to_all | solution.py:397
  44.9 2.0 %copy-done.1 = bf16[3,3,640,320]{2,3,1,0:T(8,128)(2,1)S(1)} copy-done((bf16[3,3,640,320]{2,3,1,0:T(8,128)(2,1)S(1)}, bf16[3,3,640,320]{2,3,1,0:T(8,128)(2,1)}, u32[]{:S(2)}) %copy-start.1) | copy-done | bytes 3686424
  50.9 8.4 %all-to-all-start.1 = ((bf16[8,80,128]{2,1,0:T(8,128)(2,1)}), bf16[8,80,128]{2,1,0:T(8,128)(2,1)S(1)}, u32[]{:S(2)}, u32[]{:S(2)}) async-start(bf16[8,80,128]{2,1,0:T(8,128)(2,1)} %shard_map.100.refs_3_), calls=%async_computation.1 | async-start | bytes 327680 | tf_op jit(solution)/shard_map/all_to_all | solution.py:415
  59.3 2.1 %collective-permute-start.17 = (bf16[3,320,128]{2,1,0:T(8,128)(2,1)S(1)}, bf16[3,320,128]{2,1,0:T(8,128)(2,1)S(1)}, u32[]{:S(2)}, u32[]{:S(2)}) collective-permute-start(bf16[3,320,128]{2,1,0:T(8,128)(2,1)S(1)} %shard_map.102.refs_1_), channel_id=1, source_target_pairs={{0,8},{4,12},{8,0},{12,4},{16,24},{20,28},{24,16},{28,20},{32,40},... | collective-permute-start | bytes 737288 | tf_op jit(solution)/shard_map/ppermute | solution.py:377
  61.4 2.0 %copy-done.2 = bf16[3,3,640,320]{2,3,1,0:T(8,128)(2,1)S(1)} copy-done((bf16[3,3,640,320]{2,3,1,0:T(8,128)(2,1)S(1)}, bf16[3,3,640,320]{2,3,1,0:T(8,128)(2,1)}, u32[]{:S(2)}) %copy-start.2) | copy-done | bytes 3686424
  63.4 1.9 %shard_map.99 = (bf16[160,128]{1,0:T(8,128)(2,1)S(1)}, bf16[160,128]{1,0:T(8,128)(2,1)S(1)}, bf16[160,128]{1,0:T(8,128)(2,1)S(1)}, bf16[160,128]{1,0:T(8,128)(2,1)S(1)}) custom-call(s32[5]{0:T(128)S(1)} %stack.23.refs_0_, bf16[320,128]{1,0:T(8,128)(2,1)S(1)} %collective-permute-done.10.refs_1_.refs_2_, ...), custom_call_target="tpu_custom_call" | custom-call | flops 30000001024 | bytes 3932180 | tf_op jit(solution)/shard_map/pallas_call | solution.py:64
  66.5 2.5 %collective-permute-start.13 = (bf16[160,128]{1,0:T(8,128)(2,1)S(1)}, bf16[160,128]{1,0:T(8,128)(2,1)S(1)}, u32[]{:S(2)}, u32[]{:S(2)}) collective-permute-start(bf16[160,128]{1,0:T(8,128)(2,1)S(1)} %get-tuple-element.45), channel_id=1, source_target_pairs={{0,2},{1,3},{2,0},{3,1},{4,6},{5,7},{6,4},{7,5},{8,10},{9,11},{10,... | collective-permute-start | bytes 122888 | tf_op jit(solution)/shard_map/ppermute | solution.py:374
  70.5 2.8 %collective-permute-start.18 = (bf16[5,320,128]{2,1,0:T(8,128)(2,1)S(1)}, bf16[5,320,128]{2,1,0:T(8,128)(2,1)S(1)}, u32[]{:S(2)}, u32[]{:S(2)}) collective-permute-start(bf16[5,320,128]{2,1,0:T(8,128)(2,1)S(1)} %get-tuple-element.47.refs_1_), channel_id=1, source_target_pairs={{0,16},{4,20},{8,24},{12,28},{16,0},{20,4},{24,8},{28,12},{32,48},... | collective-permute-start | bytes 1228808 | tf_op jit(solution)/shard_map/ppermute | solution.py:377
  74.1 9.1 %collective-permute-done.18.refs_2_ = bf16[5,320,128]{2,1,0:T(8,128)(2,1)S(1)} collective-permute-done((bf16[5,320,128]{2,1,0:T(8,128)(2,1)S(1)}, bf16[5,320,128]{2,1,0:T(8,128)(2,1)S(1)}, u32[]{:S(2)}, u32[]{:S(2)}) %collective-permute-start.18) | collective-permute-done | bytes 409632 | tf_op jit(solution)/shard_map/ppermute | solution.py:377
  85.2 3.6 %shard_map.106 = (bf16[2,96,320]{2,1,0:T(8,128)(2,1)S(1)}, bf16[2,96,320]{2,1,0:T(8,128)(2,1)}, bf16[2,96,320]{2,1,0:T(8,128)(2,1)}, bf16[2,96,320]{2,1,0:T(8,128)(2,1)S(1)}) custom-call(s32[5]{0:T(128)S(1)} %stack.23.refs_0_, bf16[5,320,128]{2,1,0:T(8,128)(2,1)S(1)} %copy-done.7, bf16[5,320,128]{2,1,0:T(8,128)(2,1)S(1)} %collective-permute-done.18.refs_2_, ...), custom_call_target="tpu_custom_call" | custom-call | bytes 2580500 | tf_op jit(solution)/shard_map/pallas_call | solution.py:64
  89.0 3.9 %collective-permute-start.21 = (bf16[3,160,128]{2,1,0:T(8,128)(2,1)S(1)}, bf16[3,160,128]{2,1,0:T(8,128)(2,1)S(1)}, u32[]{:S(2)}, u32[]{:S(2)}) collective-permute-start(bf16[3,160,128]{2,1,0:T(8,128)(2,1)S(1)} %shard_map.107.refs_5_.refs_1_), channel_id=1, source_target_pairs={{0,16},{4,20},{8,24},{12,28},{16,0},{20,4},{24,8},{28,12},{32,48},... | collective-permute-start | bytes 368648 | tf_op jit(solution)/shard_map/ppermute | solution.py:377
  93.6 1.8 %shard_map.108.refs_5_.refs_0_ = bf16[2,256,640]{2,1,0:T(8,128)(2,1)S(1)} custom-call(s32[5]{0:T(128)S(1)} %stack.23.refs_0_, bf16[160,128]{1,0:T(8,128)(2,1)S(1)} %collective-permute-done.15.refs_1_, bf16[160,128]{1,0:T(8,128)(2,1)S(1)} %shard_map.101.refs_0_.refs_2_, bf16[160,128]{1,0:T(8,128)(2,1)S(1)} %collective-permute-done.16.refs_2_.refs_3_, ...), custom_call_target="tpu_custom_call" | custom-call | flops 30000001024 | bytes 1966100 | tf_op jit(solution)/shard_map/pallas_call | solution.py:64
  95.5 3.4 %collective-permute-done.21.refs_3_ = bf16[3,160,128]{2,1,0:T(8,128)(2,1)S(1)} collective-permute-done((bf16[3,160,128]{2,1,0:T(8,128)(2,1)S(1)}, bf16[3,160,128]{2,1,0:T(8,128)(2,1)S(1)}, u32[]{:S(2)}, u32[]{:S(2)}) %collective-permute-start.21) | collective-permute-done | bytes 122912 | tf_op jit(solution)/shard_map/ppermute | solution.py:377
  98.9 2.2 %collective-permute-done.22.refs_4_ = bf16[3,160,128]{2,1,0:T(8,128)(2,1)S(1)} collective-permute-done((bf16[3,160,128]{2,1,0:T(8,128)(2,1)S(1)}, bf16[3,160,128]{2,1,0:T(8,128)(2,1)S(1)}, u32[]{:S(2)}, u32[]{:S(2)}) %collective-permute-start.22) | collective-permute-done | bytes 122912 | tf_op jit(solution)/shard_map/ppermute | solution.py:377
  102.9 6.3 %all-to-all-start.2 = ((bf16[4,2,64,640]{3,2,1,0:T(8,128)(2,1)}), bf16[4,2,64,640]{3,2,1,0:T(8,128)(2,1)}, u32[]{:S(2)}, u32[]{:S(2)}) async-start(bf16[4,2,64,640]{3,2,1,0:T(8,128)(2,1)} %shard_map.110), calls=%async_computation.2 | async-start | bytes 1310720 | tf_op jit(solution)/shard_map/all_to_all | solution.py:472
  110.7 17.1 %collective-permute-start.29 = (bf16[2,96,320]{2,1,0:T(8,128)(2,1)}, bf16[2,96,320]{2,1,0:T(8,128)(2,1)S(1)}, u32[]{:S(2)}, u32[]{:S(2)}) collective-permute-start(bf16[2,96,320]{2,1,0:T(8,128)(2,1)} %get-tuple-element.60), channel_id=1, source_target_pairs={{0,64},{4,68},{8,72},{12,76},{16,80},{20,84},{24,88},{28,92},{32,9... | collective-permute-start | bytes 368648 | tf_op jit(solution)/shard_map/ppermute | solution.py:434
  129.0 2.2 %shard_map.111 = (bf16[2,96,160]{2,1,0:T(8,128)(2,1)S(1)}, bf16[2,96,160]{2,1,0:T(8,128)(2,1)S(1)}, bf16[2,96,160]{2,1,0:T(8,128)(2,1)S(1)}, bf16[2,96,160]{2,1,0:T(8,128)(2,1)S(1)}) custom-call(s32[5]{0:T(128)S(1)} %stack.23.refs_0_, bf16[3,160,128]{2,1,0:T(8,128)(2,1)S(1)} %shard_map.107.refs_5_.refs_1_, ...), custom_call_target="tpu_custom_call" | custom-call | bytes 2662420 | tf_op jit(solution)/shard_map/pallas_call | solution.py:64
  131.2 2.1 %collective-permute-start.24 = (bf16[2,96,160]{2,1,0:T(8,128)(2,1)S(1)}, bf16[2,96,160]{2,1,0:T(8,128)(2,1)S(1)}, u32[]{:S(2)}, u32[]{:S(2)}) collective-permute-start(bf16[2,96,160]{2,1,0:T(8,128)(2,1)S(1)} %get-tuple-element.54), channel_id=1, source_target_pairs={{0,32},{4,36},{8,40},{12,44},{16,48},{20,52},{24,56},{28,60},{32,6... | collective-permute-start | bytes 184328 | tf_op jit(solution)/shard_map/ppermute | solution.py:434
  133.3 2.8 %collective-permute-start.26 = (bf16[2,96,160]{2,1,0:T(8,128)(2,1)S(1)}, bf16[2,96,160]{2,1,0:T(8,128)(2,1)S(1)}, u32[]{:S(2)}, u32[]{:S(2)}) collective-permute-start(bf16[2,96,160]{2,1,0:T(8,128)(2,1)S(1)} %get-tuple-element.56), channel_id=1, source_target_pairs={{0,96},{4,100},{8,104},{12,108},{16,112},{20,116},{24,120},{28,124... | collective-permute-start | bytes 184328 | tf_op jit(solution)/shard_map/ppermute | solution.py:434
  136.7 2.6 %collective-permute-start.31 = (bf16[96,320]{1,0:T(8,128)(2,1)S(1)}, bf16[96,320]{1,0:T(8,128)(2,1)S(1)}, u32[]{:S(2)}, u32[]{:S(2)}) collective-permute-start(bf16[96,320]{1,0:T(8,128)(2,1)S(1)} %get-tuple-element.63), channel_id=1, source_target_pairs={{0,128},{4,132},{8,136},{12,140},{16,144},{20,148},{24,152},{28,15... | collective-permute-start | bytes 184328 | tf_op jit(solution)/shard_map/ppermute | solution.py:377
  140.6 2.8 %collective-permute-start.27 = (bf16[96,160]{1,0:T(8,128)(2,1)S(1)}, bf16[96,160]{1,0:T(8,128)(2,1)S(1)}, u32[]{:S(2)}, u32[]{:S(2)}) collective-permute-start(bf16[96,160]{1,0:T(8,128)(2,1)S(1)} %get-tuple-element.58), channel_id=1, source_target_pairs={{0,128},{4,132},{8,136},{12,140},{16,144},{20,148},{24,152},{28,15... | collective-permute-start | bytes 92168 | tf_op jit(solution)/shard_map/ppermute | solution.py:377
  143.4 1.7 %collective-permute-done.31.refs_1_ = bf16[96,320]{1,0:T(8,128)(2,1)S(1)} collective-permute-done((bf16[96,320]{1,0:T(8,128)(2,1)S(1)}, bf16[96,320]{1,0:T(8,128)(2,1)S(1)}, u32[]{:S(2)}, u32[]{:S(2)}) %collective-permute-start.31) | collective-permute-done | bytes 61472 | tf_op jit(solution)/shard_map/ppermute | solution.py:377
  147.1 1.9 %collective-permute-done.27.refs_1_ = bf16[96,160]{1,0:T(8,128)(2,1)S(1)} collective-permute-done((bf16[96,160]{1,0:T(8,128)(2,1)S(1)}, bf16[96,160]{1,0:T(8,128)(2,1)S(1)}, u32[]{:S(2)}, u32[]{:S(2)}) %collective-permute-start.27) | collective-permute-done | bytes 30752 | tf_op jit(solution)/shard_map/ppermute | solution.py:377
  (89 shorter events, 31.8 us)
Async XLA Ops:
  0.6 13.9 %collective-permute-start = (bf16[2,64,640]{2,1,0:T(8,128)(2,1)}, bf16[2,64,640]{2,1,0:T(8,128)(2,1)S(1)}, u32[]{:S(2)}, u32[]{:S(2)}) collective-permute-start(bf16[2,64,640]{2,1,0:T(8,128)(2,1)} %refs_1_.3), channel_id=1, source_target_pairs={{0,1},{1,2},{2,3},{3,0},{4,5},{5,6},{6,7},{7,4},{8,9},{9,10},{10,1... | collective-permute-start | bytes 491528 | tf_op jit(solution)/shard_map/ppermute | solution.py:374
  2.6 14.3 %collective-permute-start.1 = (bf16[2,64,640]{2,1,0:T(8,128)(2,1)}, bf16[2,64,640]{2,1,0:T(8,128)(2,1)S(1)}, u32[]{:S(2)}, u32[]{:S(2)}) collective-permute-start(bf16[2,64,640]{2,1,0:T(8,128)(2,1)} %refs_1_.3), channel_id=1, source_target_pairs={{0,2},{1,3},{2,0},{3,1},{4,6},{5,7},{6,4},{7,5},{8,10},{9,11},{10,... | collective-permute-start | bytes 491528 | tf_op jit(solution)/shard_map/ppermute | solution.py:374
  4.9 14.0 %collective-permute-start.2 = (bf16[2,64,640]{2,1,0:T(8,128)(2,1)}, bf16[2,64,640]{2,1,0:T(8,128)(2,1)S(1)}, u32[]{:S(2)}, u32[]{:S(2)}) collective-permute-start(bf16[2,64,640]{2,1,0:T(8,128)(2,1)} %refs_1_.3), channel_id=1, source_target_pairs={{0,3},{1,0},{2,1},{3,2},{4,7},{5,4},{6,5},{7,6},{8,11},{9,8},{10,9... | collective-permute-start | bytes 491528 | tf_op jit(solution)/shard_map/ppermute | solution.py:374
  23.4 9.8 %collective-permute-start.4 = (bf16[160,128]{1,0:T(8,128)(2,1)S(1)}, bf16[160,128]{1,0:T(8,128)(2,1)S(1)}, u32[]{:S(2)}, u32[]{:S(2)}) collective-permute-start(bf16[160,128]{1,0:T(8,128)(2,1)S(1)} %get-tuple-element.36), channel_id=1, source_target_pairs={{4,8},{8,4},{12,16},{16,12},{20,24},{24,20},{28,32},{32,28},{36,40... | collective-permute-start | bytes 122888 | tf_op jit(solution)/shard_map/ppermute | solution.py:380
  27.2 17.7 %all-to-all-start = ((bf16[8,80,512]{2,1,0:T(8,128)(2,1)}), bf16[8,80,512]{2,1,0:T(8,128)(2,1)S(1)}, u32[]{:S(2)}, u32[]{:S(2)}) async-start(bf16[8,80,512]{2,1,0:T(8,128)(2,1)} %shard_map.94.refs_3_), calls=%async_computation | async-start | bytes 1310720 | tf_op jit(solution)/shard_map/all_to_all | solution.py:397
  33.2 4.1 %collective-permute-start.5 = (bf16[160,128]{1,0:T(8,128)(2,1)S(1)}, bf16[160,128]{1,0:T(8,128)(2,1)S(1)}, u32[]{:S(2)}, u32[]{:S(2)}) collective-permute-start(bf16[160,128]{1,0:T(8,128)(2,1)S(1)} %shard_map.95.refs_1_), channel_id=1, source_target_pairs={{0,1},{1,2},{2,3},{3,0},{4,5},{5,6},{6,7},{7,4},{8,9},{9,10},{10,1... | collective-permute-start | bytes 122888 | tf_op jit(solution)/shard_map/ppermute | solution.py:374
  33.3 5.5 %collective-permute-start.6 = (bf16[160,128]{1,0:T(8,128)(2,1)S(1)}, bf16[160,128]{1,0:T(8,128)(2,1)S(1)}, u32[]{:S(2)}, u32[]{:S(2)}) collective-permute-start(bf16[160,128]{1,0:T(8,128)(2,1)S(1)} %shard_map.95.refs_1_), channel_id=1, source_target_pairs={{0,2},{1,3},{2,0},{3,1},{4,6},{5,7},{6,4},{7,5},{8,10},{9,11},{10,... | collective-permute-start | bytes 122888 | tf_op jit(solution)/shard_map/ppermute | solution.py:374
  34.7 5.8 %collective-permute-start.7 = (bf16[160,128]{1,0:T(8,128)(2,1)S(1)}, bf16[160,128]{1,0:T(8,128)(2,1)S(1)}, u32[]{:S(2)}, u32[]{:S(2)}) collective-permute-start(bf16[160,128]{1,0:T(8,128)(2,1)S(1)} %shard_map.95.refs_1_), channel_id=1, source_target_pairs={{0,3},{1,0},{2,1},{3,2},{4,7},{5,4},{6,5},{7,6},{8,11},{9,8},{10,9... | collective-permute-start | bytes 122888 | tf_op jit(solution)/shard_map/ppermute | solution.py:374
  41.8 5.6 %collective-permute-start.8 = (bf16[320,128]{1,0:T(8,128)(2,1)S(1)}, bf16[320,128]{1,0:T(8,128)(2,1)S(1)}, u32[]{:S(2)}, u32[]{:S(2)}) collective-permute-start(bf16[320,128]{1,0:T(8,128)(2,1)S(1)} %get-tuple-element.39), channel_id=1, source_target_pairs={{0,4},{4,0},{8,12},{12,8},{16,20},{20,16},{24,28},{28,24},{32,36},... | collective-permute-start | bytes 245768 | tf_op jit(solution)/shard_map/ppermute | solution.py:377
  42.0 5.5 %collective-permute-start.9 = (bf16[320,128]{1,0:T(8,128)(2,1)S(1)}, bf16[320,128]{1,0:T(8,128)(2,1)S(1)}, u32[]{:S(2)}, u32[]{:S(2)}) collective-permute-start(bf16[320,128]{1,0:T(8,128)(2,1)S(1)} %get-tuple-element.40), channel_id=1, source_target_pairs={{4,8},{8,4},{12,16},{16,12},{20,24},{24,20},{28,32},{32,28},{36,40... | collective-permute-start | bytes 245768 | tf_op jit(solution)/shard_map/ppermute | solution.py:380
  48.9 10.4 %collective-permute-start.11 = (bf16[320,128]{1,0:T(8,128)(2,1)S(1)}, bf16[320,128]{1,0:T(8,128)(2,1)S(1)}, u32[]{:S(2)}, u32[]{:S(2)}) collective-permute-start(bf16[320,128]{1,0:T(8,128)(2,1)S(1)} %get-tuple-element.42.refs_2_.refs_0_), channel_id=1, source_target_pairs={{4,8},{8,4},{12,16},{16,12},{20,24},{24,20},{28,32},{32,28},{36,40... | collective-permute-start | bytes 245768 | tf_op jit(solution)/shard_map/ppermute | solution.py:380
  50.9 22.4 %all-to-all-start.1 = ((bf16[8,80,128]{2,1,0:T(8,128)(2,1)}), bf16[8,80,128]{2,1,0:T(8,128)(2,1)S(1)}, u32[]{:S(2)}, u32[]{:S(2)}) async-start(bf16[8,80,128]{2,1,0:T(8,128)(2,1)} %shard_map.100.refs_3_), calls=%async_computation.1 | async-start | bytes 327680 | tf_op jit(solution)/shard_map/all_to_all | solution.py:415
  59.3 10.6 %collective-permute-start.17 = (bf16[3,320,128]{2,1,0:T(8,128)(2,1)S(1)}, bf16[3,320,128]{2,1,0:T(8,128)(2,1)S(1)}, u32[]{:S(2)}, u32[]{:S(2)}) collective-permute-start(bf16[3,320,128]{2,1,0:T(8,128)(2,1)S(1)} %shard_map.102.refs_1_), channel_id=1, source_target_pairs={{0,8},{4,12},{8,0},{12,4},{16,24},{20,28},{24,16},{28,20},{32,40},... | collective-permute-start | bytes 737288 | tf_op jit(solution)/shard_map/ppermute | solution.py:377
  65.4 4.5 %collective-permute-start.12 = (bf16[160,128]{1,0:T(8,128)(2,1)S(1)}, bf16[160,128]{1,0:T(8,128)(2,1)S(1)}, u32[]{:S(2)}, u32[]{:S(2)}) collective-permute-start(bf16[160,128]{1,0:T(8,128)(2,1)S(1)} %get-tuple-element.44), channel_id=1, source_target_pairs={{0,1},{1,2},{2,3},{3,0},{4,5},{5,6},{6,7},{7,4},{8,9},{9,10},{10,1... | collective-permute-start | bytes 122888 | tf_op jit(solution)/shard_map/ppermute | solution.py:374
  66.5 6.7 %collective-permute-start.13 = (bf16[160,128]{1,0:T(8,128)(2,1)S(1)}, bf16[160,128]{1,0:T(8,128)(2,1)S(1)}, u32[]{:S(2)}, u32[]{:S(2)}) collective-permute-start(bf16[160,128]{1,0:T(8,128)(2,1)S(1)} %get-tuple-element.45), channel_id=1, source_target_pairs={{0,2},{1,3},{2,0},{3,1},{4,6},{5,7},{6,4},{7,5},{8,10},{9,11},{10,... | collective-permute-start | bytes 122888 | tf_op jit(solution)/shard_map/ppermute | solution.py:374
  69.0 4.3 %collective-permute-start.14 = (bf16[160,128]{1,0:T(8,128)(2,1)S(1)}, bf16[160,128]{1,0:T(8,128)(2,1)S(1)}, u32[]{:S(2)}, u32[]{:S(2)}) collective-permute-start(bf16[160,128]{1,0:T(8,128)(2,1)S(1)} %get-tuple-element.46), channel_id=1, source_target_pairs={{0,3},{1,0},{2,1},{3,2},{4,7},{5,4},{6,5},{7,6},{8,11},{9,8},{10,9... | collective-permute-start | bytes 122888 | tf_op jit(solution)/shard_map/ppermute | solution.py:374
  70.5 12.7 %collective-permute-start.18 = (bf16[5,320,128]{2,1,0:T(8,128)(2,1)S(1)}, bf16[5,320,128]{2,1,0:T(8,128)(2,1)S(1)}, u32[]{:S(2)}, u32[]{:S(2)}) collective-permute-start(bf16[5,320,128]{2,1,0:T(8,128)(2,1)S(1)} %get-tuple-element.47.refs_1_), channel_id=1, source_target_pairs={{0,16},{4,20},{8,24},{12,28},{16,0},{20,4},{24,8},{28,12},{32,48},... | collective-permute-start | bytes 1228808 | tf_op jit(solution)/shard_map/ppermute | solution.py:377
  73.3 15.5 %collective-permute-start.15 = (bf16[160,128]{1,0:T(8,128)(2,1)S(1)}, bf16[160,128]{1,0:T(8,128)(2,1)S(1)}, u32[]{:S(2)}, u32[]{:S(2)}) collective-permute-start(bf16[160,128]{1,0:T(8,128)(2,1)S(1)} %shard_map.101.refs_0_.refs_2_), channel_id=1, source_target_pairs={{0,4},{4,0},{8,12},{12,8},{16,20},{20,16},{24,28},{28,24},{32,36},... | collective-permute-start | bytes 122888 | tf_op jit(solution)/shard_map/ppermute | solution.py:377
  73.4 15.4 %collective-permute-start.16 = (bf16[160,128]{1,0:T(8,128)(2,1)S(1)}, bf16[160,128]{1,0:T(8,128)(2,1)S(1)}, u32[]{:S(2)}, u32[]{:S(2)}) collective-permute-start(bf16[160,128]{1,0:T(8,128)(2,1)S(1)} %shard_map.101.refs_0_.refs_2_), channel_id=1, source_target_pairs={{4,8},{8,4},{12,16},{16,12},{20,24},{24,20},{28,32},{32,28},{36,40... | collective-permute-start | bytes 122888 | tf_op jit(solution)/shard_map/ppermute | solution.py:380
  83.8 1.4 collective-permute-start.19
  88.8 6.6 %collective-permute-start.20 = (bf16[3,160,128]{2,1,0:T(8,128)(2,1)S(1)}, bf16[3,160,128]{2,1,0:T(8,128)(2,1)S(1)}, u32[]{:S(2)}, u32[]{:S(2)}) collective-permute-start(bf16[3,160,128]{2,1,0:T(8,128)(2,1)S(1)} %shard_map.107.refs_5_.refs_1_), channel_id=1, source_target_pairs={{0,8},{4,12},{8,0},{12,4},{16,24},{20,28},{24,16},{28,20},{32,40},... | collective-permute-start | bytes 368648 | tf_op jit(solution)/shard_map/ppermute | solution.py:377
  89.0 10.0 %collective-permute-start.21 = (bf16[3,160,128]{2,1,0:T(8,128)(2,1)S(1)}, bf16[3,160,128]{2,1,0:T(8,128)(2,1)S(1)}, u32[]{:S(2)}, u32[]{:S(2)}) collective-permute-start(bf16[3,160,128]{2,1,0:T(8,128)(2,1)S(1)} %shard_map.107.refs_5_.refs_1_), channel_id=1, source_target_pairs={{0,16},{4,20},{8,24},{12,28},{16,0},{20,4},{24,8},{28,12},{32,48},... | collective-permute-start | bytes 368648 | tf_op jit(solution)/shard_map/ppermute | solution.py:377
  92.8 8.2 %collective-permute-start.22 = (bf16[3,160,128]{2,1,0:T(8,128)(2,1)S(1)}, bf16[3,160,128]{2,1,0:T(8,128)(2,1)S(1)}, u32[]{:S(2)}, u32[]{:S(2)}) collective-permute-start(bf16[3,160,128]{2,1,0:T(8,128)(2,1)S(1)} %shard_map.107.refs_5_.refs_1_), channel_id=1, source_target_pairs={{0,24},{4,28},{8,16},{12,20},{16,8},{20,12},{24,0},{28,4},{32,56},... | collective-permute-start | bytes 368648 | tf_op jit(solution)/shard_map/ppermute | solution.py:377
  102.9 43.1 %all-to-all-start.2 = ((bf16[4,2,64,640]{3,2,1,0:T(8,128)(2,1)}), bf16[4,2,64,640]{3,2,1,0:T(8,128)(2,1)}, u32[]{:S(2)}, u32[]{:S(2)}) async-start(bf16[4,2,64,640]{3,2,1,0:T(8,128)(2,1)} %shard_map.110), calls=%async_computation.2 | async-start | bytes 1310720 | tf_op jit(solution)/shard_map/all_to_all | solution.py:472
  109.1 24.2 %collective-permute-start.28 = (bf16[2,96,320]{2,1,0:T(8,128)(2,1)}, bf16[2,96,320]{2,1,0:T(8,128)(2,1)S(1)}, u32[]{:S(2)}, u32[]{:S(2)}) collective-permute-start(bf16[2,96,320]{2,1,0:T(8,128)(2,1)} %get-tuple-element.59), channel_id=1, source_target_pairs={{0,32},{4,36},{8,40},{12,44},{16,48},{20,52},{24,56},{28,60},{32,6... | collective-permute-start | bytes 368648 | tf_op jit(solution)/shard_map/ppermute | solution.py:434
  110.7 25.4 %collective-permute-start.29 = (bf16[2,96,320]{2,1,0:T(8,128)(2,1)}, bf16[2,96,320]{2,1,0:T(8,128)(2,1)S(1)}, u32[]{:S(2)}, u32[]{:S(2)}) collective-permute-start(bf16[2,96,320]{2,1,0:T(8,128)(2,1)} %get-tuple-element.60), channel_id=1, source_target_pairs={{0,64},{4,68},{8,72},{12,76},{16,80},{20,84},{24,88},{28,92},{32,9... | collective-permute-start | bytes 368648 | tf_op jit(solution)/shard_map/ppermute | solution.py:434
  127.8 8.3 %collective-permute-start.30 = (bf16[2,96,320]{2,1,0:T(8,128)(2,1)S(1)}, bf16[2,96,320]{2,1,0:T(8,128)(2,1)S(1)}, u32[]{:S(2)}, u32[]{:S(2)}) collective-permute-start(bf16[2,96,320]{2,1,0:T(8,128)(2,1)S(1)} %get-tuple-element.61), channel_id=1, source_target_pairs={{0,96},{4,100},{8,104},{12,108},{16,112},{20,116},{24,120},{28,124... | collective-permute-start | bytes 368648 | tf_op jit(solution)/shard_map/ppermute | solution.py:434
  131.2 8.2 %collective-permute-start.24 = (bf16[2,96,160]{2,1,0:T(8,128)(2,1)S(1)}, bf16[2,96,160]{2,1,0:T(8,128)(2,1)S(1)}, u32[]{:S(2)}, u32[]{:S(2)}) collective-permute-start(bf16[2,96,160]{2,1,0:T(8,128)(2,1)S(1)} %get-tuple-element.54), channel_id=1, source_target_pairs={{0,32},{4,36},{8,40},{12,44},{16,48},{20,52},{24,56},{28,60},{32,6... | collective-permute-start | bytes 184328 | tf_op jit(solution)/shard_map/ppermute | solution.py:434
  133.3 6.2 %collective-permute-start.25 = (bf16[2,96,160]{2,1,0:T(8,128)(2,1)S(1)}, bf16[2,96,160]{2,1,0:T(8,128)(2,1)S(1)}, u32[]{:S(2)}, u32[]{:S(2)}) collective-permute-start(bf16[2,96,160]{2,1,0:T(8,128)(2,1)S(1)} %get-tuple-element.55), channel_id=1, source_target_pairs={{0,64},{4,68},{8,72},{12,76},{16,80},{20,84},{24,88},{28,92},{32,9... | collective-permute-start | bytes 184328 | tf_op jit(solution)/shard_map/ppermute | solution.py:434
  133.3 6.7 %collective-permute-start.26 = (bf16[2,96,160]{2,1,0:T(8,128)(2,1)S(1)}, bf16[2,96,160]{2,1,0:T(8,128)(2,1)S(1)}, u32[]{:S(2)}, u32[]{:S(2)}) collective-permute-start(bf16[2,96,160]{2,1,0:T(8,128)(2,1)S(1)} %get-tuple-element.56), channel_id=1, source_target_pairs={{0,96},{4,100},{8,104},{12,108},{16,112},{20,116},{24,120},{28,124... | collective-permute-start | bytes 184328 | tf_op jit(solution)/shard_map/ppermute | solution.py:434
  136.7 8.4 %collective-permute-start.31 = (bf16[96,320]{1,0:T(8,128)(2,1)S(1)}, bf16[96,320]{1,0:T(8,128)(2,1)S(1)}, u32[]{:S(2)}, u32[]{:S(2)}) collective-permute-start(bf16[96,320]{1,0:T(8,128)(2,1)S(1)} %get-tuple-element.63), channel_id=1, source_target_pairs={{0,128},{4,132},{8,136},{12,140},{16,144},{20,148},{24,152},{28,15... | collective-permute-start | bytes 184328 | tf_op jit(solution)/shard_map/ppermute | solution.py:377
  140.6 8.4 %collective-permute-start.27 = (bf16[96,160]{1,0:T(8,128)(2,1)S(1)}, bf16[96,160]{1,0:T(8,128)(2,1)S(1)}, u32[]{:S(2)}, u32[]{:S(2)}) collective-permute-start(bf16[96,160]{1,0:T(8,128)(2,1)S(1)} %get-tuple-element.58), channel_id=1, source_target_pairs={{0,128},{4,132},{8,136},{12,140},{16,144},{20,148},{24,152},{28,15... | collective-permute-start | bytes 92168 | tf_op jit(solution)/shard_map/ppermute | solution.py:377
  (15 other events, 39.0 us)

commit v14 on v12

--- a/solution.py
+++ b/solution.py
@@ -109,8 +109,8 @@
         other[...] = down
 
 
-def fine_forward(at, mine, got1, got2, got3, w, x, own, partner, other):
-    for s, piece in enumerate((mine, got1, got2, got3)):
+def fine_forward(at, mine, got2, got1, got3, w, x, own, partner, other):
+    for s, piece in ((0, mine), (2, got2), (1, got1), (3, got3)):
         x[jnp.bitwise_and(at[4] - s, 3)] = piece[...]
     deep = own.shape[1]
     rows = fine_rows(x)
@@ -380,7 +380,8 @@
         other = lax.ppermute(to_other, "wide", [(i, i - 1 + 2 * (i % 2)) for i in range(1, wide - 1)])
         return swap(to_partner, 1), other
 
-    got = [across(latent, s) for s in (1, 2, 3)]
+    two = across(latent, 2)
+    got = [two, across(latent, 1), across(latent, 3)]
     x, own, partner, other = call(
         fine_forward,
         [shape((pieces,) + latent.shape), shape((fine, deep), F32), shape((fine, deep)), shape((fine, deep))],

time: 148 us -> 147 us (level)
  waiting for transfers between devices: 35.8 us -> 34.1 us
    ppermute x9, starting transfers between devices: 13.3 us -> 15.5 us  [across(): lax.ppermute(v, 'narrow', [(i, (i + step) % pieces) for i in range(pieces)])]
  transfers between devices with their start and end apart: 35 -> 35, of which waited for: 15 -> 13; matrix products, arithmetic and copies ran while one was open for 1% -> 1% of each run, Pallas kernels for 12% -> 12%
where the time goes in v14:
time: 147 us
  starting transfers between devices  79.3 us (54%)
  waiting for transfers between devices  34.1 us (23%)
  Pallas kernels  22 us (15%)
  local copies, waits for them, and re-layouts  9.13 us (6%)
    ppermute x6, starting transfers between devices, halves(): lax.ppermute(parts[s], 'wide', [(i, i // 32 * 32 + (i // 8 + s) % 4 * 8 +...  22.9 us
    pallas_call x23, Pallas kernels, call(): pl.pallas_call(kernel, out_shape=outs, in_specs=[smem if a.dtype == jnp.i...  22 us
    ppermute x13, starting transfers between devices, swap(): return lax.ppermute(v, 'wide', [(i, i ^ bit) for i in range(wide)])  18.6 us
    ppermute x13, waiting for transfers between devices, swap(): return lax.ppermute(v, 'wide', [(i, i ^ bit) for i in range(wide)])  16.8 us
    ppermute x9, starting transfers between devices, across(): lax.ppermute(v, 'narrow', [(i, (i + step) % pieces) for i in range(pieces)])  15.5 us
    ppermute x9, waiting for transfers between devices, across(): lax.ppermute(v, 'narrow', [(i, (i + step) % pieces) for i in range(pieces)])  15.2 us
    unnamed x30, local copies, waits for them, and re-layouts  9.05 us
    all_to_all x1, starting transfers between devices, on_device(): deep_slab = lax.all_to_all(deep_pre, 'wide', 0, 0, axis_index_groups=near)  8.2 us
  transfers between devices with their start and end apart: 35, of which 13 were waited for; matrix products, arithmetic and copies ran while one was open for 1% of the time, Pallas kernels for 12%

profile of v14, /device:TPU:32, one launch (start us, length us, event | category | flops | bytes accessed | tf_op | source)
XLA Modules:
  0.0 146.7 jit_solution(16985196163327818345)
XLA Ops:
  0.6 3.4 %collective-permute-start = (bf16[2,64,640]{2,1,0:T(8,128)(2,1)}, bf16[2,64,640]{2,1,0:T(8,128)(2,1)S(1)}, u32[]{:S(2)}, u32[]{:S(2)}) collective-permute-start(bf16[2,64,640]{2,1,0:T(8,128)(2,1)} %refs_1_.3), channel_id=1, source_target_pairs={{0,2},{1,3},{2,0},{3,1},{4,6},{5,7},{6,4},{7,5},{8,10},{9,11},{10,... | collective-permute-start | bytes 491528 | tf_op jit(solution)/shard_map/ppermute | solution.py:374
  4.0 2.0 %collective-permute-start.2 = (bf16[2,64,640]{2,1,0:T(8,128)(2,1)}, bf16[2,64,640]{2,1,0:T(8,128)(2,1)S(1)}, u32[]{:S(2)}, u32[]{:S(2)}) collective-permute-start(bf16[2,64,640]{2,1,0:T(8,128)(2,1)} %refs_1_.3), channel_id=1, source_target_pairs={{0,3},{1,0},{2,1},{3,2},{4,7},{5,4},{6,5},{7,6},{8,11},{9,8},{10,9... | collective-permute-start | bytes 491528 | tf_op jit(solution)/shard_map/ppermute | solution.py:374
  6.1 5.7 %collective-permute-done.refs_2_ = bf16[2,64,640]{2,1,0:T(8,128)(2,1)S(1)} collective-permute-done((bf16[2,64,640]{2,1,0:T(8,128)(2,1)}, bf16[2,64,640]{2,1,0:T(8,128)(2,1)S(1)}, u32[]{:S(2)}, u32[]{:S(2)}) %collective-permute-start) | collective-permute-done | bytes 163872 | tf_op jit(solution)/shard_map/ppermute | solution.py:374
  11.8 6.1 %collective-permute-done.1.refs_3_ = bf16[2,64,640]{2,1,0:T(8,128)(2,1)S(1)} collective-permute-done((bf16[2,64,640]{2,1,0:T(8,128)(2,1)}, bf16[2,64,640]{2,1,0:T(8,128)(2,1)S(1)}, u32[]{:S(2)}, u32[]{:S(2)}) %collective-permute-start.1) | collective-permute-done | bytes 163872 | tf_op jit(solution)/shard_map/ppermute | solution.py:374
  20.3 1.9 %shard_map.93 = (bf16[4,2,64,640]{3,2,1,0:T(8,128)(2,1)S(1)}, f32[160,128]{1,0:T(8,128)S(1)}, bf16[160,128]{1,0:T(8,128)(2,1)S(1)}, bf16[160,128]{1,0:T(8,128)(2,1)S(1)}) custom-call(s32[5]{0:T(128)S(1)} %stack.23.refs_0_, bf16[2,64,640]{2,1,0:T(8,128)(2,1)S(1)} %copy-done.10, bf16[2,64,640]{2,1,0:T(8,128)(2,1)S(1)} %collective-permute-done.refs_2_, ...), custom_call_target="tpu_custom_call" | custom-call | flops 30000001024 | bytes 2498580 | tf_op jit(solution)/shard_map/pallas_call | solution.py:64
  23.5 2.6 %shard_map.94.refs_3_ = bf16[8,80,512]{2,1,0:T(8,128)(2,1)} custom-call(bf16[4,2,64,640]{3,2,1,0:T(8,128)(2,1)S(1)} %get-tuple-element.37.refs_0_, bf16[640,640]{1,0:T(8,128)(2,1)S(1)} %copy-done.4, bf16[160,128]{1,0:T(8,128)(2,1)S(1)} %collective-permute-done.3.refs_2_.refs_1_), custom_call_target="tpu_custom_call" | custom-call | bytes 1474560 | tf_op jit(solution)/shard_map/pallas_call | solution.py:64
  26.1 6.0 %all-to-all-start = ((bf16[8,80,512]{2,1,0:T(8,128)(2,1)}), bf16[8,80,512]{2,1,0:T(8,128)(2,1)S(1)}, u32[]{:S(2)}, u32[]{:S(2)}) async-start(bf16[8,80,512]{2,1,0:T(8,128)(2,1)} %shard_map.94.refs_3_), calls=%async_computation | async-start | bytes 1310720 | tf_op jit(solution)/shard_map/all_to_all | solution.py:398
  32.1 2.4 %collective-permute-start.5 = (bf16[160,128]{1,0:T(8,128)(2,1)S(1)}, bf16[160,128]{1,0:T(8,128)(2,1)S(1)}, u32[]{:S(2)}, u32[]{:S(2)}) collective-permute-start(bf16[160,128]{1,0:T(8,128)(2,1)S(1)} %shard_map.95.refs_1_), channel_id=1, source_target_pairs={{0,1},{1,2},{2,3},{3,0},{4,5},{5,6},{6,7},{7,4},{8,9},{9,10},{10,1... | collective-permute-start | bytes 122888 | tf_op jit(solution)/shard_map/ppermute | solution.py:374
  37.8 1.8 %collective-permute-done.6.refs_3_ = bf16[160,128]{1,0:T(8,128)(2,1)S(1)} collective-permute-done((bf16[160,128]{1,0:T(8,128)(2,1)S(1)}, bf16[160,128]{1,0:T(8,128)(2,1)S(1)}, u32[]{:S(2)}, u32[]{:S(2)}) %collective-permute-start.6) | collective-permute-done | bytes 40992 | tf_op jit(solution)/shard_map/ppermute | solution.py:374
  41.8 2.1 %all-to-all-done.refs_2_.refs_0_ = bf16[8,80,512]{2,1,0:T(8,128)(2,1)S(1)} async-done(((bf16[8,80,512]{2,1,0:T(8,128)(2,1)}), bf16[8,80,512]{2,1,0:T(8,128)(2,1)S(1)}, u32[]{:S(2)}, u32[]{:S(2)}) %all-to-all-start) | async-done | bytes 655392 | tf_op jit(solution)/shard_map/all_to_all | solution.py:398
  43.8 2.0 %copy-done.1 = bf16[3,3,640,320]{2,3,1,0:T(8,128)(2,1)S(1)} copy-done((bf16[3,3,640,320]{2,3,1,0:T(8,128)(2,1)S(1)}, bf16[3,3,640,320]{2,3,1,0:T(8,128)(2,1)}, u32[]{:S(2)}) %copy-start.1) | copy-done | bytes 3686424
  50.7 8.2 %all-to-all-start.1 = ((bf16[8,80,128]{2,1,0:T(8,128)(2,1)}), bf16[8,80,128]{2,1,0:T(8,128)(2,1)S(1)}, u32[]{:S(2)}, u32[]{:S(2)}) async-start(bf16[8,80,128]{2,1,0:T(8,128)(2,1)} %shard_map.100.refs_3_), calls=%async_computation.1 | async-start | bytes 327680 | tf_op jit(solution)/shard_map/all_to_all | solution.py:416
  58.9 2.1 %collective-permute-start.17 = (bf16[3,320,128]{2,1,0:T(8,128)(2,1)S(1)}, bf16[3,320,128]{2,1,0:T(8,128)(2,1)S(1)}, u32[]{:S(2)}, u32[]{:S(2)}) collective-permute-start(bf16[3,320,128]{2,1,0:T(8,128)(2,1)S(1)} %shard_map.103.refs_1_), channel_id=1, source_target_pairs={{0,8},{4,12},{8,0},{12,4},{16,24},{20,28},{24,16},{28,20},{32,40},... | collective-permute-start | bytes 737288 | tf_op jit(solution)/shard_map/ppermute | solution.py:377
  61.0 2.0 %copy-done.2 = bf16[3,3,640,320]{2,3,1,0:T(8,128)(2,1)S(1)} copy-done((bf16[3,3,640,320]{2,3,1,0:T(8,128)(2,1)S(1)}, bf16[3,3,640,320]{2,3,1,0:T(8,128)(2,1)}, u32[]{:S(2)}) %copy-start.2) | copy-done | bytes 3686424
  63.0 1.9 %shard_map.99 = (bf16[160,128]{1,0:T(8,128)(2,1)S(1)}, bf16[160,128]{1,0:T(8,128)(2,1)S(1)}, bf16[160,128]{1,0:T(8,128)(2,1)S(1)}, bf16[160,128]{1,0:T(8,128)(2,1)S(1)}) custom-call(s32[5]{0:T(128)S(1)} %stack.23.refs_0_, bf16[320,128]{1,0:T(8,128)(2,1)S(1)} %collective-permute-done.10.refs_1_.refs_2_, ...), custom_call_target="tpu_custom_call" | custom-call | flops 30000001024 | bytes 3932180 | tf_op jit(solution)/shard_map/pallas_call | solution.py:64
  66.2 2.9 %collective-permute-start.13 = (bf16[160,128]{1,0:T(8,128)(2,1)S(1)}, bf16[160,128]{1,0:T(8,128)(2,1)S(1)}, u32[]{:S(2)}, u32[]{:S(2)}) collective-permute-start(bf16[160,128]{1,0:T(8,128)(2,1)S(1)} %get-tuple-element.45), channel_id=1, source_target_pairs={{0,2},{1,3},{2,0},{3,1},{4,6},{5,7},{6,4},{7,5},{8,10},{9,11},{10,... | collective-permute-start | bytes 122888 | tf_op jit(solution)/shard_map/ppermute | solution.py:374
  69.2 1.9 %collective-permute-start.14 = (bf16[160,128]{1,0:T(8,128)(2,1)S(1)}, bf16[160,128]{1,0:T(8,128)(2,1)S(1)}, u32[]{:S(2)}, u32[]{:S(2)}) collective-permute-start(bf16[160,128]{1,0:T(8,128)(2,1)S(1)} %get-tuple-element.46), channel_id=1, source_target_pairs={{0,3},{1,0},{2,1},{3,2},{4,7},{5,4},{6,5},{7,6},{8,11},{9,8},{10,9... | collective-permute-start | bytes 122888 | tf_op jit(solution)/shard_map/ppermute | solution.py:374
  71.7 2.8 %collective-permute-start.18 = (bf16[5,320,128]{2,1,0:T(8,128)(2,1)S(1)}, bf16[5,320,128]{2,1,0:T(8,128)(2,1)S(1)}, u32[]{:S(2)}, u32[]{:S(2)}) collective-permute-start(bf16[5,320,128]{2,1,0:T(8,128)(2,1)S(1)} %get-tuple-element.49.refs_1_), channel_id=1, source_target_pairs={{0,16},{4,20},{8,24},{12,28},{16,0},{20,4},{24,8},{28,12},{32,48},... | collective-permute-start | bytes 1228808 | tf_op jit(solution)/shard_map/ppermute | solution.py:377
  76.1 8.1 %collective-permute-done.18.refs_2_ = bf16[5,320,128]{2,1,0:T(8,128)(2,1)S(1)} collective-permute-done((bf16[5,320,128]{2,1,0:T(8,128)(2,1)S(1)}, bf16[5,320,128]{2,1,0:T(8,128)(2,1)S(1)}, u32[]{:S(2)}, u32[]{:S(2)}) %collective-permute-start.18) | collective-permute-done | bytes 409632 | tf_op jit(solution)/shard_map/ppermute | solution.py:377
  85.1 3.6 %collective-permute-start.20 = (bf16[3,160,128]{2,1,0:T(8,128)(2,1)S(1)}, bf16[3,160,128]{2,1,0:T(8,128)(2,1)S(1)}, u32[]{:S(2)}, u32[]{:S(2)}) collective-permute-start(bf16[3,160,128]{2,1,0:T(8,128)(2,1)S(1)} %shard_map.106.refs_5_.refs_7_.refs_1_), channel_id=1, source_target_pairs={{0,16},{4,20},{8,24},{12,28},{16,0},{20,4},{24,8},{28,12},{32,48},... | collective-permute-start | bytes 368648 | tf_op jit(solution)/shard_map/ppermute | solution.py:377
  89.7 1.8 %shard_map.107.refs_5_.refs_0_ = bf16[2,256,640]{2,1,0:T(8,128)(2,1)S(1)} custom-call(s32[5]{0:T(128)S(1)} %stack.23.refs_0_, bf16[160,128]{1,0:T(8,128)(2,1)S(1)} %collective-permute-done.15.refs_1_, bf16[160,128]{1,0:T(8,128)(2,1)S(1)} %shard_map.101.refs_0_.refs_2_, bf16[160,128]{1,0:T(8,128)(2,1)S(1)} %collective-permute-done.16.refs_2_.refs_3_, ...), custom_call_target="tpu_custom_call" | custom-call | flops 30000001024 | bytes 1966100 | tf_op jit(solution)/shard_map/pallas_call | solution.py:64
  91.6 2.9 %shard_map.108 = (bf16[2,96,320]{2,1,0:T(8,128)(2,1)S(1)}, bf16[2,96,320]{2,1,0:T(8,128)(2,1)S(1)}, bf16[2,96,320]{2,1,0:T(8,128)(2,1)S(1)}, bf16[2,96,320]{2,1,0:T(8,128)(2,1)S(1)}) custom-call(s32[5]{0:T(128)S(1)} %stack.23.refs_0_, bf16[5,320,128]{2,1,0:T(8,128)(2,1)S(1)} %copy-done.7, bf16[5,320,128]{2,1,0:T(8,128)(2,1)S(1)} %collective-permute-done.18.refs_2_, ...), custom_call_target="tpu_custom_call" | custom-call | bytes 2580500 | tf_op jit(solution)/shard_map/pallas_call | solution.py:64
  95.4 2.5 %collective-permute-done.21.refs_4_ = bf16[3,160,128]{2,1,0:T(8,128)(2,1)S(1)} collective-permute-done((bf16[3,160,128]{2,1,0:T(8,128)(2,1)S(1)}, bf16[3,160,128]{2,1,0:T(8,128)(2,1)S(1)}, u32[]{:S(2)}, u32[]{:S(2)}) %collective-permute-start.21) | collective-permute-done | bytes 122912 | tf_op jit(solution)/shard_map/ppermute | solution.py:377
  99.6 5.4 %all-to-all-start.2 = ((bf16[4,2,64,640]{3,2,1,0:T(8,128)(2,1)}), bf16[4,2,64,640]{3,2,1,0:T(8,128)(2,1)}, u32[]{:S(2)}, u32[]{:S(2)}) async-start(bf16[4,2,64,640]{3,2,1,0:T(8,128)(2,1)} %shard_map.110), calls=%async_computation.2 | async-start | bytes 1310720 | tf_op jit(solution)/shard_map/all_to_all | solution.py:473
  105.0 2.1 %collective-permute-start.28 = (bf16[2,96,320]{2,1,0:T(8,128)(2,1)S(1)}, bf16[2,96,320]{2,1,0:T(8,128)(2,1)S(1)}, u32[]{:S(2)}, u32[]{:S(2)}) collective-permute-start(bf16[2,96,320]{2,1,0:T(8,128)(2,1)S(1)} %copy-done.12), channel_id=1, source_target_pairs={{0,32},{4,36},{8,40},{12,44},{16,48},{20,52},{24,56},{28,60},{32,6... | collective-permute-start | bytes 368648 | tf_op jit(solution)/shard_map/ppermute | solution.py:436
  107.1 15.9 %collective-permute-start.29 = (bf16[2,96,320]{2,1,0:T(8,128)(2,1)S(1)}, bf16[2,96,320]{2,1,0:T(8,128)(2,1)S(1)}, u32[]{:S(2)}, u32[]{:S(2)}) collective-permute-start(bf16[2,96,320]{2,1,0:T(8,128)(2,1)S(1)} %get-tuple-element.60), channel_id=1, source_target_pairs={{0,64},{4,68},{8,72},{12,76},{16,80},{20,84},{24,88},{28,92},{32,9... | collective-permute-start | bytes 368648 | tf_op jit(solution)/shard_map/ppermute | solution.py:436
  124.2 2.2 %shard_map.111 = (bf16[2,96,160]{2,1,0:T(8,128)(2,1)S(1)}, bf16[2,96,160]{2,1,0:T(8,128)(2,1)S(1)}, bf16[2,96,160]{2,1,0:T(8,128)(2,1)S(1)}, bf16[2,96,160]{2,1,0:T(8,128)(2,1)S(1)}) custom-call(s32[5]{0:T(128)S(1)} %stack.23.refs_0_, bf16[3,160,128]{2,1,0:T(8,128)(2,1)S(1)} %shard_map.106.refs_5_.refs_7_.refs_1_, ...), custom_call_target="tpu_custom_call" | custom-call | bytes 2662420 | tf_op jit(solution)/shard_map/pallas_call | solution.py:64
  126.5 2.1 %collective-permute-start.24 = (bf16[2,96,160]{2,1,0:T(8,128)(2,1)S(1)}, bf16[2,96,160]{2,1,0:T(8,128)(2,1)S(1)}, u32[]{:S(2)}, u32[]{:S(2)}) collective-permute-start(bf16[2,96,160]{2,1,0:T(8,128)(2,1)S(1)} %get-tuple-element.54), channel_id=1, source_target_pairs={{0,32},{4,36},{8,40},{12,44},{16,48},{20,52},{24,56},{28,60},{32,6... | collective-permute-start | bytes 184328 | tf_op jit(solution)/shard_map/ppermute | solution.py:436
  128.6 2.8 %collective-permute-start.26 = (bf16[2,96,160]{2,1,0:T(8,128)(2,1)S(1)}, bf16[2,96,160]{2,1,0:T(8,128)(2,1)S(1)}, u32[]{:S(2)}, u32[]{:S(2)}) collective-permute-start(bf16[2,96,160]{2,1,0:T(8,128)(2,1)S(1)} %get-tuple-element.56), channel_id=1, source_target_pairs={{0,96},{4,100},{8,104},{12,108},{16,112},{20,116},{24,120},{28,124... | collective-permute-start | bytes 184328 | tf_op jit(solution)/shard_map/ppermute | solution.py:436
  132.0 4.8 %collective-permute-start.31 = (bf16[96,320]{1,0:T(8,128)(2,1)S(1)}, bf16[96,320]{1,0:T(8,128)(2,1)S(1)}, u32[]{:S(2)}, u32[]{:S(2)}) collective-permute-start(bf16[96,320]{1,0:T(8,128)(2,1)S(1)} %get-tuple-element.63), channel_id=1, source_target_pairs={{0,128},{4,132},{8,136},{12,140},{16,144},{20,148},{24,152},{28,15... | collective-permute-start | bytes 184328 | tf_op jit(solution)/shard_map/ppermute | solution.py:377
  137.4 2.5 %collective-permute-start.27 = (bf16[96,160]{1,0:T(8,128)(2,1)S(1)}, bf16[96,160]{1,0:T(8,128)(2,1)S(1)}, u32[]{:S(2)}, u32[]{:S(2)}) collective-permute-start(bf16[96,160]{1,0:T(8,128)(2,1)S(1)} %get-tuple-element.58), channel_id=1, source_target_pairs={{0,128},{4,132},{8,136},{12,140},{16,144},{20,148},{24,152},{28,15... | collective-permute-start | bytes 92168 | tf_op jit(solution)/shard_map/ppermute | solution.py:377
  143.2 2.8 %collective-permute-done.27.refs_1_ = bf16[96,160]{1,0:T(8,128)(2,1)S(1)} collective-permute-done((bf16[96,160]{1,0:T(8,128)(2,1)S(1)}, bf16[96,160]{1,0:T(8,128)(2,1)S(1)}, u32[]{:S(2)}, u32[]{:S(2)}) %collective-permute-start.27) | collective-permute-done | bytes 30752 | tf_op jit(solution)/shard_map/ppermute | solution.py:377
  (93 shorter events, 28.5 us)
Async XLA Ops:
  0.6 11.1 %collective-permute-start = (bf16[2,64,640]{2,1,0:T(8,128)(2,1)}, bf16[2,64,640]{2,1,0:T(8,128)(2,1)S(1)}, u32[]{:S(2)}, u32[]{:S(2)}) collective-permute-start(bf16[2,64,640]{2,1,0:T(8,128)(2,1)} %refs_1_.3), channel_id=1, source_target_pairs={{0,2},{1,3},{2,0},{3,1},{4,6},{5,7},{6,4},{7,5},{8,10},{9,11},{10,... | collective-permute-start | bytes 491528 | tf_op jit(solution)/shard_map/ppermute | solution.py:374
  4.0 13.9 %collective-permute-start.1 = (bf16[2,64,640]{2,1,0:T(8,128)(2,1)}, bf16[2,64,640]{2,1,0:T(8,128)(2,1)S(1)}, u32[]{:S(2)}, u32[]{:S(2)}) collective-permute-start(bf16[2,64,640]{2,1,0:T(8,128)(2,1)} %refs_1_.3), channel_id=1, source_target_pairs={{0,1},{1,2},{2,3},{3,0},{4,5},{5,6},{6,7},{7,4},{8,9},{9,10},{10,1... | collective-permute-start | bytes 491528 | tf_op jit(solution)/shard_map/ppermute | solution.py:374
  4.0 13.8 %collective-permute-start.2 = (bf16[2,64,640]{2,1,0:T(8,128)(2,1)}, bf16[2,64,640]{2,1,0:T(8,128)(2,1)S(1)}, u32[]{:S(2)}, u32[]{:S(2)}) collective-permute-start(bf16[2,64,640]{2,1,0:T(8,128)(2,1)} %refs_1_.3), channel_id=1, source_target_pairs={{0,3},{1,0},{2,1},{3,2},{4,7},{5,4},{6,5},{7,6},{8,11},{9,8},{10,9... | collective-permute-start | bytes 491528 | tf_op jit(solution)/shard_map/ppermute | solution.py:374
  22.3 9.8 %collective-permute-start.4 = (bf16[160,128]{1,0:T(8,128)(2,1)S(1)}, bf16[160,128]{1,0:T(8,128)(2,1)S(1)}, u32[]{:S(2)}, u32[]{:S(2)}) collective-permute-start(bf16[160,128]{1,0:T(8,128)(2,1)S(1)} %get-tuple-element.36), channel_id=1, source_target_pairs={{4,8},{8,4},{12,16},{16,12},{20,24},{24,20},{28,32},{32,28},{36,40... | collective-permute-start | bytes 122888 | tf_op jit(solution)/shard_map/ppermute | solution.py:380
  26.1 17.7 %all-to-all-start = ((bf16[8,80,512]{2,1,0:T(8,128)(2,1)}), bf16[8,80,512]{2,1,0:T(8,128)(2,1)S(1)}, u32[]{:S(2)}, u32[]{:S(2)}) async-start(bf16[8,80,512]{2,1,0:T(8,128)(2,1)} %shard_map.94.refs_3_), calls=%async_computation | async-start | bytes 1310720 | tf_op jit(solution)/shard_map/all_to_all | solution.py:398
  32.1 5.7 %collective-permute-start.5 = (bf16[160,128]{1,0:T(8,128)(2,1)S(1)}, bf16[160,128]{1,0:T(8,128)(2,1)S(1)}, u32[]{:S(2)}, u32[]{:S(2)}) collective-permute-start(bf16[160,128]{1,0:T(8,128)(2,1)S(1)} %shard_map.95.refs_1_), channel_id=1, source_target_pairs={{0,1},{1,2},{2,3},{3,0},{4,5},{5,6},{6,7},{7,4},{8,9},{9,10},{10,1... | collective-permute-start | bytes 122888 | tf_op jit(solution)/shard_map/ppermute | solution.py:374
  34.6 5.0 %collective-permute-start.6 = (bf16[160,128]{1,0:T(8,128)(2,1)S(1)}, bf16[160,128]{1,0:T(8,128)(2,1)S(1)}, u32[]{:S(2)}, u32[]{:S(2)}) collective-permute-start(bf16[160,128]{1,0:T(8,128)(2,1)S(1)} %shard_map.95.refs_1_), channel_id=1, source_target_pairs={{0,2},{1,3},{2,0},{3,1},{4,6},{5,7},{6,4},{7,5},{8,10},{9,11},{10,... | collective-permute-start | bytes 122888 | tf_op jit(solution)/shard_map/ppermute | solution.py:374
  34.6 5.0 %collective-permute-start.7 = (bf16[160,128]{1,0:T(8,128)(2,1)S(1)}, bf16[160,128]{1,0:T(8,128)(2,1)S(1)}, u32[]{:S(2)}, u32[]{:S(2)}) collective-permute-start(bf16[160,128]{1,0:T(8,128)(2,1)S(1)} %shard_map.95.refs_1_), channel_id=1, source_target_pairs={{0,3},{1,0},{2,1},{3,2},{4,7},{5,4},{6,5},{7,6},{8,11},{9,8},{10,9... | collective-permute-start | bytes 122888 | tf_op jit(solution)/shard_map/ppermute | solution.py:374
  41.0 5.4 %collective-permute-start.8 = (bf16[320,128]{1,0:T(8,128)(2,1)S(1)}, bf16[320,128]{1,0:T(8,128)(2,1)S(1)}, u32[]{:S(2)}, u32[]{:S(2)}) collective-permute-start(bf16[320,128]{1,0:T(8,128)(2,1)S(1)} %get-tuple-element.39), channel_id=1, source_target_pairs={{0,4},{4,0},{8,12},{12,8},{16,20},{20,16},{24,28},{28,24},{32,36},... | collective-permute-start | bytes 245768 | tf_op jit(solution)/shard_map/ppermute | solution.py:377
  41.1 5.3 %collective-permute-start.9 = (bf16[320,128]{1,0:T(8,128)(2,1)S(1)}, bf16[320,128]{1,0:T(8,128)(2,1)S(1)}, u32[]{:S(2)}, u32[]{:S(2)}) collective-permute-start(bf16[320,128]{1,0:T(8,128)(2,1)S(1)} %get-tuple-element.40), channel_id=1, source_target_pairs={{4,8},{8,4},{12,16},{16,12},{20,24},{24,20},{28,32},{32,28},{36,40... | collective-permute-start | bytes 245768 | tf_op jit(solution)/shard_map/ppermute | solution.py:380
  48.6 10.2 %collective-permute-start.11 = (bf16[320,128]{1,0:T(8,128)(2,1)S(1)}, bf16[320,128]{1,0:T(8,128)(2,1)S(1)}, u32[]{:S(2)}, u32[]{:S(2)}) collective-permute-start(bf16[320,128]{1,0:T(8,128)(2,1)S(1)} %get-tuple-element.42.refs_2_.refs_0_), channel_id=1, source_target_pairs={{4,8},{8,4},{12,16},{16,12},{20,24},{24,20},{28,32},{32,28},{36,40... | collective-permute-start | bytes 245768 | tf_op jit(solution)/shard_map/ppermute | solution.py:380
  50.7 23.8 %all-to-all-start.1 = ((bf16[8,80,128]{2,1,0:T(8,128)(2,1)}), bf16[8,80,128]{2,1,0:T(8,128)(2,1)S(1)}, u32[]{:S(2)}, u32[]{:S(2)}) async-start(bf16[8,80,128]{2,1,0:T(8,128)(2,1)} %shard_map.100.refs_3_), calls=%async_computation.1 | async-start | bytes 327680 | tf_op jit(solution)/shard_map/all_to_all | solution.py:416
  58.9 12.2 %collective-permute-start.17 = (bf16[3,320,128]{2,1,0:T(8,128)(2,1)S(1)}, bf16[3,320,128]{2,1,0:T(8,128)(2,1)S(1)}, u32[]{:S(2)}, u32[]{:S(2)}) collective-permute-start(bf16[3,320,128]{2,1,0:T(8,128)(2,1)S(1)} %shard_map.103.refs_1_), channel_id=1, source_target_pairs={{0,8},{4,12},{8,0},{12,4},{16,24},{20,28},{24,16},{28,20},{32,40},... | collective-permute-start | bytes 737288 | tf_op jit(solution)/shard_map/ppermute | solution.py:377
  65.0 6.1 %collective-permute-start.12 = (bf16[160,128]{1,0:T(8,128)(2,1)S(1)}, bf16[160,128]{1,0:T(8,128)(2,1)S(1)}, u32[]{:S(2)}, u32[]{:S(2)}) collective-permute-start(bf16[160,128]{1,0:T(8,128)(2,1)S(1)} %get-tuple-element.44), channel_id=1, source_target_pairs={{0,1},{1,2},{2,3},{3,0},{4,5},{5,6},{6,7},{7,4},{8,9},{9,10},{10,1... | collective-permute-start | bytes 122888 | tf_op jit(solution)/shard_map/ppermute | solution.py:374
  66.2 8.2 %collective-permute-start.13 = (bf16[160,128]{1,0:T(8,128)(2,1)S(1)}, bf16[160,128]{1,0:T(8,128)(2,1)S(1)}, u32[]{:S(2)}, u32[]{:S(2)}) collective-permute-start(bf16[160,128]{1,0:T(8,128)(2,1)S(1)} %get-tuple-element.45), channel_id=1, source_target_pairs={{0,2},{1,3},{2,0},{3,1},{4,6},{5,7},{6,4},{7,5},{8,10},{9,11},{10,... | collective-permute-start | bytes 122888 | tf_op jit(solution)/shard_map/ppermute | solution.py:374
  69.2 5.3 %collective-permute-start.14 = (bf16[160,128]{1,0:T(8,128)(2,1)S(1)}, bf16[160,128]{1,0:T(8,128)(2,1)S(1)}, u32[]{:S(2)}, u32[]{:S(2)}) collective-permute-start(bf16[160,128]{1,0:T(8,128)(2,1)S(1)} %get-tuple-element.46), channel_id=1, source_target_pairs={{0,3},{1,0},{2,1},{3,2},{4,7},{5,4},{6,5},{7,6},{8,11},{9,8},{10,9... | collective-permute-start | bytes 122888 | tf_op jit(solution)/shard_map/ppermute | solution.py:374
  71.7 12.5 %collective-permute-start.18 = (bf16[5,320,128]{2,1,0:T(8,128)(2,1)S(1)}, bf16[5,320,128]{2,1,0:T(8,128)(2,1)S(1)}, u32[]{:S(2)}, u32[]{:S(2)}) collective-permute-start(bf16[5,320,128]{2,1,0:T(8,128)(2,1)S(1)} %get-tuple-element.49.refs_1_), channel_id=1, source_target_pairs={{0,16},{4,20},{8,24},{12,28},{16,0},{20,4},{24,8},{28,12},{32,48},... | collective-permute-start | bytes 1228808 | tf_op jit(solution)/shard_map/ppermute | solution.py:377
  74.5 10.4 %collective-permute-start.15 = (bf16[160,128]{1,0:T(8,128)(2,1)S(1)}, bf16[160,128]{1,0:T(8,128)(2,1)S(1)}, u32[]{:S(2)}, u32[]{:S(2)}) collective-permute-start(bf16[160,128]{1,0:T(8,128)(2,1)S(1)} %shard_map.101.refs_0_.refs_2_), channel_id=1, source_target_pairs={{0,4},{4,0},{8,12},{12,8},{16,20},{20,16},{24,28},{28,24},{32,36},... | collective-permute-start | bytes 122888 | tf_op jit(solution)/shard_map/ppermute | solution.py:377
  74.6 10.3 %collective-permute-start.16 = (bf16[160,128]{1,0:T(8,128)(2,1)S(1)}, bf16[160,128]{1,0:T(8,128)(2,1)S(1)}, u32[]{:S(2)}, u32[]{:S(2)}) collective-permute-start(bf16[160,128]{1,0:T(8,128)(2,1)S(1)} %shard_map.101.refs_0_.refs_2_), channel_id=1, source_target_pairs={{4,8},{8,4},{12,16},{16,12},{20,24},{24,20},{28,32},{32,28},{36,40... | collective-permute-start | bytes 122888 | tf_op jit(solution)/shard_map/ppermute | solution.py:380
  84.8 6.7 %collective-permute-start.22 = (bf16[320,128]{1,0:T(8,128)(2,1)S(1)}, bf16[320,128]{1,0:T(8,128)(2,1)S(1)}, u32[]{:S(2)}, u32[]{:S(2)}) collective-permute-start(bf16[320,128]{1,0:T(8,128)(2,1)S(1)} %shard_map.105.refs_4_.refs_3_), channel_id=1, source_target_pairs={{0,4},{4,0},{8,12},{12,8},{16,20},{20,16},{24,28},{28,24},{32,36},... | collective-permute-start | bytes 245768 | tf_op jit(solution)/shard_map/ppermute | solution.py:377
  85.0 10.2 %collective-permute-start.19 = (bf16[3,160,128]{2,1,0:T(8,128)(2,1)S(1)}, bf16[3,160,128]{2,1,0:T(8,128)(2,1)S(1)}, u32[]{:S(2)}, u32[]{:S(2)}) collective-permute-start(bf16[3,160,128]{2,1,0:T(8,128)(2,1)S(1)} %shard_map.106.refs_5_.refs_7_.refs_1_), channel_id=1, source_target_pairs={{0,8},{4,12},{8,0},{12,4},{16,24},{20,28},{24,16},{28,20},{32,40},... | collective-permute-start | bytes 368648 | tf_op jit(solution)/shard_map/ppermute | solution.py:377
  85.1 10.3 %collective-permute-start.20 = (bf16[3,160,128]{2,1,0:T(8,128)(2,1)S(1)}, bf16[3,160,128]{2,1,0:T(8,128)(2,1)S(1)}, u32[]{:S(2)}, u32[]{:S(2)}) collective-permute-start(bf16[3,160,128]{2,1,0:T(8,128)(2,1)S(1)} %shard_map.106.refs_5_.refs_7_.refs_1_), channel_id=1, source_target_pairs={{0,16},{4,20},{8,24},{12,28},{16,0},{20,4},{24,8},{28,12},{32,48},... | collective-permute-start | bytes 368648 | tf_op jit(solution)/shard_map/ppermute | solution.py:377
  88.6 9.2 %collective-permute-start.21 = (bf16[3,160,128]{2,1,0:T(8,128)(2,1)S(1)}, bf16[3,160,128]{2,1,0:T(8,128)(2,1)S(1)}, u32[]{:S(2)}, u32[]{:S(2)}) collective-permute-start(bf16[3,160,128]{2,1,0:T(8,128)(2,1)S(1)} %shard_map.106.refs_5_.refs_7_.refs_1_), channel_id=1, source_target_pairs={{0,24},{4,28},{8,16},{12,20},{16,8},{20,12},{24,0},{28,4},{32,56},... | collective-permute-start | bytes 368648 | tf_op jit(solution)/shard_map/ppermute | solution.py:377
  99.6 42.4 %all-to-all-start.2 = ((bf16[4,2,64,640]{3,2,1,0:T(8,128)(2,1)}), bf16[4,2,64,640]{3,2,1,0:T(8,128)(2,1)}, u32[]{:S(2)}, u32[]{:S(2)}) async-start(bf16[4,2,64,640]{3,2,1,0:T(8,128)(2,1)} %shard_map.110), calls=%async_computation.2 | async-start | bytes 1310720 | tf_op jit(solution)/shard_map/all_to_all | solution.py:473
  105.0 23.6 %collective-permute-start.28 = (bf16[2,96,320]{2,1,0:T(8,128)(2,1)S(1)}, bf16[2,96,320]{2,1,0:T(8,128)(2,1)S(1)}, u32[]{:S(2)}, u32[]{:S(2)}) collective-permute-start(bf16[2,96,320]{2,1,0:T(8,128)(2,1)S(1)} %copy-done.12), channel_id=1, source_target_pairs={{0,32},{4,36},{8,40},{12,44},{16,48},{20,52},{24,56},{28,60},{32,6... | collective-permute-start | bytes 368648 | tf_op jit(solution)/shard_map/ppermute | solution.py:436
  107.1 24.2 %collective-permute-start.29 = (bf16[2,96,320]{2,1,0:T(8,128)(2,1)S(1)}, bf16[2,96,320]{2,1,0:T(8,128)(2,1)S(1)}, u32[]{:S(2)}, u32[]{:S(2)}) collective-permute-start(bf16[2,96,320]{2,1,0:T(8,128)(2,1)S(1)} %get-tuple-element.60), channel_id=1, source_target_pairs={{0,64},{4,68},{8,72},{12,76},{16,80},{20,84},{24,88},{28,92},{32,9... | collective-permute-start | bytes 368648 | tf_op jit(solution)/shard_map/ppermute | solution.py:436
  123.0 8.3 %collective-permute-start.30 = (bf16[2,96,320]{2,1,0:T(8,128)(2,1)S(1)}, bf16[2,96,320]{2,1,0:T(8,128)(2,1)S(1)}, u32[]{:S(2)}, u32[]{:S(2)}) collective-permute-start(bf16[2,96,320]{2,1,0:T(8,128)(2,1)S(1)} %get-tuple-element.61), channel_id=1, source_target_pairs={{0,96},{4,100},{8,104},{12,108},{16,112},{20,116},{24,120},{28,124... | collective-permute-start | bytes 368648 | tf_op jit(solution)/shard_map/ppermute | solution.py:436
  126.5 10.4 %collective-permute-start.24 = (bf16[2,96,160]{2,1,0:T(8,128)(2,1)S(1)}, bf16[2,96,160]{2,1,0:T(8,128)(2,1)S(1)}, u32[]{:S(2)}, u32[]{:S(2)}) collective-permute-start(bf16[2,96,160]{2,1,0:T(8,128)(2,1)S(1)} %get-tuple-element.54), channel_id=1, source_target_pairs={{0,32},{4,36},{8,40},{12,44},{16,48},{20,52},{24,56},{28,60},{32,6... | collective-permute-start | bytes 184328 | tf_op jit(solution)/shard_map/ppermute | solution.py:436
  128.6 8.3 %collective-permute-start.25 = (bf16[2,96,160]{2,1,0:T(8,128)(2,1)S(1)}, bf16[2,96,160]{2,1,0:T(8,128)(2,1)S(1)}, u32[]{:S(2)}, u32[]{:S(2)}) collective-permute-start(bf16[2,96,160]{2,1,0:T(8,128)(2,1)S(1)} %get-tuple-element.55), channel_id=1, source_target_pairs={{0,64},{4,68},{8,72},{12,76},{16,80},{20,84},{24,88},{28,92},{32,9... | collective-permute-start | bytes 184328 | tf_op jit(solution)/shard_map/ppermute | solution.py:436
  128.6 8.2 %collective-permute-start.26 = (bf16[2,96,160]{2,1,0:T(8,128)(2,1)S(1)}, bf16[2,96,160]{2,1,0:T(8,128)(2,1)S(1)}, u32[]{:S(2)}, u32[]{:S(2)}) collective-permute-start(bf16[2,96,160]{2,1,0:T(8,128)(2,1)S(1)} %get-tuple-element.56), channel_id=1, source_target_pairs={{0,96},{4,100},{8,104},{12,108},{16,112},{20,116},{24,120},{28,124... | collective-permute-start | bytes 184328 | tf_op jit(solution)/shard_map/ppermute | solution.py:436
  132.0 9.2 %collective-permute-start.31 = (bf16[96,320]{1,0:T(8,128)(2,1)S(1)}, bf16[96,320]{1,0:T(8,128)(2,1)S(1)}, u32[]{:S(2)}, u32[]{:S(2)}) collective-permute-start(bf16[96,320]{1,0:T(8,128)(2,1)S(1)} %get-tuple-element.63), channel_id=1, source_target_pairs={{0,128},{4,132},{8,136},{12,140},{16,144},{20,148},{24,152},{28,15... | collective-permute-start | bytes 184328 | tf_op jit(solution)/shard_map/ppermute | solution.py:377
  137.4 8.5 %collective-permute-start.27 = (bf16[96,160]{1,0:T(8,128)(2,1)S(1)}, bf16[96,160]{1,0:T(8,128)(2,1)S(1)}, u32[]{:S(2)}, u32[]{:S(2)}) collective-permute-start(bf16[96,160]{1,0:T(8,128)(2,1)S(1)} %get-tuple-element.58), channel_id=1, source_target_pairs={{0,128},{4,132},{8,136},{12,140},{16,144},{20,148},{24,152},{28,15... | collective-permute-start | bytes 92168 | tf_op jit(solution)/shard_map/ppermute | solution.py:377
  (17 other events, 65.5 us)
